TPU v7x, 32 devices: a whole 2x2x4 slice. The times are simulated.
32 devices in a mesh: rhs: 16 (over z, y, x), node: 2 (over core).
Axes of the slice: x: 2, y: 2, z: 4, core: 2. Of those that a mesh axis runs over, the one named last changes fastest.
Arguments:
- right_side: float32 [2048, 4096], P('node', 'rhs'), may hold values from -6 to 6
- diag_inv: float32 [8, 256, 256], P('node', 'rhs'), may hold values from -1 to 1
- lower: float32 [8, 256, 256], P('node', 'rhs'), may hold values from -0.4375 to 0.4375
- factor_pattern: int32 [8, 4, 4], P('node'), may hold values 0 or 1
- jacobian: float32 [8, 256, 768], P('node', 'rhs'), may hold values from -0.078125 to 0.078125
- jacobian_pattern: int32 [8, 4, 12], P('node'), may hold values 0 or 1
Outputs:
- solution: float32 [2048, 4096], P('node', 'rhs')
- residual: float32 [2048, 4096], P('node', 'rhs')
All inputs are finite; a program needn't handle non-finite values. No bound on the sum of `factor_pattern` or of `jacobian_pattern` on one device may be relied on, other than what follows from the above.
Results may differ from a plain program's by a relative error of at most 0.00021.
Values sent between devices are 32-bit elements; how exact they have to be, the bound alone decides.
No kernel may reach another device: no remote copies, remote signals or barrier semaphores. Data moves between devices by JAX's collectives and lax.ppermute only.
A program may use at most 64 MiB of HBM per device.

v0:
```python
import jax
import jax.numpy as jnp
from jax import lax
from jax.sharding import PartitionSpec as P

HIGHEST_PREC = lax.Precision.HIGHEST
TRANSPOSED = (((0,), (0,)), ((), ()))


def carried_in(value, axis, combine, identity, reverse):
    devices, position = (lax.axis_size(axis), lax.axis_index(axis))
    everything = jax.tree.map(lambda part: lax.all_gather(part, axis), value)
    start = jax.tree.map(
        lambda part, zero: jnp.broadcast_to(jnp.asarray(zero, part.dtype), part.shape),
        value,
        identity,
    )

    def step(k, before):
        at = devices - 1 - k if reverse else k
        reached = at > position if reverse else at < position
        new = combine(before, jax.tree.map(lambda part: part[at], everything))
        return jax.tree.map(lambda a, b: jnp.where(reached, a, b), new, before)

    return lax.fori_loop(0, devices, step, start)


def extended(cells, sides, width):
    for axis, dim in sides:
        count = lax.axis_size(axis)
        ends = count - 1
        head = lax.slice_in_dim(cells, 0, width, axis=dim)
        tail = lax.slice_in_dim(cells, cells.shape[dim] - width, cells.shape[dim], axis=dim)
        cells = jnp.concatenate(
            [
                lax.ppermute(tail, axis, [(i, (i + 1) % count) for i in range(ends)]),
                cells,
                lax.ppermute(head, axis, [((i + 1) % count, i) for i in range(ends)]),
            ],
            axis=dim,
        )
    return cells


def apply_pattern(blocks, pattern):
    supers, row_count, col_count = blocks.shape
    block_size = row_count // pattern.shape[1]
    shaped = blocks.reshape(supers, pattern.shape[1], block_size, pattern.shape[2], block_size)
    weights = pattern.astype(jnp.float32)[:, :, None, :, None]
    return (shaped * weights).reshape(supers, row_count, col_count)


def sweep_down(inverse, masked, rhs_blocks, incoming):

    def advance(previous, inputs):
        inv_block, low_block, rhs_block = inputs
        coupled = jnp.dot(low_block, previous, precision=HIGHEST_PREC)
        solved = jnp.dot(inv_block, rhs_block - coupled, precision=HIGHEST_PREC)
        return (solved, solved)

    outgoing, values = lax.scan(advance, incoming, (inverse, masked, rhs_blocks))
    return (values, outgoing)


def sweep_up(inverse, masked, forward_blocks, incoming):

    def advance(entering, inputs):
        inv_block, low_block, forward_block = inputs
        solved = lax.dot_general(
            inv_block, forward_block - entering, TRANSPOSED, precision=HIGHEST_PREC
        )
        passed = lax.dot_general(low_block, solved, TRANSPOSED, precision=HIGHEST_PREC)
        return (passed, solved)

    outgoing, values = lax.scan(advance, incoming, (inverse, masked, forward_blocks), reverse=True)
    return (values, outgoing)


def compose(earlier, latter):
    matrix_part = jnp.dot(latter[0], earlier[0], precision=HIGHEST_PREC)
    offset_part = latter[1] + jnp.dot(latter[0], earlier[1], precision=HIGHEST_PREC)
    return (matrix_part, offset_part)


def jacobian_product(portion, pattern, windows):
    supers, row_count, col_count = portion.shape
    block_count = pattern.shape[1]
    block_size = col_count // pattern.shape[2]
    row_ids = lax.iota(jnp.int32, row_count)
    onehot = (row_ids[:, None] // block_size == lax.iota(jnp.int32, block_count)[None, :]).astype(
        jnp.float32
    )
    weights = jnp.einsum("ra,sac->src", onehot, pattern.astype(jnp.float32))
    shaped = portion.reshape(supers, row_count, pattern.shape[2], block_size)
    masked = (shaped * weights[:, :, :, None]).reshape(supers, row_count, col_count)
    return jnp.einsum("sij,sjr->sir", masked, windows, precision=HIGHEST_PREC)


def on_device(right_side, diag_inv, lower, factor_pattern, jacobian, jacobian_pattern):
    supers = diag_inv.shape[0]
    panel_rows = diag_inv.shape[2]
    columns = right_side.shape[1]
    rhs_blocks = right_side.reshape(supers, panel_rows, columns)
    inverse, lower_all = (
        lax.all_gather(diag_inv, "rhs", axis=1, tiled=True),
        lax.all_gather(lower, "rhs", axis=1, tiled=True),
    )
    masked = apply_pattern(lower_all, factor_pattern)
    zero_state = jnp.zeros((panel_rows, columns), jnp.float32)
    unit_matrix = jnp.eye(panel_rows, dtype=jnp.float32)
    extra_zero = jnp.zeros((supers, panel_rows, panel_rows), jnp.float32)
    start_state = jnp.concatenate([zero_state, unit_matrix], axis=1)
    identity_pair = (unit_matrix, zero_state)
    values, outgoing = sweep_down(
        inverse, masked, jnp.concatenate([rhs_blocks, extra_zero], axis=2), start_state
    )
    entering = carried_in(
        (outgoing[:, columns:], outgoing[:, :columns]), "node", compose, identity_pair, False
    )
    forward = values[:, :, :columns] + jnp.einsum(
        "sij,jr->sir", values[:, :, columns:], entering[1], precision=HIGHEST_PREC
    )
    values, outgoing = sweep_up(
        inverse, masked, jnp.concatenate([forward, extra_zero], axis=2), start_state
    )
    entering = carried_in(
        (outgoing[:, columns:], outgoing[:, :columns]), "node", compose, identity_pair, True
    )
    solution = values[:, :, :columns] + jnp.einsum(
        "sij,jr->sir", values[:, :, columns:], entering[1], precision=HIGHEST_PREC
    )
    span = supers * panel_rows
    flattened = solution.reshape(span, columns)
    padded = extended(flattened, (("node", 0),), panel_rows)
    before = padded[:span].reshape(supers, panel_rows, columns)
    after = padded[2 * panel_rows :].reshape(supers, panel_rows, columns)
    windows = jnp.concatenate([before, solution, after], axis=1)
    product = jacobian_product(
        lax.all_gather(jacobian, "rhs", axis=1, tiled=True), jacobian_pattern, windows
    )
    residual = rhs_blocks - product
    return (flattened, residual.reshape(span, columns))


def solution(mesh):
    in_specs = (
        P("node", "rhs"),
        P("node", "rhs", None),
        P("node", "rhs", None),
        P("node", None, None),
        P("node", "rhs", None),
        P("node", None, None),
    )
    out_specs = (P("node", "rhs"), P("node", "rhs"))
    return jax.shard_map(
        on_device, mesh=mesh, in_specs=in_specs, out_specs=out_specs, check_vma=False
    )
```

profile of v0, /device:TPU:0, one launch (start us, length us, event | category | flops | bytes accessed | tf_op | source)
XLA Modules:
  0.0 215.2 jit_solution(17715827684277653077)
XLA Ops:
  8.7 1.7 copy.11
  11.2 1.7 mul.22
  12.9 2.6 %mul.23 = f32[4,256,256]{2,1,0:T(8,128)S(1)} reshape(f32[4,4,64,4,64]{4,3,2,1,0:T(4,128)} %mul.22) | data formatting | bytes 2097152 | tf_op jit(solution)/shard_map/mul | solution.py:50
  17.2 51.2 %all-gather.8.cloned.1.call-done = f32[4,256,256]{2,1,0:T(8,128)} async-done(((f32[4,16,256]{2,1,0:T(8,128)}), f32[4,256,256]{2,1,0:T(8,128)}) %all-gather.8.cloned.1.call-update) | async-done | bytes 1048592 | tf_op jit(solution)/shard_map/all_gather | solution.py:106
  69.9 55.3 %all-gather.10.cloned.1.call-done = f32[4,256,256]{2,1,0:T(8,128)} async-done(((f32[4,16,256]{2,1,0:T(8,128)}), f32[4,256,256]{2,1,0:T(8,128)}) %all-gather.10.cloned.1.call-update) | async-done | bytes 1048592 | tf_op jit(solution)/shard_map/all_gather | solution.py:105
  126.8 12.4 %while.58 = (s32[]{:T(128)}, f32[256,512]{1,0:T(8,128)S(1)}, f32[4,256,512]{2,1,0:T(8,128)}, f32[4,256,256]{2,1,0:T(8,128)S(1)}, f32[4,256,512]{2,1,0:T(8,128)}, /*index=5*/f32[4,256,256]{2,1,0:T(8,128)S(1)}, s32[]{:T(128)}) while((s32[]{:T(128)}, f32[256,512]{1,0:T(8,128)S(1)}, f32[4,256,512]{2,1,0:T(8,128)}, f32[4,256,256]{2,1,0:T(8,128)S(1)}, ...), condition=%wide.region_1.2_spmd, body=%wide.region_0.1_spmd.sunk | while | flops 805437440 | bytes 3672141 | solution.py:61
  139.3 2.2 %all-gather.1 = f32[512,256]{1,0:T(8,128)S(1)} all-gather(f32[256,256]{1,0:T(8,128)S(1)} %get-tuple-element.480), channel_id=3, replica_groups=mesh['rhs'=16,'node'=2] {'node'}, dimensions={0}, use_global_device_ids=true | all-gather | bytes 786432 | tf_op jit(solution)/shard_map/all_gather | solution.py:12
  141.5 2.3 %all-gather = f32[512,256]{1,0:T(8,128)} all-gather(f32[256,256]{1,0:T(8,128)S(1)} %get-tuple-element.481), channel_id=2, replica_groups=mesh['rhs'=16,'node'=2] {'node'}, dimensions={0}, use_global_device_ids=true | all-gather | bytes 786432 | tf_op jit(solution)/shard_map/all_gather | solution.py:12
  143.8 2.8 %while.60 = (s32[]{:T(128)}, f32[256,256]{1,0:T(8,128)S(1)}, s32[]{:T(128)}, f32[2,256,256]{2,1,0:T(8,128)}, f32[2,256,256]{2,1,0:T(8,128)S(1)}, /*index=5*/s32[]{:T(128)}, s32[]{:T(128)}) while((s32[]{:T(128)}, f32[256,256]{1,0:T(8,128)S(1)}, s32[]{:T(128)}, f32[2,256,256]{2,1,0:T(8,128)}, f32[2,256,256]{2,1,0:T(8,128)S(1)}, ...), condition=%wide.region_3.4_spmd.clone, body=%wide.region_2.3_spmd.clone.sunk | while | flops 201588736 | bytes 1837663 | solution.py:25
  146.6 2.5 %convolution_add_fusion.3 = f32[4,256,256]{2,1,0:T(8,128)S(1)} fusion(f32[4,256,512]{2,1,0:T(8,128)} %get-tuple-element.384, f32[256,256]{1,0:T(8,128)S(1)} %get-tuple-element.386), kind=kOutput, calls=%fused_computation.46 | convolution fusion | flops 805568512 | bytes 3407872 | tf_op jit(solution)/shard_map/sij,jr->sir/dot_general | solution.py:120
  152.4 12.7 %while.59 = (s32[]{:T(128)}, f32[256,512]{1,0:T(8,128)S(1)}, f32[4,256,512]{2,1,0:T(8,128)}, f32[4,256,256]{2,1,0:T(8,128)S(1)}, f32[4,256,256]{2,1,0:T(8,128)S(...) while((s32[]{:T(128)}, f32[256,512]{1,0:T(8,128)S(1)}, f32[4,256,512]{2,1,0:T(8,128)}, ...), condition=%wide.region_5.6_spmd, body=%wide.region_4.5_spmd.sunk | while | flops 805437440 | bytes 3671653 | solution.py:75
  152.4 2.5 %bitcast_dynamic-update-slice_fusion.5 = (f32[4,256,512]{2,1,0:T(8,128)}, f32[256,512]{1,0:T(8,128)S(1)}) fusion(f32[4,256,512]{2,1,0:T(8,128)} %get-tuple-element.678, s32[]{:T(128)S(6)} %sub.54, f32[256,512]{1,0:T(8,128)S(1)} %get-tuple-element.677, f32[4,256,512]{2,1,0:T(8,128)} %get-tuple-element.689, f32[4,256,256]{2,1,0:T(8,128)S(1)} %get-tuple-element.688), kind=kOutput, calls=%fused_computation.9.clone.1 | convolution fusion | flops 402784256 | bytes 2360832 | tf_op jit(solution)/shard_map/while/body/eval_jaxpr/dot_general | solution.py:69
  155.5 2.5 %bitcast_dynamic-update-slice_fusion.5 = (f32[4,256,512]{2,1,0:T(8,128)}, f32[256,512]{1,0:T(8,128)S(1)}) fusion(f32[4,256,512]{2,1,0:T(8,128)} %get-tuple-element.678, s32[]{:T(128)S(6)} %sub.54, f32[256,512]{1,0:T(8,128)S(1)} %get-tuple-element.677, f32[4,256,512]{2,1,0:T(8,128)} %get-tuple-element.689, f32[4,256,256]{2,1,0:T(8,128)S(1)} %get-tuple-element.688), kind=kOutput, calls=%fused_computation.9.clone.1 | convolution fusion | flops 402784256 | bytes 2360832 | tf_op jit(solution)/shard_map/while/body/eval_jaxpr/dot_general | solution.py:69
  158.7 2.5 %bitcast_dynamic-update-slice_fusion.5 = (f32[4,256,512]{2,1,0:T(8,128)}, f32[256,512]{1,0:T(8,128)S(1)}) fusion(f32[4,256,512]{2,1,0:T(8,128)} %get-tuple-element.678, s32[]{:T(128)S(6)} %sub.54, f32[256,512]{1,0:T(8,128)S(1)} %get-tuple-element.677, f32[4,256,512]{2,1,0:T(8,128)} %get-tuple-element.689, f32[4,256,256]{2,1,0:T(8,128)S(1)} %get-tuple-element.688), kind=kOutput, calls=%fused_computation.9.clone.1 | convolution fusion | flops 402784256 | bytes 2360832 | tf_op jit(solution)/shard_map/while/body/eval_jaxpr/dot_general | solution.py:69
  161.9 2.5 %bitcast_dynamic-update-slice_fusion.5 = (f32[4,256,512]{2,1,0:T(8,128)}, f32[256,512]{1,0:T(8,128)S(1)}) fusion(f32[4,256,512]{2,1,0:T(8,128)} %get-tuple-element.678, s32[]{:T(128)S(6)} %sub.54, f32[256,512]{1,0:T(8,128)S(1)} %get-tuple-element.677, f32[4,256,512]{2,1,0:T(8,128)} %get-tuple-element.689, f32[4,256,256]{2,1,0:T(8,128)S(1)} %get-tuple-element.688), kind=kOutput, calls=%fused_computation.9.clone.1 | convolution fusion | flops 402784256 | bytes 2360832 | tf_op jit(solution)/shard_map/while/body/eval_jaxpr/dot_general | solution.py:69
  165.1 2.2 %all-gather.2 = f32[512,256]{1,0:T(8,128)S(1)} all-gather(f32[256,256]{1,0:T(8,128)S(1)} %get-tuple-element.479), channel_id=4, replica_groups=mesh['rhs'=16,'node'=2] {'node'}, dimensions={0}, use_global_device_ids=true | all-gather | bytes 786432 | tf_op jit(solution)/shard_map/all_gather | solution.py:12
  167.3 2.2 %all-gather.3 = f32[512,256]{1,0:T(8,128)S(1)} all-gather(f32[256,256]{1,0:T(8,128)S(1)} %get-tuple-element.478), channel_id=5, replica_groups=mesh['rhs'=16,'node'=2] {'node'}, dimensions={0}, use_global_device_ids=true | all-gather | bytes 786432 | tf_op jit(solution)/shard_map/all_gather | solution.py:12
  170.3 2.5 %convolution_add_fusion.2 = f32[4,256,256]{2,1,0:T(8,128)S(1)} fusion(f32[4,256,512]{2,1,0:T(8,128)} %get-tuple-element.387, f32[256,256]{1,0:T(8,128)S(1)} %get-tuple-element.389), kind=kOutput, calls=%fused_computation.45 | convolution fusion | flops 805568512 | bytes 3407872 | tf_op jit(solution)/shard_map/sij,jr->sir/dot_general | solution.py:129
  172.9 2.1 collective-permute-start
  176.8 1.7 collective-permute-done.1
  178.7 16.5 %all-gather.12.cloned.1.call-done = f32[4,256,768]{2,0,1:T(4,128)} async-done(((f32[4,16,768]{2,0,1:T(4,128)}), f32[4,256,768]{2,0,1:T(4,128)}) %all-gather.12.cloned.1.call-update) | async-done | bytes 3145744 | tf_op jit(solution)/shard_map/all_gather | solution.py:139
  195.2 4.9 %copy.12 = f32[4,256,768]{1,2,0:T(8,128)} copy(f32[4,256,768]{2,0,1:T(4,128)} %all-gather.12.cloned.1.call-done) | data formatting | bytes 6291456 | tf_op jit(solution)/shard_map/all_gather | solution.py:139
  200.1 2.2 %bitcast_multiply_fusion = f32[4,256,768]{1,2,0:T(8,128)S(1)} fusion(f32[4,256,768]{1,2,0:T(8,128)} %copy.12, f32[4,256,12]{1,2,0:T(8,128)S(1)} %convolution_bitcast_fusion), kind=kLoop, calls=%fused_computation.44 | loop fusion | flops 786432 | bytes 6340608 | tf_op jit(solution)/shard_map/mul | solution.py:95
  202.3 6.4 %fusion.38 = f32[4,256,256]{2,1,0:T(8,128)} fusion(f32[4,256,256]{2,1,0:T(8,128)S(1)} %bitcast.106, f32[4,256,768]{1,2,0:T(8,128)S(1)} %bitcast_multiply_fusion, f32[4,256,256]{2,1,0:T(8,128)S(1)} %bitcast.104, f32[4,256,256]{2,1,0:T(8,128)S(1)} %convolution_add_fusion.2, f32[4,256,256]{2,1,0:T(8,128)S(1)} %bitcast.103), kind=kOutput, calls=%fused_computation.47 | convolution fusion | flops 2417754112 | bytes 8388608 | tf_op jit(solution)/shard_map/sij,sjr->sir/dot_general | solution.py:96
  (61 shorter events, 31.6 us)
Async XLA Ops:
  7.2 61.3 %all-gather.8.cloned.1.call-start = ((), (), s32[]{:S(2)}) async-start(), calls=%async_computation | async-start | bytes 1114112 | tf_op jit(solution)/shard_map/all_gather | solution.py:106
  7.9 117.3 %all-gather.10.cloned.1.call-start = ((), (), s32[]{:S(2)}) async-start(), calls=%async_computation.1 | async-start | bytes 1114112 | tf_op jit(solution)/shard_map/all_gather | solution.py:105
  8.6 186.5 %all-gather.12.cloned.1.call-start = ((), (), s32[]{:S(2)}) async-start(), calls=%async_computation.2 | async-start | bytes 3342336 | tf_op jit(solution)/shard_map/all_gather | solution.py:139
  12.9 2.6 %copy-start.5 = (f32[1024,256]{1,0:T(8,128)S(1)}, f32[1024,256]{1,0:T(8,128)}, u32[]{:S(2)}) copy-start(f32[1024,256]{1,0:T(8,128)} %param.14) | copy-start | bytes 3145732
  15.6 1.7 copy-start
  68.4 58.4 %copy-start.2 = (f32[256,512]{1,0:T(8,128)S(1)}, f32[256,512]{1,0:T(8,128)}, u32[]{:S(2)}) copy-start(f32[256,512]{1,0:T(8,128)} %copy-done) | copy-start | bytes 1572868
  125.2 1.6 copy-start.4
  149.1 3.3 %copy-start.1 = (f32[256,512]{1,0:T(8,128)S(1)}, f32[256,512]{1,0:T(8,128)}, u32[]{:S(2)}) copy-start(f32[256,512]{1,0:T(8,128)} %copy-done) | copy-start | bytes 1572868
  170.3 6.2 %copy-start.7 = (s32[4,4,12]{2,1,0:T(4,128)S(1)}, s32[4,4,12]{2,1,0:T(4,128)}, u32[]{:S(2)}) copy-start(s32[4,4,12]{2,1,0:T(4,128)} %param.19) | copy-start | bytes 2308
  172.9 29.4 %copy-start.3 = (f32[4,256,256]{2,1,0:T(8,128)}, f32[4,256,256]{2,1,0:T(8,128)S(1)}, u32[]{:S(2)}) copy-start(f32[4,256,256]{2,1,0:T(8,128)S(1)} %convolution_add_fusion.2) | copy-start | bytes 3145732
  172.9 3.8 %collective-permute-start = (f32[256,256]{1,0:T(8,128)S(1)}, f32[256,256]{1,0:T(8,128)S(1)}, u32[]{:S(2)}, u32[]{:S(2)}) collective-permute-start(f32[256,256]{1,0:T(8,128)S(1)} %get-tuple-element.476), channel_id=1, source_target_pairs={{0,1},{2,3},{4,5},{6,7},{8,9},{10,11},{12,13},{14,15},{16,17},{18,... | collective-permute-start | bytes 786440 | tf_op jit(solution)/shard_map/ppermute | solution.py:36
  175.1 3.4 %collective-permute-start.1 = (f32[256,256]{1,0:T(8,128)S(1)}, f32[256,256]{1,0:T(8,128)S(1)}, u32[]{:S(2)}, u32[]{:S(2)}) collective-permute-start(f32[256,256]{1,0:T(8,128)S(1)} %get-tuple-element.477), channel_id=1, source_target_pairs={{1,0},{3,2},{5,4},{7,6},{9,8},{11,10},{13,12},{15,14},{17,16},{19,... | collective-permute-start | bytes 786440 | tf_op jit(solution)/shard_map/ppermute | solution.py:38
  200.1 2.2 %copy-start.6 = (f32[1024,256]{1,0:T(8,128)S(1)}, f32[1024,256]{1,0:T(8,128)}, u32[]{:S(2)}) copy-start(f32[1024,256]{1,0:T(8,128)} %param.14) | copy-start | bytes 3145732
Sparse Core Ops, SparseCore 0:
  10.7 57.6 all-gather.7
  71.2 53.9 all-gather.9
  128.0 67.1 all-gather.11
where the time goes:
time: 216 us; the launch traced here: 215 us
  waiting for transfers between devices  126 us (58%)
  matrix products  40.1 us (19%)
  local copies, waits for them, and re-layouts  17.6 us (8%)
  between operations  14 us (6%)
  blocking collectives  8.83 us (4%)
  other arithmetic  4.61 us (2%)
  starting transfers between devices  3.7 us (2%)
    all_gather x1, waiting for transfers between devices, on_device(): lax.all_gather(diag_inv, 'rhs', axis=1, tiled=True)  55.3 us
    all_gather x1, waiting for transfers between devices, on_device(): lax.all_gather(lower, 'rhs', axis=1, tiled=True)  51.2 us
    all_gather x1, waiting for transfers between devices, on_device(): lax.all_gather(jacobian, 'rhs', axis=1, tiled=True)  16.5 us
    dot_general x4, matrix products, advance(): lax.dot_general(inv_block, forward_block - entering, TRANSPOSED, precisio...  10 us
    all_gather x4, blocking collectives, carried_in(): everything = jax.tree.map(lambda part: lax.all_gather(part, axis), value)  8.83 us
    dot_general x4, matrix products, advance(): coupled = jnp.dot(low_block, previous, precision=HIGHEST_PREC)  6.63 us
    dot_general x1, matrix products, jacobian_product(): return jnp.einsum('sij,sjr->sir', masked, windows, precision=HIGHEST_PREC)  6.38 us
    dot_general x4, matrix products, advance(): solved = jnp.dot(inv_block, rhs_block - coupled, precision=HIGHEST_PREC)  5.76 us
  transfers between devices with their start and end apart: 5, of which 4 were waited for; matrix products, arithmetic and copies ran while one was open for 23% of the time, Pallas kernels for 0%

commit v1 on v0

v1 whole, which is shorter than its diff:
```python
import functools

import jax
import jax.numpy as jnp
from jax import lax
from jax.experimental import pallas as pl
from jax.experimental.pallas import tpu as pltpu
from jax.sharding import PartitionSpec as P

VMEM = pl.BlockSpec(memory_space=pltpu.VMEM)
SMEM = pl.BlockSpec(memory_space=pltpu.SMEM)
ANY = pl.BlockSpec(memory_space=pl.ANY)
VMEM_LIMIT = 48 * 2**20
PLAIN = (((1,), (0,)), ((), ()))


def split(value):
    high = value.astype(jnp.bfloat16)
    return high, (value - high.astype(jnp.float32)).astype(jnp.bfloat16)


def product(left, right, dims=PLAIN):
    dot = functools.partial(lax.dot_general, dimension_numbers=dims, preferred_element_type=jnp.float32)
    return dot(left[0], right[1]) + dot(left[1], right[0]) + dot(left[0], right[0])


def gather_rows(part, axis):
    count = lax.axis_size(axis)
    parts = part.shape[0]
    half = parts // 2
    if count < 4 or count & (count - 1):
        everything = lax.all_gather(part, axis, axis=1)
        return [(everything, 0, [(place, place) for place in range(count)])], False

    def across(value, mask):
        return lax.ppermute(value, axis, [(i, i ^ mask) for i in range(count)])

    lines = [0] + [high << 2 for high in range(1, count >> 2)]
    own = jnp.stack([part] + [across(part, mask) for mask in lines[1:]], axis=1)
    first, second = across(own, 1), across(own, 2)
    third = [across(first[:half], 2), across(second[half:], 1)]

    def slots(low):
        return [(place, mask | low) for place, mask in enumerate(lines)]

    return [
        (own, 0, slots(0)),
        (first, 0, slots(1)),
        (second, 0, slots(2)),
        (third[0], 0, slots(3)),
        (third[1], half, slots(3)),
    ], True


def place_rows(pieces, refs, relative, axis, panels, sem):
    me = lax.axis_index(axis)
    rows = pieces[0][0].shape[2]
    copies = []
    for (array, start, slots), ref in zip(pieces, refs):
        for place, mask in slots:
            owner = me ^ mask if relative else mask
            at = pl.multiple_of(owner * rows, rows) if relative else owner * rows
            copies.append(
                pltpu.make_async_copy(
                    ref.at[:, place],
                    panels.at[pl.ds(start, array.shape[0]), pl.ds(at, rows), :],
                    sem.at[len(copies)],
                )
            )
    for copy in copies:
        copy.start()
    return copies


def shapes(arrays):
    return [jax.ShapeDtypeStruct(shape, jnp.float32) for shape in arrays]


def solve(pieces, relative, right_side, weights, node, nodes, supers, size):
    columns = right_side.shape[1]
    extra = 0 if nodes == 1 else 1 if nodes == 2 else 2
    width = columns + extra * size
    n = len(pieces)
    n_copies = sum(len(slots) for _, _, slots in pieces)

    def kernel(*refs):
        node_ref, weights_ref, rhs_ref = refs[:3]
        piece_refs = refs[3 : 3 + n]
        sol_ref = refs[3 + n]
        extra_refs = refs[4 + n : 4 + n + extra]
        down_ref, up_ref, panels, forward, sem = refs[4 + n + extra :]
        copies = place_rows(pieces, piece_refs, relative, "rhs", panels, sem)
        index = node_ref[0]
        below = jnp.where(index > 0, 1.0, 0.0)
        above = jnp.where(index < nodes - 1, 1.0, 0.0)
        on_diagonal = lax.broadcasted_iota(jnp.int32, (size, size), 0) == lax.broadcasted_iota(
            jnp.int32, (size, size), 1
        )
        zeros = jnp.zeros((size, size), jnp.float32)
        for copy in copies:
            copy.wait()

        def masked(s):
            tall = panels[supers + s]
            blocks = weights_ref.shape[1]
            step = size // blocks
            return jnp.concatenate(
                [tall[a * step : (a + 1) * step] * weights_ref[s, a : a + 1, :] for a in range(blocks)], axis=0
            )

        previous = None
        for s in range(supers):
            own = rhs_ref[s * size : (s + 1) * size, :]
            low = masked(s)
            panels[supers + s] = low
            if s == 0:
                parts = [own]
                if extra:
                    parts.append(low * -below)
                if extra == 2:
                    parts.append(zeros)
                target = jnp.concatenate(parts, axis=1)
            else:
                target = jnp.concatenate([own] + [zeros] * extra, axis=1) - product(split(low), split(previous))
            previous = product(split(panels[s]), split(target))
            forward[s] = previous
        down_ref[...] = previous

        entering = None
        for s in reversed(range(supers)):
            target = forward[s]
            if s == supers - 1:
                if extra:
                    unit = jnp.where(on_diagonal, above, 0.0)
                    shift = [jnp.zeros((size, columns), jnp.float32)] + [zeros] * (extra - 1) + [unit]
                    target = target - jnp.concatenate(shift, axis=1)
            else:
                target = target - entering
            solved = product(split(panels[s].T), split(target))
            sol_ref[s * size : (s + 1) * size, :] = solved[:, :columns]
            for e, ref in enumerate(extra_refs):
                ref[s * size : (s + 1) * size, :] = solved[:, columns + e * size : columns + (e + 1) * size]
            if s > 0 or nodes > 1:
                entering = product(split(panels[supers + s].T), split(solved))
        up_ref[...] = entering if nodes > 1 else previous

    span = supers * size
    out = pl.pallas_call(
        kernel,
        out_shape=shapes([(span, columns)] + [(span, size)] * extra + [(size, width)] * 2),
        in_specs=[SMEM, VMEM, VMEM] + [ANY] * n,
        out_specs=[VMEM] * (3 + extra),
        scratch_shapes=[
            pltpu.VMEM((2 * supers, size, size), jnp.float32),
            pltpu.VMEM((supers, size, width), jnp.float32),
            pltpu.SemaphoreType.DMA((n_copies,)),
        ],
        compiler_params=pltpu.CompilerParams(vmem_limit_bytes=VMEM_LIMIT),
        cost_estimate=pl.CostEstimate(
            flops=6 * 4 * supers * size * size * width, bytes_accessed=16 * span * size, transcendentals=0
        ),
        name="solve",
    )(node, weights, right_side, *[array for array, _, _ in pieces])
    return out[0], out[1 : 1 + extra], out[1 + extra], out[2 + extra]


def finish(sol, part, own_mail, mail, node, size):
    span, columns = sol.shape

    def kernel(node_ref, sol_ref, part_ref, own_ref, mail_ref, out_ref, before_ref, after_ref):
        lower_one = node_ref[0] == 0
        down = jnp.where(lower_one, own_ref[0], mail_ref[0])
        offset = jnp.where(lower_one, mail_ref[0], own_ref[0])
        matrix = jnp.where(lower_one, mail_ref[1], own_ref[1])
        up = offset + product(split(matrix), split(down))
        mine = split(jnp.where(lower_one, up, down))
        other = split(jnp.where(lower_one, down, up))
        for at in range(0, span, size):
            out_ref[at : at + size, :] = sol_ref[at : at + size, :] + product(
                split(part_ref[at : at + size, :]), mine
            )
        beside = mail_ref[2] + product(split(mail_ref[3]), other)
        before_ref[...] = jnp.where(lower_one, 0.0, beside)
        after_ref[...] = jnp.where(lower_one, beside, 0.0)

    return pl.pallas_call(
        kernel,
        out_shape=shapes([(span, columns), (size, columns), (size, columns)]),
        in_specs=[SMEM] + [VMEM] * 4,
        out_specs=[VMEM] * 3,
        compiler_params=pltpu.CompilerParams(vmem_limit_bytes=VMEM_LIMIT),
        cost_estimate=pl.CostEstimate(
            flops=6 * (span + 2 * size) * size * columns, bytes_accessed=20 * span * columns, transcendentals=0
        ),
        name="finish",
    )(node, sol, part, own_mail, mail)


def subtract_product(pieces, relative, right_side, sol, before, after, weights, supers, size):
    span, columns = sol.shape
    wide = weights.shape[2]
    blocks = weights.shape[1]
    step = size // blocks
    n = len(pieces)
    n_copies = sum(len(slots) for _, _, slots in pieces)

    def kernel(*refs):
        weights_ref, rhs_ref, sol_ref, before_ref, after_ref = refs[:5]
        piece_refs = refs[5 : 5 + n]
        out_ref, panels, high, low, sem = refs[5 + n :]
        copies = place_rows(pieces, piece_refs, relative, "rhs", panels, sem)
        for at, value in (
            (0, before_ref[...]),
            (size + span, after_ref[...]),
            *((size + s * size, sol_ref[s * size : (s + 1) * size, :]) for s in range(supers)),
        ):
            high[at : at + size, :], low[at : at + size, :] = split(value)
        for copy in copies:
            copy.wait()
        for s in range(supers):
            rows = panels[s]
            panel = jnp.concatenate(
                [rows[a * step : (a + 1) * step] * weights_ref[s, a : a + 1, :] for a in range(blocks)], axis=0
            )
            window = pl.ds(s * size, wide)
            out_ref[s * size : (s + 1) * size, :] = rhs_ref[s * size : (s + 1) * size, :] - product(
                split(panel), (high[window, :], low[window, :])
            )

    return pl.pallas_call(
        kernel,
        out_shape=shapes([(span, columns)])[0],
        in_specs=[VMEM] * 5 + [ANY] * n,
        out_specs=VMEM,
        scratch_shapes=[
            pltpu.VMEM((supers, size, wide), jnp.float32),
            pltpu.VMEM((span + 2 * size, columns), jnp.bfloat16),
            pltpu.VMEM((span + 2 * size, columns), jnp.bfloat16),
            pltpu.SemaphoreType.DMA((n_copies,)),
        ],
        compiler_params=pltpu.CompilerParams(vmem_limit_bytes=VMEM_LIMIT),
        cost_estimate=pl.CostEstimate(
            flops=6 * span * wide * columns, bytes_accessed=4 * span * (wide + 3 * columns), transcendentals=0
        ),
        name="residual",
    )(weights, right_side, sol, before, after, *[array for array, _, _ in pieces])


def dot(left, right):
    return jnp.dot(left, right, precision=lax.Precision.HIGHEST)


def on_device(right_side, diag_inv, lower, factor_pattern, jacobian, jacobian_pattern):
    supers, rows, size = diag_inv.shape
    columns = right_side.shape[1]
    span = supers * size
    nodes = lax.axis_size("node")
    node = jnp.reshape(lax.axis_index("node").astype(jnp.int32), (1,))

    def widened(pattern):
        return jnp.repeat(pattern.astype(jnp.float32), size // factor_pattern.shape[2], axis=2)

    factor, relative = gather_rows(jnp.concatenate([diag_inv, lower], axis=0), "rhs")
    jacobians, _ = gather_rows(jacobian, "rhs")

    sol, parts, down, up = solve(
        factor, relative, right_side, widened(factor_pattern), node, nodes, supers, size
    )
    empty = jnp.zeros((size, columns), jnp.float32)
    if nodes == 1:
        before, after = empty, empty
    elif nodes == 2:
        last, first = slice(span - size, span), slice(0, size)
        is_lower = lax.axis_index("node") == 0
        own_mail = jnp.where(
            is_lower,
            jnp.stack([down[:, :columns], down[:, columns:], sol[last], parts[0][last]]),
            jnp.stack([up[:, :columns], up[:, columns:], sol[first], parts[0][first]]),
        )
        mail = lax.ppermute(own_mail, "node", [(0, 1), (1, 0)])
        sol, before, after = finish(sol, parts[0], own_mail, mail, node, size)
    else:
        upwards = [(i, i + 1) for i in range(nodes - 1)]
        downwards = [(i + 1, i) for i in range(nodes - 1)]
        below = above = empty
        for _ in range(nodes - 1):
            below = lax.ppermute(
                down[:, :columns] + dot(down[:, columns : columns + size], below), "node", upwards
            )
        for _ in range(nodes - 1):
            leaving = up[:, :columns] + dot(up[:, columns : columns + size], below)
            above = lax.ppermute(leaving + dot(up[:, columns + size :], above), "node", downwards)
        sol = sol + dot(parts[0], below) + dot(parts[1], above)
        before = lax.ppermute(sol[span - size :], "node", upwards)
        after = lax.ppermute(sol[:size], "node", downwards)
    residual = subtract_product(
        jacobians, relative, right_side, sol, before, after, widened(jacobian_pattern), supers, size
    )
    return sol, residual


def solution(mesh):
    in_specs = (
        P("node", "rhs"),
        P("node", "rhs", None),
        P("node", "rhs", None),
        P("node", None, None),
        P("node", "rhs", None),
        P("node", None, None),
    )
    out_specs = (P("node", "rhs"), P("node", "rhs"))
    return jax.shard_map(on_device, mesh=mesh, in_specs=in_specs, out_specs=out_specs, check_vma=False)
```

time: 216 us -> 76 us (0.35)
  the two profiles are of different devices: /device:TPU:0 before, /device:TPU:16 now
where the time goes in v1:
time: 76 us; the launch traced here: 75.5 us
  waiting for transfers between devices  31.1 us (41%)
  starting transfers between devices  16.2 us (21%)
  Pallas kernels  15.1 us (20%)
  local copies, waits for them, and re-layouts  10.8 us (14%)
  other arithmetic  1.46 us (2%)
  between operations  0.8 us (1%)
    ppermute x14, waiting for transfers between devices, across(): return lax.ppermute(value, axis, [(i, i ^ mask) for i in range(count)])  31.1 us
    ppermute x14, starting transfers between devices, across(): return lax.ppermute(value, axis, [(i, i ^ mask) for i in range(count)])  16.1 us
    unnamed x37, local copies, waits for them, and re-layouts  8.56 us
    pallas_call x1, Pallas kernels, solve(): pl.pallas_call(kernel, out_shape=shapes([(span, columns)] + [(span, size)...  7.24 us
    pallas_call x1, Pallas kernels, subtract_product(): pl.pallas_call(kernel, out_shape=shapes([(span, columns)])[0], in_specs=[...  4.63 us
    pallas_call x1, Pallas kernels, finish(): pl.pallas_call(kernel, out_shape=shapes([(span, columns), (size, columns)...  3.27 us
    slice x4, local copies, waits for them, and re-layouts, gather_rows(): third = [across(first[:half], 2), across(second[half:], 1)]  1.69 us
  transfers between devices with their start and end apart: 15, of which 9 were waited for; matrix products, arithmetic and copies ran while one was open for 5% of the time, Pallas kernels for 14%

profile of v1, /device:TPU:16, one launch (start us, length us, event | category | flops | bytes accessed | tf_op | source)
XLA Modules:
  0.0 75.5 jit_solution(1006477934748075698)
XLA Ops:
  1.5 1.6 %collective-permute-start = (f32[8,16,256]{2,1,0:T(8,128)S(1)}, f32[8,16,256]{2,1,0:T(8,128)S(1)}, u32[]{:S(2)}, u32[]{:S(2)}) collective-permute-start(f32[8,16,256]{2,1,0:T(8,128)S(1)} %constant_dynamic-update-slice_fusion), channel_id=1, source_target_pairs={{0,8},{2,10},{4,12},{6,14},{8,0},{10,2},{12,4},{14,6},{16,24},{18,... | collective-permute-start | bytes 393224 | tf_op jit(solution)/shard_map/ppermute | solution.py:36
  3.5 1.6 %collective-permute-start.2 = (f32[8,16,256]{2,1,0:T(8,128)S(1)}, f32[8,16,256]{2,1,0:T(8,128)S(1)}, u32[]{:S(2)}, u32[]{:S(2)}) collective-permute-start(f32[8,16,256]{2,1,0:T(8,128)S(1)} %constant_dynamic-update-slice_fusion), channel_id=1, source_target_pairs={{0,24},{2,26},{4,28},{6,30},{8,16},{10,18},{12,20},{14,22},{16,8},... | collective-permute-start | bytes 393224 | tf_op jit(solution)/shard_map/ppermute | solution.py:36
  5.1 2.9 %collective-permute-done = f32[8,16,256]{2,1,0:T(8,128)S(1)} collective-permute-done((f32[8,16,256]{2,1,0:T(8,128)S(1)}, f32[8,16,256]{2,1,0:T(8,128)S(1)}, u32[]{:S(2)}, u32[]{:S(2)}) %collective-permute-start) | collective-permute-done | bytes 131104 | tf_op jit(solution)/shard_map/ppermute | solution.py:36
  8.0 5.1 %collective-permute-done.1 = f32[8,16,256]{2,1,0:T(8,128)S(1)} collective-permute-done((f32[8,16,256]{2,1,0:T(8,128)S(1)}, f32[8,16,256]{2,1,0:T(8,128)S(1)}, u32[]{:S(2)}, u32[]{:S(2)}) %collective-permute-start.1) | collective-permute-done | bytes 131104 | tf_op jit(solution)/shard_map/ppermute | solution.py:36
  13.1 3.4 %collective-permute-done.2 = f32[8,16,256]{2,1,0:T(8,128)S(1)} collective-permute-done((f32[8,16,256]{2,1,0:T(8,128)S(1)}, f32[8,16,256]{2,1,0:T(8,128)S(1)}, u32[]{:S(2)}, u32[]{:S(2)}) %collective-permute-start.2) | collective-permute-done | bytes 131104 | tf_op jit(solution)/shard_map/ppermute | solution.py:36
  16.5 1.6 %collective-permute-start.3 = (f32[8,4,16,256]{3,2,1,0:T(8,128)S(1)}, f32[8,4,16,256]{3,2,1,0:T(8,128)S(1)}, u32[]{:S(2)}, u32[]{:S(2)}) collective-permute-start(f32[8,4,16,256]{3,2,1,0:T(8,128)S(1)} %pad_maximum_fusion.1.refs_3_), channel_id=1, source_target_pairs={{0,2},{2,0},{4,6},{6,4},{8,10},{10,8},{12,14},{14,12},{16,18},{18,... | collective-permute-start | bytes 1572872 | tf_op jit(solution)/shard_map/ppermute | solution.py:36
  18.1 1.5 %collective-permute-start.4 = (f32[8,4,16,256]{3,2,1,0:T(8,128)S(1)}, f32[8,4,16,256]{3,2,1,0:T(8,128)S(1)}, u32[]{:S(2)}, u32[]{:S(2)}) collective-permute-start(f32[8,4,16,256]{3,2,1,0:T(8,128)S(1)} %pad_maximum_fusion.1.refs_3_), channel_id=1, source_target_pairs={{0,4},{2,6},{4,0},{6,2},{8,12},{10,14},{12,8},{14,10},{16,20},{18,... | collective-permute-start | bytes 1572872 | tf_op jit(solution)/shard_map/ppermute | solution.py:36
  19.6 1.9 %collective-permute-start.9 = (f32[4,16,768]{2,1,0:T(8,128)S(1)}, f32[4,16,768]{2,1,0:T(8,128)}, u32[]{:S(2)}, u32[]{:S(2)}) collective-permute-start(f32[4,16,768]{2,1,0:T(8,128)S(1)} %copy-done.14), channel_id=1, source_target_pairs={{0,16},{2,18},{4,20},{6,22},{8,24},{10,26},{12,28},{14,30},{16,0},... | collective-permute-start | bytes 589832 | tf_op jit(solution)/shard_map/ppermute | solution.py:36
  21.5 1.6 %collective-permute-start.10 = (f32[4,16,768]{2,1,0:T(8,128)S(1)}, f32[4,16,768]{2,1,0:T(8,128)}, u32[]{:S(2)}, u32[]{:S(2)}) collective-permute-start(f32[4,16,768]{2,1,0:T(8,128)S(1)} %copy-done.14), channel_id=1, source_target_pairs={{0,24},{2,26},{4,28},{6,30},{8,16},{10,18},{12,20},{14,22},{16,8},... | collective-permute-start | bytes 589832 | tf_op jit(solution)/shard_map/ppermute | solution.py:36
  23.1 6.2 %collective-permute-done.3.refs_4_ = f32[8,4,16,256]{3,2,1,0:T(8,128)S(1)} collective-permute-done((f32[8,4,16,256]{3,2,1,0:T(8,128)S(1)}, f32[8,4,16,256]{3,2,1,0:T(8,128)S(1)}, u32[]{:S(2)}, u32[]{:S(2)}) %collective-permute-start.3) | collective-permute-done | bytes 524320 | tf_op jit(solution)/shard_map/ppermute | solution.py:36
  29.3 1.6 %collective-permute-start.5 = (f32[4,4,16,256]{3,2,1,0:T(8,128)S(1)}, f32[4,4,16,256]{3,2,1,0:T(8,128)S(1)}, u32[]{:S(2)}, u32[]{:S(2)}) collective-permute-start(f32[4,4,16,256]{3,2,1,0:T(8,128)S(1)} %slice.48), channel_id=1, source_target_pairs={{0,4},{2,6},{4,0},{6,2},{8,12},{10,14},{12,8},{14,10},{16,20},{18,... | collective-permute-start | bytes 786440 | tf_op jit(solution)/shard_map/ppermute | solution.py:36
  30.9 1.6 %collective-permute-start.6 = (f32[4,4,16,256]{3,2,1,0:T(8,128)S(1)}, f32[4,4,16,256]{3,2,1,0:T(8,128)S(1)}, u32[]{:S(2)}, u32[]{:S(2)}) collective-permute-start(f32[4,4,16,256]{3,2,1,0:T(8,128)S(1)} %slice.49), channel_id=1, source_target_pairs={{0,2},{2,0},{4,6},{6,4},{8,10},{10,8},{12,14},{14,12},{16,18},{18,... | collective-permute-start | bytes 786440 | tf_op jit(solution)/shard_map/ppermute | solution.py:36
  32.7 1.3 %collective-permute-done.9 = f32[4,16,768]{2,1,0:T(8,128)} collective-permute-done((f32[4,16,768]{2,1,0:T(8,128)S(1)}, f32[4,16,768]{2,1,0:T(8,128)}, u32[]{:S(2)}, u32[]{:S(2)}) %collective-permute-start.9) | collective-permute-done | bytes 196640 | tf_op jit(solution)/shard_map/ppermute | solution.py:36
  33.9 4.7 %collective-permute-done.10 = f32[4,16,768]{2,1,0:T(8,128)} collective-permute-done((f32[4,16,768]{2,1,0:T(8,128)S(1)}, f32[4,16,768]{2,1,0:T(8,128)}, u32[]{:S(2)}, u32[]{:S(2)}) %collective-permute-start.10) | collective-permute-done | bytes 196640 | tf_op jit(solution)/shard_map/ppermute | solution.py:36
  38.7 1.3 %pad_maximum_fusion.refs_5_ = f32[4,4,16,768]{3,2,1,0:T(8,128)S(1)} fusion(f32[4,1,16,768]{3,2,1,0:T(8,128)} %bitcast.19, f32[4,1,16,768]{3,2,1,0:T(8,128)} %bitcast.18, f32[4,1,16,768]{3,2,1,0:T(8,128)} %bitcast.17, f32[4,1,16,768]{3,2,1,0:T(8,128)} %bitcast.32), kind=kLoop, calls=%fused_computation.1 | loop fusion | flops 589824 | bytes 1572864 | tf_op jit(solution)/shard_map/stack | solution.py:39
  42.8 1.0 %copy-done.9 = f32[8,4,16,256]{3,2,1,0:T(8,128)S(1)} copy-done((f32[8,4,16,256]{3,2,1,0:T(8,128)S(1)}, f32[8,4,16,256]{3,2,1,0:T(8,128)}, u32[]{:S(2)}) %copy-start.9) | copy-done | bytes 524312
  45.7 7.2 %solve.1 = (f32[1024,256]{1,0:T(8,128)S(1)}, f32[1024,256]{1,0:T(8,128)S(1)}, f32[256,512]{1,0:T(8,128)S(1)}, f32[256,512]{1,0:T(8,128)S(1)}) custom-call(s32[1]{0:T(128)} %bitcast.refs_0_.node_ref, f32[4,4,256]{2,1,0:T(4,128)S(1)} %reshape.14.refs_1_, f32[1024,256]{1,0:T(8,128)} %refs_1_.1, f32[8,4,16,256]{3,2,1,0:T(8,128)S(1)} %pad_maximum_fusion.1.refs_3_, ...), custom_call_target="tpu_custom_call" | custom-call | flops 3221225472 | bytes 4194304 | tf_op jit(solution)/shard_map/solve/pallas_call | solution.py:148
  54.3 4.1 %collective-permute-done.11.refs_6_ = f32[4,4,16,768]{3,2,1,0:T(8,128)S(1)} collective-permute-done((f32[4,4,16,768]{3,2,1,0:T(8,128)S(1)}, f32[4,4,16,768]{3,2,1,0:T(8,128)S(1)}, u32[]{:S(2)}, u32[]{:S(2)}) %collective-permute-start.11) | collective-permute-done | bytes 786464 | tf_op jit(solution)/shard_map/ppermute | solution.py:36
  61.7 1.2 %copy-done.1 = f32[1024,256]{1,0:T(8,128)S(1)} copy-done((f32[1024,256]{1,0:T(8,128)S(1)}, f32[1024,256]{1,0:T(8,128)}, u32[]{:S(2)}) %copy-start.1) | copy-done | bytes 1048600
  62.9 3.3 %finish.1 = (f32[1024,256]{1,0:T(8,128)}, f32[256,256]{1,0:T(8,128)S(1)}, f32[256,256]{1,0:T(8,128)S(1)}) custom-call(s32[1]{0:T(128)} %bitcast.refs_0_.node_ref, f32[1024,256]{1,0:T(8,128)S(1)} %get-tuple-element.9.sol_ref, f32[1024,256]{1,0:T(8,128)S(1)} %copy-done.1, f32[4,256,256]{2,1,0:T(8,128)S(1)} %maximum_select_fusion.own_ref, ...), custom_call_target="tpu_custom_call" | custom-call | flops 603979776 | bytes 5242880 | tf_op jit(solution)/shard_map/finish/pallas_call | solution.py:186
  66.2 2.2 %collective-permute-done.13.refs_8_ = f32[2,4,16,768]{3,2,1,0:T(8,128)S(1)} collective-permute-done((f32[2,4,16,768]{3,2,1,0:T(8,128)}, f32[2,4,16,768]{3,2,1,0:T(8,128)S(1)}, u32[]{:S(2)}, u32[]{:S(2)}) %collective-permute-start.13) | collective-permute-done | bytes 393248 | tf_op jit(solution)/shard_map/ppermute | solution.py:36
  68.4 1.2 %collective-permute-done.14.refs_9_ = f32[2,4,16,768]{3,2,1,0:T(8,128)} collective-permute-done((f32[2,4,16,768]{3,2,1,0:T(8,128)}, f32[2,4,16,768]{3,2,1,0:T(8,128)}, u32[]{:S(2)}, u32[]{:S(2)}) %collective-permute-start.14) | collective-permute-done | bytes 393248 | tf_op jit(solution)/shard_map/ppermute | solution.py:36
  69.6 1.2 %copy-done.7 = f32[1024,256]{1,0:T(8,128)S(1)} copy-done((f32[1024,256]{1,0:T(8,128)S(1)}, f32[1024,256]{1,0:T(8,128)}, u32[]{:S(2)}) %copy-start.7) | copy-done | bytes 1048600
  70.9 4.6 %residual.1 = f32[1024,256]{1,0:T(8,128)} custom-call(f32[4,4,768]{2,1,0:T(4,128)S(1)} %reshape.15.refs_0_, f32[1024,256]{1,0:T(8,128)S(1)} %copy-done.6, f32[1024,256]{1,0:T(8,128)S(1)} %copy-done.7, f32[256,256]{1,0:T(8,128)S(1)} %get-tuple-element.14.refs_3_, f32[256,256]{1,0:T(8,128)S(1)} %get-tuple-element.15.refs_4_, ...), custom_call_target="tpu_custom_call" | custom-call | flops 1207959552 | bytes 6291456 | tf_op jit(solution)/shard_map/residual/pallas_call | solution.py:230
  (62 shorter events, 10.8 us)
Async XLA Ops:
  1.5 6.4 %collective-permute-start = (f32[8,16,256]{2,1,0:T(8,128)S(1)}, f32[8,16,256]{2,1,0:T(8,128)S(1)}, u32[]{:S(2)}, u32[]{:S(2)}) collective-permute-start(f32[8,16,256]{2,1,0:T(8,128)S(1)} %constant_dynamic-update-slice_fusion), channel_id=1, source_target_pairs={{0,8},{2,10},{4,12},{6,14},{8,0},{10,2},{12,4},{14,6},{16,24},{18,... | collective-permute-start | bytes 393224 | tf_op jit(solution)/shard_map/ppermute | solution.py:36
  3.2 9.9 %collective-permute-start.1 = (f32[8,16,256]{2,1,0:T(8,128)S(1)}, f32[8,16,256]{2,1,0:T(8,128)S(1)}, u32[]{:S(2)}, u32[]{:S(2)}) collective-permute-start(f32[8,16,256]{2,1,0:T(8,128)S(1)} %constant_dynamic-update-slice_fusion), channel_id=1, source_target_pairs={{0,16},{2,18},{4,20},{6,22},{8,24},{10,26},{12,28},{14,30},{16,0},... | collective-permute-start | bytes 393224 | tf_op jit(solution)/shard_map/ppermute | solution.py:36
  3.5 13.0 %collective-permute-start.2 = (f32[8,16,256]{2,1,0:T(8,128)S(1)}, f32[8,16,256]{2,1,0:T(8,128)S(1)}, u32[]{:S(2)}, u32[]{:S(2)}) collective-permute-start(f32[8,16,256]{2,1,0:T(8,128)S(1)} %constant_dynamic-update-slice_fusion), channel_id=1, source_target_pairs={{0,24},{2,26},{4,28},{6,30},{8,16},{10,18},{12,20},{14,22},{16,8},... | collective-permute-start | bytes 393224 | tf_op jit(solution)/shard_map/ppermute | solution.py:36
  16.5 3.1 %copy-start.14 = (f32[4,16,768]{2,1,0:T(8,128)S(1)}, f32[4,16,768]{2,1,0:T(8,128)}, u32[]{:S(2)}) copy-start(f32[4,16,768]{2,1,0:T(8,128)} %param.10) | copy-start | bytes 589828
  16.5 12.8 %collective-permute-start.3 = (f32[8,4,16,256]{3,2,1,0:T(8,128)S(1)}, f32[8,4,16,256]{3,2,1,0:T(8,128)S(1)}, u32[]{:S(2)}, u32[]{:S(2)}) collective-permute-start(f32[8,4,16,256]{3,2,1,0:T(8,128)S(1)} %pad_maximum_fusion.1.refs_3_), channel_id=1, source_target_pairs={{0,2},{2,0},{4,6},{6,4},{8,10},{10,8},{12,14},{14,12},{16,18},{18,... | collective-permute-start | bytes 1572872 | tf_op jit(solution)/shard_map/ppermute | solution.py:36
  18.1 12.8 %collective-permute-start.4 = (f32[8,4,16,256]{3,2,1,0:T(8,128)S(1)}, f32[8,4,16,256]{3,2,1,0:T(8,128)S(1)}, u32[]{:S(2)}, u32[]{:S(2)}) collective-permute-start(f32[8,4,16,256]{3,2,1,0:T(8,128)S(1)} %pad_maximum_fusion.1.refs_3_), channel_id=1, source_target_pairs={{0,4},{2,6},{4,0},{6,2},{8,12},{10,14},{12,8},{14,10},{16,20},{18,... | collective-permute-start | bytes 1572872 | tf_op jit(solution)/shard_map/ppermute | solution.py:36
  19.6 13.1 %collective-permute-start.8 = (f32[4,16,768]{2,1,0:T(8,128)S(1)}, f32[4,16,768]{2,1,0:T(8,128)}, u32[]{:S(2)}, u32[]{:S(2)}) collective-permute-start(f32[4,16,768]{2,1,0:T(8,128)S(1)} %copy-done.14), channel_id=1, source_target_pairs={{0,8},{2,10},{4,12},{6,14},{8,0},{10,2},{12,4},{14,6},{16,24},{18,... | collective-permute-start | bytes 589832 | tf_op jit(solution)/shard_map/ppermute | solution.py:36
  19.6 14.3 %collective-permute-start.9 = (f32[4,16,768]{2,1,0:T(8,128)S(1)}, f32[4,16,768]{2,1,0:T(8,128)}, u32[]{:S(2)}, u32[]{:S(2)}) collective-permute-start(f32[4,16,768]{2,1,0:T(8,128)S(1)} %copy-done.14), channel_id=1, source_target_pairs={{0,16},{2,18},{4,20},{6,22},{8,24},{10,26},{12,28},{14,30},{16,0},... | collective-permute-start | bytes 589832 | tf_op jit(solution)/shard_map/ppermute | solution.py:36
  21.5 17.1 %collective-permute-start.10 = (f32[4,16,768]{2,1,0:T(8,128)S(1)}, f32[4,16,768]{2,1,0:T(8,128)}, u32[]{:S(2)}, u32[]{:S(2)}) collective-permute-start(f32[4,16,768]{2,1,0:T(8,128)S(1)} %copy-done.14), channel_id=1, source_target_pairs={{0,24},{2,26},{4,28},{6,30},{8,16},{10,18},{12,20},{14,22},{16,8},... | collective-permute-start | bytes 589832 | tf_op jit(solution)/shard_map/ppermute | solution.py:36
  29.3 12.1 %collective-permute-start.5 = (f32[4,4,16,256]{3,2,1,0:T(8,128)S(1)}, f32[4,4,16,256]{3,2,1,0:T(8,128)S(1)}, u32[]{:S(2)}, u32[]{:S(2)}) collective-permute-start(f32[4,4,16,256]{3,2,1,0:T(8,128)S(1)} %slice.48), channel_id=1, source_target_pairs={{0,4},{2,6},{4,0},{6,2},{8,12},{10,14},{12,8},{14,10},{16,20},{18,... | collective-permute-start | bytes 786440 | tf_op jit(solution)/shard_map/ppermute | solution.py:36
  30.9 9.0 %copy-start.8 = (f32[8,4,16,256]{3,2,1,0:T(8,128)}, f32[8,4,16,256]{3,2,1,0:T(8,128)S(1)}, u32[]{:S(2)}) copy-start(f32[8,4,16,256]{3,2,1,0:T(8,128)S(1)} %collective-permute-done.4.refs_5_) | copy-start | bytes 1572868
  30.9 1.6 %copy-start.16 = (s32[4,4,4]{2,1,0:T(4,128)S(1)}, s32[4,4,4]{2,1,0:T(4,128)}, u32[]{:S(2)}) copy-start(s32[4,4,4]{2,1,0:T(4,128)} %param.9) | copy-start | bytes 772
  30.9 11.2 %collective-permute-start.6 = (f32[4,4,16,256]{3,2,1,0:T(8,128)S(1)}, f32[4,4,16,256]{3,2,1,0:T(8,128)S(1)}, u32[]{:S(2)}, u32[]{:S(2)}) collective-permute-start(f32[4,4,16,256]{3,2,1,0:T(8,128)S(1)} %slice.49), channel_id=1, source_target_pairs={{0,2},{2,0},{4,6},{6,4},{8,10},{10,8},{12,14},{14,12},{16,18},{18,... | collective-permute-start | bytes 786440 | tf_op jit(solution)/shard_map/ppermute | solution.py:36
  40.0 18.4 %collective-permute-start.11 = (f32[4,4,16,768]{3,2,1,0:T(8,128)S(1)}, f32[4,4,16,768]{3,2,1,0:T(8,128)S(1)}, u32[]{:S(2)}, u32[]{:S(2)}) collective-permute-start(f32[4,4,16,768]{3,2,1,0:T(8,128)S(1)} %pad_maximum_fusion.refs_5_), channel_id=1, source_target_pairs={{0,2},{2,0},{4,6},{6,4},{8,10},{10,8},{12,14},{14,12},{16,18},{18,... | collective-permute-start | bytes 2359304 | tf_op jit(solution)/shard_map/ppermute | solution.py:36
  40.6 19.2 %collective-permute-start.12 = (f32[4,4,16,768]{3,2,1,0:T(8,128)S(1)}, f32[4,4,16,768]{3,2,1,0:T(8,128)S(1)}, u32[]{:S(2)}, u32[]{:S(2)}) collective-permute-start(f32[4,4,16,768]{3,2,1,0:T(8,128)S(1)} %pad_maximum_fusion.refs_5_), channel_id=1, source_target_pairs={{0,4},{2,6},{4,0},{6,2},{8,12},{10,14},{12,8},{14,10},{16,20},{18,... | collective-permute-start | bytes 2359304 | tf_op jit(solution)/shard_map/ppermute | solution.py:36
  54.2 7.5 %collective-permute-start.7 = (f32[4,256,256]{2,1,0:T(8,128)S(1)}, f32[4,256,256]{2,1,0:T(8,128)}, u32[]{:S(2)}, u32[]{:S(2)}) collective-permute-start(f32[4,256,256]{2,1,0:T(8,128)S(1)} %maximum_select_fusion.own_ref), channel_id=1, source_target_pairs={{0,1},{1,0},{2,3},{3,2},{4,5},{5,4},{6,7},{7,6},{8,9},{9,8},{10,11... | collective-permute-start | bytes 3145736 | tf_op jit(solution)/shard_map/ppermute | solution.py:280
  58.4 2.2 %copy-start.2 = (f32[4,4,16,768]{3,2,1,0:T(8,128)}, f32[4,4,16,768]{3,2,1,0:T(8,128)S(1)}, u32[]{:S(2)}) copy-start(f32[4,4,16,768]{3,2,1,0:T(8,128)S(1)} %collective-permute-done.11.refs_6_) | copy-start | bytes 2359300
  59.2 2.3 %copy-start.17 = (s32[4,4,12]{2,1,0:T(4,128)S(1)}, s32[4,4,12]{2,1,0:T(4,128)}, u32[]{:S(2)}) copy-start(s32[4,4,12]{2,1,0:T(4,128)} %param.11) | copy-start | bytes 2308
  59.2 9.2 %collective-permute-start.13 = (f32[2,4,16,768]{3,2,1,0:T(8,128)}, f32[2,4,16,768]{3,2,1,0:T(8,128)S(1)}, u32[]{:S(2)}, u32[]{:S(2)}) collective-permute-start(f32[2,4,16,768]{3,2,1,0:T(8,128)} %slice.50), channel_id=1, source_target_pairs={{0,4},{2,6},{4,0},{6,2},{8,12},{10,14},{12,8},{14,10},{16,20},{18,... | collective-permute-start | bytes 1179656 | tf_op jit(solution)/shard_map/ppermute | solution.py:36
  59.7 1.8 %copy-start.4 = (f32[4,4,16,768]{3,2,1,0:T(8,128)}, f32[4,4,16,768]{3,2,1,0:T(8,128)S(1)}, u32[]{:S(2)}) copy-start(f32[4,4,16,768]{3,2,1,0:T(8,128)S(1)} %collective-permute-done.12.refs_7_) | copy-start | bytes 2359300
  60.6 9.1 %collective-permute-start.14 = (f32[2,4,16,768]{3,2,1,0:T(8,128)}, f32[2,4,16,768]{3,2,1,0:T(8,128)}, u32[]{:S(2)}, u32[]{:S(2)}) collective-permute-start(f32[2,4,16,768]{3,2,1,0:T(8,128)} %slice.51), channel_id=1, source_target_pairs={{0,2},{2,0},{4,6},{6,4},{8,10},{10,8},{12,14},{14,12},{16,18},{18,... | collective-permute-start | bytes 1179656 | tf_op jit(solution)/shard_map/ppermute | solution.py:36
  62.9 6.7 %copy-start.3 = (f32[4,4,16,768]{3,2,1,0:T(8,128)S(1)}, f32[4,4,16,768]{3,2,1,0:T(8,128)}, u32[]{:S(2)}) copy-start(f32[4,4,16,768]{3,2,1,0:T(8,128)} %copy-done.2) | copy-start | bytes 2359300
  62.9 6.7 %copy-start.5 = (f32[4,4,16,768]{3,2,1,0:T(8,128)S(1)}, f32[4,4,16,768]{3,2,1,0:T(8,128)}, u32[]{:S(2)}) copy-start(f32[4,4,16,768]{3,2,1,0:T(8,128)} %copy-done.4) | copy-start | bytes 2359300
  62.9 6.7 %copy-start.6 = (f32[1024,256]{1,0:T(8,128)S(1)}, f32[1024,256]{1,0:T(8,128)}, u32[]{:S(2)}) copy-start(f32[1024,256]{1,0:T(8,128)} %refs_1_.1) | copy-start | bytes 3145732
  (9 other events, 8.7 us)

commit v2 on v1

--- a/solution.py
+++ b/solution.py
@@ -24,46 +24,105 @@
     return dot(left[0], right[1]) + dot(left[1], right[0]) + dot(left[0], right[0])
 
 
-def gather_rows(part, axis):
-    count = lax.axis_size(axis)
-    parts = part.shape[0]
-    half = parts // 2
-    if count < 4 or count & (count - 1):
-        everything = lax.all_gather(part, axis, axis=1)
-        return [(everything, 0, [(place, place) for place in range(count)])], False
-
-    def across(value, mask):
-        return lax.ppermute(value, axis, [(i, i ^ mask) for i in range(count)])
-
-    lines = [0] + [high << 2 for high in range(1, count >> 2)]
-    own = jnp.stack([part] + [across(part, mask) for mask in lines[1:]], axis=1)
-    first, second = across(own, 1), across(own, 2)
-    third = [across(first[:half], 2), across(second[half:], 1)]
-
-    def slots(low):
-        return [(place, mask | low) for place, mask in enumerate(lines)]
-
-    return [
-        (own, 0, slots(0)),
-        (first, 0, slots(1)),
-        (second, 0, slots(2)),
-        (third[0], 0, slots(3)),
-        (third[1], half, slots(3)),
-    ], True
+def across(value, axis, mask):
+    return lax.ppermute(value, axis, [(i, i ^ mask) for i in range(lax.axis_size(axis))])
+
+
+def line_masks(axis):
+    high = lax.axis_size(axis) // 4
+    return [4 * (step - 1) for step in iter_halves(high)]
+
+
+def iter_halves(step):
+    while step > 1:
+        yield step
+        step //= 2
+
+
+def spread(held, masks, axis):
+    for mask in masks:
+        held = jnp.concatenate([held, across(held, axis, mask)])
+    return held
+
+
+def line_order(masks):
+    order = [0]
+    for mask in masks:
+        order += [mask ^ other for other in order]
+    return order
+
+
+def around(held, axis):
+    return across(held, axis, 1), across(held, axis, 2)
+
+
+def onward(first, second, axis):
+    half = first.shape[1] // 2
+    return across(first[:, :half], axis, 2), across(second[:, half:], axis, 1)
+
+
+def piece(array, order, low, start=0, column=0):
+    return array, [mask | low for mask in order], start, column
+
+
+def pieces_of(own, first, second, third, order, column=0):
+    half = third[0].shape[1]
+    return ([piece(own, order, 0, 0, column)] if own is not None else []) + [
+        piece(first, order, 1, 0, column),
+        piece(second, order, 2, 0, column),
+        piece(third[0], order, 3, 0, column),
+        piece(third[1], order, 3, half, column),
+    ]
+
+
+def gather_whole(part, axis):
+    everything = lax.all_gather(part, axis)
+    return [piece(everything, list(range(lax.axis_size(axis))), 0)]
+
+
+def gather_panels(factor_part, jacobian, right_side, axis):
+    masks = line_masks(axis)
+    order = line_order(masks)
+    factor_part, jacobian = factor_part[None], jacobian[None]
+    everything = jnp.concatenate([factor_part, jacobian], axis=3)
+    split_at = factor_part.shape[3]
+
+    factor_line = spread(factor_part, masks[:1], axis)
+    own = around(everything, axis)
+    jacobian, factor_line = lax.optimization_barrier((jacobian, factor_line))
+    factor_line = spread(factor_line, masks[1:], axis)
+    jacobian_line = spread(jacobian, masks[:1], axis)
+    factor_line, own = lax.optimization_barrier((factor_line, own))
+    own_third = onward(*own, axis)
+    factor_rest = around(factor_line[1:], axis)
+    jacobian_line = spread(jacobian_line, masks[1:], axis)
+    factor_rest, jacobian_line = lax.optimization_barrier((factor_rest, jacobian_line))
+    factor_third = onward(*factor_rest, axis)
+    jacobian_rest = around(jacobian_line[1:], axis)
+    late, jacobian_line = lax.optimization_barrier((right_side, jacobian_line))
+    jacobian_third = onward(*jacobian_rest, axis)
+
+    factor = [piece(factor_line, order, 0)]
+    factor += pieces_of(None, *own, own_third, order[:1])
+    factor += pieces_of(None, *factor_rest, factor_third, order[1:])
+    jacobians = [piece(jacobian_line, order, 0)]
+    jacobians += pieces_of(None, *own, own_third, order[:1], split_at)
+    jacobians += pieces_of(None, *jacobian_rest, jacobian_third, order[1:])
+    return factor, jacobians, late
 
 
 def place_rows(pieces, refs, relative, axis, panels, sem):
     me = lax.axis_index(axis)
-    rows = pieces[0][0].shape[2]
+    wide = panels.shape[2]
     copies = []
-    for (array, start, slots), ref in zip(pieces, refs):
-        for place, mask in slots:
-            owner = me ^ mask if relative else mask
-            at = pl.multiple_of(owner * rows, rows) if relative else owner * rows
+    for (array, owners, start, column), ref in zip(pieces, refs):
+        parts, rows = array.shape[1:3]
+        for place, owner in enumerate(owners):
+            at = pl.multiple_of((me ^ owner) * rows, rows) if relative else owner * rows
             copies.append(
                 pltpu.make_async_copy(
-                    ref.at[:, place],
-                    panels.at[pl.ds(start, array.shape[0]), pl.ds(at, rows), :],
+                    ref.at[place, :, :, pl.ds(column, wide)],
+                    panels.at[pl.ds(start, parts), pl.ds(at, rows), :],
                     sem.at[len(copies)],
                 )
             )
@@ -81,7 +140,7 @@
     extra = 0 if nodes == 1 else 1 if nodes == 2 else 2
     width = columns + extra * size
     n = len(pieces)
-    n_copies = sum(len(slots) for _, _, slots in pieces)
+    n_copies = sum(len(owners) for _, owners, _, _ in pieces)
 
     def kernel(*refs):
         node_ref, weights_ref, rhs_ref = refs[:3]
@@ -101,7 +160,7 @@
             copy.wait()
 
         def masked(s):
-            tall = panels[supers + s]
+            tall = panels[s, :, size:]
             blocks = weights_ref.shape[1]
             step = size // blocks
             return jnp.concatenate(
@@ -112,7 +171,7 @@
         for s in range(supers):
             own = rhs_ref[s * size : (s + 1) * size, :]
             low = masked(s)
-            panels[supers + s] = low
+            panels[s, :, size:] = low
             if s == 0:
                 parts = [own]
                 if extra:
@@ -122,7 +181,7 @@
                 target = jnp.concatenate(parts, axis=1)
             else:
                 target = jnp.concatenate([own] + [zeros] * extra, axis=1) - product(split(low), split(previous))
-            previous = product(split(panels[s]), split(target))
+            previous = product(split(panels[s, :, :size]), split(target))
             forward[s] = previous
         down_ref[...] = previous
 
@@ -136,12 +195,12 @@
                     target = target - jnp.concatenate(shift, axis=1)
             else:
                 target = target - entering
-            solved = product(split(panels[s].T), split(target))
+            solved = product(split(panels[s, :, :size].T), split(target))
             sol_ref[s * size : (s + 1) * size, :] = solved[:, :columns]
             for e, ref in enumerate(extra_refs):
                 ref[s * size : (s + 1) * size, :] = solved[:, columns + e * size : columns + (e + 1) * size]
             if s > 0 or nodes > 1:
-                entering = product(split(panels[supers + s].T), split(solved))
+                entering = product(split(panels[s, :, size:].T), split(solved))
         up_ref[...] = entering if nodes > 1 else previous
 
     span = supers * size
@@ -151,23 +210,23 @@
         in_specs=[SMEM, VMEM, VMEM] + [ANY] * n,
         out_specs=[VMEM] * (3 + extra),
         scratch_shapes=[
-            pltpu.VMEM((2 * supers, size, size), jnp.float32),
+            pltpu.VMEM((supers, size, 2 * size), jnp.float32),
             pltpu.VMEM((supers, size, width), jnp.float32),
             pltpu.SemaphoreType.DMA((n_copies,)),
         ],
         compiler_params=pltpu.CompilerParams(vmem_limit_bytes=VMEM_LIMIT),
         cost_estimate=pl.CostEstimate(
-            flops=6 * 4 * supers * size * size * width, bytes_accessed=16 * span * size, transcendentals=0
+            flops=4 * supers * size * size * width, bytes_accessed=span * size, transcendentals=0
         ),
         name="solve",
-    )(node, weights, right_side, *[array for array, _, _ in pieces])
+    )(node, weights, right_side, *[array for array, *_ in pieces])
     return out[0], out[1 : 1 + extra], out[1 + extra], out[2 + extra]
 
 
-def finish(sol, part, own_mail, mail, node, size):
+def finish(sol, part, own_mail, mail, beside_mail, node, size):
     span, columns = sol.shape
 
-    def kernel(node_ref, sol_ref, part_ref, own_ref, mail_ref, out_ref, before_ref, after_ref):
+    def kernel(node_ref, sol_ref, part_ref, own_ref, mail_ref, beside_ref, out_ref, before_ref, after_ref):
         lower_one = node_ref[0] == 0
         down = jnp.where(lower_one, own_ref[0], mail_ref[0])
         offset = jnp.where(lower_one, mail_ref[0], own_ref[0])
@@ -179,21 +238,21 @@
             out_ref[at : at + size, :] = sol_ref[at : at + size, :] + product(
                 split(part_ref[at : at + size, :]), mine
             )
-        beside = mail_ref[2] + product(split(mail_ref[3]), other)
+        beside = beside_ref[0] + product(split(beside_ref[1]), other)
         before_ref[...] = jnp.where(lower_one, 0.0, beside)
         after_ref[...] = jnp.where(lower_one, beside, 0.0)
 
     return pl.pallas_call(
         kernel,
         out_shape=shapes([(span, columns), (size, columns), (size, columns)]),
-        in_specs=[SMEM] + [VMEM] * 4,
+        in_specs=[SMEM] + [VMEM] * 5,
         out_specs=[VMEM] * 3,
         compiler_params=pltpu.CompilerParams(vmem_limit_bytes=VMEM_LIMIT),
         cost_estimate=pl.CostEstimate(
-            flops=6 * (span + 2 * size) * size * columns, bytes_accessed=20 * span * columns, transcendentals=0
+            flops=1 * (span + 2 * size) * size * columns, bytes_accessed=span * columns, transcendentals=0
         ),
         name="finish",
-    )(node, sol, part, own_mail, mail)
+    )(node, sol, part, own_mail, mail, beside_mail)
 
 
 def subtract_product(pieces, relative, right_side, sol, before, after, weights, supers, size):
@@ -202,7 +261,7 @@
     blocks = weights.shape[1]
     step = size // blocks
     n = len(pieces)
-    n_copies = sum(len(slots) for _, _, slots in pieces)
+    n_copies = sum(len(owners) for _, owners, _, _ in pieces)
 
     def kernel(*refs):
         weights_ref, rhs_ref, sol_ref, before_ref, after_ref = refs[:5]
@@ -243,7 +302,7 @@
             flops=6 * span * wide * columns, bytes_accessed=4 * span * (wide + 3 * columns), transcendentals=0
         ),
         name="residual",
-    )(weights, right_side, sol, before, after, *[array for array, _, _ in pieces])
+    )(weights, right_side, sol, before, after, *[array for array, *_ in pieces])
 
 
 def dot(left, right):
@@ -260,11 +319,18 @@
     def widened(pattern):
         return jnp.repeat(pattern.astype(jnp.float32), size // factor_pattern.shape[2], axis=2)
 
-    factor, relative = gather_rows(jnp.concatenate([diag_inv, lower], axis=0), "rhs")
-    jacobians, _ = gather_rows(jacobian, "rhs")
+    factor_part = jnp.concatenate([diag_inv, lower], axis=2)
+    count = lax.axis_size("rhs")
+    relative = count >= 8 and not count & (count - 1)
+    late = right_side
+    if relative:
+        factor, jacobians, late = gather_panels(factor_part, jacobian, right_side, "rhs")
+    else:
+        factor = gather_whole(factor_part, "rhs")
+        jacobians = gather_whole(jacobian, "rhs")
 
     sol, parts, down, up = solve(
-        factor, relative, right_side, widened(factor_pattern), node, nodes, supers, size
+        factor, relative, late, widened(factor_pattern), node, nodes, supers, size
     )
     empty = jnp.zeros((size, columns), jnp.float32)
     if nodes == 1:
@@ -272,13 +338,15 @@
     elif nodes == 2:
         last, first = slice(span - size, span), slice(0, size)
         is_lower = lax.axis_index("node") == 0
-        own_mail = jnp.where(
-            is_lower,
-            jnp.stack([down[:, :columns], down[:, columns:], sol[last], parts[0][last]]),
-            jnp.stack([up[:, :columns], up[:, columns:], sol[first], parts[0][first]]),
-        )
-        mail = lax.ppermute(own_mail, "node", [(0, 1), (1, 0)])
-        sol, before, after = finish(sol, parts[0], own_mail, mail, node, size)
+        own_mail = [
+            jnp.where(is_lower, jnp.stack(lower_mail), jnp.stack(upper_mail))
+            for lower_mail, upper_mail in (
+                ([down[:, :columns], down[:, columns:]], [up[:, :columns], up[:, columns:]]),
+                ([sol[last], parts[0][last]], [sol[first], parts[0][first]]),
+            )
+        ]
+        mail = [lax.ppermute(letter, "node", [(0, 1), (1, 0)]) for letter in own_mail]
+        sol, before, after = finish(sol, parts[0], own_mail[0], *mail, node, size)
     else:
         upwards = [(i, i + 1) for i in range(nodes - 1)]
         downwards = [(i + 1, i) for i in range(nodes - 1)]

time: 76 us -> 82 us (1.079)
  the two profiles are of different devices: /device:TPU:16 before, /device:TPU:0 now
where the time goes in v2:
time: 82 us; the launch traced here: 81.5 us
  starting transfers between devices  27 us (33%)
  waiting for transfers between devices  23.8 us (29%)
  Pallas kernels  15.4 us (19%)
  local copies, waits for them, and re-layouts  12.4 us (15%)
  other arithmetic  1.97 us (2%)
  between operations  0.96 us (1%)
    ppermute x16, starting transfers between devices, across(): lax.ppermute(value, axis, [(i, i ^ mask) for i in range(lax.axis_size(axi...  26.4 us
    ppermute x16, waiting for transfers between devices, across(): lax.ppermute(value, axis, [(i, i ^ mask) for i in range(lax.axis_size(axi...  23.8 us
    unnamed x58, local copies, waits for them, and re-layouts  8.69 us
    pallas_call x1, Pallas kernels, solve(): pl.pallas_call(kernel, out_shape=shapes([(span, columns)] + [(span, size)...  7.64 us
    pallas_call x1, Pallas kernels, subtract_product(): pl.pallas_call(kernel, out_shape=shapes([(span, columns)])[0], in_specs=[...  4.5 us
    pallas_call x1, Pallas kernels, finish(): pl.pallas_call(kernel, out_shape=shapes([(span, columns), (size, columns)...  3.23 us
  transfers between devices with their start and end apart: 18, of which 10 were waited for; matrix products, arithmetic and copies ran while one was open for 6% of the time, Pallas kernels for 13%

profile of v2, /device:TPU:0, one launch (start us, length us, event | category | flops | bytes accessed | tf_op | source)
XLA Modules:
  0.0 81.5 jit_solution(6016781076930683631)
XLA Ops:
  1.5 5.1 %collective-permute-start = (f32[1,4,16,512]{3,2,1,0:T(8,128)S(1)}, f32[1,4,16,512]{3,2,1,0:T(8,128)S(1)}, u32[]{:S(2)}, u32[]{:S(2)}) collective-permute-start(f32[1,4,16,512]{3,2,1,0:T(8,128)S(1)} %maximum_bitcast_fusion), channel_id=1, source_target_pairs={{0,24},{2,26},{4,28},{6,30},{8,16},{10,18},{12,20},{14,22},{16,8},... | collective-permute-start | bytes 393224 | tf_op jit(solution)/shard_map/ppermute | solution.py:28
  6.6 3.6 %collective-permute-done = f32[1,4,16,512]{3,2,1,0:T(8,128)S(1)} collective-permute-done((f32[1,4,16,512]{3,2,1,0:T(8,128)S(1)}, f32[1,4,16,512]{3,2,1,0:T(8,128)S(1)}, u32[]{:S(2)}, u32[]{:S(2)}) %collective-permute-start) | collective-permute-done | bytes 131104 | tf_op jit(solution)/shard_map/ppermute | solution.py:28
  10.3 3.6 %collective-permute-start.6 = (f32[1,4,16,768]{3,2,1,0:T(8,128)S(1)}, f32[1,4,16,768]{3,2,1,0:T(8,128)S(1)}, u32[]{:S(2)}, u32[]{:S(2)}) collective-permute-start(f32[1,4,16,768]{3,2,1,0:T(8,128)S(1)} %bitcast.20), channel_id=1, source_target_pairs={{0,24},{2,26},{4,28},{6,30},{8,16},{10,18},{12,20},{14,22},{16,8},... | collective-permute-start | bytes 589832 | tf_op jit(solution)/shard_map/ppermute | solution.py:28
  14.4 1.6 %collective-permute-start.2 = (f32[1,4,16,1280]{3,2,1,0:T(8,128)S(1)}, f32[1,4,16,1280]{3,2,1,0:T(8,128)S(1)}, u32[]{:S(2)}, u32[]{:S(2)}) collective-permute-start(f32[1,4,16,1280]{3,2,1,0:T(8,128)S(1)} %pad_maximum_fusion.3), channel_id=1, source_target_pairs={{0,2},{2,0},{4,6},{6,4},{8,10},{10,8},{12,14},{14,12},{16,18},{18,... | collective-permute-start | bytes 983048 | tf_op jit(solution)/shard_map/ppermute | solution.py:28
  15.9 1.5 %collective-permute-start.3 = (f32[1,4,16,1280]{3,2,1,0:T(8,128)S(1)}, f32[1,4,16,1280]{3,2,1,0:T(8,128)S(1)}, u32[]{:S(2)}, u32[]{:S(2)}) collective-permute-start(f32[1,4,16,1280]{3,2,1,0:T(8,128)S(1)} %pad_maximum_fusion.3), channel_id=1, source_target_pairs={{0,4},{2,6},{4,0},{6,2},{8,12},{10,14},{12,8},{14,10},{16,20},{18,... | collective-permute-start | bytes 983048 | tf_op jit(solution)/shard_map/ppermute | solution.py:28
  17.4 2.5 %collective-permute-done.6 = f32[1,4,16,768]{3,2,1,0:T(8,128)S(1)} collective-permute-done((f32[1,4,16,768]{3,2,1,0:T(8,128)S(1)}, f32[1,4,16,768]{3,2,1,0:T(8,128)S(1)}, u32[]{:S(2)}, u32[]{:S(2)}) %collective-permute-start.6) | collective-permute-done | bytes 196640 | tf_op jit(solution)/shard_map/ppermute | solution.py:28
  20.0 3.0 %collective-permute-start.7 = (f32[2,4,16,768]{3,2,1,0:T(8,128)S(1)}, f32[2,4,16,768]{3,2,1,0:T(8,128)S(1)}, u32[]{:S(2)}, u32[]{:S(2)}) collective-permute-start(f32[2,4,16,768]{3,2,1,0:T(8,128)S(1)} %pad_maximum_fusion.2), channel_id=1, source_target_pairs={{0,8},{2,10},{4,12},{6,14},{8,0},{10,2},{12,4},{14,6},{16,24},{18,... | collective-permute-start | bytes 1179656 | tf_op jit(solution)/shard_map/ppermute | solution.py:28
  24.0 1.4 %collective-permute-start.4 = (f32[3,4,16,512]{3,2,1,0:T(8,128)S(1)}, f32[3,4,16,512]{3,2,1,0:T(8,128)S(1)}, u32[]{:S(2)}, u32[]{:S(2)}) collective-permute-start(f32[3,4,16,512]{3,2,1,0:T(8,128)S(1)} %slice.48), channel_id=1, source_target_pairs={{0,2},{2,0},{4,6},{6,4},{8,10},{10,8},{12,14},{14,12},{16,18},{18,... | collective-permute-start | bytes 1179656 | tf_op jit(solution)/shard_map/ppermute | solution.py:28
  25.4 1.5 %collective-permute-start.5 = (f32[3,4,16,512]{3,2,1,0:T(8,128)S(1)}, f32[3,4,16,512]{3,2,1,0:T(8,128)S(1)}, u32[]{:S(2)}, u32[]{:S(2)}) collective-permute-start(f32[3,4,16,512]{3,2,1,0:T(8,128)S(1)} %slice.48), channel_id=1, source_target_pairs={{0,4},{2,6},{4,0},{6,2},{8,12},{10,14},{12,8},{14,10},{16,20},{18,... | collective-permute-start | bytes 1179656 | tf_op jit(solution)/shard_map/ppermute | solution.py:28
  26.9 5.4 %collective-permute-done.7 = f32[2,4,16,768]{3,2,1,0:T(8,128)S(1)} collective-permute-done((f32[2,4,16,768]{3,2,1,0:T(8,128)S(1)}, f32[2,4,16,768]{3,2,1,0:T(8,128)S(1)}, u32[]{:S(2)}, u32[]{:S(2)}) %collective-permute-start.7) | collective-permute-done | bytes 393248 | tf_op jit(solution)/shard_map/ppermute | solution.py:28
  32.4 2.3 %collective-permute-done.4.refs_8_ = f32[3,4,16,512]{3,2,1,0:T(8,128)S(1)} collective-permute-done((f32[3,4,16,512]{3,2,1,0:T(8,128)S(1)}, f32[3,4,16,512]{3,2,1,0:T(8,128)S(1)}, u32[]{:S(2)}, u32[]{:S(2)}) %collective-permute-start.4) | collective-permute-done | bytes 393248 | tf_op jit(solution)/shard_map/ppermute | solution.py:28
  35.5 1.6 %collective-permute-start.10 = (f32[3,2,16,512]{3,2,1,0:T(8,128)S(1)}, f32[3,2,16,512]{3,2,1,0:T(8,128)S(1)}, u32[]{:S(2)}, u32[]{:S(2)}) collective-permute-start(f32[3,2,16,512]{3,2,1,0:T(8,128)S(1)} %slice.51), channel_id=1, source_target_pairs={{0,4},{2,6},{4,0},{6,2},{8,12},{10,14},{12,8},{14,10},{16,20},{18,... | collective-permute-start | bytes 589832 | tf_op jit(solution)/shard_map/ppermute | solution.py:28
  37.7 1.0 %collective-permute-start.8 = (f32[1,2,16,1280]{3,2,1,0:T(8,128)S(1)}, f32[1,2,16,1280]{3,2,1,0:T(8,128)S(1)}, u32[]{:S(2)}, u32[]{:S(2)}) collective-permute-start(f32[1,2,16,1280]{3,2,1,0:T(8,128)S(1)} %slice.49), channel_id=1, source_target_pairs={{0,4},{2,6},{4,0},{6,2},{8,12},{10,14},{12,8},{14,10},{16,20},{18,... | collective-permute-start | bytes 491528 | tf_op jit(solution)/shard_map/ppermute | solution.py:28
  38.8 1.2 %collective-permute-start.9 = (f32[1,2,16,1280]{3,2,1,0:T(8,128)S(1)}, f32[1,2,16,1280]{3,2,1,0:T(8,128)S(1)}, u32[]{:S(2)}, u32[]{:S(2)}) collective-permute-start(f32[1,2,16,1280]{3,2,1,0:T(8,128)S(1)} %slice.50), channel_id=1, source_target_pairs={{0,2},{2,0},{4,6},{6,4},{8,10},{10,8},{12,14},{14,12},{16,18},{18,... | collective-permute-start | bytes 491528 | tf_op jit(solution)/shard_map/ppermute | solution.py:28
  41.2 2.9 %collective-permute-done.8.refs_6_.refs_8_ = f32[1,2,16,1280]{3,2,1,0:T(8,128)S(1)} collective-permute-done((f32[1,2,16,1280]{3,2,1,0:T(8,128)S(1)}, f32[1,2,16,1280]{3,2,1,0:T(8,128)S(1)}, u32[]{:S(2)}, u32[]{:S(2)}) %collective-permute-start.8) | collective-permute-done | bytes 163872 | tf_op jit(solution)/shard_map/ppermute | solution.py:28
  44.7 1.5 %collective-permute-start.15 = (f32[3,4,16,768]{3,2,1,0:T(8,128)S(1)}, f32[3,4,16,768]{3,2,1,0:T(8,128)S(1)}, u32[]{:S(2)}, u32[]{:S(2)}) collective-permute-start(f32[3,4,16,768]{3,2,1,0:T(8,128)S(1)} %slice.61), channel_id=1, source_target_pairs={{0,4},{2,6},{4,0},{6,2},{8,12},{10,14},{12,8},{14,10},{16,20},{18,... | collective-permute-start | bytes 1769480 | tf_op jit(solution)/shard_map/ppermute | solution.py:28
  46.3 2.3 %collective-permute-done.9.refs_7_.refs_9_ = f32[1,2,16,1280]{3,2,1,0:T(8,128)S(1)} collective-permute-done((f32[1,2,16,1280]{3,2,1,0:T(8,128)S(1)}, f32[1,2,16,1280]{3,2,1,0:T(8,128)S(1)}, u32[]{:S(2)}, u32[]{:S(2)}) %collective-permute-start.9) | collective-permute-done | bytes 163872 | tf_op jit(solution)/shard_map/ppermute | solution.py:28
  55.3 7.6 %solve.1 = (f32[1024,256]{1,0:T(8,128)S(1)}, f32[1024,256]{1,0:T(8,128)S(1)}, f32[256,512]{1,0:T(8,128)S(1)}, f32[256,512]{1,0:T(8,128)S(1)}) custom-call(s32[1]{0:T(128)} %bitcast.refs_0_.node_ref, f32[4,4,256]{2,1,0:T(4,128)S(1)} %reshape.14.refs_1_, f32[1024,256]{1,0:T(8,128)} %refs_1_.1, f32[4,4,16,512]{3,2,1,0:T(8,128)S(1)} %pad_maximum_fusion.1.refs_3_, ...), custom_call_target="tpu_custom_call" | custom-call | flops 536870912 | bytes 262144 | tf_op jit(solution)/shard_map/solve/pallas_call | solution.py:207
  68.4 1.0 %reshape.15.refs_0_ = f32[4,4,768]{2,1,0:T(4,128)S(1)} reshape(f32[4,4,12,64]{3,2,1,0:T(8,128)} %broadcast_in_dim.15) | data formatting | bytes 98304 | tf_op jit(solution)/shard_map/reshape | solution.py:320
  69.5 3.2 %finish.1 = (f32[1024,256]{1,0:T(8,128)}, f32[256,256]{1,0:T(8,128)S(1)}, f32[256,256]{1,0:T(8,128)S(1)}) custom-call(s32[1]{0:T(128)} %bitcast.refs_0_.node_ref, f32[1024,256]{1,0:T(8,128)S(1)} %get-tuple-element.28.sol_ref, f32[1024,256]{1,0:T(8,128)S(1)} %get-tuple-element.29.part_ref, f32[2,256,256]{2,1,0:T(8,128)S(1)} %maximum_select_fusion.own_ref, ...), custom_call_target="tpu_custom_call" | custom-call | flops 100663296 | bytes 262144 | tf_op jit(solution)/shard_map/finish/pallas_call | solution.py:245
  72.7 1.9 %collective-permute-done.16.refs_12_ = f32[3,2,16,768]{3,2,1,0:T(8,128)} collective-permute-done((f32[3,2,16,768]{3,2,1,0:T(8,128)}, f32[3,2,16,768]{3,2,1,0:T(8,128)}, u32[]{:S(2)}, u32[]{:S(2)}) %collective-permute-start.16) | collective-permute-done | bytes 294944 | tf_op jit(solution)/shard_map/ppermute | solution.py:28
  74.7 1.1 %collective-permute-done.17.refs_13_ = f32[3,2,16,768]{3,2,1,0:T(8,128)} collective-permute-done((f32[3,2,16,768]{3,2,1,0:T(8,128)}, f32[3,2,16,768]{3,2,1,0:T(8,128)}, u32[]{:S(2)}, u32[]{:S(2)}) %collective-permute-start.17) | collective-permute-done | bytes 294944 | tf_op jit(solution)/shard_map/ppermute | solution.py:28
  75.8 1.2 %copy-done.11 = f32[1024,256]{1,0:T(8,128)S(1)} copy-done((f32[1024,256]{1,0:T(8,128)S(1)}, f32[1024,256]{1,0:T(8,128)}, u32[]{:S(2)}) %copy-start.11) | copy-done | bytes 1048600
  77.0 4.5 %residual.1 = f32[1024,256]{1,0:T(8,128)} custom-call(f32[4,4,768]{2,1,0:T(4,128)S(1)} %reshape.15.refs_0_, f32[1024,256]{1,0:T(8,128)S(1)} %copy-done, f32[1024,256]{1,0:T(8,128)S(1)} %copy-done.11, f32[256,256]{1,0:T(8,128)S(1)} %get-tuple-element.33.refs_3_, f32[256,256]{1,0:T(8,128)S(1)} %get-tuple-element.34.refs_4_, ...), custom_call_target="tpu_custom_call" | custom-call | flops 1207959552 | bytes 6291456 | tf_op jit(solution)/shard_map/residual/pallas_call | solution.py:289
  (97 shorter events, 17.9 us)
Async XLA Ops:
  1.5 8.8 %copy-start.26 = (f32[4,16,768]{2,1,0:T(8,128)S(1)}, f32[4,16,768]{2,1,0:T(8,128)}, u32[]{:S(2)}) copy-start(f32[4,16,768]{2,1,0:T(8,128)} %param.10) | copy-start | bytes 589828
  1.5 8.7 %collective-permute-start = (f32[1,4,16,512]{3,2,1,0:T(8,128)S(1)}, f32[1,4,16,512]{3,2,1,0:T(8,128)S(1)}, u32[]{:S(2)}, u32[]{:S(2)}) collective-permute-start(f32[1,4,16,512]{3,2,1,0:T(8,128)S(1)} %maximum_bitcast_fusion), channel_id=1, source_target_pairs={{0,24},{2,26},{4,28},{6,30},{8,16},{10,18},{12,20},{14,22},{16,8},... | collective-permute-start | bytes 393224 | tf_op jit(solution)/shard_map/ppermute | solution.py:28
  10.3 9.7 %collective-permute-start.6 = (f32[1,4,16,768]{3,2,1,0:T(8,128)S(1)}, f32[1,4,16,768]{3,2,1,0:T(8,128)S(1)}, u32[]{:S(2)}, u32[]{:S(2)}) collective-permute-start(f32[1,4,16,768]{3,2,1,0:T(8,128)S(1)} %bitcast.20), channel_id=1, source_target_pairs={{0,24},{2,26},{4,28},{6,30},{8,16},{10,18},{12,20},{14,22},{16,8},... | collective-permute-start | bytes 589832 | tf_op jit(solution)/shard_map/ppermute | solution.py:28
  13.9 10.0 %collective-permute-start.1 = (f32[2,4,16,512]{3,2,1,0:T(8,128)S(1)}, f32[2,4,16,512]{3,2,1,0:T(8,128)S(1)}, u32[]{:S(2)}, u32[]{:S(2)}) collective-permute-start(f32[2,4,16,512]{3,2,1,0:T(8,128)S(1)} %pad_maximum_fusion.4), channel_id=1, source_target_pairs={{0,8},{2,10},{4,12},{6,14},{8,0},{10,2},{12,4},{14,6},{16,24},{18,... | collective-permute-start | bytes 786440 | tf_op jit(solution)/shard_map/ppermute | solution.py:28
  14.4 9.6 %collective-permute-start.2 = (f32[1,4,16,1280]{3,2,1,0:T(8,128)S(1)}, f32[1,4,16,1280]{3,2,1,0:T(8,128)S(1)}, u32[]{:S(2)}, u32[]{:S(2)}) collective-permute-start(f32[1,4,16,1280]{3,2,1,0:T(8,128)S(1)} %pad_maximum_fusion.3), channel_id=1, source_target_pairs={{0,2},{2,0},{4,6},{6,4},{8,10},{10,8},{12,14},{14,12},{16,18},{18,... | collective-permute-start | bytes 983048 | tf_op jit(solution)/shard_map/ppermute | solution.py:28
  15.9 8.0 %collective-permute-start.3 = (f32[1,4,16,1280]{3,2,1,0:T(8,128)S(1)}, f32[1,4,16,1280]{3,2,1,0:T(8,128)S(1)}, u32[]{:S(2)}, u32[]{:S(2)}) collective-permute-start(f32[1,4,16,1280]{3,2,1,0:T(8,128)S(1)} %pad_maximum_fusion.3), channel_id=1, source_target_pairs={{0,4},{2,6},{4,0},{6,2},{8,12},{10,14},{12,8},{14,10},{16,20},{18,... | collective-permute-start | bytes 983048 | tf_op jit(solution)/shard_map/ppermute | solution.py:28
  20.0 12.3 %collective-permute-start.7 = (f32[2,4,16,768]{3,2,1,0:T(8,128)S(1)}, f32[2,4,16,768]{3,2,1,0:T(8,128)S(1)}, u32[]{:S(2)}, u32[]{:S(2)}) collective-permute-start(f32[2,4,16,768]{3,2,1,0:T(8,128)S(1)} %pad_maximum_fusion.2), channel_id=1, source_target_pairs={{0,8},{2,10},{4,12},{6,14},{8,0},{10,2},{12,4},{14,6},{16,24},{18,... | collective-permute-start | bytes 1179656 | tf_op jit(solution)/shard_map/ppermute | solution.py:28
  23.9 13.8 %copy-start.1 = (f32[1,4,16,1280]{3,2,1,0:T(8,128)}, f32[1,4,16,1280]{3,2,1,0:T(8,128)S(1)}, u32[]{:S(2)}) copy-start(f32[1,4,16,1280]{3,2,1,0:T(8,128)S(1)} %collective-permute-done.2.refs_4_.refs_6_) | copy-start | bytes 983044
  24.0 14.8 %copy-start.4 = (f32[1,4,16,1280]{3,2,1,0:T(8,128)}, f32[1,4,16,1280]{3,2,1,0:T(8,128)S(1)}, u32[]{:S(2)}) copy-start(f32[1,4,16,1280]{3,2,1,0:T(8,128)S(1)} %collective-permute-done.3.refs_5_.refs_7_) | copy-start | bytes 983044
  24.0 10.7 %collective-permute-start.4 = (f32[3,4,16,512]{3,2,1,0:T(8,128)S(1)}, f32[3,4,16,512]{3,2,1,0:T(8,128)S(1)}, u32[]{:S(2)}, u32[]{:S(2)}) collective-permute-start(f32[3,4,16,512]{3,2,1,0:T(8,128)S(1)} %slice.48), channel_id=1, source_target_pairs={{0,2},{2,0},{4,6},{6,4},{8,10},{10,8},{12,14},{14,12},{16,18},{18,... | collective-permute-start | bytes 1179656 | tf_op jit(solution)/shard_map/ppermute | solution.py:28
  25.4 10.1 %collective-permute-start.5 = (f32[3,4,16,512]{3,2,1,0:T(8,128)S(1)}, f32[3,4,16,512]{3,2,1,0:T(8,128)S(1)}, u32[]{:S(2)}, u32[]{:S(2)}) collective-permute-start(f32[3,4,16,512]{3,2,1,0:T(8,128)S(1)} %slice.48), channel_id=1, source_target_pairs={{0,4},{2,6},{4,0},{6,2},{8,12},{10,14},{12,8},{14,10},{16,20},{18,... | collective-permute-start | bytes 1179656 | tf_op jit(solution)/shard_map/ppermute | solution.py:28
  35.5 13.7 %collective-permute-start.10 = (f32[3,2,16,512]{3,2,1,0:T(8,128)S(1)}, f32[3,2,16,512]{3,2,1,0:T(8,128)S(1)}, u32[]{:S(2)}, u32[]{:S(2)}) collective-permute-start(f32[3,2,16,512]{3,2,1,0:T(8,128)S(1)} %slice.51), channel_id=1, source_target_pairs={{0,4},{2,6},{4,0},{6,2},{8,12},{10,14},{12,8},{14,10},{16,20},{18,... | collective-permute-start | bytes 589832 | tf_op jit(solution)/shard_map/ppermute | solution.py:28
  37.1 12.8 %collective-permute-start.11 = (f32[3,2,16,512]{3,2,1,0:T(8,128)S(1)}, f32[3,2,16,512]{3,2,1,0:T(8,128)S(1)}, u32[]{:S(2)}, u32[]{:S(2)}) collective-permute-start(f32[3,2,16,512]{3,2,1,0:T(8,128)S(1)} %slice.52), channel_id=1, source_target_pairs={{0,2},{2,0},{4,6},{6,4},{8,10},{10,8},{12,14},{14,12},{16,18},{18,... | collective-permute-start | bytes 589832 | tf_op jit(solution)/shard_map/ppermute | solution.py:28
  37.7 6.3 %collective-permute-start.8 = (f32[1,2,16,1280]{3,2,1,0:T(8,128)S(1)}, f32[1,2,16,1280]{3,2,1,0:T(8,128)S(1)}, u32[]{:S(2)}, u32[]{:S(2)}) collective-permute-start(f32[1,2,16,1280]{3,2,1,0:T(8,128)S(1)} %slice.49), channel_id=1, source_target_pairs={{0,4},{2,6},{4,0},{6,2},{8,12},{10,14},{12,8},{14,10},{16,20},{18,... | collective-permute-start | bytes 491528 | tf_op jit(solution)/shard_map/ppermute | solution.py:28
  38.8 9.8 %collective-permute-start.9 = (f32[1,2,16,1280]{3,2,1,0:T(8,128)S(1)}, f32[1,2,16,1280]{3,2,1,0:T(8,128)S(1)}, u32[]{:S(2)}, u32[]{:S(2)}) collective-permute-start(f32[1,2,16,1280]{3,2,1,0:T(8,128)S(1)} %slice.50), channel_id=1, source_target_pairs={{0,2},{2,0},{4,6},{6,4},{8,10},{10,8},{12,14},{14,12},{16,18},{18,... | collective-permute-start | bytes 491528 | tf_op jit(solution)/shard_map/ppermute | solution.py:28
  40.1 10.5 %copy-start.2 = (f32[1,4,16,1280]{3,2,1,0:T(8,128)S(1)}, f32[1,4,16,1280]{3,2,1,0:T(8,128)}, u32[]{:S(2)}) copy-start(f32[1,4,16,1280]{3,2,1,0:T(8,128)} %copy-done.1) | copy-start | bytes 983044
  40.1 10.5 %copy-start.5 = (f32[1,4,16,1280]{3,2,1,0:T(8,128)S(1)}, f32[1,4,16,1280]{3,2,1,0:T(8,128)}, u32[]{:S(2)}) copy-start(f32[1,4,16,1280]{3,2,1,0:T(8,128)} %copy-done.4) | copy-start | bytes 983044
  40.1 10.5 %copy-start.13 = (f32[3,4,16,512]{3,2,1,0:T(8,128)S(1)}, f32[3,4,16,512]{3,2,1,0:T(8,128)}, u32[]{:S(2)}) copy-start(f32[3,4,16,512]{3,2,1,0:T(8,128)} %copy-done.12) | copy-start | bytes 1179652
  40.2 24.4 %collective-permute-start.14 = (f32[3,4,16,768]{3,2,1,0:T(8,128)S(1)}, f32[3,4,16,768]{3,2,1,0:T(8,128)S(1)}, u32[]{:S(2)}, u32[]{:S(2)}) collective-permute-start(f32[3,4,16,768]{3,2,1,0:T(8,128)S(1)} %slice.61), channel_id=1, source_target_pairs={{0,2},{2,0},{4,6},{6,4},{8,10},{10,8},{12,14},{14,12},{16,18},{18,... | collective-permute-start | bytes 1769480 | tf_op jit(solution)/shard_map/ppermute | solution.py:28
  44.7 21.2 %collective-permute-start.15 = (f32[3,4,16,768]{3,2,1,0:T(8,128)S(1)}, f32[3,4,16,768]{3,2,1,0:T(8,128)S(1)}, u32[]{:S(2)}, u32[]{:S(2)}) collective-permute-start(f32[3,4,16,768]{3,2,1,0:T(8,128)S(1)} %slice.61), channel_id=1, source_target_pairs={{0,4},{2,6},{4,0},{6,2},{8,12},{10,14},{12,8},{14,10},{16,20},{18,... | collective-permute-start | bytes 1769480 | tf_op jit(solution)/shard_map/ppermute | solution.py:28
  63.9 5.6 %collective-permute-start.13 = (f32[2,256,256]{2,1,0:T(8,128)}, f32[2,256,256]{2,1,0:T(8,128)}, u32[]{:S(2)}, u32[]{:S(2)}) collective-permute-start(f32[2,256,256]{2,1,0:T(8,128)} %maximum_select_fusion.1), channel_id=1, source_target_pairs={{0,1},{1,0},{2,3},{3,2},{4,5},{5,4},{6,7},{7,6},{8,9},{9,8},{10,11... | collective-permute-start | bytes 1572872 | tf_op jit(solution)/shard_map/ppermute | solution.py:348
  64.1 5.4 %collective-permute-start.12 = (f32[2,256,256]{2,1,0:T(8,128)S(1)}, f32[2,256,256]{2,1,0:T(8,128)}, u32[]{:S(2)}, u32[]{:S(2)}) collective-permute-start(f32[2,256,256]{2,1,0:T(8,128)S(1)} %maximum_select_fusion.own_ref), channel_id=1, source_target_pairs={{0,1},{1,0},{2,3},{3,2},{4,5},{5,4},{6,7},{7,6},{8,9},{9,8},{10,11... | collective-permute-start | bytes 1572872 | tf_op jit(solution)/shard_map/ppermute | solution.py:348
  65.4 9.3 %collective-permute-start.16 = (f32[3,2,16,768]{3,2,1,0:T(8,128)}, f32[3,2,16,768]{3,2,1,0:T(8,128)}, u32[]{:S(2)}, u32[]{:S(2)}) collective-permute-start(f32[3,2,16,768]{3,2,1,0:T(8,128)} %slice.64), channel_id=1, source_target_pairs={{0,4},{2,6},{4,0},{6,2},{8,12},{10,14},{12,8},{14,10},{16,20},{18,... | collective-permute-start | bytes 884744 | tf_op jit(solution)/shard_map/ppermute | solution.py:28
  66.8 9.0 %collective-permute-start.17 = (f32[3,2,16,768]{3,2,1,0:T(8,128)}, f32[3,2,16,768]{3,2,1,0:T(8,128)}, u32[]{:S(2)}, u32[]{:S(2)}) collective-permute-start(f32[3,2,16,768]{3,2,1,0:T(8,128)} %slice.65), channel_id=1, source_target_pairs={{0,2},{2,0},{4,6},{6,4},{8,10},{10,8},{12,14},{14,12},{16,18},{18,... | collective-permute-start | bytes 884744 | tf_op jit(solution)/shard_map/ppermute | solution.py:28
  (23 other events, 64.3 us)

commit v3 on v2

--- a/solution.py
+++ b/solution.py
@@ -10,7 +10,7 @@
 VMEM = pl.BlockSpec(memory_space=pltpu.VMEM)
 SMEM = pl.BlockSpec(memory_space=pltpu.SMEM)
 ANY = pl.BlockSpec(memory_space=pl.ANY)
-VMEM_LIMIT = 48 * 2**20
+VMEM_LIMIT = 20 * 2**20
 PLAIN = (((1,), (0,)), ((), ()))
 
 
@@ -58,20 +58,18 @@
 
 def onward(first, second, axis):
     half = first.shape[1] // 2
-    return across(first[:, :half], axis, 2), across(second[:, half:], axis, 1)
+    return (first,), (second,), (across(first[:, :half], axis, 2), across(second[:, half:], axis, 1))
 
 
 def piece(array, order, low, start=0, column=0):
     return array, [mask | low for mask in order], start, column
 
 
-def pieces_of(own, first, second, third, order, column=0):
-    half = third[0].shape[1]
-    return ([piece(own, order, 0, 0, column)] if own is not None else []) + [
-        piece(first, order, 1, 0, column),
-        piece(second, order, 2, 0, column),
-        piece(third[0], order, 3, 0, column),
-        piece(third[1], order, 3, half, column),
+def pieces_of(neighbours, order, column=0):
+    return [
+        piece(array, order, low, start, column)
+        for low, halves in enumerate(neighbours, 1)
+        for array, start in zip(halves, (0, halves[0].shape[1]))
     ]
 
 
@@ -89,25 +87,21 @@
 
     factor_line = spread(factor_part, masks[:1], axis)
     own = around(everything, axis)
-    jacobian, factor_line = lax.optimization_barrier((jacobian, factor_line))
+    (jacobian, factor_line), own = lax.optimization_barrier(((jacobian, factor_line), own))
     factor_line = spread(factor_line, masks[1:], axis)
-    jacobian_line = spread(jacobian, masks[:1], axis)
+    jacobian_line = spread(jacobian, masks, axis)
+    own = onward(*own, axis)
     factor_line, own = lax.optimization_barrier((factor_line, own))
-    own_third = onward(*own, axis)
-    factor_rest = around(factor_line[1:], axis)
-    jacobian_line = spread(jacobian_line, masks[1:], axis)
-    factor_rest, jacobian_line = lax.optimization_barrier((factor_rest, jacobian_line))
-    factor_third = onward(*factor_rest, axis)
-    jacobian_rest = around(jacobian_line[1:], axis)
+    factor_rest = onward(*around(factor_line[1:], axis), axis)
     late, jacobian_line = lax.optimization_barrier((right_side, jacobian_line))
-    jacobian_third = onward(*jacobian_rest, axis)
+    jacobian_rest = onward(*around(jacobian_line[1:], axis), axis)
 
     factor = [piece(factor_line, order, 0)]
-    factor += pieces_of(None, *own, own_third, order[:1])
-    factor += pieces_of(None, *factor_rest, factor_third, order[1:])
+    factor += pieces_of(own, order[:1])
+    factor += pieces_of(factor_rest, order[1:])
     jacobians = [piece(jacobian_line, order, 0)]
-    jacobians += pieces_of(None, *own, own_third, order[:1], split_at)
-    jacobians += pieces_of(None, *jacobian_rest, jacobian_third, order[1:])
+    jacobians += pieces_of(own, order[:1], split_at)
+    jacobians += pieces_of(jacobian_rest, order[1:])
     return factor, jacobians, late
 
 

time: 82 us -> 74.7 us (0.911)
  starting transfers between devices: 27 us -> 22.7 us
  waiting for transfers between devices: 23.8 us -> 20.6 us
  Pallas kernels: 15.4 us -> 14.2 us
  other arithmetic: 1.97 us -> 3.13 us
    ppermute x16, starting transfers between devices: 26.4 us -> 22.2 us  [across(): lax.ppermute(value, axis, [(i, i ^ mask) for i in range(lax.axis_size(axi...]
    ppermute x16, waiting for transfers between devices: 23.8 us -> 20.6 us  [across(): lax.ppermute(value, axis, [(i, i ^ mask) for i in range(lax.axis_size(axi...]
    pallas_call x1, Pallas kernels: 7.64 us -> 6.42 us  [solve(): pl.pallas_call(kernel, out_shape=shapes([(span, columns)] + [(span, size)...]
    concatenate x4, other arithmetic: 0.13 us -> 1.25 us  [spread(): held = jnp.concatenate([held, across(held, axis, mask)])]
    unnamed x58 -> x62, local copies, waits for them, and re-layouts: 8.69 us -> 8.23 us
  transfers between devices with their start and end apart: 18 -> 18, of which waited for: 10 -> 11; matrix products, arithmetic and copies ran while one was open for 6% -> 9% of each run, Pallas kernels for 13% -> 13%
where the time goes in v3:
time: 74.7 us; the launch traced here: 74.3 us
  starting transfers between devices  22.7 us (30%)
  waiting for transfers between devices  20.6 us (28%)
  Pallas kernels  14.2 us (19%)
  local copies, waits for them, and re-layouts  12.7 us (17%)
  other arithmetic  3.13 us (4%)
  between operations  0.96 us (1%)
    ppermute x16, starting transfers between devices, across(): lax.ppermute(value, axis, [(i, i ^ mask) for i in range(lax.axis_size(axi...  22.2 us
    ppermute x16, waiting for transfers between devices, across(): lax.ppermute(value, axis, [(i, i ^ mask) for i in range(lax.axis_size(axi...  20.6 us
    unnamed x62, local copies, waits for them, and re-layouts  8.23 us
    pallas_call x1, Pallas kernels, solve(): pl.pallas_call(kernel, out_shape=shapes([(span, columns)] + [(span, size)...  6.42 us
    pallas_call x1, Pallas kernels, subtract_product(): pl.pallas_call(kernel, out_shape=shapes([(span, columns)])[0], in_specs=[...  4.5 us
    pallas_call x1, Pallas kernels, finish(): pl.pallas_call(kernel, out_shape=shapes([(span, columns), (size, columns)...  3.23 us
    slice x3, local copies, waits for them, and re-layouts, onward(): second[:, half:]  1.53 us
  transfers between devices with their start and end apart: 18, of which 11 were waited for; matrix products, arithmetic and copies ran while one was open for 9% of the time, Pallas kernels for 13%

profile of v3, /device:TPU:0, one launch (start us, length us, event | category | flops | bytes accessed | tf_op | source)
XLA Modules:
  0.0 74.3 jit_solution(14135929797535375139)
XLA Ops:
  1.6 3.0 %collective-permute-start.1 = (f32[1,4,16,1280]{3,2,1,0:T(8,128)S(1)}, f32[1,4,16,1280]{3,2,1,0:T(8,128)S(1)}, u32[]{:S(2)}, u32[]{:S(2)}) collective-permute-start(f32[1,4,16,1280]{3,2,1,0:T(8,128)S(1)} %pad_maximum_fusion.3), channel_id=1, source_target_pairs={{0,2},{2,0},{4,6},{6,4},{8,10},{10,8},{12,14},{14,12},{16,18},{18,... | collective-permute-start | bytes 983048 | tf_op jit(solution)/shard_map/ppermute | solution.py:28
  4.7 1.5 %collective-permute-start.2 = (f32[1,4,16,1280]{3,2,1,0:T(8,128)S(1)}, f32[1,4,16,1280]{3,2,1,0:T(8,128)S(1)}, u32[]{:S(2)}, u32[]{:S(2)}) collective-permute-start(f32[1,4,16,1280]{3,2,1,0:T(8,128)S(1)} %pad_maximum_fusion.3), channel_id=1, source_target_pairs={{0,4},{2,6},{4,0},{6,2},{8,12},{10,14},{12,8},{14,10},{16,20},{18,... | collective-permute-start | bytes 983048 | tf_op jit(solution)/shard_map/ppermute | solution.py:28
  6.2 3.6 %collective-permute-start = (f32[1,4,16,512]{3,2,1,0:T(8,128)S(1)}, f32[1,4,16,512]{3,2,1,0:T(8,128)S(1)}, u32[]{:S(2)}, u32[]{:S(2)}) collective-permute-start(f32[1,4,16,512]{3,2,1,0:T(8,128)S(1)} %maximum_bitcast_fusion), channel_id=1, source_target_pairs={{0,24},{2,26},{4,28},{6,30},{8,16},{10,18},{12,20},{14,22},{16,8},... | collective-permute-start | bytes 393224 | tf_op jit(solution)/shard_map/ppermute | solution.py:28
  9.8 3.2 %collective-permute-done = f32[1,4,16,512]{3,2,1,0:T(8,128)S(1)} collective-permute-done((f32[1,4,16,512]{3,2,1,0:T(8,128)S(1)}, f32[1,4,16,512]{3,2,1,0:T(8,128)S(1)}, u32[]{:S(2)}, u32[]{:S(2)}) %collective-permute-start) | collective-permute-done | bytes 131104 | tf_op jit(solution)/shard_map/ppermute | solution.py:28
  13.8 1.6 %collective-permute-start.5 = (f32[2,4,16,512]{3,2,1,0:T(8,128)S(1)}, f32[2,4,16,512]{3,2,1,0:T(8,128)S(1)}, u32[]{:S(2)}, u32[]{:S(2)}) collective-permute-start(f32[2,4,16,512]{3,2,1,0:T(8,128)S(1)} %pad_maximum_fusion.4), channel_id=1, source_target_pairs={{0,8},{2,10},{4,12},{6,14},{8,0},{10,2},{12,4},{14,6},{16,24},{18,... | collective-permute-start | bytes 786440 | tf_op jit(solution)/shard_map/ppermute | solution.py:28
  15.4 2.7 %collective-permute-start.3 = (f32[1,4,16,768]{3,2,1,0:T(8,128)S(1)}, f32[1,4,16,768]{3,2,1,0:T(8,128)S(1)}, u32[]{:S(2)}, u32[]{:S(2)}) collective-permute-start(f32[1,4,16,768]{3,2,1,0:T(8,128)S(1)} %bitcast.21), channel_id=1, source_target_pairs={{0,24},{2,26},{4,28},{6,30},{8,16},{10,18},{12,20},{14,22},{16,8},... | collective-permute-start | bytes 589832 | tf_op jit(solution)/shard_map/ppermute | solution.py:28
  18.1 1.3 %collective-permute-start.6 = (f32[1,2,16,1280]{3,2,1,0:T(8,128)S(1)}, f32[1,2,16,1280]{3,2,1,0:T(8,128)S(1)}, u32[]{:S(2)}, u32[]{:S(2)}) collective-permute-start(f32[1,2,16,1280]{3,2,1,0:T(8,128)S(1)} %slice.48), channel_id=1, source_target_pairs={{0,4},{2,6},{4,0},{6,2},{8,12},{10,14},{12,8},{14,10},{16,20},{18,... | collective-permute-start | bytes 491528 | tf_op jit(solution)/shard_map/ppermute | solution.py:28
  20.1 2.0 %collective-permute-done.5 = f32[2,4,16,512]{3,2,1,0:T(8,128)S(1)} collective-permute-done((f32[2,4,16,512]{3,2,1,0:T(8,128)S(1)}, f32[2,4,16,512]{3,2,1,0:T(8,128)S(1)}, u32[]{:S(2)}, u32[]{:S(2)}) %collective-permute-start.5) | collective-permute-done | bytes 262176 | tf_op jit(solution)/shard_map/ppermute | solution.py:28
  22.2 1.3 %collective-permute-done.6.refs_6_.refs_8_ = f32[1,2,16,1280]{3,2,1,0:T(8,128)S(1)} collective-permute-done((f32[1,2,16,1280]{3,2,1,0:T(8,128)S(1)}, f32[1,2,16,1280]{3,2,1,0:T(8,128)S(1)}, u32[]{:S(2)}, u32[]{:S(2)}) %collective-permute-start.6) | collective-permute-done | bytes 163872 | tf_op jit(solution)/shard_map/ppermute | solution.py:28
  23.5 1.4 %collective-permute-done.7.refs_7_.refs_9_ = f32[1,2,16,1280]{3,2,1,0:T(8,128)S(1)} collective-permute-done((f32[1,2,16,1280]{3,2,1,0:T(8,128)S(1)}, f32[1,2,16,1280]{3,2,1,0:T(8,128)S(1)}, u32[]{:S(2)}, u32[]{:S(2)}) %collective-permute-start.7) | collective-permute-done | bytes 163872 | tf_op jit(solution)/shard_map/ppermute | solution.py:28
  27.4 6.2 %collective-permute-done.8.refs_8_ = f32[3,4,16,512]{3,2,1,0:T(8,128)S(1)} collective-permute-done((f32[3,4,16,512]{3,2,1,0:T(8,128)S(1)}, f32[3,4,16,512]{3,2,1,0:T(8,128)S(1)}, u32[]{:S(2)}, u32[]{:S(2)}) %collective-permute-start.8) | collective-permute-done | bytes 393248 | tf_op jit(solution)/shard_map/ppermute | solution.py:28
  34.2 1.3 %collective-permute-done.9.refs_9_ = f32[3,4,16,512]{3,2,1,0:T(8,128)S(1)} collective-permute-done((f32[3,4,16,512]{3,2,1,0:T(8,128)S(1)}, f32[3,4,16,512]{3,2,1,0:T(8,128)S(1)}, u32[]{:S(2)}, u32[]{:S(2)}) %collective-permute-start.9) | collective-permute-done | bytes 393248 | tf_op jit(solution)/shard_map/ppermute | solution.py:28
  36.3 1.9 %collective-permute-start.11 = (f32[3,2,16,512]{3,2,1,0:T(8,128)}, f32[3,2,16,512]{3,2,1,0:T(8,128)S(1)}, u32[]{:S(2)}, u32[]{:S(2)}) collective-permute-start(f32[3,2,16,512]{3,2,1,0:T(8,128)} %slice.65), channel_id=1, source_target_pairs={{0,2},{2,0},{4,6},{6,4},{8,10},{10,8},{12,14},{14,12},{16,18},{18,... | collective-permute-start | bytes 589832 | tf_op jit(solution)/shard_map/ppermute | solution.py:28
  38.4 1.2 %pad_maximum_fusion.refs_5_ = f32[4,4,16,768]{3,2,1,0:T(8,128)S(1)} fusion(f32[2,4,16,768]{3,2,1,0:T(8,128)} %collective-permute-done.4, f32[1,4,16,768]{3,2,1,0:T(8,128)S(1)} %collective-permute-done.3, f32[1,4,16,768]{3,2,1,0:T(8,128)S(1)} %bitcast.23), kind=kLoop, calls=%fused_computation | loop fusion | flops 393216 | bytes 1572864 | tf_op jit(solution)/shard_map/concatenate | solution.py:44
  39.8 1.1 %collective-permute-start.15 = (f32[3,4,16,768]{3,2,1,0:T(8,128)S(1)}, f32[3,4,16,768]{3,2,1,0:T(8,128)S(1)}, u32[]{:S(2)}, u32[]{:S(2)}) collective-permute-start(f32[3,4,16,768]{3,2,1,0:T(8,128)S(1)} %slice.61), channel_id=1, source_target_pairs={{0,4},{2,6},{4,0},{6,2},{8,12},{10,14},{12,8},{14,10},{16,20},{18,... | collective-permute-start | bytes 1769480 | tf_op jit(solution)/shard_map/ppermute | solution.py:28
  42.2 2.0 %collective-permute-done.11.refs_11_ = f32[3,2,16,512]{3,2,1,0:T(8,128)S(1)} collective-permute-done((f32[3,2,16,512]{3,2,1,0:T(8,128)}, f32[3,2,16,512]{3,2,1,0:T(8,128)S(1)}, u32[]{:S(2)}, u32[]{:S(2)}) %collective-permute-start.11) | collective-permute-done | bytes 196640 | tf_op jit(solution)/shard_map/ppermute | solution.py:28
  47.7 6.4 %solve.1 = (f32[1024,256]{1,0:T(8,128)S(1)}, f32[1024,256]{1,0:T(8,128)S(1)}, f32[256,512]{1,0:T(8,128)S(1)}, f32[256,512]{1,0:T(8,128)S(1)}) custom-call(s32[1]{0:T(128)} %bitcast.refs_0_.node_ref, f32[4,4,256]{2,1,0:T(4,128)S(1)} %reshape.14.refs_1_, f32[1024,256]{1,0:T(8,128)S(1)} %copy-done, f32[4,4,16,512]{3,2,1,0:T(8,128)S(1)} %pad_maximum_fusion.1.refs_3_, ...), custom_call_target="tpu_custom_call" | custom-call | flops 536870912 | bytes 262144 | tf_op jit(solution)/shard_map/solve/pallas_call | solution.py:201
  57.5 1.3 %collective-permute-start.16 = (f32[3,2,16,768]{3,2,1,0:T(8,128)}, f32[3,2,16,768]{3,2,1,0:T(8,128)}, u32[]{:S(2)}, u32[]{:S(2)}) collective-permute-start(f32[3,2,16,768]{3,2,1,0:T(8,128)} %slice.66), channel_id=1, source_target_pairs={{0,4},{2,6},{4,0},{6,2},{8,12},{10,14},{12,8},{14,10},{16,20},{18,... | collective-permute-start | bytes 884744 | tf_op jit(solution)/shard_map/ppermute | solution.py:28
  61.3 1.0 %reshape.15.refs_0_ = f32[4,4,768]{2,1,0:T(4,128)S(1)} reshape(f32[4,4,12,64]{3,2,1,0:T(8,128)} %broadcast_in_dim.15) | data formatting | bytes 98304 | tf_op jit(solution)/shard_map/reshape | solution.py:314
  62.3 1.2 %copy-done.2 = f32[1024,256]{1,0:T(8,128)S(1)} copy-done((f32[1024,256]{1,0:T(8,128)S(1)}, f32[1024,256]{1,0:T(8,128)}, u32[]{:S(2)}) %copy-start.2) | copy-done | bytes 1048600
  63.6 3.2 %finish.1 = (f32[1024,256]{1,0:T(8,128)}, f32[256,256]{1,0:T(8,128)S(1)}, f32[256,256]{1,0:T(8,128)S(1)}) custom-call(s32[1]{0:T(128)} %bitcast.refs_0_.node_ref, f32[1024,256]{1,0:T(8,128)S(1)} %get-tuple-element.30.sol_ref, f32[1024,256]{1,0:T(8,128)S(1)} %copy-done.2, f32[2,256,256]{2,1,0:T(8,128)S(1)} %maximum_select_fusion.own_ref, ...), custom_call_target="tpu_custom_call" | custom-call | flops 100663296 | bytes 262144 | tf_op jit(solution)/shard_map/finish/pallas_call | solution.py:239
  66.8 1.7 %collective-permute-done.17.refs_13_ = f32[3,2,16,768]{3,2,1,0:T(8,128)} collective-permute-done((f32[3,2,16,768]{3,2,1,0:T(8,128)}, f32[3,2,16,768]{3,2,1,0:T(8,128)}, u32[]{:S(2)}, u32[]{:S(2)}) %collective-permute-start.17) | collective-permute-done | bytes 294944 | tf_op jit(solution)/shard_map/ppermute | solution.py:28
  68.6 1.2 %copy-done.13 = f32[1024,256]{1,0:T(8,128)S(1)} copy-done((f32[1024,256]{1,0:T(8,128)S(1)}, f32[1024,256]{1,0:T(8,128)}, u32[]{:S(2)}) %copy-start.13) | copy-done | bytes 1048600
  69.8 4.5 %residual.1 = f32[1024,256]{1,0:T(8,128)} custom-call(f32[4,4,768]{2,1,0:T(4,128)S(1)} %reshape.15.refs_0_, f32[1024,256]{1,0:T(8,128)S(1)} %copy-done, f32[1024,256]{1,0:T(8,128)S(1)} %copy-done.13, f32[256,256]{1,0:T(8,128)S(1)} %get-tuple-element.35.refs_3_, f32[256,256]{1,0:T(8,128)S(1)} %get-tuple-element.36.refs_4_, ...), custom_call_target="tpu_custom_call" | custom-call | flops 1207959552 | bytes 6291456 | tf_op jit(solution)/shard_map/residual/pallas_call | solution.py:283
  (101 shorter events, 17.2 us)
Async XLA Ops:
  1.6 11.4 %collective-permute-start.1 = (f32[1,4,16,1280]{3,2,1,0:T(8,128)S(1)}, f32[1,4,16,1280]{3,2,1,0:T(8,128)S(1)}, u32[]{:S(2)}, u32[]{:S(2)}) collective-permute-start(f32[1,4,16,1280]{3,2,1,0:T(8,128)S(1)} %pad_maximum_fusion.3), channel_id=1, source_target_pairs={{0,2},{2,0},{4,6},{6,4},{8,10},{10,8},{12,14},{14,12},{16,18},{18,... | collective-permute-start | bytes 983048 | tf_op jit(solution)/shard_map/ppermute | solution.py:28
  4.7 9.2 %collective-permute-start.2 = (f32[1,4,16,1280]{3,2,1,0:T(8,128)S(1)}, f32[1,4,16,1280]{3,2,1,0:T(8,128)S(1)}, u32[]{:S(2)}, u32[]{:S(2)}) collective-permute-start(f32[1,4,16,1280]{3,2,1,0:T(8,128)S(1)} %pad_maximum_fusion.3), channel_id=1, source_target_pairs={{0,4},{2,6},{4,0},{6,2},{8,12},{10,14},{12,8},{14,10},{16,20},{18,... | collective-permute-start | bytes 983048 | tf_op jit(solution)/shard_map/ppermute | solution.py:28
  6.2 6.8 %collective-permute-start = (f32[1,4,16,512]{3,2,1,0:T(8,128)S(1)}, f32[1,4,16,512]{3,2,1,0:T(8,128)S(1)}, u32[]{:S(2)}, u32[]{:S(2)}) collective-permute-start(f32[1,4,16,512]{3,2,1,0:T(8,128)S(1)} %maximum_bitcast_fusion), channel_id=1, source_target_pairs={{0,24},{2,26},{4,28},{6,30},{8,16},{10,18},{12,20},{14,22},{16,8},... | collective-permute-start | bytes 393224 | tf_op jit(solution)/shard_map/ppermute | solution.py:28
  13.0 6.5 %copy-start.3 = (f32[1,4,16,1280]{3,2,1,0:T(8,128)}, f32[1,4,16,1280]{3,2,1,0:T(8,128)S(1)}, u32[]{:S(2)}) copy-start(f32[1,4,16,1280]{3,2,1,0:T(8,128)S(1)} %collective-permute-done.1.refs_4_.refs_6_) | copy-start | bytes 983044
  13.8 5.7 %copy-start.6 = (f32[1,4,16,1280]{3,2,1,0:T(8,128)}, f32[1,4,16,1280]{3,2,1,0:T(8,128)S(1)}, u32[]{:S(2)}) copy-start(f32[1,4,16,1280]{3,2,1,0:T(8,128)S(1)} %collective-permute-done.2.refs_5_.refs_7_) | copy-start | bytes 983044
  13.8 8.3 %collective-permute-start.5 = (f32[2,4,16,512]{3,2,1,0:T(8,128)S(1)}, f32[2,4,16,512]{3,2,1,0:T(8,128)S(1)}, u32[]{:S(2)}, u32[]{:S(2)}) collective-permute-start(f32[2,4,16,512]{3,2,1,0:T(8,128)S(1)} %pad_maximum_fusion.4), channel_id=1, source_target_pairs={{0,8},{2,10},{4,12},{6,14},{8,0},{10,2},{12,4},{14,6},{16,24},{18,... | collective-permute-start | bytes 786440 | tf_op jit(solution)/shard_map/ppermute | solution.py:28
  15.4 11.5 %collective-permute-start.3 = (f32[1,4,16,768]{3,2,1,0:T(8,128)S(1)}, f32[1,4,16,768]{3,2,1,0:T(8,128)S(1)}, u32[]{:S(2)}, u32[]{:S(2)}) collective-permute-start(f32[1,4,16,768]{3,2,1,0:T(8,128)S(1)} %bitcast.21), channel_id=1, source_target_pairs={{0,24},{2,26},{4,28},{6,30},{8,16},{10,18},{12,20},{14,22},{16,8},... | collective-permute-start | bytes 589832 | tf_op jit(solution)/shard_map/ppermute | solution.py:28
  18.1 5.4 %collective-permute-start.6 = (f32[1,2,16,1280]{3,2,1,0:T(8,128)S(1)}, f32[1,2,16,1280]{3,2,1,0:T(8,128)S(1)}, u32[]{:S(2)}, u32[]{:S(2)}) collective-permute-start(f32[1,2,16,1280]{3,2,1,0:T(8,128)S(1)} %slice.48), channel_id=1, source_target_pairs={{0,4},{2,6},{4,0},{6,2},{8,12},{10,14},{12,8},{14,10},{16,20},{18,... | collective-permute-start | bytes 491528 | tf_op jit(solution)/shard_map/ppermute | solution.py:28
  19.5 5.4 %collective-permute-start.7 = (f32[1,2,16,1280]{3,2,1,0:T(8,128)S(1)}, f32[1,2,16,1280]{3,2,1,0:T(8,128)S(1)}, u32[]{:S(2)}, u32[]{:S(2)}) collective-permute-start(f32[1,2,16,1280]{3,2,1,0:T(8,128)S(1)} %slice.49), channel_id=1, source_target_pairs={{0,2},{2,0},{4,6},{6,4},{8,10},{10,8},{12,14},{14,12},{16,18},{18,... | collective-permute-start | bytes 491528 | tf_op jit(solution)/shard_map/ppermute | solution.py:28
  25.6 8.1 %collective-permute-start.8 = (f32[3,4,16,512]{3,2,1,0:T(8,128)S(1)}, f32[3,4,16,512]{3,2,1,0:T(8,128)S(1)}, u32[]{:S(2)}, u32[]{:S(2)}) collective-permute-start(f32[3,4,16,512]{3,2,1,0:T(8,128)S(1)} %slice.50), channel_id=1, source_target_pairs={{0,2},{2,0},{4,6},{6,4},{8,10},{10,8},{12,14},{14,12},{16,18},{18,... | collective-permute-start | bytes 1179656 | tf_op jit(solution)/shard_map/ppermute | solution.py:28
  26.1 9.4 %collective-permute-start.9 = (f32[3,4,16,512]{3,2,1,0:T(8,128)S(1)}, f32[3,4,16,512]{3,2,1,0:T(8,128)S(1)}, u32[]{:S(2)}, u32[]{:S(2)}) collective-permute-start(f32[3,4,16,512]{3,2,1,0:T(8,128)S(1)} %slice.50), channel_id=1, source_target_pairs={{0,4},{2,6},{4,0},{6,2},{8,12},{10,14},{12,8},{14,10},{16,20},{18,... | collective-permute-start | bytes 1179656 | tf_op jit(solution)/shard_map/ppermute | solution.py:28
  27.0 11.5 %collective-permute-start.4 = (f32[2,4,16,768]{3,2,1,0:T(8,128)S(1)}, f32[2,4,16,768]{3,2,1,0:T(8,128)}, u32[]{:S(2)}, u32[]{:S(2)}) collective-permute-start(f32[2,4,16,768]{3,2,1,0:T(8,128)S(1)} %pad_maximum_fusion.2), channel_id=1, source_target_pairs={{0,8},{2,10},{4,12},{6,14},{8,0},{10,2},{12,4},{14,6},{16,24},{18,... | collective-permute-start | bytes 1179656 | tf_op jit(solution)/shard_map/ppermute | solution.py:28
  33.7 7.9 %collective-permute-start.10 = (f32[3,2,16,512]{3,2,1,0:T(8,128)S(1)}, f32[3,2,16,512]{3,2,1,0:T(8,128)S(1)}, u32[]{:S(2)}, u32[]{:S(2)}) collective-permute-start(f32[3,2,16,512]{3,2,1,0:T(8,128)S(1)} %slice.64), channel_id=1, source_target_pairs={{0,4},{2,6},{4,0},{6,2},{8,12},{10,14},{12,8},{14,10},{16,20},{18,... | collective-permute-start | bytes 589832 | tf_op jit(solution)/shard_map/ppermute | solution.py:28
  36.3 7.9 %collective-permute-start.11 = (f32[3,2,16,512]{3,2,1,0:T(8,128)}, f32[3,2,16,512]{3,2,1,0:T(8,128)S(1)}, u32[]{:S(2)}, u32[]{:S(2)}) collective-permute-start(f32[3,2,16,512]{3,2,1,0:T(8,128)} %slice.65), channel_id=1, source_target_pairs={{0,2},{2,0},{4,6},{6,4},{8,10},{10,8},{12,14},{14,12},{16,18},{18,... | collective-permute-start | bytes 589832 | tf_op jit(solution)/shard_map/ppermute | solution.py:28
  38.4 6.5 %copy-start = (f32[1024,256]{1,0:T(8,128)S(1)}, f32[1024,256]{1,0:T(8,128)}, u32[]{:S(2)}) copy-start(f32[1024,256]{1,0:T(8,128)} %refs_1_.1) | copy-start | bytes 3145732
  38.4 6.5 %copy-start.17 = (f32[3,4,16,512]{3,2,1,0:T(8,128)S(1)}, f32[3,4,16,512]{3,2,1,0:T(8,128)}, u32[]{:S(2)}) copy-start(f32[3,4,16,512]{3,2,1,0:T(8,128)} %copy-done.16) | copy-start | bytes 1179652
  38.4 6.5 %copy-start.19 = (f32[1,2,16,1280]{3,2,1,0:T(8,128)S(1)}, f32[1,2,16,1280]{3,2,1,0:T(8,128)}, u32[]{:S(2)}) copy-start(f32[1,2,16,1280]{3,2,1,0:T(8,128)} %copy-done.18) | copy-start | bytes 491524
  39.6 5.3 %copy-start.4 = (f32[1,4,16,1280]{3,2,1,0:T(8,128)S(1)}, f32[1,4,16,1280]{3,2,1,0:T(8,128)}, u32[]{:S(2)}) copy-start(f32[1,4,16,1280]{3,2,1,0:T(8,128)} %copy-done.3) | copy-start | bytes 983044
  39.7 17.0 %collective-permute-start.14 = (f32[3,4,16,768]{3,2,1,0:T(8,128)S(1)}, f32[3,4,16,768]{3,2,1,0:T(8,128)S(1)}, u32[]{:S(2)}, u32[]{:S(2)}) collective-permute-start(f32[3,4,16,768]{3,2,1,0:T(8,128)S(1)} %slice.61), channel_id=1, source_target_pairs={{0,2},{2,0},{4,6},{6,4},{8,10},{10,8},{12,14},{14,12},{16,18},{18,... | collective-permute-start | bytes 1769480 | tf_op jit(solution)/shard_map/ppermute | solution.py:28
  39.8 18.9 %collective-permute-start.15 = (f32[3,4,16,768]{3,2,1,0:T(8,128)S(1)}, f32[3,4,16,768]{3,2,1,0:T(8,128)S(1)}, u32[]{:S(2)}, u32[]{:S(2)}) collective-permute-start(f32[3,4,16,768]{3,2,1,0:T(8,128)S(1)} %slice.61), channel_id=1, source_target_pairs={{0,4},{2,6},{4,0},{6,2},{8,12},{10,14},{12,8},{14,10},{16,20},{18,... | collective-permute-start | bytes 1769480 | tf_op jit(solution)/shard_map/ppermute | solution.py:28
  56.0 6.3 %collective-permute-start.13 = (f32[2,256,256]{2,1,0:T(8,128)}, f32[2,256,256]{2,1,0:T(8,128)}, u32[]{:S(2)}, u32[]{:S(2)}) collective-permute-start(f32[2,256,256]{2,1,0:T(8,128)} %maximum_select_fusion.1), channel_id=1, source_target_pairs={{0,1},{1,0},{2,3},{3,2},{4,5},{5,4},{6,7},{7,6},{8,9},{9,8},{10,11... | collective-permute-start | bytes 1572872 | tf_op jit(solution)/shard_map/ppermute | solution.py:342
  56.1 6.1 %collective-permute-start.12 = (f32[2,256,256]{2,1,0:T(8,128)S(1)}, f32[2,256,256]{2,1,0:T(8,128)}, u32[]{:S(2)}, u32[]{:S(2)}) collective-permute-start(f32[2,256,256]{2,1,0:T(8,128)S(1)} %maximum_select_fusion.own_ref), channel_id=1, source_target_pairs={{0,1},{1,0},{2,3},{3,2},{4,5},{5,4},{6,7},{7,6},{8,9},{9,8},{10,11... | collective-permute-start | bytes 1572872 | tf_op jit(solution)/shard_map/ppermute | solution.py:342
  57.5 9.3 %collective-permute-start.16 = (f32[3,2,16,768]{3,2,1,0:T(8,128)}, f32[3,2,16,768]{3,2,1,0:T(8,128)}, u32[]{:S(2)}, u32[]{:S(2)}) collective-permute-start(f32[3,2,16,768]{3,2,1,0:T(8,128)} %slice.66), channel_id=1, source_target_pairs={{0,4},{2,6},{4,0},{6,2},{8,12},{10,14},{12,8},{14,10},{16,20},{18,... | collective-permute-start | bytes 884744 | tf_op jit(solution)/shard_map/ppermute | solution.py:28
  59.5 9.0 %collective-permute-start.17 = (f32[3,2,16,768]{3,2,1,0:T(8,128)}, f32[3,2,16,768]{3,2,1,0:T(8,128)}, u32[]{:S(2)}, u32[]{:S(2)}) collective-permute-start(f32[3,2,16,768]{3,2,1,0:T(8,128)} %slice.67), channel_id=1, source_target_pairs={{0,2},{2,0},{4,6},{6,4},{8,10},{10,8},{12,14},{14,12},{16,18},{18,... | collective-permute-start | bytes 884744 | tf_op jit(solution)/shard_map/ppermute | solution.py:28
  (25 other events, 66.9 us)

commit v4 on v3

v4 whole, which is shorter than its diff:
```python
import functools

import jax
import jax.numpy as jnp
from jax import lax
from jax.experimental import pallas as pl
from jax.experimental.pallas import tpu as pltpu
from jax.sharding import PartitionSpec as P

VMEM = pl.BlockSpec(memory_space=pltpu.VMEM)
SMEM = pl.BlockSpec(memory_space=pltpu.SMEM)
ANY = pl.BlockSpec(memory_space=pl.ANY)
VMEM_LIMIT = 20 * 2**20
PLAIN = (((1,), (0,)), ((), ()))


def split(value):
    high = value.astype(jnp.bfloat16)
    return high, (value - high.astype(jnp.float32)).astype(jnp.bfloat16)


def product(left, right, dims=PLAIN):
    dot = functools.partial(lax.dot_general, dimension_numbers=dims, preferred_element_type=jnp.float32)
    return dot(left[0], right[1]) + dot(left[1], right[0]) + dot(left[0], right[0])


def across(value, axis, mask):
    return lax.ppermute(value, axis, [(i, i ^ mask) for i in range(lax.axis_size(axis))])


def line_masks(axis):
    high = lax.axis_size(axis) // 4
    return [4 * (step - 1) for step in iter_halves(high)]


def iter_halves(step):
    while step > 1:
        yield step
        step //= 2


def spread(held, masks, axis):
    for mask in masks:
        held = jnp.concatenate([held, across(held, axis, mask)])
    return held


def line_order(masks):
    order = [0]
    for mask in masks:
        order += [mask ^ other for other in order]
    return order


def around(held, axis):
    return across(held, axis, 1), across(held, axis, 2)


def onward(first, second, axis):
    half = first.shape[1] // 2
    return (first,), (second,), (across(first[:, :half], axis, 2), across(second[:, half:], axis, 1))


def piece(array, order, low, start=0, column=0):
    return array, [mask | low for mask in order], start, column


def pieces_of(neighbours, order, column=0):
    return [
        piece(array, order, low, start, column)
        for low, halves in enumerate(neighbours, 1)
        for array, start in zip(halves, (0, halves[0].shape[1]))
    ]


def gather_whole(part, axis):
    everything = lax.all_gather(part, axis)
    return [piece(everything, list(range(lax.axis_size(axis))), 0)]


def gather_panels(factor_part, jacobian, right_side, axis):
    masks = line_masks(axis)
    order = line_order(masks)
    factor_part, jacobian = factor_part[None], jacobian[None]
    everything = jnp.concatenate([factor_part, jacobian], axis=3)
    split_at = factor_part.shape[3]

    factor_line = spread(factor_part, masks[:1], axis)
    own = around(everything, axis)
    (jacobian, factor_line), own = lax.optimization_barrier(((jacobian, factor_line), own))
    factor_line = spread(factor_line, masks[1:], axis)
    jacobian_line = spread(jacobian, masks[:1], axis)
    own = onward(*own, axis)
    factor_line, jacobian_line, own = lax.optimization_barrier((factor_line, jacobian_line, own))
    factor_rest = around(factor_line[1:], axis)
    jacobian_line = spread(jacobian_line, masks[1:], axis)
    late, jacobian_line, _ = lax.optimization_barrier((right_side, jacobian_line, factor_rest))
    factor_rest = onward(*factor_rest, axis)
    jacobian_rest = onward(*around(jacobian_line[1:], axis), axis)

    factor = [piece(factor_line, order, 0)]
    factor += pieces_of(own, order[:1])
    factor += pieces_of(factor_rest, order[1:])
    jacobians = [piece(jacobian_line, order, 0)]
    jacobians += pieces_of(own, order[:1], split_at)
    jacobians += pieces_of(jacobian_rest, order[1:])
    return factor, jacobians, late


def place_rows(pieces, refs, relative, axis, panels, sem):
    me = lax.axis_index(axis)
    wide = panels.shape[2]
    copies = []
    for (array, owners, start, column), ref in zip(pieces, refs):
        parts, rows = array.shape[1:3]
        for place, owner in enumerate(owners):
            at = pl.multiple_of((me ^ owner) * rows, rows) if relative else owner * rows
            copies.append(
                pltpu.make_async_copy(
                    ref.at[place, :, :, pl.ds(column, wide)],
                    panels.at[pl.ds(start, parts), pl.ds(at, rows), :],
                    sem.at[len(copies)],
                )
            )
    for copy in copies:
        copy.start()
    return copies


def shapes(arrays):
    return [jax.ShapeDtypeStruct(shape, jnp.float32) for shape in arrays]


def masked(rows, pattern_ref, s, block_rows):
    wide = rows.shape[1]
    blocks = wide // pattern_ref.shape[2]
    together = max(1, 128 // blocks)
    lane = lax.broadcasted_iota(jnp.int32, (1, together * blocks), 1)
    bands = []
    for a in range(pattern_ref.shape[1]):
        weights = []
        for first in range(0, pattern_ref.shape[2], together):
            chosen = pattern_ref[s, a, first]
            weight = jnp.full(lane.shape, chosen.astype(jnp.float32))
            for c in range(1, min(together, pattern_ref.shape[2] - first)):
                weight = jnp.where(lane >= c * blocks, pattern_ref[s, a, first + c].astype(jnp.float32), weight)
            weights.append(weight)
        weights = jnp.concatenate(weights, axis=1)[:, :wide]
        bands.append(rows[a * block_rows : (a + 1) * block_rows] * weights)
    return jnp.concatenate(bands, axis=0)


def solve(pieces, relative, right_side, pattern, nodes, supers, size):
    columns = right_side.shape[1]
    extra = 0 if nodes == 1 else 1 if nodes == 2 else 2
    width = columns + extra * size
    n = len(pieces)
    n_copies = sum(len(owners) for _, owners, _, _ in pieces)

    def kernel(*refs):
        pattern_ref, rhs_ref = refs[:2]
        piece_refs = refs[2 : 2 + n]
        sol_ref = refs[2 + n]
        extra_refs = refs[3 + n : 3 + n + extra]
        down_ref, up_ref, panels, forward, sem = refs[3 + n + extra :]
        copies = place_rows(pieces, piece_refs, relative, "rhs", panels, sem)
        index = lax.axis_index("node")
        below = jnp.where(index > 0, 1.0, 0.0)
        above = jnp.where(index < nodes - 1, 1.0, 0.0)
        on_diagonal = lax.broadcasted_iota(jnp.int32, (size, size), 0) == lax.broadcasted_iota(
            jnp.int32, (size, size), 1
        )
        zeros = jnp.zeros((size, size), jnp.float32)
        for copy in copies:
            copy.wait()

        previous = None
        for s in range(supers):
            own = rhs_ref[s * size : (s + 1) * size, :]
            low = masked(panels[s, :, size:], pattern_ref, s, size // pattern_ref.shape[1])
            panels[s, :, size:] = low
            if s == 0:
                parts = [own]
                if extra:
                    parts.append(low * -below)
                if extra == 2:
                    parts.append(zeros)
                target = jnp.concatenate(parts, axis=1)
            else:
                target = jnp.concatenate([own] + [zeros] * extra, axis=1) - product(split(low), split(previous))
            previous = product(split(panels[s, :, :size]), split(target))
            forward[s] = previous

        entering = None
        for s in reversed(range(supers)):
            target = forward[s]
            if s == supers - 1:
                if extra:
                    unit = jnp.where(on_diagonal, above, 0.0)
                    shift = [jnp.zeros((size, columns), jnp.float32)] + [zeros] * (extra - 1) + [unit]
                    target = target - jnp.concatenate(shift, axis=1)
            else:
                target = target - entering
            solved = product(split(panels[s, :, :size].T), split(target))
            sol_ref[s * size : (s + 1) * size, :] = solved[:, :columns]
            for e, ref in enumerate(extra_refs):
                ref[s * size : (s + 1) * size, :] = solved[:, columns + e * size : columns + (e + 1) * size]
            if s > 0 or nodes > 1:
                entering = product(split(panels[s, :, size:].T), split(solved))

        if nodes == 2:
            upper = index == 1
            span = supers * size
            down_ref[0] = jnp.where(upper, entering[:, :columns], forward[supers - 1, :, :columns])
            down_ref[1] = entering[:, columns:]
            up_ref[0] = jnp.where(upper, sol_ref[:size, :], sol_ref[span - size :, :])
            up_ref[1] = jnp.where(upper, extra_refs[0][:size, :], extra_refs[0][span - size :, :])
        else:
            down_ref[...] = forward[supers - 1]
            up_ref[...] = entering if nodes > 1 else forward[0]

    span = supers * size
    leaving = (2, size, columns) if nodes == 2 else (size, width)
    out = pl.pallas_call(
        kernel,
        out_shape=shapes([(span, columns)] + [(span, size)] * extra + [leaving] * 2),
        in_specs=[SMEM, VMEM] + [ANY] * n,
        out_specs=[VMEM] * (3 + extra),
        scratch_shapes=[
            pltpu.VMEM((supers, size, 2 * size), jnp.float32),
            pltpu.VMEM((supers, size, width), jnp.float32),
            pltpu.SemaphoreType.DMA((n_copies,)),
        ],
        compiler_params=pltpu.CompilerParams(vmem_limit_bytes=VMEM_LIMIT),
        cost_estimate=pl.CostEstimate(
            flops=4 * supers * size * size * width, bytes_accessed=span * size, transcendentals=0
        ),
        name="solve",
    )(pattern, right_side, *[array for array, *_ in pieces])
    return out[0], out[1 : 1 + extra], out[1 + extra], out[2 + extra]


def finish(sol, part, own_mail, mail, beside_mail, supers):
    span, columns = sol.shape
    size = span // supers

    def kernel(sol_ref, part_ref, own_ref, mail_ref, beside_ref, out_ref, high_ref, low_ref):
        lower_one = lax.axis_index("node") == 0
        down = jnp.where(lower_one, own_ref[0], mail_ref[0])
        offset = jnp.where(lower_one, mail_ref[0], own_ref[0])
        matrix = jnp.where(lower_one, mail_ref[1], own_ref[1])
        up = offset + product(split(matrix), split(down))
        mine = split(jnp.where(lower_one, up, down))
        other = split(jnp.where(lower_one, down, up))

        def window(at, value):
            high_ref[at : at + size, :], low_ref[at : at + size, :] = split(value)

        for at in range(0, span, size):
            value = sol_ref[at : at + size, :] + product(split(part_ref[at : at + size, :]), mine)
            out_ref[at : at + size, :] = value
            window(at + size, value)
        beside = beside_ref[0] + product(split(beside_ref[1]), other)
        window(0, jnp.where(lower_one, 0.0, beside))
        window(size + span, jnp.where(lower_one, beside, 0.0))

    windows = jax.ShapeDtypeStruct((span + 2 * size, columns), jnp.bfloat16)
    return pl.pallas_call(
        kernel,
        out_shape=shapes([(span, columns)]) + [windows, windows],
        in_specs=[VMEM] * 5,
        out_specs=[VMEM] * 3,
        compiler_params=pltpu.CompilerParams(vmem_limit_bytes=VMEM_LIMIT),
        cost_estimate=pl.CostEstimate(
            flops=(span + 2 * size) * size * columns, bytes_accessed=span * columns, transcendentals=0
        ),
        name="finish",
    )(sol, part, own_mail, mail, beside_mail)


def split_windows(sol, before, after):
    span, columns = sol.shape
    size = before.shape[0]

    def kernel(sol_ref, before_ref, after_ref, high_ref, low_ref):
        for at, value in ((0, before_ref[...]), (size, sol_ref[...]), (size + span, after_ref[...])):
            high, low = split(value)
            high_ref[at : at + value.shape[0], :], low_ref[at : at + value.shape[0], :] = high, low

    windows = jax.ShapeDtypeStruct((span + 2 * size, columns), jnp.bfloat16)
    return pl.pallas_call(kernel, out_shape=[windows, windows], name="windows")(sol, before, after)


def subtract_product(pieces, relative, right_side, high, low, pattern, supers, size):
    span, columns = right_side.shape
    wide = 3 * size
    n = len(pieces)
    n_copies = sum(len(owners) for _, owners, _, _ in pieces)

    def kernel(*refs):
        pattern_ref, rhs_ref, high_ref, low_ref = refs[:4]
        piece_refs = refs[4 : 4 + n]
        out_ref, panels, sem = refs[4 + n :]
        for copy in place_rows(pieces, piece_refs, relative, "rhs", panels, sem):
            copy.wait()
        for s in range(supers):
            panel = masked(panels[s], pattern_ref, s, size // pattern_ref.shape[1])
            window = pl.ds(s * size, wide)
            out_ref[s * size : (s + 1) * size, :] = rhs_ref[s * size : (s + 1) * size, :] - product(
                split(panel), (high_ref[window, :], low_ref[window, :])
            )

    return pl.pallas_call(
        kernel,
        out_shape=shapes([(span, columns)])[0],
        in_specs=[SMEM] + [VMEM] * 3 + [ANY] * n,
        out_specs=VMEM,
        scratch_shapes=[
            pltpu.VMEM((supers, size, wide), jnp.float32),
            pltpu.SemaphoreType.DMA((n_copies,)),
        ],
        compiler_params=pltpu.CompilerParams(vmem_limit_bytes=VMEM_LIMIT),
        cost_estimate=pl.CostEstimate(
            flops=6 * span * wide * columns, bytes_accessed=4 * span * (wide + 3 * columns), transcendentals=0
        ),
        name="residual",
    )(pattern, right_side, high, low, *[array for array, *_ in pieces])


def dot(left, right):
    return jnp.dot(left, right, precision=lax.Precision.HIGHEST)


def on_device(right_side, diag_inv, lower, factor_pattern, jacobian, jacobian_pattern):
    supers, rows, size = diag_inv.shape
    columns = right_side.shape[1]
    span = supers * size
    nodes = lax.axis_size("node")

    factor_part = jnp.concatenate([diag_inv, lower], axis=2)
    count = lax.axis_size("rhs")
    relative = count >= 8 and not count & (count - 1)
    late = right_side
    if relative:
        factor, jacobians, late = gather_panels(factor_part, jacobian, right_side, "rhs")
    else:
        factor = gather_whole(factor_part, "rhs")
        jacobians = gather_whole(jacobian, "rhs")

    sol, parts, down, up = solve(factor, relative, late, factor_pattern, nodes, supers, size)
    if nodes == 2:
        mail = [lax.ppermute(letter, "node", [(0, 1), (1, 0)]) for letter in (down, up)]
        sol, high, low = finish(sol, parts[0], down, *mail, supers)
    else:
        before = after = jnp.zeros((size, columns), jnp.float32)
        if nodes > 1:
            upwards = [(i, i + 1) for i in range(nodes - 1)]
            downwards = [(i + 1, i) for i in range(nodes - 1)]
            below = above = before
            for _ in range(nodes - 1):
                below = lax.ppermute(
                    down[:, :columns] + dot(down[:, columns : columns + size], below), "node", upwards
                )
            for _ in range(nodes - 1):
                leaving = up[:, :columns] + dot(up[:, columns : columns + size], below)
                above = lax.ppermute(leaving + dot(up[:, columns + size :], above), "node", downwards)
            sol = sol + dot(parts[0], below) + dot(parts[1], above)
            before = lax.ppermute(sol[span - size :], "node", upwards)
            after = lax.ppermute(sol[:size], "node", downwards)
        high, low = split_windows(sol, before, after)
    residual = subtract_product(jacobians, relative, right_side, high, low, jacobian_pattern, supers, size)
    return sol, residual


def solution(mesh):
    in_specs = (
        P("node", "rhs"),
        P("node", "rhs", None),
        P("node", "rhs", None),
        P("node", None, None),
        P("node", "rhs", None),
        P("node", None, None),
    )
    out_specs = (P("node", "rhs"), P("node", "rhs"))
    return jax.shard_map(on_device, mesh=mesh, in_specs=in_specs, out_specs=out_specs, check_vma=False)
```

time: 74.7 us -> 78.3 us (1.048)
  waiting for transfers between devices: 20.6 us -> 36.9 us
  local copies, waits for them, and re-layouts: 12.7 us -> 0.23 us
  starting transfers between devices: 22.7 us -> 25.4 us
  other arithmetic: 3.13 us -> 1.08 us
    ppermute x16, waiting for transfers between devices: 20.6 us -> 36.9 us  [across(): lax.ppermute(value, axis, [(i, i ^ mask) for i in range(lax.axis_size(axi...]
    unnamed x62 -> x8, local copies, waits for them, and re-layouts: 8.23 us -> 0.07 us
    ppermute x16, starting transfers between devices: 22.2 us -> 24.8 us  [across(): lax.ppermute(value, axis, [(i, i ^ mask) for i in range(lax.axis_size(axi...]
    slice x3, local copies, waits for them, and re-layouts: 1.53 us -> 0.05 us  [onward(): second[:, half:]]
    pallas_call x1, Pallas kernels: 3.23 us -> 1.95 us  [finish(): pl.pallas_call(kernel, out_shape=shapes([(span, columns)]) + [windows, wi...]
    concatenate x4, other arithmetic: 1.25 us -> 0.14 us  [spread(): held = jnp.concatenate([held, across(held, axis, mask)])]
    reshape x2 -> x0, local copies, waits for them, and re-layouts: 1.09 us -> none  [widened(): jnp.repeat(pattern.astype(jnp.float32), size // factor_pattern.shape[2],...]
    select_n x2 -> x0, other arithmetic: 0.93 us -> none  [on_device(): jnp.where(is_lower, jnp.stack(lower_mail), jnp.stack(upper_mail))]
  transfers between devices with their start and end apart: 18 -> 18, of which waited for: 11 -> 10; matrix products, arithmetic and copies ran while one was open for 9% -> 0% of each run, Pallas kernels for 13% -> 12%
where the time goes in v4:
time: 78.3 us; the launch traced here: 78.1 us
  waiting for transfers between devices  36.9 us (47%)
  starting transfers between devices  25.4 us (32%)
  Pallas kernels  13.7 us (17%)
  other arithmetic  1.08 us (1%)
    ppermute x16, waiting for transfers between devices, across(): lax.ppermute(value, axis, [(i, i ^ mask) for i in range(lax.axis_size(axi...  36.9 us
    ppermute x16, starting transfers between devices, across(): lax.ppermute(value, axis, [(i, i ^ mask) for i in range(lax.axis_size(axi...  24.8 us
    pallas_call x1, Pallas kernels, solve(): pl.pallas_call(kernel, out_shape=shapes([(span, columns)] + [(span, size)...  7.16 us
    pallas_call x1, Pallas kernels, subtract_product(): pl.pallas_call(kernel, out_shape=shapes([(span, columns)])[0], in_specs=[...  4.61 us
    pallas_call x1, Pallas kernels, finish(): pl.pallas_call(kernel, out_shape=shapes([(span, columns)]) + [windows, wi...  1.95 us
  transfers between devices with their start and end apart: 18, of which 10 were waited for; matrix products, arithmetic and copies ran while one was open for 0% of the time, Pallas kernels for 12%

profile of v4, /device:TPU:0, one launch (start us, length us, event | category | flops | bytes accessed | tf_op | source)
XLA Modules:
  0.0 78.1 jit_solution(3723404918934905533)
XLA Ops:
  0.6 0.9 %maximum_bitcast_fusion = f32[1,4,16,512]{3,2,1,0:T(8,128)S(1)} fusion(f32[4,16,256]{2,1,0:T(8,128)} %param.8, f32[4,16,256]{2,1,0:T(8,128)} %param.7), kind=kLoop, calls=%fused_computation.5 | loop fusion | flops 32768 | bytes 262144 | tf_op jit(solution)/shard_map/broadcast_in_dim | solution.py:84
  1.6 3.0 %collective-permute-start.1 = (f32[1,4,16,1280]{3,2,1,0:T(8,128)S(1)}, f32[1,4,16,1280]{3,2,1,0:T(8,128)S(1)}, u32[]{:S(2)}, u32[]{:S(2)}) collective-permute-start(f32[1,4,16,1280]{3,2,1,0:T(8,128)S(1)} %pad_maximum_fusion.3), channel_id=1, source_target_pairs={{0,2},{2,0},{4,6},{6,4},{8,10},{10,8},{12,14},{14,12},{16,18},{18,... | collective-permute-start | bytes 983048 | tf_op jit(solution)/shard_map/ppermute | solution.py:28
  4.7 1.5 %collective-permute-start.2 = (f32[1,4,16,1280]{3,2,1,0:T(8,128)S(1)}, f32[1,4,16,1280]{3,2,1,0:T(8,128)S(1)}, u32[]{:S(2)}, u32[]{:S(2)}) collective-permute-start(f32[1,4,16,1280]{3,2,1,0:T(8,128)S(1)} %pad_maximum_fusion.3), channel_id=1, source_target_pairs={{0,4},{2,6},{4,0},{6,2},{8,12},{10,14},{12,8},{14,10},{16,20},{18,... | collective-permute-start | bytes 983048 | tf_op jit(solution)/shard_map/ppermute | solution.py:28
  6.2 3.6 %collective-permute-start = (f32[1,4,16,512]{3,2,1,0:T(8,128)S(1)}, f32[1,4,16,512]{3,2,1,0:T(8,128)S(1)}, u32[]{:S(2)}, u32[]{:S(2)}) collective-permute-start(f32[1,4,16,512]{3,2,1,0:T(8,128)S(1)} %maximum_bitcast_fusion), channel_id=1, source_target_pairs={{0,24},{2,26},{4,28},{6,30},{8,16},{10,18},{12,20},{14,22},{16,8},... | collective-permute-start | bytes 393224 | tf_op jit(solution)/shard_map/ppermute | solution.py:28
  9.8 3.2 %collective-permute-done = f32[1,4,16,512]{3,2,1,0:T(8,128)S(1)} collective-permute-done((f32[1,4,16,512]{3,2,1,0:T(8,128)S(1)}, f32[1,4,16,512]{3,2,1,0:T(8,128)S(1)}, u32[]{:S(2)}, u32[]{:S(2)}) %collective-permute-start) | collective-permute-done | bytes 131104 | tf_op jit(solution)/shard_map/ppermute | solution.py:28
  13.0 0.8 %collective-permute-done.2.refs_4_.refs_6_ = f32[1,4,16,1280]{3,2,1,0:T(8,128)S(1)} collective-permute-done((f32[1,4,16,1280]{3,2,1,0:T(8,128)S(1)}, f32[1,4,16,1280]{3,2,1,0:T(8,128)S(1)}, u32[]{:S(2)}, u32[]{:S(2)}) %collective-permute-start.2) | collective-permute-done | bytes 327712 | tf_op jit(solution)/shard_map/ppermute | solution.py:28
  13.8 3.6 %collective-permute-start.4 = (f32[1,4,16,768]{3,2,1,0:T(8,128)S(1)}, f32[1,4,16,768]{3,2,1,0:T(8,128)S(1)}, u32[]{:S(2)}, u32[]{:S(2)}) collective-permute-start(f32[1,4,16,768]{3,2,1,0:T(8,128)S(1)} %bitcast.4), channel_id=1, source_target_pairs={{0,24},{2,26},{4,28},{6,30},{8,16},{10,18},{12,20},{14,22},{16,8},... | collective-permute-start | bytes 589832 | tf_op jit(solution)/shard_map/ppermute | solution.py:28
  17.4 1.6 %collective-permute-start.5 = (f32[1,2,16,1280]{3,2,1,0:T(8,128)S(1)}, f32[1,2,16,1280]{3,2,1,0:T(8,128)S(1)}, u32[]{:S(2)}, u32[]{:S(2)}) collective-permute-start(f32[1,2,16,1280]{3,2,1,0:T(8,128)S(1)} %slice.24), channel_id=1, source_target_pairs={{0,4},{2,6},{4,0},{6,2},{8,12},{10,14},{12,8},{14,10},{16,20},{18,... | collective-permute-start | bytes 491528 | tf_op jit(solution)/shard_map/ppermute | solution.py:28
  19.6 3.8 %collective-permute-done.4 = f32[1,4,16,768]{3,2,1,0:T(8,128)S(1)} collective-permute-done((f32[1,4,16,768]{3,2,1,0:T(8,128)S(1)}, f32[1,4,16,768]{3,2,1,0:T(8,128)S(1)}, u32[]{:S(2)}, u32[]{:S(2)}) %collective-permute-start.4) | collective-permute-done | bytes 196640 | tf_op jit(solution)/shard_map/ppermute | solution.py:28
  23.5 3.4 %collective-permute-done.3 = f32[2,4,16,512]{3,2,1,0:T(8,128)S(1)} collective-permute-done((f32[2,4,16,512]{3,2,1,0:T(8,128)S(1)}, f32[2,4,16,512]{3,2,1,0:T(8,128)S(1)}, u32[]{:S(2)}, u32[]{:S(2)}) %collective-permute-start.3) | collective-permute-done | bytes 262176 | tf_op jit(solution)/shard_map/ppermute | solution.py:28
  26.9 1.8 %collective-permute-start.7 = (f32[2,4,16,768]{3,2,1,0:T(8,128)S(1)}, f32[2,4,16,768]{3,2,1,0:T(8,128)S(1)}, u32[]{:S(2)}, u32[]{:S(2)}) collective-permute-start(f32[2,4,16,768]{3,2,1,0:T(8,128)S(1)} %pad_maximum_fusion.2), channel_id=1, source_target_pairs={{0,8},{2,10},{4,12},{6,14},{8,0},{10,2},{12,4},{14,6},{16,24},{18,... | collective-permute-start | bytes 1179656 | tf_op jit(solution)/shard_map/ppermute | solution.py:28
  29.4 1.5 %collective-permute-start.9 = (f32[3,4,16,512]{3,2,1,0:T(8,128)S(1)}, f32[3,4,16,512]{3,2,1,0:T(8,128)S(1)}, u32[]{:S(2)}, u32[]{:S(2)}) collective-permute-start(f32[3,4,16,512]{3,2,1,0:T(8,128)S(1)} %slice.26), channel_id=1, source_target_pairs={{0,4},{2,6},{4,0},{6,2},{8,12},{10,14},{12,8},{14,10},{16,20},{18,... | collective-permute-start | bytes 1179656 | tf_op jit(solution)/shard_map/ppermute | solution.py:28
  30.9 6.2 %collective-permute-done.7 = f32[2,4,16,768]{3,2,1,0:T(8,128)S(1)} collective-permute-done((f32[2,4,16,768]{3,2,1,0:T(8,128)S(1)}, f32[2,4,16,768]{3,2,1,0:T(8,128)S(1)}, u32[]{:S(2)}, u32[]{:S(2)}) %collective-permute-start.7) | collective-permute-done | bytes 393248 | tf_op jit(solution)/shard_map/ppermute | solution.py:28
  37.7 1.4 %collective-permute-start.14 = (f32[3,4,16,768]{3,2,1,0:T(8,128)S(1)}, f32[3,4,16,768]{3,2,1,0:T(8,128)S(1)}, u32[]{:S(2)}, u32[]{:S(2)}) collective-permute-start(f32[3,4,16,768]{3,2,1,0:T(8,128)S(1)} %slice.29), channel_id=1, source_target_pairs={{0,2},{2,0},{4,6},{6,4},{8,10},{10,8},{12,14},{14,12},{16,18},{18,... | collective-permute-start | bytes 1769480 | tf_op jit(solution)/shard_map/ppermute | solution.py:28
  39.1 1.5 %collective-permute-start.15 = (f32[3,4,16,768]{3,2,1,0:T(8,128)S(1)}, f32[3,4,16,768]{3,2,1,0:T(8,128)S(1)}, u32[]{:S(2)}, u32[]{:S(2)}) collective-permute-start(f32[3,4,16,768]{3,2,1,0:T(8,128)S(1)} %slice.29), channel_id=1, source_target_pairs={{0,4},{2,6},{4,0},{6,2},{8,12},{10,14},{12,8},{14,10},{16,20},{18,... | collective-permute-start | bytes 1769480 | tf_op jit(solution)/shard_map/ppermute | solution.py:28
  41.3 0.8 collective-permute-start.11
  42.0 13.5 %collective-permute-done.10.refs_9_ = f32[3,2,16,512]{3,2,1,0:T(8,128)S(1)} collective-permute-done((f32[3,2,16,512]{3,2,1,0:T(8,128)S(1)}, f32[3,2,16,512]{3,2,1,0:T(8,128)S(1)}, u32[]{:S(2)}, u32[]{:S(2)}) %collective-permute-start.10) | collective-permute-done | bytes 196640 | tf_op jit(solution)/shard_map/ppermute | solution.py:28
  55.5 7.2 %solve.1 = (f32[1024,256]{1,0:T(8,128)S(1)}, f32[1024,256]{1,0:T(8,128)S(1)}, f32[2,256,256]{2,1,0:T(8,128)S(1)}, f32[2,256,256]{2,1,0:T(8,128)S(1)}) custom-call(s32[4,4,4]{2,1,0:T(4,128)S(1)} %copy-done.1, f32[1024,256]{1,0:T(8,128)S(1)} %copy-done, f32[4,4,16,512]{3,2,1,0:T(8,128)S(1)} %pad_maximum_fusion.1.refs_2_, ...), custom_call_target="tpu_custom_call" | custom-call | flops 536870912 | bytes 262144 | tf_op jit(solution)/shard_map/solve/pallas_call | solution.py:224
  63.3 1.4 %collective-permute-start.16 = (f32[3,2,16,768]{3,2,1,0:T(8,128)S(1)}, f32[3,2,16,768]{3,2,1,0:T(8,128)S(1)}, u32[]{:S(2)}, u32[]{:S(2)}) collective-permute-start(f32[3,2,16,768]{3,2,1,0:T(8,128)S(1)} %slice.34), channel_id=1, source_target_pairs={{0,4},{2,6},{4,0},{6,2},{8,12},{10,14},{12,8},{14,10},{16,20},{18,... | collective-permute-start | bytes 884744 | tf_op jit(solution)/shard_map/ppermute | solution.py:28
  64.7 1.3 %collective-permute-start.17 = (f32[3,2,16,768]{3,2,1,0:T(8,128)S(1)}, f32[3,2,16,768]{3,2,1,0:T(8,128)S(1)}, u32[]{:S(2)}, u32[]{:S(2)}) collective-permute-start(f32[3,2,16,768]{3,2,1,0:T(8,128)S(1)} %slice.35), channel_id=1, source_target_pairs={{0,2},{2,0},{4,6},{6,4},{8,10},{10,8},{12,14},{14,12},{16,18},{18,... | collective-permute-start | bytes 884744 | tf_op jit(solution)/shard_map/ppermute | solution.py:28
  66.1 2.0 %finish.1 = (f32[1024,256]{1,0:T(8,128)}, bf16[1536,256]{1,0:T(8,128)(2,1)S(1)}, bf16[1536,256]{1,0:T(8,128)(2,1)S(1)}) custom-call(f32[1024,256]{1,0:T(8,128)S(1)} %get-tuple-element.32.sol_ref, f32[1024,256]{1,0:T(8,128)S(1)} %get-tuple-element.33.part_ref, f32[2,256,256]{2,1,0:T(8,128)S(1)} %get-tuple-element.34.own_ref, ...), custom_call_target="tpu_custom_call" | custom-call | flops 100663296 | bytes 262144 | tf_op jit(solution)/shard_map/finish/pallas_call | solution.py:268
  68.0 4.3 %collective-permute-done.16.refs_11_ = f32[3,2,16,768]{3,2,1,0:T(8,128)S(1)} collective-permute-done((f32[3,2,16,768]{3,2,1,0:T(8,128)S(1)}, f32[3,2,16,768]{3,2,1,0:T(8,128)S(1)}, u32[]{:S(2)}, u32[]{:S(2)}) %collective-permute-start.16) | collective-permute-done | bytes 294944 | tf_op jit(solution)/shard_map/ppermute | solution.py:28
  72.4 1.1 %collective-permute-done.17.refs_12_ = f32[3,2,16,768]{3,2,1,0:T(8,128)S(1)} collective-permute-done((f32[3,2,16,768]{3,2,1,0:T(8,128)S(1)}, f32[3,2,16,768]{3,2,1,0:T(8,128)S(1)}, u32[]{:S(2)}, u32[]{:S(2)}) %collective-permute-start.17) | collective-permute-done | bytes 294944 | tf_op jit(solution)/shard_map/ppermute | solution.py:28
  73.5 4.6 %residual.1 = f32[1024,256]{1,0:T(8,128)} custom-call(s32[4,4,12]{2,1,0:T(4,128)S(1)} %copy-done.2, f32[1024,256]{1,0:T(8,128)S(1)} %copy-done, bf16[1536,256]{1,0:T(8,128)(2,1)S(1)} %get-tuple-element.37.refs_2_, bf16[1536,256]{1,0:T(8,128)(2,1)S(1)} %get-tuple-element.38.refs_3_, f32[4,4,16,768]{3,2,1,0:T(8,128)S(1)} %pad_maximum_fusion.refs_4_, ...), custom_call_target="tpu_custom_call" | custom-call | flops 1207959552 | bytes 6291456 | tf_op jit(solution)/shard_map/residual/pallas_call | solution.py:313
  (37 shorter events, 3.4 us)
Async XLA Ops:
  0.6 1.0 %copy-start.3 = (f32[4,16,768]{2,1,0:T(8,128)S(1)}, f32[4,16,768]{2,1,0:T(8,128)}, u32[]{:S(2)}) copy-start(f32[4,16,768]{2,1,0:T(8,128)} %param.10) | copy-start | bytes 589828
  1.6 11.4 %collective-permute-start.1 = (f32[1,4,16,1280]{3,2,1,0:T(8,128)S(1)}, f32[1,4,16,1280]{3,2,1,0:T(8,128)S(1)}, u32[]{:S(2)}, u32[]{:S(2)}) collective-permute-start(f32[1,4,16,1280]{3,2,1,0:T(8,128)S(1)} %pad_maximum_fusion.3), channel_id=1, source_target_pairs={{0,2},{2,0},{4,6},{6,4},{8,10},{10,8},{12,14},{14,12},{16,18},{18,... | collective-permute-start | bytes 983048 | tf_op jit(solution)/shard_map/ppermute | solution.py:28
  4.7 9.2 %collective-permute-start.2 = (f32[1,4,16,1280]{3,2,1,0:T(8,128)S(1)}, f32[1,4,16,1280]{3,2,1,0:T(8,128)S(1)}, u32[]{:S(2)}, u32[]{:S(2)}) collective-permute-start(f32[1,4,16,1280]{3,2,1,0:T(8,128)S(1)} %pad_maximum_fusion.3), channel_id=1, source_target_pairs={{0,4},{2,6},{4,0},{6,2},{8,12},{10,14},{12,8},{14,10},{16,20},{18,... | collective-permute-start | bytes 983048 | tf_op jit(solution)/shard_map/ppermute | solution.py:28
  6.2 6.8 %collective-permute-start = (f32[1,4,16,512]{3,2,1,0:T(8,128)S(1)}, f32[1,4,16,512]{3,2,1,0:T(8,128)S(1)}, u32[]{:S(2)}, u32[]{:S(2)}) collective-permute-start(f32[1,4,16,512]{3,2,1,0:T(8,128)S(1)} %maximum_bitcast_fusion), channel_id=1, source_target_pairs={{0,24},{2,26},{4,28},{6,30},{8,16},{10,18},{12,20},{14,22},{16,8},... | collective-permute-start | bytes 393224 | tf_op jit(solution)/shard_map/ppermute | solution.py:28
  13.8 9.6 %collective-permute-start.4 = (f32[1,4,16,768]{3,2,1,0:T(8,128)S(1)}, f32[1,4,16,768]{3,2,1,0:T(8,128)S(1)}, u32[]{:S(2)}, u32[]{:S(2)}) collective-permute-start(f32[1,4,16,768]{3,2,1,0:T(8,128)S(1)} %bitcast.4), channel_id=1, source_target_pairs={{0,24},{2,26},{4,28},{6,30},{8,16},{10,18},{12,20},{14,22},{16,8},... | collective-permute-start | bytes 589832 | tf_op jit(solution)/shard_map/ppermute | solution.py:28
  17.4 9.4 %collective-permute-start.3 = (f32[2,4,16,512]{3,2,1,0:T(8,128)S(1)}, f32[2,4,16,512]{3,2,1,0:T(8,128)S(1)}, u32[]{:S(2)}, u32[]{:S(2)}) collective-permute-start(f32[2,4,16,512]{3,2,1,0:T(8,128)S(1)} %pad_maximum_fusion.4), channel_id=1, source_target_pairs={{0,8},{2,10},{4,12},{6,14},{8,0},{10,2},{12,4},{14,6},{16,24},{18,... | collective-permute-start | bytes 786440 | tf_op jit(solution)/shard_map/ppermute | solution.py:28
  17.4 9.5 %collective-permute-start.5 = (f32[1,2,16,1280]{3,2,1,0:T(8,128)S(1)}, f32[1,2,16,1280]{3,2,1,0:T(8,128)S(1)}, u32[]{:S(2)}, u32[]{:S(2)}) collective-permute-start(f32[1,2,16,1280]{3,2,1,0:T(8,128)S(1)} %slice.24), channel_id=1, source_target_pairs={{0,4},{2,6},{4,0},{6,2},{8,12},{10,14},{12,8},{14,10},{16,20},{18,... | collective-permute-start | bytes 491528 | tf_op jit(solution)/shard_map/ppermute | solution.py:28
  19.0 7.9 %collective-permute-start.6 = (f32[1,2,16,1280]{3,2,1,0:T(8,128)S(1)}, f32[1,2,16,1280]{3,2,1,0:T(8,128)S(1)}, u32[]{:S(2)}, u32[]{:S(2)}) collective-permute-start(f32[1,2,16,1280]{3,2,1,0:T(8,128)S(1)} %slice.25), channel_id=1, source_target_pairs={{0,2},{2,0},{4,6},{6,4},{8,10},{10,8},{12,14},{14,12},{16,18},{18,... | collective-permute-start | bytes 491528 | tf_op jit(solution)/shard_map/ppermute | solution.py:28
  26.9 10.1 %collective-permute-start.7 = (f32[2,4,16,768]{3,2,1,0:T(8,128)S(1)}, f32[2,4,16,768]{3,2,1,0:T(8,128)S(1)}, u32[]{:S(2)}, u32[]{:S(2)}) collective-permute-start(f32[2,4,16,768]{3,2,1,0:T(8,128)S(1)} %pad_maximum_fusion.2), channel_id=1, source_target_pairs={{0,8},{2,10},{4,12},{6,14},{8,0},{10,2},{12,4},{14,6},{16,24},{18,... | collective-permute-start | bytes 1179656 | tf_op jit(solution)/shard_map/ppermute | solution.py:28
  28.7 8.6 %collective-permute-start.8 = (f32[3,4,16,512]{3,2,1,0:T(8,128)S(1)}, f32[3,4,16,512]{3,2,1,0:T(8,128)S(1)}, u32[]{:S(2)}, u32[]{:S(2)}) collective-permute-start(f32[3,4,16,512]{3,2,1,0:T(8,128)S(1)} %slice.26), channel_id=1, source_target_pairs={{0,2},{2,0},{4,6},{6,4},{8,10},{10,8},{12,14},{14,12},{16,18},{18,... | collective-permute-start | bytes 1179656 | tf_op jit(solution)/shard_map/ppermute | solution.py:28
  29.4 8.3 %collective-permute-start.9 = (f32[3,4,16,512]{3,2,1,0:T(8,128)S(1)}, f32[3,4,16,512]{3,2,1,0:T(8,128)S(1)}, u32[]{:S(2)}, u32[]{:S(2)}) collective-permute-start(f32[3,4,16,512]{3,2,1,0:T(8,128)S(1)} %slice.26), channel_id=1, source_target_pairs={{0,4},{2,6},{4,0},{6,2},{8,12},{10,14},{12,8},{14,10},{16,20},{18,... | collective-permute-start | bytes 1179656 | tf_op jit(solution)/shard_map/ppermute | solution.py:28
  37.1 18.4 %copy-start = (f32[1024,256]{1,0:T(8,128)S(1)}, f32[1024,256]{1,0:T(8,128)}, u32[]{:S(2)}) copy-start(f32[1024,256]{1,0:T(8,128)} %refs_1_.2) | copy-start | bytes 3145732
  37.7 25.6 %collective-permute-start.14 = (f32[3,4,16,768]{3,2,1,0:T(8,128)S(1)}, f32[3,4,16,768]{3,2,1,0:T(8,128)S(1)}, u32[]{:S(2)}, u32[]{:S(2)}) collective-permute-start(f32[3,4,16,768]{3,2,1,0:T(8,128)S(1)} %slice.29), channel_id=1, source_target_pairs={{0,2},{2,0},{4,6},{6,4},{8,10},{10,8},{12,14},{14,12},{16,18},{18,... | collective-permute-start | bytes 1769480 | tf_op jit(solution)/shard_map/ppermute | solution.py:28
  39.1 25.6 %collective-permute-start.15 = (f32[3,4,16,768]{3,2,1,0:T(8,128)S(1)}, f32[3,4,16,768]{3,2,1,0:T(8,128)S(1)}, u32[]{:S(2)}, u32[]{:S(2)}) collective-permute-start(f32[3,4,16,768]{3,2,1,0:T(8,128)S(1)} %slice.29), channel_id=1, source_target_pairs={{0,4},{2,6},{4,0},{6,2},{8,12},{10,14},{12,8},{14,10},{16,20},{18,... | collective-permute-start | bytes 1769480 | tf_op jit(solution)/shard_map/ppermute | solution.py:28
  40.7 14.9 %copy-start.1 = (s32[4,4,4]{2,1,0:T(4,128)S(1)}, s32[4,4,4]{2,1,0:T(4,128)}, u32[]{:S(2)}) copy-start(s32[4,4,4]{2,1,0:T(4,128)} %refs_0_.2) | copy-start | bytes 772
  40.7 14.8 %collective-permute-start.10 = (f32[3,2,16,512]{3,2,1,0:T(8,128)S(1)}, f32[3,2,16,512]{3,2,1,0:T(8,128)S(1)}, u32[]{:S(2)}, u32[]{:S(2)}) collective-permute-start(f32[3,2,16,512]{3,2,1,0:T(8,128)S(1)} %slice.32), channel_id=1, source_target_pairs={{0,4},{2,6},{4,0},{6,2},{8,12},{10,14},{12,8},{14,10},{16,20},{18,... | collective-permute-start | bytes 589832 | tf_op jit(solution)/shard_map/ppermute | solution.py:28
  41.3 14.3 %collective-permute-start.11 = (f32[3,2,16,512]{3,2,1,0:T(8,128)S(1)}, f32[3,2,16,512]{3,2,1,0:T(8,128)S(1)}, u32[]{:S(2)}, u32[]{:S(2)}) collective-permute-start(f32[3,2,16,512]{3,2,1,0:T(8,128)S(1)} %slice.33), channel_id=1, source_target_pairs={{0,2},{2,0},{4,6},{6,4},{8,10},{10,8},{12,14},{14,12},{16,18},{18,... | collective-permute-start | bytes 589832 | tf_op jit(solution)/shard_map/ppermute | solution.py:28
  62.7 3.4 %collective-permute-start.12 = (f32[2,256,256]{2,1,0:T(8,128)S(1)}, f32[2,256,256]{2,1,0:T(8,128)S(1)}, u32[]{:S(2)}, u32[]{:S(2)}) collective-permute-start(f32[2,256,256]{2,1,0:T(8,128)S(1)} %get-tuple-element.34.own_ref), channel_id=1, source_target_pairs={{0,1},{1,0},{2,3},{3,2},{4,5},{5,4},{6,7},{7,6},{8,9},{9,8},{10,11... | collective-permute-start | bytes 1572872 | tf_op jit(solution)/shard_map/ppermute | solution.py:352
  62.8 3.3 %collective-permute-start.13 = (f32[2,256,256]{2,1,0:T(8,128)S(1)}, f32[2,256,256]{2,1,0:T(8,128)S(1)}, u32[]{:S(2)}, u32[]{:S(2)}) collective-permute-start(f32[2,256,256]{2,1,0:T(8,128)S(1)} %get-tuple-element.35), channel_id=1, source_target_pairs={{0,1},{1,0},{2,3},{3,2},{4,5},{5,4},{6,7},{7,6},{8,9},{9,8},{10,11... | collective-permute-start | bytes 1572872 | tf_op jit(solution)/shard_map/ppermute | solution.py:352
  63.3 9.1 %collective-permute-start.16 = (f32[3,2,16,768]{3,2,1,0:T(8,128)S(1)}, f32[3,2,16,768]{3,2,1,0:T(8,128)S(1)}, u32[]{:S(2)}, u32[]{:S(2)}) collective-permute-start(f32[3,2,16,768]{3,2,1,0:T(8,128)S(1)} %slice.34), channel_id=1, source_target_pairs={{0,4},{2,6},{4,0},{6,2},{8,12},{10,14},{12,8},{14,10},{16,20},{18,... | collective-permute-start | bytes 884744 | tf_op jit(solution)/shard_map/ppermute | solution.py:28
  64.7 8.8 %collective-permute-start.17 = (f32[3,2,16,768]{3,2,1,0:T(8,128)S(1)}, f32[3,2,16,768]{3,2,1,0:T(8,128)S(1)}, u32[]{:S(2)}, u32[]{:S(2)}) collective-permute-start(f32[3,2,16,768]{3,2,1,0:T(8,128)S(1)} %slice.35), channel_id=1, source_target_pairs={{0,2},{2,0},{4,6},{6,4},{8,10},{10,8},{12,14},{14,12},{16,18},{18,... | collective-permute-start | bytes 884744 | tf_op jit(solution)/shard_map/ppermute | solution.py:28
  66.1 7.4 %copy-start.2 = (s32[4,4,12]{2,1,0:T(4,128)S(1)}, s32[4,4,12]{2,1,0:T(4,128)}, u32[]{:S(2)}) copy-start(s32[4,4,12]{2,1,0:T(4,128)} %refs_0_.3) | copy-start | bytes 2308

commit v5 on v4

--- a/solution.py
+++ b/solution.py
@@ -86,16 +86,15 @@
     split_at = factor_part.shape[3]
 
     factor_line = spread(factor_part, masks[:1], axis)
+    jacobian_line = spread(jacobian, masks[:1], axis)
     own = around(everything, axis)
-    (jacobian, factor_line), own = lax.optimization_barrier(((jacobian, factor_line), own))
+    jacobian_line, own = lax.optimization_barrier((jacobian_line, own))
+    own = onward(*own, axis)
     factor_line = spread(factor_line, masks[1:], axis)
-    jacobian_line = spread(jacobian, masks[:1], axis)
-    own = onward(*own, axis)
-    factor_line, jacobian_line, own = lax.optimization_barrier((factor_line, jacobian_line, own))
-    factor_rest = around(factor_line[1:], axis)
+    factor_line, own = lax.optimization_barrier((factor_line, own))
+    factor_rest = onward(*around(factor_line[1:], axis), axis)
     jacobian_line = spread(jacobian_line, masks[1:], axis)
-    late, jacobian_line, _ = lax.optimization_barrier((right_side, jacobian_line, factor_rest))
-    factor_rest = onward(*factor_rest, axis)
+    late, jacobian_line = lax.optimization_barrier((right_side, jacobian_line))
     jacobian_rest = onward(*around(jacobian_line[1:], axis), axis)
 
     factor = [piece(factor_line, order, 0)]
@@ -233,7 +232,7 @@
         ],
         compiler_params=pltpu.CompilerParams(vmem_limit_bytes=VMEM_LIMIT),
         cost_estimate=pl.CostEstimate(
-            flops=4 * supers * size * size * width, bytes_accessed=span * size, transcendentals=0
+            flops=16 * supers * size * size * width, bytes_accessed=span * size, transcendentals=0
         ),
         name="solve",
     )(pattern, right_side, *[array for array, *_ in pieces])

time: 78.3 us -> 68.5 us (0.87)
  waiting for transfers between devices: 36.9 us -> 25.3 us
  starting transfers between devices: 25.4 us -> 27.3 us
    ppermute x16, waiting for transfers between devices: 36.9 us -> 25.2 us  [across(): lax.ppermute(value, axis, [(i, i ^ mask) for i in range(lax.axis_size(axi...]
    ppermute x16, starting transfers between devices: 24.8 us -> 26.7 us  [across(): lax.ppermute(value, axis, [(i, i ^ mask) for i in range(lax.axis_size(axi...]
  transfers between devices with their start and end apart: 18 -> 18, of which waited for: 10 -> 12; matrix products, arithmetic and copies ran while one was open for 0% -> 0% of each run, Pallas kernels for 12% -> 13%
where the time goes in v5:
time: 68.5 us; the launch traced here: 68.3 us
  starting transfers between devices  27.3 us (40%)
  waiting for transfers between devices  25.3 us (37%)
  Pallas kernels  13.7 us (20%)
  other arithmetic  1.07 us (2%)
  between operations  0.77 us (1%)
    ppermute x16, starting transfers between devices, across(): lax.ppermute(value, axis, [(i, i ^ mask) for i in range(lax.axis_size(axi...  26.7 us
    ppermute x16, waiting for transfers between devices, across(): lax.ppermute(value, axis, [(i, i ^ mask) for i in range(lax.axis_size(axi...  25.2 us
    pallas_call x1, Pallas kernels, solve(): pl.pallas_call(kernel, out_shape=shapes([(span, columns)] + [(span, size)...  7.14 us
    pallas_call x1, Pallas kernels, subtract_product(): pl.pallas_call(kernel, out_shape=shapes([(span, columns)])[0], in_specs=[...  4.61 us
    pallas_call x1, Pallas kernels, finish(): pl.pallas_call(kernel, out_shape=shapes([(span, columns)]) + [windows, wi...  1.96 us
  transfers between devices with their start and end apart: 18, of which 12 were waited for; matrix products, arithmetic and copies ran while one was open for 0% of the time, Pallas kernels for 13%

profile of v5, /device:TPU:0, one launch (start us, length us, event | category | flops | bytes accessed | tf_op | source)
XLA Modules:
  0.0 68.3 jit_solution(8598964991554250450)
XLA Ops:
  1.6 5.1 %collective-permute-start.4 = (f32[1,4,16,512]{3,2,1,0:T(8,128)S(1)}, f32[1,4,16,512]{3,2,1,0:T(8,128)S(1)}, u32[]{:S(2)}, u32[]{:S(2)}) collective-permute-start(f32[1,4,16,512]{3,2,1,0:T(8,128)S(1)} %maximum_bitcast_fusion), channel_id=1, source_target_pairs={{0,24},{2,26},{4,28},{6,30},{8,16},{10,18},{12,20},{14,22},{16,8},... | collective-permute-start | bytes 393224 | tf_op jit(solution)/shard_map/ppermute | solution.py:28
  6.7 1.6 %collective-permute-start.1 = (f32[1,4,16,1280]{3,2,1,0:T(8,128)S(1)}, f32[1,4,16,1280]{3,2,1,0:T(8,128)S(1)}, u32[]{:S(2)}, u32[]{:S(2)}) collective-permute-start(f32[1,4,16,1280]{3,2,1,0:T(8,128)S(1)} %pad_maximum_fusion.3), channel_id=1, source_target_pairs={{0,2},{2,0},{4,6},{6,4},{8,10},{10,8},{12,14},{14,12},{16,18},{18,... | collective-permute-start | bytes 983048 | tf_op jit(solution)/shard_map/ppermute | solution.py:28
  8.3 1.5 %collective-permute-start.2 = (f32[1,4,16,1280]{3,2,1,0:T(8,128)S(1)}, f32[1,4,16,1280]{3,2,1,0:T(8,128)S(1)}, u32[]{:S(2)}, u32[]{:S(2)}) collective-permute-start(f32[1,4,16,1280]{3,2,1,0:T(8,128)S(1)} %pad_maximum_fusion.3), channel_id=1, source_target_pairs={{0,4},{2,6},{4,0},{6,2},{8,12},{10,14},{12,8},{14,10},{16,20},{18,... | collective-permute-start | bytes 983048 | tf_op jit(solution)/shard_map/ppermute | solution.py:28
  10.3 6.0 %collective-permute-start.5 = (f32[2,4,16,512]{3,2,1,0:T(8,128)S(1)}, f32[2,4,16,512]{3,2,1,0:T(8,128)S(1)}, u32[]{:S(2)}, u32[]{:S(2)}) collective-permute-start(f32[2,4,16,512]{3,2,1,0:T(8,128)S(1)} %pad_maximum_fusion.4), channel_id=1, source_target_pairs={{0,8},{2,10},{4,12},{6,14},{8,0},{10,2},{12,4},{14,6},{16,24},{18,... | collective-permute-start | bytes 786440 | tf_op jit(solution)/shard_map/ppermute | solution.py:28
  16.3 3.2 %collective-permute-done = f32[1,4,16,768]{3,2,1,0:T(8,128)S(1)} collective-permute-done((f32[1,4,16,768]{3,2,1,0:T(8,128)S(1)}, f32[1,4,16,768]{3,2,1,0:T(8,128)S(1)}, u32[]{:S(2)}, u32[]{:S(2)}) %collective-permute-start) | collective-permute-done | bytes 196640 | tf_op jit(solution)/shard_map/ppermute | solution.py:28
  20.1 1.1 %collective-permute-start.7 = (f32[1,2,16,1280]{3,2,1,0:T(8,128)S(1)}, f32[1,2,16,1280]{3,2,1,0:T(8,128)S(1)}, u32[]{:S(2)}, u32[]{:S(2)}) collective-permute-start(f32[1,2,16,1280]{3,2,1,0:T(8,128)S(1)} %slice.25), channel_id=1, source_target_pairs={{0,2},{2,0},{4,6},{6,4},{8,10},{10,8},{12,14},{14,12},{16,18},{18,... | collective-permute-start | bytes 491528 | tf_op jit(solution)/shard_map/ppermute | solution.py:28
  21.2 1.4 %collective-permute-done.5 = f32[2,4,16,512]{3,2,1,0:T(8,128)S(1)} collective-permute-done((f32[2,4,16,512]{3,2,1,0:T(8,128)S(1)}, f32[2,4,16,512]{3,2,1,0:T(8,128)S(1)}, u32[]{:S(2)}, u32[]{:S(2)}) %collective-permute-start.5) | collective-permute-done | bytes 262176 | tf_op jit(solution)/shard_map/ppermute | solution.py:28
  22.7 2.7 %collective-permute-done.6.refs_5_.refs_7_ = f32[1,2,16,1280]{3,2,1,0:T(8,128)S(1)} collective-permute-done((f32[1,2,16,1280]{3,2,1,0:T(8,128)S(1)}, f32[1,2,16,1280]{3,2,1,0:T(8,128)S(1)}, u32[]{:S(2)}, u32[]{:S(2)}) %collective-permute-start.6) | collective-permute-done | bytes 163872 | tf_op jit(solution)/shard_map/ppermute | solution.py:28
  25.4 1.5 %collective-permute-done.7.refs_6_.refs_8_ = f32[1,2,16,1280]{3,2,1,0:T(8,128)S(1)} collective-permute-done((f32[1,2,16,1280]{3,2,1,0:T(8,128)S(1)}, f32[1,2,16,1280]{3,2,1,0:T(8,128)S(1)}, u32[]{:S(2)}, u32[]{:S(2)}) %collective-permute-start.7) | collective-permute-done | bytes 163872 | tf_op jit(solution)/shard_map/ppermute | solution.py:28
  26.9 1.5 %collective-permute-start.8 = (f32[3,4,16,512]{3,2,1,0:T(8,128)S(1)}, f32[3,4,16,512]{3,2,1,0:T(8,128)S(1)}, u32[]{:S(2)}, u32[]{:S(2)}) collective-permute-start(f32[3,4,16,512]{3,2,1,0:T(8,128)S(1)} %slice.26), channel_id=1, source_target_pairs={{0,2},{2,0},{4,6},{6,4},{8,10},{10,8},{12,14},{14,12},{16,18},{18,... | collective-permute-start | bytes 1179656 | tf_op jit(solution)/shard_map/ppermute | solution.py:28
  28.4 1.0 %collective-permute-start.9 = (f32[3,4,16,512]{3,2,1,0:T(8,128)S(1)}, f32[3,4,16,512]{3,2,1,0:T(8,128)S(1)}, u32[]{:S(2)}, u32[]{:S(2)}) collective-permute-start(f32[3,4,16,512]{3,2,1,0:T(8,128)S(1)} %slice.26), channel_id=1, source_target_pairs={{0,4},{2,6},{4,0},{6,2},{8,12},{10,14},{12,8},{14,10},{16,20},{18,... | collective-permute-start | bytes 1179656 | tf_op jit(solution)/shard_map/ppermute | solution.py:28
  29.3 0.9 %collective-permute-start.3 = (f32[2,4,16,768]{3,2,1,0:T(8,128)S(1)}, f32[2,4,16,768]{3,2,1,0:T(8,128)S(1)}, u32[]{:S(2)}, u32[]{:S(2)}) collective-permute-start(f32[2,4,16,768]{3,2,1,0:T(8,128)S(1)} %pad_maximum_fusion.2), channel_id=1, source_target_pairs={{0,8},{2,10},{4,12},{6,14},{8,0},{10,2},{12,4},{14,6},{16,24},{18,... | collective-permute-start | bytes 1179656 | tf_op jit(solution)/shard_map/ppermute | solution.py:28
  30.3 6.2 %collective-permute-done.8.refs_7_ = f32[3,4,16,512]{3,2,1,0:T(8,128)S(1)} collective-permute-done((f32[3,4,16,512]{3,2,1,0:T(8,128)S(1)}, f32[3,4,16,512]{3,2,1,0:T(8,128)S(1)}, u32[]{:S(2)}, u32[]{:S(2)}) %collective-permute-start.8) | collective-permute-done | bytes 393248 | tf_op jit(solution)/shard_map/ppermute | solution.py:28
  36.5 2.6 %collective-permute-start.10 = (f32[3,2,16,512]{3,2,1,0:T(8,128)S(1)}, f32[3,2,16,512]{3,2,1,0:T(8,128)S(1)}, u32[]{:S(2)}, u32[]{:S(2)}) collective-permute-start(f32[3,2,16,512]{3,2,1,0:T(8,128)S(1)} %slice.32), channel_id=1, source_target_pairs={{0,4},{2,6},{4,0},{6,2},{8,12},{10,14},{12,8},{14,10},{16,20},{18,... | collective-permute-start | bytes 589832 | tf_op jit(solution)/shard_map/ppermute | solution.py:28
  39.1 1.0 %collective-permute-done.9.refs_8_ = f32[3,4,16,512]{3,2,1,0:T(8,128)S(1)} collective-permute-done((f32[3,4,16,512]{3,2,1,0:T(8,128)S(1)}, f32[3,4,16,512]{3,2,1,0:T(8,128)S(1)}, u32[]{:S(2)}, u32[]{:S(2)}) %collective-permute-start.9) | collective-permute-done | bytes 393248 | tf_op jit(solution)/shard_map/ppermute | solution.py:28
  40.4 2.0 %collective-permute-start.14 = (f32[3,4,16,768]{3,2,1,0:T(8,128)S(1)}, f32[3,4,16,768]{3,2,1,0:T(8,128)S(1)}, u32[]{:S(2)}, u32[]{:S(2)}) collective-permute-start(f32[3,4,16,768]{3,2,1,0:T(8,128)S(1)} %slice.29), channel_id=1, source_target_pairs={{0,2},{2,0},{4,6},{6,4},{8,10},{10,8},{12,14},{14,12},{16,18},{18,... | collective-permute-start | bytes 1769480 | tf_op jit(solution)/shard_map/ppermute | solution.py:28
  43.0 1.9 %collective-permute-done.10.refs_9_ = f32[3,2,16,512]{3,2,1,0:T(8,128)S(1)} collective-permute-done((f32[3,2,16,512]{3,2,1,0:T(8,128)S(1)}, f32[3,2,16,512]{3,2,1,0:T(8,128)S(1)}, u32[]{:S(2)}, u32[]{:S(2)}) %collective-permute-start.10) | collective-permute-done | bytes 196640 | tf_op jit(solution)/shard_map/ppermute | solution.py:28
  44.9 1.0 %collective-permute-done.11.refs_10_ = f32[3,2,16,512]{3,2,1,0:T(8,128)S(1)} collective-permute-done((f32[3,2,16,512]{3,2,1,0:T(8,128)S(1)}, f32[3,2,16,512]{3,2,1,0:T(8,128)S(1)}, u32[]{:S(2)}, u32[]{:S(2)}) %collective-permute-start.11) | collective-permute-done | bytes 196640 | tf_op jit(solution)/shard_map/ppermute | solution.py:28
  45.9 7.1 %solve.1 = (f32[1024,256]{1,0:T(8,128)S(1)}, f32[1024,256]{1,0:T(8,128)S(1)}, f32[2,256,256]{2,1,0:T(8,128)S(1)}, f32[2,256,256]{2,1,0:T(8,128)S(1)}) custom-call(s32[4,4,4]{2,1,0:T(4,128)S(1)} %copy-done.2, f32[1024,256]{1,0:T(8,128)S(1)} %copy-done, f32[4,4,16,512]{3,2,1,0:T(8,128)S(1)} %pad_maximum_fusion.1.refs_2_, ...), custom_call_target="tpu_custom_call" | custom-call | flops 2147483648 | bytes 262144 | tf_op jit(solution)/shard_map/solve/pallas_call | solution.py:223
  53.6 1.3 %collective-permute-start.16 = (f32[3,2,16,768]{3,2,1,0:T(8,128)S(1)}, f32[3,2,16,768]{3,2,1,0:T(8,128)S(1)}, u32[]{:S(2)}, u32[]{:S(2)}) collective-permute-start(f32[3,2,16,768]{3,2,1,0:T(8,128)S(1)} %slice.34), channel_id=1, source_target_pairs={{0,4},{2,6},{4,0},{6,2},{8,12},{10,14},{12,8},{14,10},{16,20},{18,... | collective-permute-start | bytes 884744 | tf_op jit(solution)/shard_map/ppermute | solution.py:28
  55.7 2.0 %finish.1 = (f32[1024,256]{1,0:T(8,128)}, bf16[1536,256]{1,0:T(8,128)(2,1)S(1)}, bf16[1536,256]{1,0:T(8,128)(2,1)S(1)}) custom-call(f32[1024,256]{1,0:T(8,128)S(1)} %get-tuple-element.28.sol_ref, f32[1024,256]{1,0:T(8,128)S(1)} %get-tuple-element.29.part_ref, f32[2,256,256]{2,1,0:T(8,128)S(1)} %get-tuple-element.30.own_ref, ...), custom_call_target="tpu_custom_call" | custom-call | flops 100663296 | bytes 262144 | tf_op jit(solution)/shard_map/finish/pallas_call | solution.py:267
  57.7 5.0 %collective-permute-done.16.refs_11_ = f32[3,2,16,768]{3,2,1,0:T(8,128)S(1)} collective-permute-done((f32[3,2,16,768]{3,2,1,0:T(8,128)S(1)}, f32[3,2,16,768]{3,2,1,0:T(8,128)S(1)}, u32[]{:S(2)}, u32[]{:S(2)}) %collective-permute-start.16) | collective-permute-done | bytes 294944 | tf_op jit(solution)/shard_map/ppermute | solution.py:28
  62.7 1.0 %collective-permute-done.17.refs_12_ = f32[3,2,16,768]{3,2,1,0:T(8,128)S(1)} collective-permute-done((f32[3,2,16,768]{3,2,1,0:T(8,128)S(1)}, f32[3,2,16,768]{3,2,1,0:T(8,128)S(1)}, u32[]{:S(2)}, u32[]{:S(2)}) %collective-permute-start.17) | collective-permute-done | bytes 294944 | tf_op jit(solution)/shard_map/ppermute | solution.py:28
  63.7 4.6 %residual.1 = f32[1024,256]{1,0:T(8,128)} custom-call(s32[4,4,12]{2,1,0:T(4,128)S(1)} %copy-done.1, f32[1024,256]{1,0:T(8,128)S(1)} %copy-done, bf16[1536,256]{1,0:T(8,128)(2,1)S(1)} %get-tuple-element.33.refs_2_, bf16[1536,256]{1,0:T(8,128)(2,1)S(1)} %get-tuple-element.34.refs_3_, f32[4,4,16,768]{3,2,1,0:T(8,128)S(1)} %pad_maximum_fusion.refs_4_, ...), custom_call_target="tpu_custom_call" | custom-call | flops 1207959552 | bytes 6291456 | tf_op jit(solution)/shard_map/residual/pallas_call | solution.py:312
  (37 shorter events, 4.5 us)
Async XLA Ops:
  0.6 6.1 %copy-start.3 = (f32[4,16,768]{2,1,0:T(8,128)S(1)}, f32[4,16,768]{2,1,0:T(8,128)}, u32[]{:S(2)}) copy-start(f32[4,16,768]{2,1,0:T(8,128)} %param.10) | copy-start | bytes 589828
  1.6 8.7 %collective-permute-start.4 = (f32[1,4,16,512]{3,2,1,0:T(8,128)S(1)}, f32[1,4,16,512]{3,2,1,0:T(8,128)S(1)}, u32[]{:S(2)}, u32[]{:S(2)}) collective-permute-start(f32[1,4,16,512]{3,2,1,0:T(8,128)S(1)} %maximum_bitcast_fusion), channel_id=1, source_target_pairs={{0,24},{2,26},{4,28},{6,30},{8,16},{10,18},{12,20},{14,22},{16,8},... | collective-permute-start | bytes 393224 | tf_op jit(solution)/shard_map/ppermute | solution.py:28
  6.7 12.7 %collective-permute-start.1 = (f32[1,4,16,1280]{3,2,1,0:T(8,128)S(1)}, f32[1,4,16,1280]{3,2,1,0:T(8,128)S(1)}, u32[]{:S(2)}, u32[]{:S(2)}) collective-permute-start(f32[1,4,16,1280]{3,2,1,0:T(8,128)S(1)} %pad_maximum_fusion.3), channel_id=1, source_target_pairs={{0,2},{2,0},{4,6},{6,4},{8,10},{10,8},{12,14},{14,12},{16,18},{18,... | collective-permute-start | bytes 983048 | tf_op jit(solution)/shard_map/ppermute | solution.py:28
  8.3 11.2 %collective-permute-start.2 = (f32[1,4,16,1280]{3,2,1,0:T(8,128)S(1)}, f32[1,4,16,1280]{3,2,1,0:T(8,128)S(1)}, u32[]{:S(2)}, u32[]{:S(2)}) collective-permute-start(f32[1,4,16,1280]{3,2,1,0:T(8,128)S(1)} %pad_maximum_fusion.3), channel_id=1, source_target_pairs={{0,4},{2,6},{4,0},{6,2},{8,12},{10,14},{12,8},{14,10},{16,20},{18,... | collective-permute-start | bytes 983048 | tf_op jit(solution)/shard_map/ppermute | solution.py:28
  9.8 9.6 %collective-permute-start = (f32[1,4,16,768]{3,2,1,0:T(8,128)S(1)}, f32[1,4,16,768]{3,2,1,0:T(8,128)S(1)}, u32[]{:S(2)}, u32[]{:S(2)}) collective-permute-start(f32[1,4,16,768]{3,2,1,0:T(8,128)S(1)} %bitcast.4), channel_id=1, source_target_pairs={{0,24},{2,26},{4,28},{6,30},{8,16},{10,18},{12,20},{14,22},{16,8},... | collective-permute-start | bytes 589832 | tf_op jit(solution)/shard_map/ppermute | solution.py:28
  10.3 12.3 %collective-permute-start.5 = (f32[2,4,16,512]{3,2,1,0:T(8,128)S(1)}, f32[2,4,16,512]{3,2,1,0:T(8,128)S(1)}, u32[]{:S(2)}, u32[]{:S(2)}) collective-permute-start(f32[2,4,16,512]{3,2,1,0:T(8,128)S(1)} %pad_maximum_fusion.4), channel_id=1, source_target_pairs={{0,8},{2,10},{4,12},{6,14},{8,0},{10,2},{12,4},{14,6},{16,24},{18,... | collective-permute-start | bytes 786440 | tf_op jit(solution)/shard_map/ppermute | solution.py:28
  19.5 5.9 %collective-permute-start.6 = (f32[1,2,16,1280]{3,2,1,0:T(8,128)S(1)}, f32[1,2,16,1280]{3,2,1,0:T(8,128)S(1)}, u32[]{:S(2)}, u32[]{:S(2)}) collective-permute-start(f32[1,2,16,1280]{3,2,1,0:T(8,128)S(1)} %slice.24), channel_id=1, source_target_pairs={{0,4},{2,6},{4,0},{6,2},{8,12},{10,14},{12,8},{14,10},{16,20},{18,... | collective-permute-start | bytes 491528 | tf_op jit(solution)/shard_map/ppermute | solution.py:28
  20.1 6.8 %collective-permute-start.7 = (f32[1,2,16,1280]{3,2,1,0:T(8,128)S(1)}, f32[1,2,16,1280]{3,2,1,0:T(8,128)S(1)}, u32[]{:S(2)}, u32[]{:S(2)}) collective-permute-start(f32[1,2,16,1280]{3,2,1,0:T(8,128)S(1)} %slice.25), channel_id=1, source_target_pairs={{0,2},{2,0},{4,6},{6,4},{8,10},{10,8},{12,14},{14,12},{16,18},{18,... | collective-permute-start | bytes 491528 | tf_op jit(solution)/shard_map/ppermute | solution.py:28
  26.9 9.6 %collective-permute-start.8 = (f32[3,4,16,512]{3,2,1,0:T(8,128)S(1)}, f32[3,4,16,512]{3,2,1,0:T(8,128)S(1)}, u32[]{:S(2)}, u32[]{:S(2)}) collective-permute-start(f32[3,4,16,512]{3,2,1,0:T(8,128)S(1)} %slice.26), channel_id=1, source_target_pairs={{0,2},{2,0},{4,6},{6,4},{8,10},{10,8},{12,14},{14,12},{16,18},{18,... | collective-permute-start | bytes 1179656 | tf_op jit(solution)/shard_map/ppermute | solution.py:28
  28.4 11.7 %collective-permute-start.9 = (f32[3,4,16,512]{3,2,1,0:T(8,128)S(1)}, f32[3,4,16,512]{3,2,1,0:T(8,128)S(1)}, u32[]{:S(2)}, u32[]{:S(2)}) collective-permute-start(f32[3,4,16,512]{3,2,1,0:T(8,128)S(1)} %slice.26), channel_id=1, source_target_pairs={{0,4},{2,6},{4,0},{6,2},{8,12},{10,14},{12,8},{14,10},{16,20},{18,... | collective-permute-start | bytes 1179656 | tf_op jit(solution)/shard_map/ppermute | solution.py:28
  29.3 11.0 %collective-permute-start.3 = (f32[2,4,16,768]{3,2,1,0:T(8,128)S(1)}, f32[2,4,16,768]{3,2,1,0:T(8,128)S(1)}, u32[]{:S(2)}, u32[]{:S(2)}) collective-permute-start(f32[2,4,16,768]{3,2,1,0:T(8,128)S(1)} %pad_maximum_fusion.2), channel_id=1, source_target_pairs={{0,8},{2,10},{4,12},{6,14},{8,0},{10,2},{12,4},{14,6},{16,24},{18,... | collective-permute-start | bytes 1179656 | tf_op jit(solution)/shard_map/ppermute | solution.py:28
  36.5 8.4 %collective-permute-start.10 = (f32[3,2,16,512]{3,2,1,0:T(8,128)S(1)}, f32[3,2,16,512]{3,2,1,0:T(8,128)S(1)}, u32[]{:S(2)}, u32[]{:S(2)}) collective-permute-start(f32[3,2,16,512]{3,2,1,0:T(8,128)S(1)} %slice.32), channel_id=1, source_target_pairs={{0,4},{2,6},{4,0},{6,2},{8,12},{10,14},{12,8},{14,10},{16,20},{18,... | collective-permute-start | bytes 589832 | tf_op jit(solution)/shard_map/ppermute | solution.py:28
  40.1 5.8 %copy-start = (f32[1024,256]{1,0:T(8,128)S(1)}, f32[1024,256]{1,0:T(8,128)}, u32[]{:S(2)}) copy-start(f32[1024,256]{1,0:T(8,128)} %refs_1_.2) | copy-start | bytes 3145732
  40.1 5.7 %collective-permute-start.11 = (f32[3,2,16,512]{3,2,1,0:T(8,128)S(1)}, f32[3,2,16,512]{3,2,1,0:T(8,128)S(1)}, u32[]{:S(2)}, u32[]{:S(2)}) collective-permute-start(f32[3,2,16,512]{3,2,1,0:T(8,128)S(1)} %slice.33), channel_id=1, source_target_pairs={{0,2},{2,0},{4,6},{6,4},{8,10},{10,8},{12,14},{14,12},{16,18},{18,... | collective-permute-start | bytes 589832 | tf_op jit(solution)/shard_map/ppermute | solution.py:28
  40.4 5.5 %copy-start.2 = (s32[4,4,4]{2,1,0:T(4,128)S(1)}, s32[4,4,4]{2,1,0:T(4,128)}, u32[]{:S(2)}) copy-start(s32[4,4,4]{2,1,0:T(4,128)} %refs_0_.2) | copy-start | bytes 772
  40.4 13.2 %collective-permute-start.14 = (f32[3,4,16,768]{3,2,1,0:T(8,128)S(1)}, f32[3,4,16,768]{3,2,1,0:T(8,128)S(1)}, u32[]{:S(2)}, u32[]{:S(2)}) collective-permute-start(f32[3,4,16,768]{3,2,1,0:T(8,128)S(1)} %slice.29), channel_id=1, source_target_pairs={{0,2},{2,0},{4,6},{6,4},{8,10},{10,8},{12,14},{14,12},{16,18},{18,... | collective-permute-start | bytes 1769480 | tf_op jit(solution)/shard_map/ppermute | solution.py:28
  42.4 12.5 %collective-permute-start.15 = (f32[3,4,16,768]{3,2,1,0:T(8,128)S(1)}, f32[3,4,16,768]{3,2,1,0:T(8,128)S(1)}, u32[]{:S(2)}, u32[]{:S(2)}) collective-permute-start(f32[3,4,16,768]{3,2,1,0:T(8,128)S(1)} %slice.29), channel_id=1, source_target_pairs={{0,4},{2,6},{4,0},{6,2},{8,12},{10,14},{12,8},{14,10},{16,20},{18,... | collective-permute-start | bytes 1769480 | tf_op jit(solution)/shard_map/ppermute | solution.py:28
  53.0 2.6 %collective-permute-start.12 = (f32[2,256,256]{2,1,0:T(8,128)S(1)}, f32[2,256,256]{2,1,0:T(8,128)S(1)}, u32[]{:S(2)}, u32[]{:S(2)}) collective-permute-start(f32[2,256,256]{2,1,0:T(8,128)S(1)} %get-tuple-element.30.own_ref), channel_id=1, source_target_pairs={{0,1},{1,0},{2,3},{3,2},{4,5},{5,4},{6,7},{7,6},{8,9},{9,8},{10,11... | collective-permute-start | bytes 1572872 | tf_op jit(solution)/shard_map/ppermute | solution.py:351
  53.1 2.6 %collective-permute-start.13 = (f32[2,256,256]{2,1,0:T(8,128)S(1)}, f32[2,256,256]{2,1,0:T(8,128)S(1)}, u32[]{:S(2)}, u32[]{:S(2)}) collective-permute-start(f32[2,256,256]{2,1,0:T(8,128)S(1)} %get-tuple-element.31), channel_id=1, source_target_pairs={{0,1},{1,0},{2,3},{3,2},{4,5},{5,4},{6,7},{7,6},{8,9},{9,8},{10,11... | collective-permute-start | bytes 1572872 | tf_op jit(solution)/shard_map/ppermute | solution.py:351
  53.6 9.1 %collective-permute-start.16 = (f32[3,2,16,768]{3,2,1,0:T(8,128)S(1)}, f32[3,2,16,768]{3,2,1,0:T(8,128)S(1)}, u32[]{:S(2)}, u32[]{:S(2)}) collective-permute-start(f32[3,2,16,768]{3,2,1,0:T(8,128)S(1)} %slice.34), channel_id=1, source_target_pairs={{0,4},{2,6},{4,0},{6,2},{8,12},{10,14},{12,8},{14,10},{16,20},{18,... | collective-permute-start | bytes 884744 | tf_op jit(solution)/shard_map/ppermute | solution.py:28
  54.9 8.8 %collective-permute-start.17 = (f32[3,2,16,768]{3,2,1,0:T(8,128)S(1)}, f32[3,2,16,768]{3,2,1,0:T(8,128)S(1)}, u32[]{:S(2)}, u32[]{:S(2)}) collective-permute-start(f32[3,2,16,768]{3,2,1,0:T(8,128)S(1)} %slice.35), channel_id=1, source_target_pairs={{0,2},{2,0},{4,6},{6,4},{8,10},{10,8},{12,14},{14,12},{16,18},{18,... | collective-permute-start | bytes 884744 | tf_op jit(solution)/shard_map/ppermute | solution.py:28
  55.7 8.0 %copy-start.1 = (s32[4,4,12]{2,1,0:T(4,128)S(1)}, s32[4,4,12]{2,1,0:T(4,128)}, u32[]{:S(2)}) copy-start(s32[4,4,12]{2,1,0:T(4,128)} %refs_0_.3) | copy-start | bytes 2308

commit v6 on v5

--- a/solution.py
+++ b/solution.py
@@ -24,100 +24,101 @@
     return dot(left[0], right[1]) + dot(left[1], right[0]) + dot(left[0], right[0])
 
 
-def across(value, axis, mask):
-    return lax.ppermute(value, axis, [(i, i ^ mask) for i in range(lax.axis_size(axis))])
-
-
-def line_masks(axis):
-    high = lax.axis_size(axis) // 4
-    return [4 * (step - 1) for step in iter_halves(high)]
-
-
-def iter_halves(step):
-    while step > 1:
-        yield step
-        step //= 2
-
-
-def spread(held, masks, axis):
-    for mask in masks:
-        held = jnp.concatenate([held, across(held, axis, mask)])
-    return held
-
-
-def line_order(masks):
-    order = [0]
-    for mask in masks:
-        order += [mask ^ other for other in order]
-    return order
+def after(held, *others):
+    return lax.optimization_barrier((held[0], [array for array, _ in others]))[0], held[1]
+
+
+def joined(*parts):
+    if len(parts) == 1:
+        return parts[0]
+    return jnp.concatenate([array for array, _ in parts]), [name for _, names in parts for name in names]
+
+
+def cut(held, begin, end):
+    return held[0][begin:end], held[1][begin:end]
+
+
+def sent(held, axis, mask):
+    array, names = held
+    swapped = lax.ppermute(array, axis, [(i, i ^ mask) for i in range(lax.axis_size(axis))])
+    return swapped, [(owner ^ mask, block) for owner, block in names]
 
 
 def around(held, axis):
-    return across(held, axis, 1), across(held, axis, 2)
-
-
-def onward(first, second, axis):
-    half = first.shape[1] // 2
-    return (first,), (second,), (across(first[:, :half], axis, 2), across(second[:, half:], axis, 1))
-
-
-def piece(array, order, low, start=0, column=0):
-    return array, [mask | low for mask in order], start, column
-
-
-def pieces_of(neighbours, order, column=0):
-    return [
-        piece(array, order, low, start, column)
-        for low, halves in enumerate(neighbours, 1)
-        for array, start in zip(halves, (0, halves[0].shape[1]))
+    return sent(held, axis, 1), sent(held, axis, 2)
+
+
+def onward(pair, axis, *more):
+    half = len(pair[0][1]) // 2
+    first, second = cut(pair[0], 0, half), cut(pair[1], half, 2 * half)
+    return joined(*more, second), joined(*more, first)
+
+
+def gather_panels(own, factor_blocks, right_side, axis):
+    steps = lax.axis_size(axis) // 4
+    masks = []
+    while steps > 1:
+        masks.append(4 * (steps - 1))
+        steps //= 2
+    count = len(own[1])
+    factor, jacobian = cut(own, 0, factor_blocks), cut(own, factor_blocks, count)
+
+    factor_line = [factor, sent(factor, axis, masks[0])]
+    jacobian_line = [jacobian, sent(jacobian, axis, masks[0])]
+    own_round = around(own, axis)
+    own_across = [sent(part, axis, mask) for part, mask in zip(onward(own_round, axis), (1, 2))]
+    for mask in masks[1:]:
+        factor_line.append(sent(joined(*factor_line), axis, mask))
+    factor_rest = after(joined(*factor_line[1:]), *own_across)
+    factor_round = around(factor_rest, axis)
+    for mask in masks[1:]:
+        jacobian_line.append(sent(joined(*jacobian_line), axis, mask))
+    early_round = around(joined(*jacobian_line[1:-1]), axis)
+    factor_across = [sent(part, axis, mask) for part, mask in zip(onward(factor_round, axis), (1, 2))]
+    late_parts = onward(early_round, axis, jacobian_line[-1])
+    late_round = [sent(part, axis, mask) for part, mask in zip(late_parts, (1, 2))]
+    size = len(jacobian_line[-1][1])
+    late_across = [
+        sent(part, axis, mask)
+        for part, mask in zip(onward([cut(part, 0, size) for part in late_round], axis), (1, 2))
     ]
-
-
-def gather_whole(part, axis):
-    everything = lax.all_gather(part, axis)
-    return [piece(everything, list(range(lax.axis_size(axis))), 0)]
-
-
-def gather_panels(factor_part, jacobian, right_side, axis):
-    masks = line_masks(axis)
-    order = line_order(masks)
-    factor_part, jacobian = factor_part[None], jacobian[None]
-    everything = jnp.concatenate([factor_part, jacobian], axis=3)
-    split_at = factor_part.shape[3]
-
-    factor_line = spread(factor_part, masks[:1], axis)
-    jacobian_line = spread(jacobian, masks[:1], axis)
-    own = around(everything, axis)
-    jacobian_line, own = lax.optimization_barrier((jacobian_line, own))
-    own = onward(*own, axis)
-    factor_line = spread(factor_line, masks[1:], axis)
-    factor_line, own = lax.optimization_barrier((factor_line, own))
-    factor_rest = onward(*around(factor_line[1:], axis), axis)
-    jacobian_line = spread(jacobian_line, masks[1:], axis)
-    late, jacobian_line = lax.optimization_barrier((right_side, jacobian_line))
-    jacobian_rest = onward(*around(jacobian_line[1:], axis), axis)
-
-    factor = [piece(factor_line, order, 0)]
-    factor += pieces_of(own, order[:1])
-    factor += pieces_of(factor_rest, order[1:])
-    jacobians = [piece(jacobian_line, order, 0)]
-    jacobians += pieces_of(own, order[:1], split_at)
-    jacobians += pieces_of(jacobian_rest, order[1:])
-    return factor, jacobians, late
+    right_side, _ = after((right_side, None), *late_parts)
+    arrived = [own, *factor_line[1:], *jacobian_line[1:], *own_round, *own_across, *factor_round, *factor_across]
+    return arrived + [*early_round, *late_round, *late_across], right_side
+
+
+def gather_whole(own, axis):
+    everything = lax.all_gather(own[0], axis, tiled=True)
+    return [(everything, [(owner, block) for owner in range(lax.axis_size(axis)) for _, block in own[1]])]
+
+
+def runs_of(pieces, begin, end):
+    chosen = []
+    for array, names in pieces:
+        runs = []
+        for at, (owner, block) in enumerate(names):
+            if not begin <= block < end:
+                continue
+            if runs and runs[-1][0] + runs[-1][1] == at and names[at - 1] == (owner, block - 1):
+                runs[-1][1] += 1
+            else:
+                runs.append([at, 1, owner, block - begin])
+        if runs:
+            chosen.append((array, runs))
+    return chosen
 
 
 def place_rows(pieces, refs, relative, axis, panels, sem):
     me = lax.axis_index(axis)
-    wide = panels.shape[2]
     copies = []
-    for (array, owners, start, column), ref in zip(pieces, refs):
-        parts, rows = array.shape[1:3]
-        for place, owner in enumerate(owners):
-            at = pl.multiple_of((me ^ owner) * rows, rows) if relative else owner * rows
+    for (array, runs), ref in zip(pieces, refs):
+        rows = array.shape[1]
+        for at, length, owner, block in runs:
+            row = pl.multiple_of((me ^ owner) * rows, rows) if relative else owner * rows
             copies.append(
                 pltpu.make_async_copy(
-                    ref.at[place, :, :, pl.ds(column, wide)],
-                    panels.at[pl.ds(start, parts), pl.ds(at, rows), :],
+                    ref.at[pl.ds(at, length)],
+                    panels.at[pl.ds(block, length), pl.ds(row, rows), :],
                     sem.at[len(copies)],
                 )
             )
@@ -154,7 +155,7 @@
     extra = 0 if nodes == 1 else 1 if nodes == 2 else 2
     width = columns + extra * size
     n = len(pieces)
-    n_copies = sum(len(owners) for _, owners, _, _ in pieces)
+    n_copies = sum(len(runs) for _, runs in pieces)
 
     def kernel(*refs):
         pattern_ref, rhs_ref = refs[:2]
@@ -176,8 +177,8 @@
         previous = None
         for s in range(supers):
             own = rhs_ref[s * size : (s + 1) * size, :]
-            low = masked(panels[s, :, size:], pattern_ref, s, size // pattern_ref.shape[1])
-            panels[s, :, size:] = low
+            low = masked(panels[supers + s], pattern_ref, s, size // pattern_ref.shape[1])
+            panels[supers + s] = low
             if s == 0:
                 parts = [own]
                 if extra:
@@ -187,7 +188,7 @@
                 target = jnp.concatenate(parts, axis=1)
             else:
                 target = jnp.concatenate([own] + [zeros] * extra, axis=1) - product(split(low), split(previous))
-            previous = product(split(panels[s, :, :size]), split(target))
+            previous = product(split(panels[s]), split(target))
             forward[s] = previous
 
         entering = None
@@ -200,12 +201,12 @@
                     target = target - jnp.concatenate(shift, axis=1)
             else:
                 target = target - entering
-            solved = product(split(panels[s, :, :size].T), split(target))
+            solved = product(split(panels[s].T), split(target))
             sol_ref[s * size : (s + 1) * size, :] = solved[:, :columns]
             for e, ref in enumerate(extra_refs):
                 ref[s * size : (s + 1) * size, :] = solved[:, columns + e * size : columns + (e + 1) * size]
             if s > 0 or nodes > 1:
-                entering = product(split(panels[s, :, size:].T), split(solved))
+                entering = product(split(panels[supers + s].T), split(solved))
 
         if nodes == 2:
             upper = index == 1
@@ -226,7 +227,7 @@
         in_specs=[SMEM, VMEM] + [ANY] * n,
         out_specs=[VMEM] * (3 + extra),
         scratch_shapes=[
-            pltpu.VMEM((supers, size, 2 * size), jnp.float32),
+            pltpu.VMEM((2 * supers, size, size), jnp.float32),
             pltpu.VMEM((supers, size, width), jnp.float32),
             pltpu.SemaphoreType.DMA((n_copies,)),
         ],
@@ -235,7 +236,7 @@
             flops=16 * supers * size * size * width, bytes_accessed=span * size, transcendentals=0
         ),
         name="solve",
-    )(pattern, right_side, *[array for array, *_ in pieces])
+    )(pattern, right_side, *[array for array, _ in pieces])
     return out[0], out[1 : 1 + extra], out[1 + extra], out[2 + extra]
 
 
@@ -294,7 +295,7 @@
     span, columns = right_side.shape
     wide = 3 * size
     n = len(pieces)
-    n_copies = sum(len(owners) for _, owners, _, _ in pieces)
+    n_copies = sum(len(runs) for _, runs in pieces)
 
     def kernel(*refs):
         pattern_ref, rhs_ref, high_ref, low_ref = refs[:4]
@@ -303,7 +304,8 @@
         for copy in place_rows(pieces, piece_refs, relative, "rhs", panels, sem):
             copy.wait()
         for s in range(supers):
-            panel = masked(panels[s], pattern_ref, s, size // pattern_ref.shape[1])
+            rows = jnp.concatenate([panels[3 * s + c] for c in range(3)], axis=1)
+            panel = masked(rows, pattern_ref, s, size // pattern_ref.shape[1])
             window = pl.ds(s * size, wide)
             out_ref[s * size : (s + 1) * size, :] = rhs_ref[s * size : (s + 1) * size, :] - product(
                 split(panel), (high_ref[window, :], low_ref[window, :])
@@ -315,7 +317,7 @@
         in_specs=[SMEM] + [VMEM] * 3 + [ANY] * n,
         out_specs=VMEM,
         scratch_shapes=[
-            pltpu.VMEM((supers, size, wide), jnp.float32),
+            pltpu.VMEM((3 * supers, size, size), jnp.float32),
             pltpu.SemaphoreType.DMA((n_copies,)),
         ],
         compiler_params=pltpu.CompilerParams(vmem_limit_bytes=VMEM_LIMIT),
@@ -323,7 +325,7 @@
             flops=6 * span * wide * columns, bytes_accessed=4 * span * (wide + 3 * columns), transcendentals=0
         ),
         name="residual",
-    )(pattern, right_side, high, low, *[array for array, *_ in pieces])
+    )(pattern, right_side, high, low, *[array for array, _ in pieces])
 
 
 def dot(left, right):
@@ -336,15 +338,18 @@
     span = supers * size
     nodes = lax.axis_size("node")
 
-    factor_part = jnp.concatenate([diag_inv, lower], axis=2)
+    own = jnp.concatenate(
+        [diag_inv, lower, jacobian.reshape(supers, rows, 3, size).swapaxes(1, 2).reshape(3 * supers, rows, size)]
+    )
+    own = own, [(0, block) for block in range(own.shape[0])]
     count = lax.axis_size("rhs")
-    relative = count >= 8 and not count & (count - 1)
-    late = right_side
+    relative = count >= 16 and not count & (count - 1)
     if relative:
-        factor, jacobians, late = gather_panels(factor_part, jacobian, right_side, "rhs")
+        arrived, late = gather_panels(own, 2 * supers, right_side, "rhs")
     else:
-        factor = gather_whole(factor_part, "rhs")
-        jacobians = gather_whole(jacobian, "rhs")
+        arrived, late = gather_whole(own, "rhs"), right_side
+    factor = runs_of(arrived, 0, 2 * supers)
+    jacobians = runs_of(arrived, 2 * supers, len(own[1]))
 
     sol, parts, down, up = solve(factor, relative, late, factor_pattern, nodes, supers, size)
     if nodes == 2:

time: 68.5 us -> 64.5 us (0.942)
  waiting for transfers between devices: 25.3 us -> 21.1 us
  Pallas kernels: 13.7 us -> 12.6 us
  local copies, waits for them, and re-layouts: 0.18 us -> 0.96 us
    ppermute x16 -> x18, waiting for transfers between devices: 25.2 us -> 21.1 us  [sent(): lax.ppermute(array, axis, [(i, i ^ mask) for i in range(lax.axis_size(axi...]
    concatenate x5 -> x7, other arithmetic: 0.15 us -> 1.15 us  [the longest x2 0.94 us: on_device(): jnp.concatenate([diag_inv, lower, jacobian.reshape(supers, rows, 3, size)...]
    broadcast_in_dim x1 -> x0, other arithmetic: 0.92 us -> none  [gather_panels(): factor_part, jacobian = (factor_part[None], jacobian[None])]
    unnamed x8 -> x12, local copies, waits for them, and re-layouts: 0.02 us -> 0.86 us
    ppermute x16 -> x18, starting transfers between devices: 26.7 us -> 27.2 us  [sent(): lax.ppermute(array, axis, [(i, i ^ mask) for i in range(lax.axis_size(axi...]
  transfers between devices with their start and end apart: 18 -> 20, of which waited for: 12 -> 10; matrix products, arithmetic and copies ran while one was open for 0% -> 1% of each run, Pallas kernels for 13% -> 13%
where the time goes in v6:
time: 64.5 us; the launch traced here: 64.4 us
  starting transfers between devices  27.8 us (43%)
  waiting for transfers between devices  21.1 us (33%)
  Pallas kernels  12.6 us (20%)
  other arithmetic  1.15 us (2%)
  local copies, waits for them, and re-layouts  0.96 us (1%)
  between operations  0.8 us (1%)
    ppermute x18, starting transfers between devices, sent(): lax.ppermute(array, axis, [(i, i ^ mask) for i in range(lax.axis_size(axi...  27.2 us
    ppermute x18, waiting for transfers between devices, sent(): lax.ppermute(array, axis, [(i, i ^ mask) for i in range(lax.axis_size(axi...  21.1 us
    pallas_call x1, Pallas kernels, solve(): pl.pallas_call(kernel, out_shape=shapes([(span, columns)] + [(span, size)...  6.69 us
    pallas_call x1, Pallas kernels, subtract_product(): pl.pallas_call(kernel, out_shape=shapes([(span, columns)])[0], in_specs=[...  3.97 us
    pallas_call x1, Pallas kernels, finish(): pl.pallas_call(kernel, out_shape=shapes([(span, columns)]) + [windows, wi...  1.96 us
  transfers between devices with their start and end apart: 20, of which 10 were waited for; matrix products, arithmetic and copies ran while one was open for 1% of the time, Pallas kernels for 13%

profile of v6, /device:TPU:0, one launch (start us, length us, event | category | flops | bytes accessed | tf_op | source)
XLA Modules:
  0.0 64.4 jit_solution(9158458392986567738)
XLA Ops:
  1.6 5.1 %collective-permute-start.4 = (f32[8,16,256]{2,1,0:T(8,128)S(1)}, f32[8,16,256]{2,1,0:T(8,128)S(1)}, u32[]{:S(2)}, u32[]{:S(2)}) collective-permute-start(f32[8,16,256]{2,1,0:T(8,128)S(1)} %pad_maximum_fusion.7), channel_id=1, source_target_pairs={{0,24},{2,26},{4,28},{6,30},{8,16},{10,18},{12,20},{14,22},{16,8},... | collective-permute-start | bytes 393224 | tf_op jit(solution)/shard_map/ppermute | solution.py:43
  7.6 1.6 %collective-permute-start.6 = (f32[20,16,256]{2,1,0:T(8,128)S(1)}, f32[20,16,256]{2,1,0:T(8,128)S(1)}, u32[]{:S(2)}, u32[]{:S(2)}) collective-permute-start(f32[20,16,256]{2,1,0:T(8,128)S(1)} %pad_maximum_fusion.4.refs_2_.refs_4_), channel_id=1, source_target_pairs={{0,2},{2,0},{4,6},{6,4},{8,10},{10,8},{12,14},{14,12},{16,18},{18,... | collective-permute-start | bytes 983048 | tf_op jit(solution)/shard_map/ppermute | solution.py:43
  9.2 1.5 %collective-permute-start.7 = (f32[20,16,256]{2,1,0:T(8,128)S(1)}, f32[20,16,256]{2,1,0:T(8,128)S(1)}, u32[]{:S(2)}, u32[]{:S(2)}) collective-permute-start(f32[20,16,256]{2,1,0:T(8,128)S(1)} %pad_maximum_fusion.4.refs_2_.refs_4_), channel_id=1, source_target_pairs={{0,4},{2,6},{4,0},{6,2},{8,12},{10,14},{12,8},{14,10},{16,20},{18,... | collective-permute-start | bytes 983048 | tf_op jit(solution)/shard_map/ppermute | solution.py:43
  10.7 2.1 %collective-permute-start.5 = (f32[16,16,256]{2,1,0:T(8,128)S(1)}, f32[16,16,256]{2,1,0:T(8,128)S(1)}, u32[]{:S(2)}, u32[]{:S(2)}) collective-permute-start(f32[16,16,256]{2,1,0:T(8,128)S(1)} %pad_maximum_fusion.5), channel_id=1, source_target_pairs={{0,8},{2,10},{4,12},{6,14},{8,0},{10,2},{12,4},{14,6},{16,24},{18,... | collective-permute-start | bytes 786440 | tf_op jit(solution)/shard_map/ppermute | solution.py:43
  12.8 2.5 %collective-permute-start = (f32[12,16,256]{2,1,0:T(8,128)S(1)}, f32[12,16,256]{2,1,0:T(8,128)S(1)}, u32[]{:S(2)}, u32[]{:S(2)}) collective-permute-start(f32[12,16,256]{2,1,0:T(8,128)S(1)} %bitcast.2), channel_id=1, source_target_pairs={{0,24},{2,26},{4,28},{6,30},{8,16},{10,18},{12,20},{14,22},{16,8},... | collective-permute-start | bytes 589832 | tf_op jit(solution)/shard_map/ppermute | solution.py:43
  15.3 1.6 %collective-permute-done.6.refs_5_.refs_7_ = f32[20,16,256]{2,1,0:T(8,128)S(1)} collective-permute-done((f32[20,16,256]{2,1,0:T(8,128)S(1)}, f32[20,16,256]{2,1,0:T(8,128)S(1)}, u32[]{:S(2)}, u32[]{:S(2)}) %collective-permute-start.6) | collective-permute-done | bytes 327712 | tf_op jit(solution)/shard_map/ppermute | solution.py:43
  16.9 1.6 %collective-permute-start.8 = (f32[10,16,256]{2,1,0:T(8,128)S(1)}, f32[10,16,256]{2,1,0:T(8,128)S(1)}, u32[]{:S(2)}, u32[]{:S(2)}) collective-permute-start(f32[10,16,256]{2,1,0:T(8,128)S(1)} %slice.52), channel_id=1, source_target_pairs={{0,4},{2,6},{4,0},{6,2},{8,12},{10,14},{12,8},{14,10},{16,20},{18,... | collective-permute-start | bytes 491528 | tf_op jit(solution)/shard_map/ppermute | solution.py:43
  18.5 1.6 %collective-permute-start.9 = (f32[10,16,256]{2,1,0:T(8,128)S(1)}, f32[10,16,256]{2,1,0:T(8,128)S(1)}, u32[]{:S(2)}, u32[]{:S(2)}) collective-permute-start(f32[10,16,256]{2,1,0:T(8,128)S(1)} %slice.53), channel_id=1, source_target_pairs={{0,2},{2,0},{4,6},{6,4},{8,10},{10,8},{12,14},{14,12},{16,18},{18,... | collective-permute-start | bytes 491528 | tf_op jit(solution)/shard_map/ppermute | solution.py:43
  20.5 1.7 %collective-permute-done.8.refs_7_.refs_10_ = f32[10,16,256]{2,1,0:T(8,128)S(1)} collective-permute-done((f32[10,16,256]{2,1,0:T(8,128)S(1)}, f32[10,16,256]{2,1,0:T(8,128)S(1)}, u32[]{:S(2)}, u32[]{:S(2)}) %collective-permute-start.8) | collective-permute-done | bytes 163872 | tf_op jit(solution)/shard_map/ppermute | solution.py:43
  22.2 1.6 %collective-permute-done.9.refs_9_ = f32[10,16,256]{2,1,0:T(8,128)S(1)} collective-permute-done((f32[10,16,256]{2,1,0:T(8,128)S(1)}, f32[10,16,256]{2,1,0:T(8,128)S(1)}, u32[]{:S(2)}, u32[]{:S(2)}) %collective-permute-start.9) | collective-permute-done | bytes 163872 | tf_op jit(solution)/shard_map/ppermute | solution.py:43
  23.8 1.1 %collective-permute-start.11 = (f32[24,16,256]{2,1,0:T(8,128)S(1)}, f32[24,16,256]{2,1,0:T(8,128)S(1)}, u32[]{:S(2)}, u32[]{:S(2)}) collective-permute-start(f32[24,16,256]{2,1,0:T(8,128)S(1)} %pad_maximum_fusion.3), channel_id=1, source_target_pairs={{0,4},{2,6},{4,0},{6,2},{8,12},{10,14},{12,8},{14,10},{16,20},{18,... | collective-permute-start | bytes 1179656 | tf_op jit(solution)/shard_map/ppermute | solution.py:43
  26.0 1.6 %collective-permute-start.2 = (f32[12,16,256]{2,1,0:T(8,128)S(1)}, f32[12,16,256]{2,1,0:T(8,128)S(1)}, u32[]{:S(2)}, u32[]{:S(2)}) collective-permute-start(f32[12,16,256]{2,1,0:T(8,128)S(1)} %collective-permute-done.refs_5_), channel_id=1, source_target_pairs={{0,4},{2,6},{4,0},{6,2},{8,12},{10,14},{12,8},{14,10},{16,20},{18,... | collective-permute-start | bytes 589832 | tf_op jit(solution)/shard_map/ppermute | solution.py:43
  28.1 7.8 %collective-permute-done.11.refs_9_ = f32[24,16,256]{2,1,0:T(8,128)S(1)} collective-permute-done((f32[24,16,256]{2,1,0:T(8,128)S(1)}, f32[24,16,256]{2,1,0:T(8,128)S(1)}, u32[]{:S(2)}, u32[]{:S(2)}) %collective-permute-start.11) | collective-permute-done | bytes 393248 | tf_op jit(solution)/shard_map/ppermute | solution.py:43
  35.9 1.6 %collective-permute-start.12 = (f32[12,16,256]{2,1,0:T(8,128)S(1)}, f32[12,16,256]{2,1,0:T(8,128)S(1)}, u32[]{:S(2)}, u32[]{:S(2)}) collective-permute-start(f32[12,16,256]{2,1,0:T(8,128)S(1)} %slice.54), channel_id=1, source_target_pairs={{0,2},{2,0},{4,6},{6,4},{8,10},{10,8},{12,14},{14,12},{16,18},{18,... | collective-permute-start | bytes 589832 | tf_op jit(solution)/shard_map/ppermute | solution.py:43
  38.1 2.0 %collective-permute-done.2.refs_12_ = f32[12,16,256]{2,1,0:T(8,128)S(1)} collective-permute-done((f32[12,16,256]{2,1,0:T(8,128)S(1)}, f32[12,16,256]{2,1,0:T(8,128)S(1)}, u32[]{:S(2)}, u32[]{:S(2)}) %collective-permute-start.2) | collective-permute-done | bytes 196640 | tf_op jit(solution)/shard_map/ppermute | solution.py:43
  40.1 1.1 %collective-permute-done.3.refs_11_ = f32[12,16,256]{2,1,0:T(8,128)S(1)} collective-permute-done((f32[12,16,256]{2,1,0:T(8,128)S(1)}, f32[12,16,256]{2,1,0:T(8,128)S(1)}, u32[]{:S(2)}, u32[]{:S(2)}) %collective-permute-start.3) | collective-permute-done | bytes 196640 | tf_op jit(solution)/shard_map/ppermute | solution.py:43
  41.4 1.0 %collective-permute-start.17 = (f32[30,16,256]{2,1,0:T(8,128)S(1)}, f32[30,16,256]{2,1,0:T(8,128)S(1)}, u32[]{:S(2)}, u32[]{:S(2)}) collective-permute-start(f32[30,16,256]{2,1,0:T(8,128)S(1)} %get-tuple-element.20), channel_id=1, source_target_pairs={{0,4},{2,6},{4,0},{6,2},{8,12},{10,14},{12,8},{14,10},{16,20},{18,... | collective-permute-start | bytes 1474568 | tf_op jit(solution)/shard_map/ppermute | solution.py:43
  42.4 1.5 %collective-permute-start.16 = (f32[30,16,256]{2,1,0:T(8,128)S(1)}, f32[30,16,256]{2,1,0:T(8,128)S(1)}, u32[]{:S(2)}, u32[]{:S(2)}) collective-permute-start(f32[30,16,256]{2,1,0:T(8,128)S(1)} %get-tuple-element.21), channel_id=1, source_target_pairs={{0,2},{2,0},{4,6},{6,4},{8,10},{10,8},{12,14},{14,12},{16,18},{18,... | collective-permute-start | bytes 1474568 | tf_op jit(solution)/shard_map/ppermute | solution.py:43
  43.8 1.6 %collective-permute-done.12.refs_10_ = f32[12,16,256]{2,1,0:T(8,128)S(1)} collective-permute-done((f32[12,16,256]{2,1,0:T(8,128)S(1)}, f32[12,16,256]{2,1,0:T(8,128)S(1)}, u32[]{:S(2)}, u32[]{:S(2)}) %collective-permute-start.12) | collective-permute-done | bytes 196640 | tf_op jit(solution)/shard_map/ppermute | solution.py:43
  45.5 6.7 %solve.1 = (f32[1024,256]{1,0:T(8,128)S(1)}, f32[1024,256]{1,0:T(8,128)S(1)}, f32[2,256,256]{2,1,0:T(8,128)S(1)}, f32[2,256,256]{2,1,0:T(8,128)S(1)}) custom-call(s32[4,4,4]{2,1,0:T(4,128)S(1)} %copy-done.2, f32[1024,256]{1,0:T(8,128)S(1)} %copy-done, f32[20,16,256]{2,1,0:T(8,128)S(1)} %pad_maximum_fusion.4.refs_2_.refs_4_, ...), custom_call_target="tpu_custom_call" | custom-call | flops 2147483648 | bytes 262144 | tf_op jit(solution)/shard_map/solve/pallas_call | solution.py:224
  53.7 1.6 %collective-permute-start.19 = (f32[12,16,256]{2,1,0:T(8,128)S(1)}, f32[12,16,256]{2,1,0:T(8,128)S(1)}, u32[]{:S(2)}, u32[]{:S(2)}) collective-permute-start(f32[12,16,256]{2,1,0:T(8,128)S(1)} %slice.57), channel_id=1, source_target_pairs={{0,4},{2,6},{4,0},{6,2},{8,12},{10,14},{12,8},{14,10},{16,20},{18,... | collective-permute-start | bytes 589832 | tf_op jit(solution)/shard_map/ppermute | solution.py:43
  55.3 2.0 %finish.1 = (f32[1024,256]{1,0:T(8,128)}, bf16[1536,256]{1,0:T(8,128)(2,1)S(1)}, bf16[1536,256]{1,0:T(8,128)(2,1)S(1)}) custom-call(f32[1024,256]{1,0:T(8,128)S(1)} %get-tuple-element.13.sol_ref, f32[1024,256]{1,0:T(8,128)S(1)} %get-tuple-element.14.part_ref, f32[2,256,256]{2,1,0:T(8,128)S(1)} %get-tuple-element.15.own_ref, ...), custom_call_target="tpu_custom_call" | custom-call | flops 100663296 | bytes 262144 | tf_op jit(solution)/shard_map/finish/pallas_call | solution.py:268
  57.3 2.4 %collective-permute-done.18.refs_15_ = f32[12,16,256]{2,1,0:T(8,128)S(1)} collective-permute-done((f32[12,16,256]{2,1,0:T(8,128)S(1)}, f32[12,16,256]{2,1,0:T(8,128)S(1)}, u32[]{:S(2)}, u32[]{:S(2)}) %collective-permute-start.18) | collective-permute-done | bytes 196640 | tf_op jit(solution)/shard_map/ppermute | solution.py:43
  60.4 4.0 %residual.1 = f32[1024,256]{1,0:T(8,128)} custom-call(s32[4,4,12]{2,1,0:T(4,128)S(1)} %copy-done.1, f32[1024,256]{1,0:T(8,128)S(1)} %copy-done, bf16[1536,256]{1,0:T(8,128)(2,1)S(1)} %get-tuple-element.18.refs_2_, bf16[1536,256]{1,0:T(8,128)(2,1)S(1)} %get-tuple-element.19.refs_3_, f32[20,16,256]{2,1,0:T(8,128)S(1)} %pad_maximum_fusion.4.refs_2_.refs_4_, ...), custom_call_target="tpu_custom_call" | custom-call | flops 1207959552 | bytes 6291456 | tf_op jit(solution)/shard_map/residual/pallas_call | solution.py:314
  (47 shorter events, 6.9 us)
Async XLA Ops:
  0.6 6.1 %copy-start.5 = (f32[4,16,768]{2,1,0:T(8,128)S(1)}, f32[4,16,768]{2,1,0:T(8,128)}, u32[]{:S(2)}) copy-start(f32[4,16,768]{2,1,0:T(8,128)} %param.10) | copy-start | bytes 589828
  1.6 9.1 %collective-permute-start.4 = (f32[8,16,256]{2,1,0:T(8,128)S(1)}, f32[8,16,256]{2,1,0:T(8,128)S(1)}, u32[]{:S(2)}, u32[]{:S(2)}) collective-permute-start(f32[8,16,256]{2,1,0:T(8,128)S(1)} %pad_maximum_fusion.7), channel_id=1, source_target_pairs={{0,24},{2,26},{4,28},{6,30},{8,16},{10,18},{12,20},{14,22},{16,8},... | collective-permute-start | bytes 393224 | tf_op jit(solution)/shard_map/ppermute | solution.py:43
  7.6 9.2 %collective-permute-start.6 = (f32[20,16,256]{2,1,0:T(8,128)S(1)}, f32[20,16,256]{2,1,0:T(8,128)S(1)}, u32[]{:S(2)}, u32[]{:S(2)}) collective-permute-start(f32[20,16,256]{2,1,0:T(8,128)S(1)} %pad_maximum_fusion.4.refs_2_.refs_4_), channel_id=1, source_target_pairs={{0,2},{2,0},{4,6},{6,4},{8,10},{10,8},{12,14},{14,12},{16,18},{18,... | collective-permute-start | bytes 983048 | tf_op jit(solution)/shard_map/ppermute | solution.py:43
  9.2 9.3 %collective-permute-start.7 = (f32[20,16,256]{2,1,0:T(8,128)S(1)}, f32[20,16,256]{2,1,0:T(8,128)S(1)}, u32[]{:S(2)}, u32[]{:S(2)}) collective-permute-start(f32[20,16,256]{2,1,0:T(8,128)S(1)} %pad_maximum_fusion.4.refs_2_.refs_4_), channel_id=1, source_target_pairs={{0,4},{2,6},{4,0},{6,2},{8,12},{10,14},{12,8},{14,10},{16,20},{18,... | collective-permute-start | bytes 983048 | tf_op jit(solution)/shard_map/ppermute | solution.py:43
  10.7 9.8 %collective-permute-start.5 = (f32[16,16,256]{2,1,0:T(8,128)S(1)}, f32[16,16,256]{2,1,0:T(8,128)S(1)}, u32[]{:S(2)}, u32[]{:S(2)}) collective-permute-start(f32[16,16,256]{2,1,0:T(8,128)S(1)} %pad_maximum_fusion.5), channel_id=1, source_target_pairs={{0,8},{2,10},{4,12},{6,14},{8,0},{10,2},{12,4},{14,6},{16,24},{18,... | collective-permute-start | bytes 786440 | tf_op jit(solution)/shard_map/ppermute | solution.py:43
  12.8 13.1 %collective-permute-start = (f32[12,16,256]{2,1,0:T(8,128)S(1)}, f32[12,16,256]{2,1,0:T(8,128)S(1)}, u32[]{:S(2)}, u32[]{:S(2)}) collective-permute-start(f32[12,16,256]{2,1,0:T(8,128)S(1)} %bitcast.2), channel_id=1, source_target_pairs={{0,24},{2,26},{4,28},{6,30},{8,16},{10,18},{12,20},{14,22},{16,8},... | collective-permute-start | bytes 589832 | tf_op jit(solution)/shard_map/ppermute | solution.py:43
  16.9 5.4 %collective-permute-start.8 = (f32[10,16,256]{2,1,0:T(8,128)S(1)}, f32[10,16,256]{2,1,0:T(8,128)S(1)}, u32[]{:S(2)}, u32[]{:S(2)}) collective-permute-start(f32[10,16,256]{2,1,0:T(8,128)S(1)} %slice.52), channel_id=1, source_target_pairs={{0,4},{2,6},{4,0},{6,2},{8,12},{10,14},{12,8},{14,10},{16,20},{18,... | collective-permute-start | bytes 491528 | tf_op jit(solution)/shard_map/ppermute | solution.py:43
  18.5 5.4 %collective-permute-start.9 = (f32[10,16,256]{2,1,0:T(8,128)S(1)}, f32[10,16,256]{2,1,0:T(8,128)S(1)}, u32[]{:S(2)}, u32[]{:S(2)}) collective-permute-start(f32[10,16,256]{2,1,0:T(8,128)S(1)} %slice.53), channel_id=1, source_target_pairs={{0,2},{2,0},{4,6},{6,4},{8,10},{10,8},{12,14},{14,12},{16,18},{18,... | collective-permute-start | bytes 491528 | tf_op jit(solution)/shard_map/ppermute | solution.py:43
  23.8 12.1 %collective-permute-start.11 = (f32[24,16,256]{2,1,0:T(8,128)S(1)}, f32[24,16,256]{2,1,0:T(8,128)S(1)}, u32[]{:S(2)}, u32[]{:S(2)}) collective-permute-start(f32[24,16,256]{2,1,0:T(8,128)S(1)} %pad_maximum_fusion.3), channel_id=1, source_target_pairs={{0,4},{2,6},{4,0},{6,2},{8,12},{10,14},{12,8},{14,10},{16,20},{18,... | collective-permute-start | bytes 1179656 | tf_op jit(solution)/shard_map/ppermute | solution.py:43
  25.0 12.5 %collective-permute-start.10 = (f32[24,16,256]{2,1,0:T(8,128)S(1)}, f32[24,16,256]{2,1,0:T(8,128)S(1)}, u32[]{:S(2)}, u32[]{:S(2)}) collective-permute-start(f32[24,16,256]{2,1,0:T(8,128)S(1)} %pad_maximum_fusion.3), channel_id=1, source_target_pairs={{0,2},{2,0},{4,6},{6,4},{8,10},{10,8},{12,14},{14,12},{16,18},{18,... | collective-permute-start | bytes 1179656 | tf_op jit(solution)/shard_map/ppermute | solution.py:43
  25.9 15.4 %collective-permute-start.1 = (f32[24,16,256]{2,1,0:T(8,128)S(1)}, f32[24,16,256]{2,1,0:T(8,128)S(1)}, u32[]{:S(2)}, u32[]{:S(2)}) collective-permute-start(f32[24,16,256]{2,1,0:T(8,128)S(1)} %pad_maximum_fusion.2), channel_id=1, source_target_pairs={{0,8},{2,10},{4,12},{6,14},{8,0},{10,2},{12,4},{14,6},{16,24},{18,... | collective-permute-start | bytes 1179656 | tf_op jit(solution)/shard_map/ppermute | solution.py:43
  26.0 14.2 %collective-permute-start.2 = (f32[12,16,256]{2,1,0:T(8,128)S(1)}, f32[12,16,256]{2,1,0:T(8,128)S(1)}, u32[]{:S(2)}, u32[]{:S(2)}) collective-permute-start(f32[12,16,256]{2,1,0:T(8,128)S(1)} %collective-permute-done.refs_5_), channel_id=1, source_target_pairs={{0,4},{2,6},{4,0},{6,2},{8,12},{10,14},{12,8},{14,10},{16,20},{18,... | collective-permute-start | bytes 589832 | tf_op jit(solution)/shard_map/ppermute | solution.py:43
  27.5 13.7 %collective-permute-start.3 = (f32[12,16,256]{2,1,0:T(8,128)S(1)}, f32[12,16,256]{2,1,0:T(8,128)S(1)}, u32[]{:S(2)}, u32[]{:S(2)}) collective-permute-start(f32[12,16,256]{2,1,0:T(8,128)S(1)} %collective-permute-done.refs_5_), channel_id=1, source_target_pairs={{0,2},{2,0},{4,6},{6,4},{8,10},{10,8},{12,14},{14,12},{16,18},{18,... | collective-permute-start | bytes 589832 | tf_op jit(solution)/shard_map/ppermute | solution.py:43
  35.9 9.5 %collective-permute-start.12 = (f32[12,16,256]{2,1,0:T(8,128)S(1)}, f32[12,16,256]{2,1,0:T(8,128)S(1)}, u32[]{:S(2)}, u32[]{:S(2)}) collective-permute-start(f32[12,16,256]{2,1,0:T(8,128)S(1)} %slice.54), channel_id=1, source_target_pairs={{0,2},{2,0},{4,6},{6,4},{8,10},{10,8},{12,14},{14,12},{16,18},{18,... | collective-permute-start | bytes 589832 | tf_op jit(solution)/shard_map/ppermute | solution.py:43
  37.5 8.0 %copy-start = (f32[1024,256]{1,0:T(8,128)S(1)}, f32[1024,256]{1,0:T(8,128)}, u32[]{:S(2)}) copy-start(f32[1024,256]{1,0:T(8,128)} %refs_1_.2) | copy-start | bytes 3145732
  37.5 7.9 %collective-permute-start.13 = (f32[12,16,256]{2,1,0:T(8,128)S(1)}, f32[12,16,256]{2,1,0:T(8,128)S(1)}, u32[]{:S(2)}, u32[]{:S(2)}) collective-permute-start(f32[12,16,256]{2,1,0:T(8,128)S(1)} %slice.55), channel_id=1, source_target_pairs={{0,4},{2,6},{4,0},{6,2},{8,12},{10,14},{12,8},{14,10},{16,20},{18,... | collective-permute-start | bytes 589832 | tf_op jit(solution)/shard_map/ppermute | solution.py:43
  41.2 4.2 %copy-start.2 = (s32[4,4,4]{2,1,0:T(4,128)S(1)}, s32[4,4,4]{2,1,0:T(4,128)}, u32[]{:S(2)}) copy-start(s32[4,4,4]{2,1,0:T(4,128)} %refs_0_.2) | copy-start | bytes 772
  41.4 11.3 %collective-permute-start.17 = (f32[30,16,256]{2,1,0:T(8,128)S(1)}, f32[30,16,256]{2,1,0:T(8,128)S(1)}, u32[]{:S(2)}, u32[]{:S(2)}) collective-permute-start(f32[30,16,256]{2,1,0:T(8,128)S(1)} %get-tuple-element.20), channel_id=1, source_target_pairs={{0,4},{2,6},{4,0},{6,2},{8,12},{10,14},{12,8},{14,10},{16,20},{18,... | collective-permute-start | bytes 1474568 | tf_op jit(solution)/shard_map/ppermute | solution.py:43
  42.4 11.3 %collective-permute-start.16 = (f32[30,16,256]{2,1,0:T(8,128)S(1)}, f32[30,16,256]{2,1,0:T(8,128)S(1)}, u32[]{:S(2)}, u32[]{:S(2)}) collective-permute-start(f32[30,16,256]{2,1,0:T(8,128)S(1)} %get-tuple-element.21), channel_id=1, source_target_pairs={{0,2},{2,0},{4,6},{6,4},{8,10},{10,8},{12,14},{14,12},{16,18},{18,... | collective-permute-start | bytes 1474568 | tf_op jit(solution)/shard_map/ppermute | solution.py:43
  52.2 3.1 %collective-permute-start.14 = (f32[2,256,256]{2,1,0:T(8,128)S(1)}, f32[2,256,256]{2,1,0:T(8,128)S(1)}, u32[]{:S(2)}, u32[]{:S(2)}) collective-permute-start(f32[2,256,256]{2,1,0:T(8,128)S(1)} %get-tuple-element.15.own_ref), channel_id=1, source_target_pairs={{0,1},{1,0},{2,3},{3,2},{4,5},{5,4},{6,7},{7,6},{8,9},{9,8},{10,11... | collective-permute-start | bytes 1572872 | tf_op jit(solution)/shard_map/ppermute | solution.py:356
  52.2 3.1 %collective-permute-start.15 = (f32[2,256,256]{2,1,0:T(8,128)S(1)}, f32[2,256,256]{2,1,0:T(8,128)S(1)}, u32[]{:S(2)}, u32[]{:S(2)}) collective-permute-start(f32[2,256,256]{2,1,0:T(8,128)S(1)} %get-tuple-element.16), channel_id=1, source_target_pairs={{0,1},{1,0},{2,3},{3,2},{4,5},{5,4},{6,7},{7,6},{8,9},{9,8},{10,11... | collective-permute-start | bytes 1572872 | tf_op jit(solution)/shard_map/ppermute | solution.py:356
  52.8 7.0 %collective-permute-start.18 = (f32[12,16,256]{2,1,0:T(8,128)S(1)}, f32[12,16,256]{2,1,0:T(8,128)S(1)}, u32[]{:S(2)}, u32[]{:S(2)}) collective-permute-start(f32[12,16,256]{2,1,0:T(8,128)S(1)} %slice.56), channel_id=1, source_target_pairs={{0,2},{2,0},{4,6},{6,4},{8,10},{10,8},{12,14},{14,12},{16,18},{18,... | collective-permute-start | bytes 589832 | tf_op jit(solution)/shard_map/ppermute | solution.py:43
  53.7 6.7 %collective-permute-start.19 = (f32[12,16,256]{2,1,0:T(8,128)S(1)}, f32[12,16,256]{2,1,0:T(8,128)S(1)}, u32[]{:S(2)}, u32[]{:S(2)}) collective-permute-start(f32[12,16,256]{2,1,0:T(8,128)S(1)} %slice.57), channel_id=1, source_target_pairs={{0,4},{2,6},{4,0},{6,2},{8,12},{10,14},{12,8},{14,10},{16,20},{18,... | collective-permute-start | bytes 589832 | tf_op jit(solution)/shard_map/ppermute | solution.py:43
  55.3 5.1 %copy-start.1 = (s32[4,4,12]{2,1,0:T(4,128)S(1)}, s32[4,4,12]{2,1,0:T(4,128)}, u32[]{:S(2)}) copy-start(s32[4,4,12]{2,1,0:T(4,128)} %refs_0_.3) | copy-start | bytes 2308
  (2 other events, 1.7 us)

commit v7 on v6

--- a/solution.py
+++ b/solution.py
@@ -63,12 +63,10 @@
     count = len(own[1])
     factor, jacobian = cut(own, 0, factor_blocks), cut(own, factor_blocks, count)
 
-    factor_line = [factor, sent(factor, axis, masks[0])]
+    factor_line = [factor] + [sent(factor, axis, 4 * high) for high in reversed(range(1, lax.axis_size(axis) // 4))]
     jacobian_line = [jacobian, sent(jacobian, axis, masks[0])]
     own_round = around(own, axis)
     own_across = [sent(part, axis, mask) for part, mask in zip(onward(own_round, axis), (1, 2))]
-    for mask in masks[1:]:
-        factor_line.append(sent(joined(*factor_line), axis, mask))
     factor_rest = after(joined(*factor_line[1:]), *own_across)
     factor_round = around(factor_rest, axis)
     for mask in masks[1:]:

time: 64.5 us -> 66.8 us (1.036)
  starting transfers between devices: 27.8 us -> 31.1 us
  waiting for transfers between devices: 21.1 us -> 20 us
  other arithmetic: 1.15 us -> 0.21 us
  local copies, waits for them, and re-layouts: 0.96 us -> 1.88 us
    ppermute x18 -> x19, starting transfers between devices: 27.2 us -> 30.5 us  [sent(): lax.ppermute(array, axis, [(i, i ^ mask) for i in range(lax.axis_size(axi...]
    ppermute x18 -> x19, waiting for transfers between devices: 21.1 us -> 20 us  [sent(): lax.ppermute(array, axis, [(i, i ^ mask) for i in range(lax.axis_size(axi...]
    concatenate x2 -> x1, other arithmetic: 0.94 us -> 0.02 us  [on_device(): jnp.concatenate([diag_inv, lower, jacobian.reshape(supers, rows, 3, size)...]
    slice x1, local copies, waits for them, and re-layouts: 0.01 us -> 0.92 us
  transfers between devices with their start and end apart: 20 -> 21, of which waited for: 10 -> 8; matrix products, arithmetic and copies ran while one was open for 1% -> 0% of each run, Pallas kernels for 13% -> 13%
where the time goes in v7:
time: 66.8 us; the launch traced here: 66.6 us
  starting transfers between devices  31.1 us (47%)
  waiting for transfers between devices  20 us (30%)
  Pallas kernels  12.6 us (19%)
  local copies, waits for them, and re-layouts  1.88 us (3%)
  between operations  0.81 us (1%)
    ppermute x19, starting transfers between devices, sent(): lax.ppermute(array, axis, [(i, i ^ mask) for i in range(lax.axis_size(axi...  30.5 us
    ppermute x19, waiting for transfers between devices, sent(): lax.ppermute(array, axis, [(i, i ^ mask) for i in range(lax.axis_size(axi...  20 us
    pallas_call x1, Pallas kernels, solve(): pl.pallas_call(kernel, out_shape=shapes([(span, columns)] + [(span, size)...  6.71 us
    pallas_call x1, Pallas kernels, subtract_product(): pl.pallas_call(kernel, out_shape=shapes([(span, columns)])[0], in_specs=[...  3.97 us
    pallas_call x1, Pallas kernels, finish(): pl.pallas_call(kernel, out_shape=shapes([(span, columns)]) + [windows, wi...  1.96 us
  transfers between devices with their start and end apart: 21, of which 8 were waited for; matrix products, arithmetic and copies ran while one was open for 0% of the time, Pallas kernels for 13%

profile of v7, /device:TPU:0, one launch (start us, length us, event | category | flops | bytes accessed | tf_op | source)
XLA Modules:
  0.0 66.6 jit_solution(5554395813299976898)
XLA Ops:
  0.6 0.9 %fusion = (f32[4,16,256]{2,1,0:T(8,128)S(1)}, f32[4,16,256]{2,1,0:T(8,128)S(1)}, f32[4,16,256]{2,1,0:T(8,128)S(1)}) fusion(f32[4,16,768]{2,1,0:T(8,128)} %param.10), kind=kLoop, calls=%fused_computation.8 | loop fusion | bytes 393216 | tf_op jit(solution)/shard_map/slice
  2.5 3.0 %collective-permute-start.7 = (f32[20,16,256]{2,1,0:T(8,128)S(1)}, f32[20,16,256]{2,1,0:T(8,128)S(1)}, u32[]{:S(2)}, u32[]{:S(2)}) collective-permute-start(f32[20,16,256]{2,1,0:T(8,128)S(1)} %pad_maximum_fusion.4.refs_2_.refs_4_), channel_id=1, source_target_pairs={{0,2},{2,0},{4,6},{6,4},{8,10},{10,8},{12,14},{14,12},{16,18},{18,... | collective-permute-start | bytes 983048 | tf_op jit(solution)/shard_map/ppermute | solution.py:43
  5.5 1.5 %collective-permute-start.8 = (f32[20,16,256]{2,1,0:T(8,128)S(1)}, f32[20,16,256]{2,1,0:T(8,128)S(1)}, u32[]{:S(2)}, u32[]{:S(2)}) collective-permute-start(f32[20,16,256]{2,1,0:T(8,128)S(1)} %pad_maximum_fusion.4.refs_2_.refs_4_), channel_id=1, source_target_pairs={{0,4},{2,6},{4,0},{6,2},{8,12},{10,14},{12,8},{14,10},{16,20},{18,... | collective-permute-start | bytes 983048 | tf_op jit(solution)/shard_map/ppermute | solution.py:43
  7.0 3.7 %collective-permute-start.4 = (f32[8,16,256]{2,1,0:T(8,128)S(1)}, f32[8,16,256]{2,1,0:T(8,128)S(1)}, u32[]{:S(2)}, u32[]{:S(2)}) collective-permute-start(f32[8,16,256]{2,1,0:T(8,128)S(1)} %constant_dynamic-update-slice_fusion), channel_id=1, source_target_pairs={{0,24},{2,26},{4,28},{6,30},{8,16},{10,18},{12,20},{14,22},{16,8},... | collective-permute-start | bytes 393224 | tf_op jit(solution)/shard_map/ppermute | solution.py:43
  11.4 1.7 %collective-permute-done.7.refs_6_.refs_7_ = f32[20,16,256]{2,1,0:T(8,128)S(1)} collective-permute-done((f32[20,16,256]{2,1,0:T(8,128)S(1)}, f32[20,16,256]{2,1,0:T(8,128)S(1)}, u32[]{:S(2)}, u32[]{:S(2)}) %collective-permute-start.7) | collective-permute-done | bytes 327712 | tf_op jit(solution)/shard_map/ppermute | solution.py:43
  13.2 3.9 %collective-permute-start = (f32[12,16,256]{2,1,0:T(8,128)S(1)}, f32[12,16,256]{2,1,0:T(8,128)S(1)}, u32[]{:S(2)}, u32[]{:S(2)}) collective-permute-start(f32[12,16,256]{2,1,0:T(8,128)S(1)} %bitcast.2), channel_id=1, source_target_pairs={{0,24},{2,26},{4,28},{6,30},{8,16},{10,18},{12,20},{14,22},{16,8},... | collective-permute-start | bytes 589832 | tf_op jit(solution)/shard_map/ppermute | solution.py:43
  17.0 1.6 %collective-permute-start.9 = (f32[10,16,256]{2,1,0:T(8,128)S(1)}, f32[10,16,256]{2,1,0:T(8,128)S(1)}, u32[]{:S(2)}, u32[]{:S(2)}) collective-permute-start(f32[10,16,256]{2,1,0:T(8,128)S(1)} %slice.52), channel_id=1, source_target_pairs={{0,4},{2,6},{4,0},{6,2},{8,12},{10,14},{12,8},{14,10},{16,20},{18,... | collective-permute-start | bytes 491528 | tf_op jit(solution)/shard_map/ppermute | solution.py:43
  18.7 1.6 %collective-permute-start.10 = (f32[10,16,256]{2,1,0:T(8,128)S(1)}, f32[10,16,256]{2,1,0:T(8,128)S(1)}, u32[]{:S(2)}, u32[]{:S(2)}) collective-permute-start(f32[10,16,256]{2,1,0:T(8,128)S(1)} %slice.53), channel_id=1, source_target_pairs={{0,2},{2,0},{4,6},{6,4},{8,10},{10,8},{12,14},{14,12},{16,18},{18,... | collective-permute-start | bytes 491528 | tf_op jit(solution)/shard_map/ppermute | solution.py:43
  20.2 6.2 %collective-permute-done.5.refs_4_ = f32[8,16,256]{2,1,0:T(8,128)S(1)} collective-permute-done((f32[8,16,256]{2,1,0:T(8,128)S(1)}, f32[8,16,256]{2,1,0:T(8,128)S(1)}, u32[]{:S(2)}, u32[]{:S(2)}) %collective-permute-start.5) | collective-permute-done | bytes 131104 | tf_op jit(solution)/shard_map/ppermute | solution.py:43
  27.6 4.8 %collective-permute-start.1 = (f32[24,16,256]{2,1,0:T(8,128)S(1)}, f32[24,16,256]{2,1,0:T(8,128)S(1)}, u32[]{:S(2)}, u32[]{:S(2)}) collective-permute-start(f32[24,16,256]{2,1,0:T(8,128)S(1)} %pad_maximum_fusion.2), channel_id=1, source_target_pairs={{0,8},{2,10},{4,12},{6,14},{8,0},{10,2},{12,4},{14,6},{16,24},{18,... | collective-permute-start | bytes 1179656 | tf_op jit(solution)/shard_map/ppermute | solution.py:43
  32.4 1.1 %collective-permute-start.2 = (f32[12,16,256]{2,1,0:T(8,128)S(1)}, f32[12,16,256]{2,1,0:T(8,128)S(1)}, u32[]{:S(2)}, u32[]{:S(2)}) collective-permute-start(f32[12,16,256]{2,1,0:T(8,128)S(1)} %collective-permute-done.refs_5_), channel_id=1, source_target_pairs={{0,4},{2,6},{4,0},{6,2},{8,12},{10,14},{12,8},{14,10},{16,20},{18,... | collective-permute-start | bytes 589832 | tf_op jit(solution)/shard_map/ppermute | solution.py:43
  33.5 1.1 %collective-permute-start.3 = (f32[12,16,256]{2,1,0:T(8,128)S(1)}, f32[12,16,256]{2,1,0:T(8,128)S(1)}, u32[]{:S(2)}, u32[]{:S(2)}) collective-permute-start(f32[12,16,256]{2,1,0:T(8,128)S(1)} %collective-permute-done.refs_5_), channel_id=1, source_target_pairs={{0,2},{2,0},{4,6},{6,4},{8,10},{10,8},{12,14},{14,12},{16,18},{18,... | collective-permute-start | bytes 589832 | tf_op jit(solution)/shard_map/ppermute | solution.py:43
  34.7 3.9 %collective-permute-done.12.refs_10_ = f32[24,16,256]{2,1,0:T(8,128)S(1)} collective-permute-done((f32[24,16,256]{2,1,0:T(8,128)S(1)}, f32[24,16,256]{2,1,0:T(8,128)S(1)}, u32[]{:S(2)}, u32[]{:S(2)}) %collective-permute-start.12) | collective-permute-done | bytes 393248 | tf_op jit(solution)/shard_map/ppermute | solution.py:43
  39.2 1.5 %collective-permute-start.14 = (f32[12,16,256]{2,1,0:T(8,128)S(1)}, f32[12,16,256]{2,1,0:T(8,128)S(1)}, u32[]{:S(2)}, u32[]{:S(2)}) collective-permute-start(f32[12,16,256]{2,1,0:T(8,128)S(1)} %slice.55), channel_id=1, source_target_pairs={{0,4},{2,6},{4,0},{6,2},{8,12},{10,14},{12,8},{14,10},{16,20},{18,... | collective-permute-start | bytes 589832 | tf_op jit(solution)/shard_map/ppermute | solution.py:43
  40.7 2.1 %collective-permute-done.2.refs_12_ = f32[12,16,256]{2,1,0:T(8,128)S(1)} collective-permute-done((f32[12,16,256]{2,1,0:T(8,128)S(1)}, f32[12,16,256]{2,1,0:T(8,128)S(1)}, u32[]{:S(2)}, u32[]{:S(2)}) %collective-permute-start.2) | collective-permute-done | bytes 196640 | tf_op jit(solution)/shard_map/ppermute | solution.py:43
  43.4 1.6 %collective-permute-start.18 = (f32[30,16,256]{2,1,0:T(8,128)S(1)}, f32[30,16,256]{2,1,0:T(8,128)S(1)}, u32[]{:S(2)}, u32[]{:S(2)}) collective-permute-start(f32[30,16,256]{2,1,0:T(8,128)S(1)} %get-tuple-element.20), channel_id=1, source_target_pairs={{0,4},{2,6},{4,0},{6,2},{8,12},{10,14},{12,8},{14,10},{16,20},{18,... | collective-permute-start | bytes 1474568 | tf_op jit(solution)/shard_map/ppermute | solution.py:43
  45.6 1.9 %collective-permute-done.13.refs_11_ = f32[12,16,256]{2,1,0:T(8,128)S(1)} collective-permute-done((f32[12,16,256]{2,1,0:T(8,128)S(1)}, f32[12,16,256]{2,1,0:T(8,128)S(1)}, u32[]{:S(2)}, u32[]{:S(2)}) %collective-permute-start.13) | collective-permute-done | bytes 196640 | tf_op jit(solution)/shard_map/ppermute | solution.py:43
  47.5 6.7 %solve.1 = (f32[1024,256]{1,0:T(8,128)S(1)}, f32[1024,256]{1,0:T(8,128)S(1)}, f32[2,256,256]{2,1,0:T(8,128)S(1)}, f32[2,256,256]{2,1,0:T(8,128)S(1)}) custom-call(s32[4,4,4]{2,1,0:T(4,128)S(1)} %copy-done.2, f32[1024,256]{1,0:T(8,128)S(1)} %copy-done, f32[20,16,256]{2,1,0:T(8,128)S(1)} %pad_maximum_fusion.4.refs_2_.refs_4_, ...), custom_call_target="tpu_custom_call" | custom-call | flops 2147483648 | bytes 262144 | tf_op jit(solution)/shard_map/solve/pallas_call | solution.py:222
  54.8 1.1 %collective-permute-start.19 = (f32[12,16,256]{2,1,0:T(8,128)S(1)}, f32[12,16,256]{2,1,0:T(8,128)S(1)}, u32[]{:S(2)}, u32[]{:S(2)}) collective-permute-start(f32[12,16,256]{2,1,0:T(8,128)S(1)} %slice.56), channel_id=1, source_target_pairs={{0,2},{2,0},{4,6},{6,4},{8,10},{10,8},{12,14},{14,12},{16,18},{18,... | collective-permute-start | bytes 589832 | tf_op jit(solution)/shard_map/ppermute | solution.py:43
  56.0 1.0 %collective-permute-start.20 = (f32[12,16,256]{2,1,0:T(8,128)S(1)}, f32[12,16,256]{2,1,0:T(8,128)S(1)}, u32[]{:S(2)}, u32[]{:S(2)}) collective-permute-start(f32[12,16,256]{2,1,0:T(8,128)S(1)} %slice.57), channel_id=1, source_target_pairs={{0,4},{2,6},{4,0},{6,2},{8,12},{10,14},{12,8},{14,10},{16,20},{18,... | collective-permute-start | bytes 589832 | tf_op jit(solution)/shard_map/ppermute | solution.py:43
  57.0 2.0 %finish.1 = (f32[1024,256]{1,0:T(8,128)}, bf16[1536,256]{1,0:T(8,128)(2,1)S(1)}, bf16[1536,256]{1,0:T(8,128)(2,1)S(1)}) custom-call(f32[1024,256]{1,0:T(8,128)S(1)} %get-tuple-element.13.sol_ref, f32[1024,256]{1,0:T(8,128)S(1)} %get-tuple-element.14.part_ref, f32[2,256,256]{2,1,0:T(8,128)S(1)} %get-tuple-element.15.own_ref, ...), custom_call_target="tpu_custom_call" | custom-call | flops 100663296 | bytes 262144 | tf_op jit(solution)/shard_map/finish/pallas_call | solution.py:266
  59.0 2.8 %collective-permute-done.19.refs_15_ = f32[12,16,256]{2,1,0:T(8,128)S(1)} collective-permute-done((f32[12,16,256]{2,1,0:T(8,128)S(1)}, f32[12,16,256]{2,1,0:T(8,128)S(1)}, u32[]{:S(2)}, u32[]{:S(2)}) %collective-permute-start.19) | collective-permute-done | bytes 196640 | tf_op jit(solution)/shard_map/ppermute | solution.py:43
  61.8 0.9 %collective-permute-done.20.refs_16_ = f32[12,16,256]{2,1,0:T(8,128)S(1)} collective-permute-done((f32[12,16,256]{2,1,0:T(8,128)S(1)}, f32[12,16,256]{2,1,0:T(8,128)S(1)}, u32[]{:S(2)}, u32[]{:S(2)}) %collective-permute-start.20) | collective-permute-done | bytes 196640 | tf_op jit(solution)/shard_map/ppermute | solution.py:43
  62.7 4.0 %residual.1 = f32[1024,256]{1,0:T(8,128)} custom-call(s32[4,4,12]{2,1,0:T(4,128)S(1)} %copy-done.1, f32[1024,256]{1,0:T(8,128)S(1)} %copy-done, bf16[1536,256]{1,0:T(8,128)(2,1)S(1)} %get-tuple-element.18.refs_2_, bf16[1536,256]{1,0:T(8,128)(2,1)S(1)} %get-tuple-element.19.refs_3_, f32[20,16,256]{2,1,0:T(8,128)S(1)} %pad_maximum_fusion.4.refs_2_.refs_4_, ...), custom_call_target="tpu_custom_call" | custom-call | flops 1207959552 | bytes 6291456 | tf_op jit(solution)/shard_map/residual/pallas_call | solution.py:312
  (47 shorter events, 5.3 us)
Async XLA Ops:
  2.5 10.7 %collective-permute-start.7 = (f32[20,16,256]{2,1,0:T(8,128)S(1)}, f32[20,16,256]{2,1,0:T(8,128)S(1)}, u32[]{:S(2)}, u32[]{:S(2)}) collective-permute-start(f32[20,16,256]{2,1,0:T(8,128)S(1)} %pad_maximum_fusion.4.refs_2_.refs_4_), channel_id=1, source_target_pairs={{0,2},{2,0},{4,6},{6,4},{8,10},{10,8},{12,14},{14,12},{16,18},{18,... | collective-permute-start | bytes 983048 | tf_op jit(solution)/shard_map/ppermute | solution.py:43
  5.5 11.6 %collective-permute-start.8 = (f32[20,16,256]{2,1,0:T(8,128)S(1)}, f32[20,16,256]{2,1,0:T(8,128)S(1)}, u32[]{:S(2)}, u32[]{:S(2)}) collective-permute-start(f32[20,16,256]{2,1,0:T(8,128)S(1)} %pad_maximum_fusion.4.refs_2_.refs_4_), channel_id=1, source_target_pairs={{0,4},{2,6},{4,0},{6,2},{8,12},{10,14},{12,8},{14,10},{16,20},{18,... | collective-permute-start | bytes 983048 | tf_op jit(solution)/shard_map/ppermute | solution.py:43
  7.0 11.7 %collective-permute-start.4 = (f32[8,16,256]{2,1,0:T(8,128)S(1)}, f32[8,16,256]{2,1,0:T(8,128)S(1)}, u32[]{:S(2)}, u32[]{:S(2)}) collective-permute-start(f32[8,16,256]{2,1,0:T(8,128)S(1)} %constant_dynamic-update-slice_fusion), channel_id=1, source_target_pairs={{0,24},{2,26},{4,28},{6,30},{8,16},{10,18},{12,20},{14,22},{16,8},... | collective-permute-start | bytes 393224 | tf_op jit(solution)/shard_map/ppermute | solution.py:43
  10.7 15.7 %collective-permute-start.5 = (f32[8,16,256]{2,1,0:T(8,128)S(1)}, f32[8,16,256]{2,1,0:T(8,128)S(1)}, u32[]{:S(2)}, u32[]{:S(2)}) collective-permute-start(f32[8,16,256]{2,1,0:T(8,128)S(1)} %constant_dynamic-update-slice_fusion), channel_id=1, source_target_pairs={{0,16},{2,18},{4,20},{6,22},{8,24},{10,26},{12,28},{14,30},{16,0},... | collective-permute-start | bytes 393224 | tf_op jit(solution)/shard_map/ppermute | solution.py:43
  10.7 15.7 %collective-permute-start.6 = (f32[8,16,256]{2,1,0:T(8,128)S(1)}, f32[8,16,256]{2,1,0:T(8,128)S(1)}, u32[]{:S(2)}, u32[]{:S(2)}) collective-permute-start(f32[8,16,256]{2,1,0:T(8,128)S(1)} %constant_dynamic-update-slice_fusion), channel_id=1, source_target_pairs={{0,8},{2,10},{4,12},{6,14},{8,0},{10,2},{12,4},{14,6},{16,24},{18,... | collective-permute-start | bytes 393224 | tf_op jit(solution)/shard_map/ppermute | solution.py:43
  13.2 14.4 %collective-permute-start = (f32[12,16,256]{2,1,0:T(8,128)S(1)}, f32[12,16,256]{2,1,0:T(8,128)S(1)}, u32[]{:S(2)}, u32[]{:S(2)}) collective-permute-start(f32[12,16,256]{2,1,0:T(8,128)S(1)} %bitcast.2), channel_id=1, source_target_pairs={{0,24},{2,26},{4,28},{6,30},{8,16},{10,18},{12,20},{14,22},{16,8},... | collective-permute-start | bytes 589832 | tf_op jit(solution)/shard_map/ppermute | solution.py:43
  17.0 9.4 %collective-permute-start.9 = (f32[10,16,256]{2,1,0:T(8,128)S(1)}, f32[10,16,256]{2,1,0:T(8,128)S(1)}, u32[]{:S(2)}, u32[]{:S(2)}) collective-permute-start(f32[10,16,256]{2,1,0:T(8,128)S(1)} %slice.52), channel_id=1, source_target_pairs={{0,4},{2,6},{4,0},{6,2},{8,12},{10,14},{12,8},{14,10},{16,20},{18,... | collective-permute-start | bytes 491528 | tf_op jit(solution)/shard_map/ppermute | solution.py:43
  18.7 7.8 %collective-permute-start.10 = (f32[10,16,256]{2,1,0:T(8,128)S(1)}, f32[10,16,256]{2,1,0:T(8,128)S(1)}, u32[]{:S(2)}, u32[]{:S(2)}) collective-permute-start(f32[10,16,256]{2,1,0:T(8,128)S(1)} %slice.53), channel_id=1, source_target_pairs={{0,2},{2,0},{4,6},{6,4},{8,10},{10,8},{12,14},{14,12},{16,18},{18,... | collective-permute-start | bytes 491528 | tf_op jit(solution)/shard_map/ppermute | solution.py:43
  26.5 12.1 %collective-permute-start.12 = (f32[24,16,256]{2,1,0:T(8,128)S(1)}, f32[24,16,256]{2,1,0:T(8,128)S(1)}, u32[]{:S(2)}, u32[]{:S(2)}) collective-permute-start(f32[24,16,256]{2,1,0:T(8,128)S(1)} %pad_maximum_fusion.3), channel_id=1, source_target_pairs={{0,4},{2,6},{4,0},{6,2},{8,12},{10,14},{12,8},{14,10},{16,20},{18,... | collective-permute-start | bytes 1179656 | tf_op jit(solution)/shard_map/ppermute | solution.py:43
  27.0 12.2 %collective-permute-start.11 = (f32[24,16,256]{2,1,0:T(8,128)S(1)}, f32[24,16,256]{2,1,0:T(8,128)S(1)}, u32[]{:S(2)}, u32[]{:S(2)}) collective-permute-start(f32[24,16,256]{2,1,0:T(8,128)S(1)} %pad_maximum_fusion.3), channel_id=1, source_target_pairs={{0,2},{2,0},{4,6},{6,4},{8,10},{10,8},{12,14},{14,12},{16,18},{18,... | collective-permute-start | bytes 1179656 | tf_op jit(solution)/shard_map/ppermute | solution.py:43
  27.6 15.7 %collective-permute-start.1 = (f32[24,16,256]{2,1,0:T(8,128)S(1)}, f32[24,16,256]{2,1,0:T(8,128)S(1)}, u32[]{:S(2)}, u32[]{:S(2)}) collective-permute-start(f32[24,16,256]{2,1,0:T(8,128)S(1)} %pad_maximum_fusion.2), channel_id=1, source_target_pairs={{0,8},{2,10},{4,12},{6,14},{8,0},{10,2},{12,4},{14,6},{16,24},{18,... | collective-permute-start | bytes 1179656 | tf_op jit(solution)/shard_map/ppermute | solution.py:43
  32.4 10.4 %collective-permute-start.2 = (f32[12,16,256]{2,1,0:T(8,128)S(1)}, f32[12,16,256]{2,1,0:T(8,128)S(1)}, u32[]{:S(2)}, u32[]{:S(2)}) collective-permute-start(f32[12,16,256]{2,1,0:T(8,128)S(1)} %collective-permute-done.refs_5_), channel_id=1, source_target_pairs={{0,4},{2,6},{4,0},{6,2},{8,12},{10,14},{12,8},{14,10},{16,20},{18,... | collective-permute-start | bytes 589832 | tf_op jit(solution)/shard_map/ppermute | solution.py:43
  33.5 9.7 %collective-permute-start.3 = (f32[12,16,256]{2,1,0:T(8,128)S(1)}, f32[12,16,256]{2,1,0:T(8,128)S(1)}, u32[]{:S(2)}, u32[]{:S(2)}) collective-permute-start(f32[12,16,256]{2,1,0:T(8,128)S(1)} %collective-permute-done.refs_5_), channel_id=1, source_target_pairs={{0,2},{2,0},{4,6},{6,4},{8,10},{10,8},{12,14},{14,12},{16,18},{18,... | collective-permute-start | bytes 589832 | tf_op jit(solution)/shard_map/ppermute | solution.py:43
  38.6 8.9 %collective-permute-start.13 = (f32[12,16,256]{2,1,0:T(8,128)S(1)}, f32[12,16,256]{2,1,0:T(8,128)S(1)}, u32[]{:S(2)}, u32[]{:S(2)}) collective-permute-start(f32[12,16,256]{2,1,0:T(8,128)S(1)} %slice.54), channel_id=1, source_target_pairs={{0,2},{2,0},{4,6},{6,4},{8,10},{10,8},{12,14},{14,12},{16,18},{18,... | collective-permute-start | bytes 589832 | tf_op jit(solution)/shard_map/ppermute | solution.py:43
  39.2 8.3 %copy-start = (f32[1024,256]{1,0:T(8,128)S(1)}, f32[1024,256]{1,0:T(8,128)}, u32[]{:S(2)}) copy-start(f32[1024,256]{1,0:T(8,128)} %refs_1_.2) | copy-start | bytes 3145732
  39.2 8.3 %collective-permute-start.14 = (f32[12,16,256]{2,1,0:T(8,128)S(1)}, f32[12,16,256]{2,1,0:T(8,128)S(1)}, u32[]{:S(2)}, u32[]{:S(2)}) collective-permute-start(f32[12,16,256]{2,1,0:T(8,128)S(1)} %slice.55), channel_id=1, source_target_pairs={{0,4},{2,6},{4,0},{6,2},{8,12},{10,14},{12,8},{14,10},{16,20},{18,... | collective-permute-start | bytes 589832 | tf_op jit(solution)/shard_map/ppermute | solution.py:43
  43.3 4.2 %copy-start.2 = (s32[4,4,4]{2,1,0:T(4,128)S(1)}, s32[4,4,4]{2,1,0:T(4,128)}, u32[]{:S(2)}) copy-start(s32[4,4,4]{2,1,0:T(4,128)} %refs_0_.2) | copy-start | bytes 772
  43.4 11.4 %collective-permute-start.18 = (f32[30,16,256]{2,1,0:T(8,128)S(1)}, f32[30,16,256]{2,1,0:T(8,128)S(1)}, u32[]{:S(2)}, u32[]{:S(2)}) collective-permute-start(f32[30,16,256]{2,1,0:T(8,128)S(1)} %get-tuple-element.20), channel_id=1, source_target_pairs={{0,4},{2,6},{4,0},{6,2},{8,12},{10,14},{12,8},{14,10},{16,20},{18,... | collective-permute-start | bytes 1474568 | tf_op jit(solution)/shard_map/ppermute | solution.py:43
  45.0 10.9 %collective-permute-start.17 = (f32[30,16,256]{2,1,0:T(8,128)S(1)}, f32[30,16,256]{2,1,0:T(8,128)S(1)}, u32[]{:S(2)}, u32[]{:S(2)}) collective-permute-start(f32[30,16,256]{2,1,0:T(8,128)S(1)} %get-tuple-element.21), channel_id=1, source_target_pairs={{0,2},{2,0},{4,6},{6,4},{8,10},{10,8},{12,14},{14,12},{16,18},{18,... | collective-permute-start | bytes 1474568 | tf_op jit(solution)/shard_map/ppermute | solution.py:43
  54.2 2.8 %collective-permute-start.15 = (f32[2,256,256]{2,1,0:T(8,128)S(1)}, f32[2,256,256]{2,1,0:T(8,128)S(1)}, u32[]{:S(2)}, u32[]{:S(2)}) collective-permute-start(f32[2,256,256]{2,1,0:T(8,128)S(1)} %get-tuple-element.15.own_ref), channel_id=1, source_target_pairs={{0,1},{1,0},{2,3},{3,2},{4,5},{5,4},{6,7},{7,6},{8,9},{9,8},{10,11... | collective-permute-start | bytes 1572872 | tf_op jit(solution)/shard_map/ppermute | solution.py:354
  54.3 2.7 %collective-permute-start.16 = (f32[2,256,256]{2,1,0:T(8,128)S(1)}, f32[2,256,256]{2,1,0:T(8,128)S(1)}, u32[]{:S(2)}, u32[]{:S(2)}) collective-permute-start(f32[2,256,256]{2,1,0:T(8,128)S(1)} %get-tuple-element.16), channel_id=1, source_target_pairs={{0,1},{1,0},{2,3},{3,2},{4,5},{5,4},{6,7},{7,6},{8,9},{9,8},{10,11... | collective-permute-start | bytes 1572872 | tf_op jit(solution)/shard_map/ppermute | solution.py:354
  54.8 7.0 %collective-permute-start.19 = (f32[12,16,256]{2,1,0:T(8,128)S(1)}, f32[12,16,256]{2,1,0:T(8,128)S(1)}, u32[]{:S(2)}, u32[]{:S(2)}) collective-permute-start(f32[12,16,256]{2,1,0:T(8,128)S(1)} %slice.56), channel_id=1, source_target_pairs={{0,2},{2,0},{4,6},{6,4},{8,10},{10,8},{12,14},{14,12},{16,18},{18,... | collective-permute-start | bytes 589832 | tf_op jit(solution)/shard_map/ppermute | solution.py:43
  56.0 6.7 %collective-permute-start.20 = (f32[12,16,256]{2,1,0:T(8,128)S(1)}, f32[12,16,256]{2,1,0:T(8,128)S(1)}, u32[]{:S(2)}, u32[]{:S(2)}) collective-permute-start(f32[12,16,256]{2,1,0:T(8,128)S(1)} %slice.57), channel_id=1, source_target_pairs={{0,4},{2,6},{4,0},{6,2},{8,12},{10,14},{12,8},{14,10},{16,20},{18,... | collective-permute-start | bytes 589832 | tf_op jit(solution)/shard_map/ppermute | solution.py:43
  57.0 5.6 %copy-start.1 = (s32[4,4,12]{2,1,0:T(4,128)S(1)}, s32[4,4,12]{2,1,0:T(4,128)}, u32[]{:S(2)}) copy-start(s32[4,4,12]{2,1,0:T(4,128)} %refs_0_.3) | copy-start | bytes 2308
  (2 other events, 1.7 us)

commit v8 on v6

--- a/solution.py
+++ b/solution.py
@@ -48,42 +48,47 @@
     return sent(held, axis, 1), sent(held, axis, 2)
 
 
-def onward(pair, axis, *more):
-    half = len(pair[0][1]) // 2
-    first, second = cut(pair[0], 0, half), cut(pair[1], half, 2 * half)
-    return joined(*more, second), joined(*more, first)
-
-
-def gather_panels(own, factor_blocks, right_side, axis):
+def onward(pair, size, more, axis):
+    half = size // 2
+    second = joined(*more, cut(pair[1], half, size))
+    first = joined(*more, cut(pair[0], 0, half))
+    return second, first
+
+
+def send_both(parts, axis):
+    return sent(parts[0], axis, 1), sent(parts[1], axis, 2)
+
+
+def gather_panels(factor, jacobian, right_side, axis):
     steps = lax.axis_size(axis) // 4
     masks = []
     while steps > 1:
         masks.append(4 * (steps - 1))
         steps //= 2
-    count = len(own[1])
-    factor, jacobian = cut(own, 0, factor_blocks), cut(own, factor_blocks, count)
+    own = joined(factor, jacobian)
+    factor_blocks = len(factor[1])
 
     factor_line = [factor, sent(factor, axis, masks[0])]
-    jacobian_line = [jacobian, sent(jacobian, axis, masks[0])]
+    jacobian_line = [jacobian, sent(after(jacobian, factor_line[1]), axis, masks[0])]
     own_round = around(own, axis)
-    own_across = [sent(part, axis, mask) for part, mask in zip(onward(own_round, axis), (1, 2))]
+    second_round = send_both(onward(own_round, len(own[1]), factor_line[1:], axis), axis)
     for mask in masks[1:]:
         factor_line.append(sent(joined(*factor_line), axis, mask))
-    factor_rest = after(joined(*factor_line[1:]), *own_across)
-    factor_round = around(factor_rest, axis)
+    rest = joined(*factor_line[2:])
+    second_last = [after(part, rest) for part in second_round]
+    third_round = send_both(onward(second_last, factor_blocks, [rest], axis), axis)
     for mask in masks[1:]:
         jacobian_line.append(sent(joined(*jacobian_line), axis, mask))
-    early_round = around(joined(*jacobian_line[1:-1]), axis)
-    factor_across = [sent(part, axis, mask) for part, mask in zip(onward(factor_round, axis), (1, 2))]
-    late_parts = onward(early_round, axis, jacobian_line[-1])
-    late_round = [sent(part, axis, mask) for part, mask in zip(late_parts, (1, 2))]
-    size = len(jacobian_line[-1][1])
-    late_across = [
-        sent(part, axis, mask)
-        for part, mask in zip(onward([cut(part, 0, size) for part in late_round], axis), (1, 2))
-    ]
+    early = joined(*jacobian_line[1:-1])
+    early_round = around(early, axis)
+    factor_parts = onward(third_round, len(rest[1]), [], axis)
+    factor_across = send_both(factor_parts, axis)
+    early_last = [after(part, *factor_parts) for part in early_round]
+    late_parts = onward(early_last, len(early[1]), jacobian_line[-1:], axis)
+    late_round = send_both(late_parts, axis)
+    late_across = send_both(onward(late_round, len(jacobian_line[-1][1]), [], axis), axis)
     right_side, _ = after((right_side, None), *late_parts)
-    arrived = [own, *factor_line[1:], *jacobian_line[1:], *own_round, *own_across, *factor_round, *factor_across]
+    arrived = [own, *factor_line[1:], *jacobian_line[1:], *own_round, *second_round, *third_round, *factor_across]
     return arrived + [*early_round, *late_round, *late_across], right_side
 
 
@@ -338,14 +343,17 @@
     span = supers * size
     nodes = lax.axis_size("node")
 
-    own = jnp.concatenate(
-        [diag_inv, lower, jacobian.reshape(supers, rows, 3, size).swapaxes(1, 2).reshape(3 * supers, rows, size)]
-    )
-    own = own, [(0, block) for block in range(own.shape[0])]
+    def blocks_of(array, begin):
+        return array, [(0, begin + block) for block in range(array.shape[0])]
+
+    factor_own = blocks_of(jnp.concatenate([diag_inv, lower]), 0)
+    shaped = jacobian.reshape(supers, rows, 3, size).swapaxes(1, 2).reshape(3 * supers, rows, size)
+    jacobian_own = blocks_of(shaped, 2 * supers)
+    own = joined(factor_own, jacobian_own)
     count = lax.axis_size("rhs")
     relative = count >= 16 and not count & (count - 1)
     if relative:
-        arrived, late = gather_panels(own, 2 * supers, right_side, "rhs")
+        arrived, late = gather_panels(factor_own, jacobian_own, right_side, "rhs")
     else:
         arrived, late = gather_whole(own, "rhs"), right_side
     factor = runs_of(arrived, 0, 2 * supers)
@@ -356,11 +364,11 @@
         mail = [lax.ppermute(letter, "node", [(0, 1), (1, 0)]) for letter in (down, up)]
         sol, high, low = finish(sol, parts[0], down, *mail, supers)
     else:
-        before = after = jnp.zeros((size, columns), jnp.float32)
+        beneath = beyond = jnp.zeros((size, columns), jnp.float32)
         if nodes > 1:
             upwards = [(i, i + 1) for i in range(nodes - 1)]
             downwards = [(i + 1, i) for i in range(nodes - 1)]
-            below = above = before
+            below = above = beneath
             for _ in range(nodes - 1):
                 below = lax.ppermute(
                     down[:, :columns] + dot(down[:, columns : columns + size], below), "node", upwards
@@ -369,9 +377,9 @@
                 leaving = up[:, :columns] + dot(up[:, columns : columns + size], below)
                 above = lax.ppermute(leaving + dot(up[:, columns + size :], above), "node", downwards)
             sol = sol + dot(parts[0], below) + dot(parts[1], above)
-            before = lax.ppermute(sol[span - size :], "node", upwards)
-            after = lax.ppermute(sol[:size], "node", downwards)
-        high, low = split_windows(sol, before, after)
+            beneath = lax.ppermute(sol[span - size :], "node", upwards)
+            beyond = lax.ppermute(sol[:size], "node", downwards)
+        high, low = split_windows(sol, beneath, beyond)
     residual = subtract_product(jacobians, relative, right_side, high, low, jacobian_pattern, supers, size)
     return sol, residual
 

time: 64.5 us -> 64.4 us (level)
  local copies, waits for them, and re-layouts: 0.96 us -> 1.87 us
  other arithmetic: 1.15 us -> 0.34 us
  waiting for transfers between devices: 21.1 us -> 20.3 us
    concatenate x3 -> x1, other arithmetic: 0.96 us -> 0.01 us  [on_device(): factor_own = blocks_of(jnp.concatenate([diag_inv, lower]), 0)]
    slice x1, local copies, waits for them, and re-layouts: 0.01 us -> 0.92 us
    ppermute x18, waiting for transfers between devices: 21.1 us -> 20.3 us  [sent(): lax.ppermute(array, axis, [(i, i ^ mask) for i in range(lax.axis_size(axi...]
  transfers between devices with their start and end apart: 20 -> 20, of which waited for: 10 -> 8; matrix products, arithmetic and copies ran while one was open for 1% -> 1% of each run, Pallas kernels for 13% -> 13%
where the time goes in v8:
time: 64.4 us; the launch traced here: 64.2 us
  starting transfers between devices  28.4 us (44%)
  waiting for transfers between devices  20.3 us (32%)
  Pallas kernels  12.5 us (19%)
  local copies, waits for them, and re-layouts  1.87 us (3%)
  between operations  0.83 us (1%)
    ppermute x18, starting transfers between devices, sent(): lax.ppermute(array, axis, [(i, i ^ mask) for i in range(lax.axis_size(axi...  27.8 us
    ppermute x18, waiting for transfers between devices, sent(): lax.ppermute(array, axis, [(i, i ^ mask) for i in range(lax.axis_size(axi...  20.3 us
    pallas_call x1, Pallas kernels, solve(): pl.pallas_call(kernel, out_shape=shapes([(span, columns)] + [(span, size)...  6.68 us
    pallas_call x1, Pallas kernels, subtract_product(): pl.pallas_call(kernel, out_shape=shapes([(span, columns)])[0], in_specs=[...  3.87 us
    pallas_call x1, Pallas kernels, finish(): pl.pallas_call(kernel, out_shape=shapes([(span, columns)]) + [windows, wi...  1.95 us
  transfers between devices with their start and end apart: 20, of which 8 were waited for; matrix products, arithmetic and copies ran while one was open for 1% of the time, Pallas kernels for 13%

profile of v8, /device:TPU:0, one launch (start us, length us, event | category | flops | bytes accessed | tf_op | source)
XLA Modules:
  0.0 64.2 jit_solution(435024897409998792)
XLA Ops:
  0.6 0.9 %fusion = (f32[4,16,256]{2,1,0:T(8,128)S(1)}, f32[4,16,256]{2,1,0:T(8,128)S(1)}, f32[4,16,256]{2,1,0:T(8,128)S(1)}) fusion(f32[4,16,768]{2,1,0:T(8,128)} %param.10), kind=kLoop, calls=%fused_computation.11 | loop fusion | bytes 393216 | tf_op jit(solution)/shard_map/slice
  1.6 0.8 %copy-done.3 = f32[4,16,256]{2,1,0:T(8,128)S(1)} copy-done((f32[4,16,256]{2,1,0:T(8,128)S(1)}, f32[4,16,256]{2,1,0:T(8,128)}, u32[]{:S(2)}) %copy-start.3) | copy-done | bytes 65560
  2.5 3.0 %collective-permute-start.5 = (f32[20,16,256]{2,1,0:T(8,128)S(1)}, f32[20,16,256]{2,1,0:T(8,128)S(1)}, u32[]{:S(2)}, u32[]{:S(2)}) collective-permute-start(f32[20,16,256]{2,1,0:T(8,128)S(1)} %pad_maximum_fusion.7.refs_2_.refs_4_), channel_id=1, source_target_pairs={{0,4},{2,6},{4,0},{6,2},{8,12},{10,14},{12,8},{14,10},{16,20},{18,... | collective-permute-start | bytes 983048 | tf_op jit(solution)/shard_map/ppermute | solution.py:43
  5.5 1.5 %collective-permute-start.8 = (f32[20,16,256]{2,1,0:T(8,128)S(1)}, f32[20,16,256]{2,1,0:T(8,128)S(1)}, u32[]{:S(2)}, u32[]{:S(2)}) collective-permute-start(f32[20,16,256]{2,1,0:T(8,128)S(1)} %pad_maximum_fusion.7.refs_2_.refs_4_), channel_id=1, source_target_pairs={{0,2},{2,0},{4,6},{6,4},{8,10},{10,8},{12,14},{14,12},{16,18},{18,... | collective-permute-start | bytes 983048 | tf_op jit(solution)/shard_map/ppermute | solution.py:43
  7.0 3.7 %collective-permute-start = (f32[8,16,256]{2,1,0:T(8,128)S(1)}, f32[8,16,256]{2,1,0:T(8,128)S(1)}, u32[]{:S(2)}, u32[]{:S(2)}) collective-permute-start(f32[8,16,256]{2,1,0:T(8,128)S(1)} %pad_maximum_fusion.10), channel_id=1, source_target_pairs={{0,24},{2,26},{4,28},{6,30},{8,16},{10,18},{12,20},{14,22},{16,8},... | collective-permute-start | bytes 393224 | tf_op jit(solution)/shard_map/ppermute | solution.py:43
  10.7 3.2 %collective-permute-done.refs_3_ = f32[8,16,256]{2,1,0:T(8,128)S(1)} collective-permute-done((f32[8,16,256]{2,1,0:T(8,128)S(1)}, f32[8,16,256]{2,1,0:T(8,128)S(1)}, u32[]{:S(2)}, u32[]{:S(2)}) %collective-permute-start) | collective-permute-done | bytes 131104 | tf_op jit(solution)/shard_map/ppermute | solution.py:43
  13.9 3.6 %collective-permute-start.1 = (f32[12,16,256]{2,1,0:T(8,128)S(1)}, f32[12,16,256]{2,1,0:T(8,128)S(1)}, u32[]{:S(2)}, u32[]{:S(2)}) collective-permute-start(f32[12,16,256]{2,1,0:T(8,128)S(1)} %bitcast.2), channel_id=1, source_target_pairs={{0,24},{2,26},{4,28},{6,30},{8,16},{10,18},{12,20},{14,22},{16,8},... | collective-permute-start | bytes 589832 | tf_op jit(solution)/shard_map/ppermute | solution.py:43
  19.3 3.8 %collective-permute-done.1.refs_5_ = f32[12,16,256]{2,1,0:T(8,128)S(1)} collective-permute-done((f32[12,16,256]{2,1,0:T(8,128)S(1)}, f32[12,16,256]{2,1,0:T(8,128)S(1)}, u32[]{:S(2)}, u32[]{:S(2)}) %collective-permute-start.1) | collective-permute-done | bytes 196640 | tf_op jit(solution)/shard_map/ppermute | solution.py:43
  23.1 2.5 %collective-permute-start.2 = (f32[24,16,256]{2,1,0:T(8,128)S(1)}, f32[24,16,256]{2,1,0:T(8,128)S(1)}, u32[]{:S(2)}, u32[]{:S(2)}) collective-permute-start(f32[24,16,256]{2,1,0:T(8,128)S(1)} %pad_maximum_fusion.2), channel_id=1, source_target_pairs={{0,8},{2,10},{4,12},{6,14},{8,0},{10,2},{12,4},{14,6},{16,24},{18,... | collective-permute-start | bytes 1179656 | tf_op jit(solution)/shard_map/ppermute | solution.py:43
  25.6 1.2 %collective-permute-done.4.refs_4_ = f32[16,16,256]{2,1,0:T(8,128)S(1)} collective-permute-done((f32[16,16,256]{2,1,0:T(8,128)S(1)}, f32[16,16,256]{2,1,0:T(8,128)S(1)}, u32[]{:S(2)}, u32[]{:S(2)}) %collective-permute-start.4) | collective-permute-done | bytes 262176 | tf_op jit(solution)/shard_map/ppermute | solution.py:43
  26.9 1.8 %collective-permute-start.7 = (f32[20,16,256]{2,1,0:T(8,128)S(1)}, f32[20,16,256]{2,1,0:T(8,128)S(1)}, u32[]{:S(2)}, u32[]{:S(2)}) collective-permute-start(f32[20,16,256]{2,1,0:T(8,128)S(1)} %get-tuple-element.31), channel_id=1, source_target_pairs={{0,4},{2,6},{4,0},{6,2},{8,12},{10,14},{12,8},{14,10},{16,20},{18,... | collective-permute-start | bytes 983048 | tf_op jit(solution)/shard_map/ppermute | solution.py:43
  29.4 1.4 %collective-permute-start.3 = (f32[12,16,256]{2,1,0:T(8,128)S(1)}, f32[12,16,256]{2,1,0:T(8,128)S(1)}, u32[]{:S(2)}, u32[]{:S(2)}) collective-permute-start(f32[12,16,256]{2,1,0:T(8,128)S(1)} %collective-permute-done.1.refs_5_), channel_id=1, source_target_pairs={{0,4},{2,6},{4,0},{6,2},{8,12},{10,14},{12,8},{14,10},{16,20},{18,... | collective-permute-start | bytes 589832 | tf_op jit(solution)/shard_map/ppermute | solution.py:43
  31.1 6.6 %collective-permute-done.7.refs_10_ = f32[20,16,256]{2,1,0:T(8,128)S(1)} collective-permute-done((f32[20,16,256]{2,1,0:T(8,128)S(1)}, f32[20,16,256]{2,1,0:T(8,128)S(1)}, u32[]{:S(2)}, u32[]{:S(2)}) %collective-permute-start.7) | collective-permute-done | bytes 327712 | tf_op jit(solution)/shard_map/ppermute | solution.py:43
  37.7 1.4 %collective-permute-start.12 = (f32[8,16,256]{2,1,0:T(8,128)S(1)}, f32[8,16,256]{2,1,0:T(8,128)S(1)}, u32[]{:S(2)}, u32[]{:S(2)}) collective-permute-start(f32[8,16,256]{2,1,0:T(8,128)S(1)} %slice.53), channel_id=1, source_target_pairs={{0,2},{2,0},{4,6},{6,4},{8,10},{10,8},{12,14},{14,12},{16,18},{18,... | collective-permute-start | bytes 393224 | tf_op jit(solution)/shard_map/ppermute | solution.py:43
  39.1 0.6 collective-permute-start.13
  39.8 1.9 %collective-permute-done.3.refs_12_ = f32[12,16,256]{2,1,0:T(8,128)S(1)} collective-permute-done((f32[12,16,256]{2,1,0:T(8,128)S(1)}, f32[12,16,256]{2,1,0:T(8,128)S(1)}, u32[]{:S(2)}, u32[]{:S(2)}) %collective-permute-start.3) | collective-permute-done | bytes 196640 | tf_op jit(solution)/shard_map/ppermute | solution.py:43
  41.8 1.8 %collective-permute-start.17 = (f32[30,16,256]{2,1,0:T(8,128)S(1)}, f32[30,16,256]{2,1,0:T(8,128)S(1)}, u32[]{:S(2)}, u32[]{:S(2)}) collective-permute-start(f32[30,16,256]{2,1,0:T(8,128)S(1)} %get-tuple-element.28), channel_id=1, source_target_pairs={{0,4},{2,6},{4,0},{6,2},{8,12},{10,14},{12,8},{14,10},{16,20},{18,... | collective-permute-start | bytes 1474568 | tf_op jit(solution)/shard_map/ppermute | solution.py:43
  43.6 1.6 %collective-permute-start.16 = (f32[30,16,256]{2,1,0:T(8,128)S(1)}, f32[30,16,256]{2,1,0:T(8,128)S(1)}, u32[]{:S(2)}, u32[]{:S(2)}) collective-permute-start(f32[30,16,256]{2,1,0:T(8,128)S(1)} %get-tuple-element.29), channel_id=1, source_target_pairs={{0,2},{2,0},{4,6},{6,4},{8,10},{10,8},{12,14},{14,12},{16,18},{18,... | collective-permute-start | bytes 1474568 | tf_op jit(solution)/shard_map/ppermute | solution.py:43
  45.6 6.7 %solve.1 = (f32[1024,256]{1,0:T(8,128)S(1)}, f32[1024,256]{1,0:T(8,128)S(1)}, f32[2,256,256]{2,1,0:T(8,128)S(1)}, f32[2,256,256]{2,1,0:T(8,128)S(1)}) custom-call(s32[4,4,4]{2,1,0:T(4,128)S(1)} %copy-done.2, f32[1024,256]{1,0:T(8,128)S(1)} %copy-done, f32[20,16,256]{2,1,0:T(8,128)S(1)} %pad_maximum_fusion.7.refs_2_.refs_4_, ...), custom_call_target="tpu_custom_call" | custom-call | flops 2147483648 | bytes 262144 | tf_op jit(solution)/shard_map/solve/pallas_call | solution.py:229
  52.9 0.7 %collective-permute-start.18 = (f32[12,16,256]{2,1,0:T(8,128)S(1)}, f32[12,16,256]{2,1,0:T(8,128)S(1)}, u32[]{:S(2)}, u32[]{:S(2)}) collective-permute-start(f32[12,16,256]{2,1,0:T(8,128)S(1)} %slice.56), channel_id=1, source_target_pairs={{0,2},{2,0},{4,6},{6,4},{8,10},{10,8},{12,14},{14,12},{16,18},{18,... | collective-permute-start | bytes 589832 | tf_op jit(solution)/shard_map/ppermute | solution.py:43
  53.7 1.6 %collective-permute-start.19 = (f32[12,16,256]{2,1,0:T(8,128)S(1)}, f32[12,16,256]{2,1,0:T(8,128)S(1)}, u32[]{:S(2)}, u32[]{:S(2)}) collective-permute-start(f32[12,16,256]{2,1,0:T(8,128)S(1)} %slice.57), channel_id=1, source_target_pairs={{0,4},{2,6},{4,0},{6,2},{8,12},{10,14},{12,8},{14,10},{16,20},{18,... | collective-permute-start | bytes 589832 | tf_op jit(solution)/shard_map/ppermute | solution.py:43
  55.3 2.0 %finish.1 = (f32[1024,256]{1,0:T(8,128)}, bf16[1536,256]{1,0:T(8,128)(2,1)S(1)}, bf16[1536,256]{1,0:T(8,128)(2,1)S(1)}) custom-call(f32[1024,256]{1,0:T(8,128)S(1)} %get-tuple-element.21.sol_ref, f32[1024,256]{1,0:T(8,128)S(1)} %get-tuple-element.22.part_ref, f32[2,256,256]{2,1,0:T(8,128)S(1)} %get-tuple-element.23.own_ref, ...), custom_call_target="tpu_custom_call" | custom-call | flops 100663296 | bytes 262144 | tf_op jit(solution)/shard_map/finish/pallas_call | solution.py:273
  57.2 2.7 %collective-permute-done.18.refs_15_ = f32[12,16,256]{2,1,0:T(8,128)S(1)} collective-permute-done((f32[12,16,256]{2,1,0:T(8,128)S(1)}, f32[12,16,256]{2,1,0:T(8,128)S(1)}, u32[]{:S(2)}, u32[]{:S(2)}) %collective-permute-start.18) | collective-permute-done | bytes 196640 | tf_op jit(solution)/shard_map/ppermute | solution.py:43
  60.3 3.9 %residual.1 = f32[1024,256]{1,0:T(8,128)} custom-call(s32[4,4,12]{2,1,0:T(4,128)S(1)} %copy-done.1, f32[1024,256]{1,0:T(8,128)S(1)} %copy-done, bf16[1536,256]{1,0:T(8,128)(2,1)S(1)} %get-tuple-element.26.refs_2_, bf16[1536,256]{1,0:T(8,128)(2,1)S(1)} %get-tuple-element.27.refs_3_, f32[20,16,256]{2,1,0:T(8,128)S(1)} %pad_maximum_fusion.7.refs_2_.refs_4_, ...), custom_call_target="tpu_custom_call" | custom-call | flops 1207959552 | bytes 6291456 | tf_op jit(solution)/shard_map/residual/pallas_call | solution.py:319
  (48 shorter events, 4.5 us)
Async XLA Ops:
  1.6 0.9 %copy-start.4 = (f32[4,16,256]{2,1,0:T(8,128)S(1)}, f32[4,16,256]{2,1,0:T(8,128)}, u32[]{:S(2)}) copy-start(f32[4,16,256]{2,1,0:T(8,128)} %param.7) | copy-start | bytes 196612
  2.5 15.0 %collective-permute-start.5 = (f32[20,16,256]{2,1,0:T(8,128)S(1)}, f32[20,16,256]{2,1,0:T(8,128)S(1)}, u32[]{:S(2)}, u32[]{:S(2)}) collective-permute-start(f32[20,16,256]{2,1,0:T(8,128)S(1)} %pad_maximum_fusion.7.refs_2_.refs_4_), channel_id=1, source_target_pairs={{0,4},{2,6},{4,0},{6,2},{8,12},{10,14},{12,8},{14,10},{16,20},{18,... | collective-permute-start | bytes 983048 | tf_op jit(solution)/shard_map/ppermute | solution.py:43
  5.5 12.0 %collective-permute-start.8 = (f32[20,16,256]{2,1,0:T(8,128)S(1)}, f32[20,16,256]{2,1,0:T(8,128)S(1)}, u32[]{:S(2)}, u32[]{:S(2)}) collective-permute-start(f32[20,16,256]{2,1,0:T(8,128)S(1)} %pad_maximum_fusion.7.refs_2_.refs_4_), channel_id=1, source_target_pairs={{0,2},{2,0},{4,6},{6,4},{8,10},{10,8},{12,14},{14,12},{16,18},{18,... | collective-permute-start | bytes 983048 | tf_op jit(solution)/shard_map/ppermute | solution.py:43
  7.0 6.9 %collective-permute-start = (f32[8,16,256]{2,1,0:T(8,128)S(1)}, f32[8,16,256]{2,1,0:T(8,128)S(1)}, u32[]{:S(2)}, u32[]{:S(2)}) collective-permute-start(f32[8,16,256]{2,1,0:T(8,128)S(1)} %pad_maximum_fusion.10), channel_id=1, source_target_pairs={{0,24},{2,26},{4,28},{6,30},{8,16},{10,18},{12,20},{14,22},{16,8},... | collective-permute-start | bytes 393224 | tf_op jit(solution)/shard_map/ppermute | solution.py:43
  13.9 9.2 %collective-permute-start.1 = (f32[12,16,256]{2,1,0:T(8,128)S(1)}, f32[12,16,256]{2,1,0:T(8,128)S(1)}, u32[]{:S(2)}, u32[]{:S(2)}) collective-permute-start(f32[12,16,256]{2,1,0:T(8,128)S(1)} %bitcast.2), channel_id=1, source_target_pairs={{0,24},{2,26},{4,28},{6,30},{8,16},{10,18},{12,20},{14,22},{16,8},... | collective-permute-start | bytes 589832 | tf_op jit(solution)/shard_map/ppermute | solution.py:43
  17.6 9.2 %collective-permute-start.6 = (f32[18,16,256]{2,1,0:T(8,128)S(1)}, f32[18,16,256]{2,1,0:T(8,128)S(1)}, u32[]{:S(2)}, u32[]{:S(2)}) collective-permute-start(f32[18,16,256]{2,1,0:T(8,128)S(1)} %get-tuple-element.36), channel_id=1, source_target_pairs={{0,2},{2,0},{4,6},{6,4},{8,10},{10,8},{12,14},{14,12},{16,18},{18,... | collective-permute-start | bytes 884744 | tf_op jit(solution)/shard_map/ppermute | solution.py:43
  18.2 8.6 %collective-permute-start.9 = (f32[18,16,256]{2,1,0:T(8,128)S(1)}, f32[18,16,256]{2,1,0:T(8,128)S(1)}, u32[]{:S(2)}, u32[]{:S(2)}) collective-permute-start(f32[18,16,256]{2,1,0:T(8,128)S(1)} %get-tuple-element.35), channel_id=1, source_target_pairs={{0,4},{2,6},{4,0},{6,2},{8,12},{10,14},{12,8},{14,10},{16,20},{18,... | collective-permute-start | bytes 884744 | tf_op jit(solution)/shard_map/ppermute | solution.py:43
  18.7 8.1 %collective-permute-start.4 = (f32[16,16,256]{2,1,0:T(8,128)S(1)}, f32[16,16,256]{2,1,0:T(8,128)S(1)}, u32[]{:S(2)}, u32[]{:S(2)}) collective-permute-start(f32[16,16,256]{2,1,0:T(8,128)S(1)} %pad_maximum_fusion.8), channel_id=1, source_target_pairs={{0,8},{2,10},{4,12},{6,14},{8,0},{10,2},{12,4},{14,6},{16,24},{18,... | collective-permute-start | bytes 786440 | tf_op jit(solution)/shard_map/ppermute | solution.py:43
  23.1 18.6 %collective-permute-start.2 = (f32[24,16,256]{2,1,0:T(8,128)S(1)}, f32[24,16,256]{2,1,0:T(8,128)S(1)}, u32[]{:S(2)}, u32[]{:S(2)}) collective-permute-start(f32[24,16,256]{2,1,0:T(8,128)S(1)} %pad_maximum_fusion.2), channel_id=1, source_target_pairs={{0,8},{2,10},{4,12},{6,14},{8,0},{10,2},{12,4},{14,6},{16,24},{18,... | collective-permute-start | bytes 1179656 | tf_op jit(solution)/shard_map/ppermute | solution.py:43
  26.9 10.7 %collective-permute-start.7 = (f32[20,16,256]{2,1,0:T(8,128)S(1)}, f32[20,16,256]{2,1,0:T(8,128)S(1)}, u32[]{:S(2)}, u32[]{:S(2)}) collective-permute-start(f32[20,16,256]{2,1,0:T(8,128)S(1)} %get-tuple-element.31), channel_id=1, source_target_pairs={{0,4},{2,6},{4,0},{6,2},{8,12},{10,14},{12,8},{14,10},{16,20},{18,... | collective-permute-start | bytes 983048 | tf_op jit(solution)/shard_map/ppermute | solution.py:43
  28.8 10.4 %collective-permute-start.10 = (f32[20,16,256]{2,1,0:T(8,128)S(1)}, f32[20,16,256]{2,1,0:T(8,128)S(1)}, u32[]{:S(2)}, u32[]{:S(2)}) collective-permute-start(f32[20,16,256]{2,1,0:T(8,128)S(1)} %get-tuple-element.30), channel_id=1, source_target_pairs={{0,2},{2,0},{4,6},{6,4},{8,10},{10,8},{12,14},{14,12},{16,18},{18,... | collective-permute-start | bytes 983048 | tf_op jit(solution)/shard_map/ppermute | solution.py:43
  29.4 12.3 %collective-permute-start.3 = (f32[12,16,256]{2,1,0:T(8,128)S(1)}, f32[12,16,256]{2,1,0:T(8,128)S(1)}, u32[]{:S(2)}, u32[]{:S(2)}) collective-permute-start(f32[12,16,256]{2,1,0:T(8,128)S(1)} %collective-permute-done.1.refs_5_), channel_id=1, source_target_pairs={{0,4},{2,6},{4,0},{6,2},{8,12},{10,14},{12,8},{14,10},{16,20},{18,... | collective-permute-start | bytes 589832 | tf_op jit(solution)/shard_map/ppermute | solution.py:43
  30.8 10.9 %collective-permute-start.11 = (f32[12,16,256]{2,1,0:T(8,128)S(1)}, f32[12,16,256]{2,1,0:T(8,128)S(1)}, u32[]{:S(2)}, u32[]{:S(2)}) collective-permute-start(f32[12,16,256]{2,1,0:T(8,128)S(1)} %collective-permute-done.1.refs_5_), channel_id=1, source_target_pairs={{0,2},{2,0},{4,6},{6,4},{8,10},{10,8},{12,14},{14,12},{16,18},{18,... | collective-permute-start | bytes 589832 | tf_op jit(solution)/shard_map/ppermute | solution.py:43
  37.7 7.5 %collective-permute-start.12 = (f32[8,16,256]{2,1,0:T(8,128)S(1)}, f32[8,16,256]{2,1,0:T(8,128)S(1)}, u32[]{:S(2)}, u32[]{:S(2)}) collective-permute-start(f32[8,16,256]{2,1,0:T(8,128)S(1)} %slice.53), channel_id=1, source_target_pairs={{0,2},{2,0},{4,6},{6,4},{8,10},{10,8},{12,14},{14,12},{16,18},{18,... | collective-permute-start | bytes 393224 | tf_op jit(solution)/shard_map/ppermute | solution.py:43
  39.1 6.5 %copy-start = (f32[1024,256]{1,0:T(8,128)S(1)}, f32[1024,256]{1,0:T(8,128)}, u32[]{:S(2)}) copy-start(f32[1024,256]{1,0:T(8,128)} %refs_1_.2) | copy-start | bytes 3145732
  39.1 6.5 %collective-permute-start.13 = (f32[8,16,256]{2,1,0:T(8,128)S(1)}, f32[8,16,256]{2,1,0:T(8,128)S(1)}, u32[]{:S(2)}, u32[]{:S(2)}) collective-permute-start(f32[8,16,256]{2,1,0:T(8,128)S(1)} %slice.55), channel_id=1, source_target_pairs={{0,4},{2,6},{4,0},{6,2},{8,12},{10,14},{12,8},{14,10},{16,20},{18,... | collective-permute-start | bytes 393224 | tf_op jit(solution)/shard_map/ppermute | solution.py:43
  41.7 4.0 %copy-start.2 = (s32[4,4,4]{2,1,0:T(4,128)S(1)}, s32[4,4,4]{2,1,0:T(4,128)}, u32[]{:S(2)}) copy-start(s32[4,4,4]{2,1,0:T(4,128)} %refs_0_.2) | copy-start | bytes 772
  41.8 11.1 %collective-permute-start.17 = (f32[30,16,256]{2,1,0:T(8,128)S(1)}, f32[30,16,256]{2,1,0:T(8,128)S(1)}, u32[]{:S(2)}, u32[]{:S(2)}) collective-permute-start(f32[30,16,256]{2,1,0:T(8,128)S(1)} %get-tuple-element.28), channel_id=1, source_target_pairs={{0,4},{2,6},{4,0},{6,2},{8,12},{10,14},{12,8},{14,10},{16,20},{18,... | collective-permute-start | bytes 1474568 | tf_op jit(solution)/shard_map/ppermute | solution.py:43
  43.6 10.0 %collective-permute-start.16 = (f32[30,16,256]{2,1,0:T(8,128)S(1)}, f32[30,16,256]{2,1,0:T(8,128)S(1)}, u32[]{:S(2)}, u32[]{:S(2)}) collective-permute-start(f32[30,16,256]{2,1,0:T(8,128)S(1)} %get-tuple-element.29), channel_id=1, source_target_pairs={{0,2},{2,0},{4,6},{6,4},{8,10},{10,8},{12,14},{14,12},{16,18},{18,... | collective-permute-start | bytes 1474568 | tf_op jit(solution)/shard_map/ppermute | solution.py:43
  52.3 2.9 %collective-permute-start.14 = (f32[2,256,256]{2,1,0:T(8,128)S(1)}, f32[2,256,256]{2,1,0:T(8,128)S(1)}, u32[]{:S(2)}, u32[]{:S(2)}) collective-permute-start(f32[2,256,256]{2,1,0:T(8,128)S(1)} %get-tuple-element.23.own_ref), channel_id=1, source_target_pairs={{0,1},{1,0},{2,3},{3,2},{4,5},{5,4},{6,7},{7,6},{8,9},{9,8},{10,11... | collective-permute-start | bytes 1572872 | tf_op jit(solution)/shard_map/ppermute | solution.py:364
  52.4 2.8 %collective-permute-start.15 = (f32[2,256,256]{2,1,0:T(8,128)S(1)}, f32[2,256,256]{2,1,0:T(8,128)S(1)}, u32[]{:S(2)}, u32[]{:S(2)}) collective-permute-start(f32[2,256,256]{2,1,0:T(8,128)S(1)} %get-tuple-element.24), channel_id=1, source_target_pairs={{0,1},{1,0},{2,3},{3,2},{4,5},{5,4},{6,7},{7,6},{8,9},{9,8},{10,11... | collective-permute-start | bytes 1572872 | tf_op jit(solution)/shard_map/ppermute | solution.py:364
  52.9 7.0 %collective-permute-start.18 = (f32[12,16,256]{2,1,0:T(8,128)S(1)}, f32[12,16,256]{2,1,0:T(8,128)S(1)}, u32[]{:S(2)}, u32[]{:S(2)}) collective-permute-start(f32[12,16,256]{2,1,0:T(8,128)S(1)} %slice.56), channel_id=1, source_target_pairs={{0,2},{2,0},{4,6},{6,4},{8,10},{10,8},{12,14},{14,12},{16,18},{18,... | collective-permute-start | bytes 589832 | tf_op jit(solution)/shard_map/ppermute | solution.py:43
  53.7 6.7 %collective-permute-start.19 = (f32[12,16,256]{2,1,0:T(8,128)S(1)}, f32[12,16,256]{2,1,0:T(8,128)S(1)}, u32[]{:S(2)}, u32[]{:S(2)}) collective-permute-start(f32[12,16,256]{2,1,0:T(8,128)S(1)} %slice.57), channel_id=1, source_target_pairs={{0,4},{2,6},{4,0},{6,2},{8,12},{10,14},{12,8},{14,10},{16,20},{18,... | collective-permute-start | bytes 589832 | tf_op jit(solution)/shard_map/ppermute | solution.py:43
  55.3 5.1 %copy-start.1 = (s32[4,4,12]{2,1,0:T(4,128)S(1)}, s32[4,4,12]{2,1,0:T(4,128)}, u32[]{:S(2)}) copy-start(s32[4,4,12]{2,1,0:T(4,128)} %refs_0_.3) | copy-start | bytes 2308
  (1 other events, 0.8 us)

commit v9 on v8

--- a/solution.py
+++ b/solution.py
@@ -89,7 +89,7 @@
     late_across = send_both(onward(late_round, len(jacobian_line[-1][1]), [], axis), axis)
     right_side, _ = after((right_side, None), *late_parts)
     arrived = [own, *factor_line[1:], *jacobian_line[1:], *own_round, *second_round, *third_round, *factor_across]
-    return arrived + [*early_round, *late_round, *late_across], right_side
+    return arrived + [*early_round, *late_round], list(late_across), right_side
 
 
 def gather_whole(own, axis):
@@ -97,14 +97,15 @@
     return [(everything, [(owner, block) for owner in range(lax.axis_size(axis)) for _, block in own[1]])]
 
 
-def runs_of(pieces, begin, end):
+def runs_of(pieces, begin, end, group):
     chosen = []
     for array, names in pieces:
         runs = []
         for at, (owner, block) in enumerate(names):
             if not begin <= block < end:
                 continue
-            if runs and runs[-1][0] + runs[-1][1] == at and names[at - 1] == (owner, block - 1):
+            follows = runs and runs[-1][0] + runs[-1][1] == at and names[at - 1] == (owner, block - 1)
+            if follows and (block - begin) % group:
                 runs[-1][1] += 1
             else:
                 runs.append([at, 1, owner, block - begin])
@@ -115,20 +116,18 @@
 
 def place_rows(pieces, refs, relative, axis, panels, sem):
     me = lax.axis_index(axis)
-    copies = []
+    placed = []
     for (array, runs), ref in zip(pieces, refs):
         rows = array.shape[1]
         for at, length, owner, block in runs:
             row = pl.multiple_of((me ^ owner) * rows, rows) if relative else owner * rows
-            copies.append(
-                pltpu.make_async_copy(
-                    ref.at[pl.ds(at, length)],
-                    panels.at[pl.ds(block, length), pl.ds(row, rows), :],
-                    sem.at[len(copies)],
-                )
-            )
-    for copy in copies:
-        copy.start()
+            source = ref.at[pl.ds(at, length)]
+            placed.append((block, source, panels.at[pl.ds(block, length), pl.ds(row, rows), :]))
+    placed.sort(key=lambda item: item[0])
+    copies = []
+    for block, source, target in placed:
+        copies.append((block, pltpu.make_async_copy(source, target, sem.at[len(copies)])))
+        copies[-1][1].start()
     return copies
 
 
@@ -136,23 +135,28 @@
     return [jax.ShapeDtypeStruct(shape, jnp.float32) for shape in arrays]
 
 
+def weights_of(pattern_ref, s, a, wide):
+    count = pattern_ref.shape[2]
+    step = wide // count
+    together = max(1, 128 // step)
+    lane = lax.broadcasted_iota(jnp.int32, (1, together * step), 1)
+    weights = []
+    for first in range(0, count, together):
+        weight = jnp.full(lane.shape, pattern_ref[s, a, first].astype(jnp.float32))
+        for c in range(1, min(together, count - first)):
+            weight = jnp.where(lane >= c * step, pattern_ref[s, a, first + c].astype(jnp.float32), weight)
+        weights.append(weight)
+    return jnp.concatenate(weights, axis=1)[:, :wide]
+
+
 def masked(rows, pattern_ref, s, block_rows):
-    wide = rows.shape[1]
-    blocks = wide // pattern_ref.shape[2]
-    together = max(1, 128 // blocks)
-    lane = lax.broadcasted_iota(jnp.int32, (1, together * blocks), 1)
-    bands = []
-    for a in range(pattern_ref.shape[1]):
-        weights = []
-        for first in range(0, pattern_ref.shape[2], together):
-            chosen = pattern_ref[s, a, first]
-            weight = jnp.full(lane.shape, chosen.astype(jnp.float32))
-            for c in range(1, min(together, pattern_ref.shape[2] - first)):
-                weight = jnp.where(lane >= c * blocks, pattern_ref[s, a, first + c].astype(jnp.float32), weight)
-            weights.append(weight)
-        weights = jnp.concatenate(weights, axis=1)[:, :wide]
-        bands.append(rows[a * block_rows : (a + 1) * block_rows] * weights)
-    return jnp.concatenate(bands, axis=0)
+    return jnp.concatenate(
+        [
+            rows[a * block_rows : (a + 1) * block_rows] * weights_of(pattern_ref, s, a, rows.shape[1])
+            for a in range(pattern_ref.shape[1])
+        ],
+        axis=0,
+    )
 
 
 def solve(pieces, relative, right_side, pattern, nodes, supers, size):
@@ -176,7 +180,7 @@
             jnp.int32, (size, size), 1
         )
         zeros = jnp.zeros((size, size), jnp.float32)
-        for copy in copies:
+        for _, copy in copies:
             copy.wait()
 
         previous = None
@@ -306,9 +310,11 @@
         pattern_ref, rhs_ref, high_ref, low_ref = refs[:4]
         piece_refs = refs[4 : 4 + n]
         out_ref, panels, sem = refs[4 + n :]
-        for copy in place_rows(pieces, piece_refs, relative, "rhs", panels, sem):
-            copy.wait()
+        copies = place_rows(pieces, piece_refs, relative, "rhs", panels, sem)
         for s in range(supers):
+            for block, copy in copies:
+                if block // 3 == s:
+                    copy.wait()
             rows = jnp.concatenate([panels[3 * s + c] for c in range(3)], axis=1)
             panel = masked(rows, pattern_ref, s, size // pattern_ref.shape[1])
             window = pl.ds(s * size, wide)
@@ -333,6 +339,59 @@
     )(pattern, right_side, high, low, *[array for array, _ in pieces])
 
 
+def subtract_rest(pieces, residual, right_side, high, low, pattern, supers, size):
+    span, columns = right_side.shape
+    wide = 3 * size
+    n = len(pieces)
+    places = {}
+    for i, (array, runs) in enumerate(pieces):
+        for at, length, owner, block in runs:
+            for step in range(length):
+                places.setdefault(owner, {})[block + step] = (i, at + step)
+    rows = pieces[0][0].shape[1]
+
+    def kernel(*refs):
+        pattern_ref, rhs_ref, high_ref, low_ref, _ = refs[:5]
+        piece_refs = refs[5 : 5 + n]
+        out_ref, held, sem = refs[5 + n :]
+        me = lax.axis_index("rhs")
+        copies = []
+        for s in range(supers):
+            bands, starts = [], []
+            for owner, blocks in places.items():
+                row = pl.multiple_of((me ^ owner) * rows, rows)
+                band = [piece_refs[i][at] for i, at in (blocks[3 * s + c] for c in range(3))]
+                a = row // (size // pattern_ref.shape[1])
+                bands.append(jnp.concatenate(band, axis=1) * weights_of(pattern_ref, s, a, wide))
+                starts.append(pl.multiple_of(s * size + row, rows))
+            window = pl.ds(s * size, wide)
+            result = product(split(jnp.concatenate(bands, axis=0)), (high_ref[window, :], low_ref[window, :]))
+            for i, start in enumerate(starts):
+                at = len(copies)
+                held[at] = rhs_ref[pl.ds(start, rows), :] - result[i * rows : (i + 1) * rows]
+                copies.append(pltpu.make_async_copy(held.at[at], out_ref.at[pl.ds(start, rows), :], sem.at[at]))
+                copies[-1].start()
+        for copy in copies:
+            copy.wait()
+
+    return pl.pallas_call(
+        kernel,
+        out_shape=shapes([(span, columns)])[0],
+        in_specs=[SMEM] + [VMEM] * 3 + [ANY] + [VMEM] * n,
+        out_specs=ANY,
+        input_output_aliases={4: 0},
+        scratch_shapes=[
+            pltpu.VMEM((supers * len(places), rows, columns), jnp.float32),
+            pltpu.SemaphoreType.DMA((supers * len(places),)),
+        ],
+        compiler_params=pltpu.CompilerParams(vmem_limit_bytes=VMEM_LIMIT),
+        cost_estimate=pl.CostEstimate(
+            flops=6 * supers * rows * len(places) * wide * columns, bytes_accessed=8 * span * size, transcendentals=0
+        ),
+        name="residual_rest",
+    )(pattern, right_side, high, low, residual, *[array for array, _ in pieces])
+
+
 def dot(left, right):
     return jnp.dot(left, right, precision=lax.Precision.HIGHEST)
 
@@ -353,11 +412,12 @@
     count = lax.axis_size("rhs")
     relative = count >= 16 and not count & (count - 1)
     if relative:
-        arrived, late = gather_panels(factor_own, jacobian_own, right_side, "rhs")
+        arrived, last, late = gather_panels(factor_own, jacobian_own, right_side, "rhs")
     else:
-        arrived, late = gather_whole(own, "rhs"), right_side
-    factor = runs_of(arrived, 0, 2 * supers)
-    jacobians = runs_of(arrived, 2 * supers, len(own[1]))
+        arrived, last, late = gather_whole(own, "rhs"), [], right_side
+    factor = runs_of(arrived, 0, 2 * supers, 2 * supers)
+    jacobians = runs_of(arrived, 2 * supers, len(own[1]), 3)
+    last = runs_of(last, 2 * supers, len(own[1]), 3)
 
     sol, parts, down, up = solve(factor, relative, late, factor_pattern, nodes, supers, size)
     if nodes == 2:
@@ -381,6 +441,8 @@
             beyond = lax.ppermute(sol[:size], "node", downwards)
         high, low = split_windows(sol, beneath, beyond)
     residual = subtract_product(jacobians, relative, right_side, high, low, jacobian_pattern, supers, size)
+    if last:
+        residual = subtract_rest(last, residual, right_side, high, low, jacobian_pattern, supers, size)
     return sol, residual
 
 

time: 64.4 us -> 66.8 us (1.037)
  Pallas kernels: 12.5 us -> 17.7 us
  waiting for transfers between devices: 20.3 us -> 18 us
    pallas_call x1, Pallas kernels: 3.87 us -> 6.75 us  [subtract_product(): pl.pallas_call(kernel, out_shape=shapes([(span, columns)])[0], in_specs=[...]
    ppermute x18, waiting for transfers between devices: 20.3 us -> 18 us  [sent(): lax.ppermute(array, axis, [(i, i ^ mask) for i in range(lax.axis_size(axi...]
    pallas_call x0 -> x1, Pallas kernels: none -> 2.26 us  [subtract_rest(): pl.pallas_call(kernel, out_shape=shapes([(span, columns)])[0], in_specs=[...]
  transfers between devices with their start and end apart: 20 -> 20, of which waited for: 8 -> 8; matrix products, arithmetic and copies ran while one was open for 1% -> 1% of each run, Pallas kernels for 13% -> 23%
where the time goes in v9:
time: 66.8 us; the launch traced here: 66.6 us
  starting transfers between devices  27.9 us (42%)
  waiting for transfers between devices  18 us (27%)
  Pallas kernels  17.7 us (26%)
  local copies, waits for them, and re-layouts  1.87 us (3%)
  between operations  0.84 us (1%)
    ppermute x18, starting transfers between devices, sent(): lax.ppermute(array, axis, [(i, i ^ mask) for i in range(lax.axis_size(axi...  27.3 us
    ppermute x18, waiting for transfers between devices, sent(): lax.ppermute(array, axis, [(i, i ^ mask) for i in range(lax.axis_size(axi...  18 us
    pallas_call x1, Pallas kernels, subtract_product(): pl.pallas_call(kernel, out_shape=shapes([(span, columns)])[0], in_specs=[...  6.75 us
    pallas_call x1, Pallas kernels, solve(): pl.pallas_call(kernel, out_shape=shapes([(span, columns)] + [(span, size)...  6.68 us
    pallas_call x1, Pallas kernels, subtract_rest(): pl.pallas_call(kernel, out_shape=shapes([(span, columns)])[0], in_specs=[...  2.26 us
    pallas_call x1, Pallas kernels, finish(): pl.pallas_call(kernel, out_shape=shapes([(span, columns)]) + [windows, wi...  1.96 us
  transfers between devices with their start and end apart: 20, of which 8 were waited for; matrix products, arithmetic and copies ran while one was open for 1% of the time, Pallas kernels for 23%

profile of v9, /device:TPU:0, one launch (start us, length us, event | category | flops | bytes accessed | tf_op | source)
XLA Modules:
  0.0 66.6 jit_solution(18104859940096168524)
XLA Ops:
  0.6 0.9 %fusion = (f32[4,16,256]{2,1,0:T(8,128)S(1)}, f32[4,16,256]{2,1,0:T(8,128)S(1)}, f32[4,16,256]{2,1,0:T(8,128)S(1)}) fusion(f32[4,16,768]{2,1,0:T(8,128)} %param.10), kind=kLoop, calls=%fused_computation.11 | loop fusion | bytes 393216 | tf_op jit(solution)/shard_map/slice
  1.6 0.8 %copy-done.3 = f32[4,16,256]{2,1,0:T(8,128)S(1)} copy-done((f32[4,16,256]{2,1,0:T(8,128)S(1)}, f32[4,16,256]{2,1,0:T(8,128)}, u32[]{:S(2)}) %copy-start.3) | copy-done | bytes 65560
  2.5 3.0 %collective-permute-start.5 = (f32[20,16,256]{2,1,0:T(8,128)S(1)}, f32[20,16,256]{2,1,0:T(8,128)S(1)}, u32[]{:S(2)}, u32[]{:S(2)}) collective-permute-start(f32[20,16,256]{2,1,0:T(8,128)S(1)} %pad_maximum_fusion.7.refs_2_.refs_4_), channel_id=1, source_target_pairs={{0,4},{2,6},{4,0},{6,2},{8,12},{10,14},{12,8},{14,10},{16,20},{18,... | collective-permute-start | bytes 983048 | tf_op jit(solution)/shard_map/ppermute | solution.py:43
  5.5 1.5 %collective-permute-start.8 = (f32[20,16,256]{2,1,0:T(8,128)S(1)}, f32[20,16,256]{2,1,0:T(8,128)S(1)}, u32[]{:S(2)}, u32[]{:S(2)}) collective-permute-start(f32[20,16,256]{2,1,0:T(8,128)S(1)} %pad_maximum_fusion.7.refs_2_.refs_4_), channel_id=1, source_target_pairs={{0,2},{2,0},{4,6},{6,4},{8,10},{10,8},{12,14},{14,12},{16,18},{18,... | collective-permute-start | bytes 983048 | tf_op jit(solution)/shard_map/ppermute | solution.py:43
  7.0 3.7 %collective-permute-start = (f32[8,16,256]{2,1,0:T(8,128)S(1)}, f32[8,16,256]{2,1,0:T(8,128)S(1)}, u32[]{:S(2)}, u32[]{:S(2)}) collective-permute-start(f32[8,16,256]{2,1,0:T(8,128)S(1)} %pad_maximum_fusion.10), channel_id=1, source_target_pairs={{0,24},{2,26},{4,28},{6,30},{8,16},{10,18},{12,20},{14,22},{16,8},... | collective-permute-start | bytes 393224 | tf_op jit(solution)/shard_map/ppermute | solution.py:43
  10.7 3.2 %collective-permute-done.refs_3_ = f32[8,16,256]{2,1,0:T(8,128)S(1)} collective-permute-done((f32[8,16,256]{2,1,0:T(8,128)S(1)}, f32[8,16,256]{2,1,0:T(8,128)S(1)}, u32[]{:S(2)}, u32[]{:S(2)}) %collective-permute-start) | collective-permute-done | bytes 131104 | tf_op jit(solution)/shard_map/ppermute | solution.py:43
  13.9 3.6 %collective-permute-start.1 = (f32[12,16,256]{2,1,0:T(8,128)S(1)}, f32[12,16,256]{2,1,0:T(8,128)S(1)}, u32[]{:S(2)}, u32[]{:S(2)}) collective-permute-start(f32[12,16,256]{2,1,0:T(8,128)S(1)} %bitcast.2), channel_id=1, source_target_pairs={{0,24},{2,26},{4,28},{6,30},{8,16},{10,18},{12,20},{14,22},{16,8},... | collective-permute-start | bytes 589832 | tf_op jit(solution)/shard_map/ppermute | solution.py:43
  19.3 3.8 %collective-permute-done.1.refs_5_ = f32[12,16,256]{2,1,0:T(8,128)S(1)} collective-permute-done((f32[12,16,256]{2,1,0:T(8,128)S(1)}, f32[12,16,256]{2,1,0:T(8,128)S(1)}, u32[]{:S(2)}, u32[]{:S(2)}) %collective-permute-start.1) | collective-permute-done | bytes 196640 | tf_op jit(solution)/shard_map/ppermute | solution.py:43
  23.1 2.5 %collective-permute-start.2 = (f32[24,16,256]{2,1,0:T(8,128)S(1)}, f32[24,16,256]{2,1,0:T(8,128)S(1)}, u32[]{:S(2)}, u32[]{:S(2)}) collective-permute-start(f32[24,16,256]{2,1,0:T(8,128)S(1)} %pad_maximum_fusion.2), channel_id=1, source_target_pairs={{0,8},{2,10},{4,12},{6,14},{8,0},{10,2},{12,4},{14,6},{16,24},{18,... | collective-permute-start | bytes 1179656 | tf_op jit(solution)/shard_map/ppermute | solution.py:43
  25.6 1.2 %collective-permute-done.4.refs_4_ = f32[16,16,256]{2,1,0:T(8,128)S(1)} collective-permute-done((f32[16,16,256]{2,1,0:T(8,128)S(1)}, f32[16,16,256]{2,1,0:T(8,128)S(1)}, u32[]{:S(2)}, u32[]{:S(2)}) %collective-permute-start.4) | collective-permute-done | bytes 262176 | tf_op jit(solution)/shard_map/ppermute | solution.py:43
  26.9 1.8 %collective-permute-start.7 = (f32[20,16,256]{2,1,0:T(8,128)S(1)}, f32[20,16,256]{2,1,0:T(8,128)S(1)}, u32[]{:S(2)}, u32[]{:S(2)}) collective-permute-start(f32[20,16,256]{2,1,0:T(8,128)S(1)} %get-tuple-element.31), channel_id=1, source_target_pairs={{0,4},{2,6},{4,0},{6,2},{8,12},{10,14},{12,8},{14,10},{16,20},{18,... | collective-permute-start | bytes 983048 | tf_op jit(solution)/shard_map/ppermute | solution.py:43
  29.4 1.4 %collective-permute-start.3 = (f32[12,16,256]{2,1,0:T(8,128)S(1)}, f32[12,16,256]{2,1,0:T(8,128)S(1)}, u32[]{:S(2)}, u32[]{:S(2)}) collective-permute-start(f32[12,16,256]{2,1,0:T(8,128)S(1)} %collective-permute-done.1.refs_5_), channel_id=1, source_target_pairs={{0,4},{2,6},{4,0},{6,2},{8,12},{10,14},{12,8},{14,10},{16,20},{18,... | collective-permute-start | bytes 589832 | tf_op jit(solution)/shard_map/ppermute | solution.py:43
  31.1 6.6 %collective-permute-done.7.refs_10_ = f32[20,16,256]{2,1,0:T(8,128)S(1)} collective-permute-done((f32[20,16,256]{2,1,0:T(8,128)S(1)}, f32[20,16,256]{2,1,0:T(8,128)S(1)}, u32[]{:S(2)}, u32[]{:S(2)}) %collective-permute-start.7) | collective-permute-done | bytes 327712 | tf_op jit(solution)/shard_map/ppermute | solution.py:43
  37.7 1.4 %collective-permute-start.12 = (f32[8,16,256]{2,1,0:T(8,128)S(1)}, f32[8,16,256]{2,1,0:T(8,128)S(1)}, u32[]{:S(2)}, u32[]{:S(2)}) collective-permute-start(f32[8,16,256]{2,1,0:T(8,128)S(1)} %slice.53), channel_id=1, source_target_pairs={{0,2},{2,0},{4,6},{6,4},{8,10},{10,8},{12,14},{14,12},{16,18},{18,... | collective-permute-start | bytes 393224 | tf_op jit(solution)/shard_map/ppermute | solution.py:43
  39.8 1.8 %collective-permute-done.3.refs_12_ = f32[12,16,256]{2,1,0:T(8,128)S(1)} collective-permute-done((f32[12,16,256]{2,1,0:T(8,128)S(1)}, f32[12,16,256]{2,1,0:T(8,128)S(1)}, u32[]{:S(2)}, u32[]{:S(2)}) %collective-permute-start.3) | collective-permute-done | bytes 196640 | tf_op jit(solution)/shard_map/ppermute | solution.py:43
  41.6 1.2 %collective-permute-done.11.refs_11_ = f32[12,16,256]{2,1,0:T(8,128)S(1)} collective-permute-done((f32[12,16,256]{2,1,0:T(8,128)S(1)}, f32[12,16,256]{2,1,0:T(8,128)S(1)}, u32[]{:S(2)}, u32[]{:S(2)}) %collective-permute-start.11) | collective-permute-done | bytes 196640 | tf_op jit(solution)/shard_map/ppermute | solution.py:43
  42.9 0.7 %collective-permute-start.16 = (f32[30,16,256]{2,1,0:T(8,128)S(1)}, f32[30,16,256]{2,1,0:T(8,128)S(1)}, u32[]{:S(2)}, u32[]{:S(2)}) collective-permute-start(f32[30,16,256]{2,1,0:T(8,128)S(1)} %get-tuple-element.29), channel_id=1, source_target_pairs={{0,2},{2,0},{4,6},{6,4},{8,10},{10,8},{12,14},{14,12},{16,18},{18,... | collective-permute-start | bytes 1474568 | tf_op jit(solution)/shard_map/ppermute | solution.py:43
  43.6 1.9 %collective-permute-start.17 = (f32[30,16,256]{2,1,0:T(8,128)S(1)}, f32[30,16,256]{2,1,0:T(8,128)S(1)}, u32[]{:S(2)}, u32[]{:S(2)}) collective-permute-start(f32[30,16,256]{2,1,0:T(8,128)S(1)} %get-tuple-element.28), channel_id=1, source_target_pairs={{0,4},{2,6},{4,0},{6,2},{8,12},{10,14},{12,8},{14,10},{16,20},{18,... | collective-permute-start | bytes 1474568 | tf_op jit(solution)/shard_map/ppermute | solution.py:43
  45.6 6.7 %solve.1 = (f32[1024,256]{1,0:T(8,128)S(1)}, f32[1024,256]{1,0:T(8,128)S(1)}, f32[2,256,256]{2,1,0:T(8,128)S(1)}, f32[2,256,256]{2,1,0:T(8,128)S(1)}) custom-call(s32[4,4,4]{2,1,0:T(4,128)S(1)} %copy-done.2, f32[1024,256]{1,0:T(8,128)S(1)} %copy-done, f32[20,16,256]{2,1,0:T(8,128)S(1)} %pad_maximum_fusion.7.refs_2_.refs_4_, ...), custom_call_target="tpu_custom_call" | custom-call | flops 2147483648 | bytes 262144 | tf_op jit(solution)/shard_map/solve/pallas_call | solution.py:233
  52.9 1.0 %collective-permute-start.18 = (f32[12,16,256]{2,1,0:T(8,128)S(1)}, f32[12,16,256]{2,1,0:T(8,128)S(1)}, u32[]{:S(2)}, u32[]{:S(2)}) collective-permute-start(f32[12,16,256]{2,1,0:T(8,128)S(1)} %slice.56), channel_id=1, source_target_pairs={{0,2},{2,0},{4,6},{6,4},{8,10},{10,8},{12,14},{14,12},{16,18},{18,... | collective-permute-start | bytes 589832 | tf_op jit(solution)/shard_map/ppermute | solution.py:43
  54.0 1.6 %collective-permute-start.19 = (f32[12,16,256]{2,1,0:T(8,128)S(1)}, f32[12,16,256]{2,1,0:T(8,128)S(1)}, u32[]{:S(2)}, u32[]{:S(2)}) collective-permute-start(f32[12,16,256]{2,1,0:T(8,128)S(1)} %slice.57), channel_id=1, source_target_pairs={{0,4},{2,6},{4,0},{6,2},{8,12},{10,14},{12,8},{14,10},{16,20},{18,... | collective-permute-start | bytes 589832 | tf_op jit(solution)/shard_map/ppermute | solution.py:43
  55.6 2.0 %finish.1 = (f32[1024,256]{1,0:T(8,128)}, bf16[1536,256]{1,0:T(8,128)(2,1)S(1)}, bf16[1536,256]{1,0:T(8,128)(2,1)S(1)}) custom-call(f32[1024,256]{1,0:T(8,128)S(1)} %get-tuple-element.21.sol_ref, f32[1024,256]{1,0:T(8,128)S(1)} %get-tuple-element.22.part_ref, f32[2,256,256]{2,1,0:T(8,128)S(1)} %get-tuple-element.23.own_ref, ...), custom_call_target="tpu_custom_call" | custom-call | flops 100663296 | bytes 262144 | tf_op jit(solution)/shard_map/finish/pallas_call | solution.py:277
  57.5 6.8 %residual.1.refs_4_ = f32[1024,256]{1,0:T(8,128)} custom-call(s32[4,4,12]{2,1,0:T(4,128)S(1)} %copy-done.1, f32[1024,256]{1,0:T(8,128)S(1)} %copy-done, bf16[1536,256]{1,0:T(8,128)(2,1)S(1)} %get-tuple-element.26.refs_2_, bf16[1536,256]{1,0:T(8,128)(2,1)S(1)} %get-tuple-element.27.refs_3_, f32[20,16,256]{2,1,0:T(8,128)S(1)} %pad_maximum_fusion.7.refs_2_.refs_4_, ...), custom_call_target="tpu_custom_call" | custom-call | flops 1207959552 | bytes 6291456 | tf_op jit(solution)/shard_map/residual/pallas_call | solution.py:325
  64.3 2.3 %residual_rest.1 = f32[1024,256]{1,0:T(8,128)} custom-call(s32[4,4,12]{2,1,0:T(4,128)S(1)} %copy-done.1, f32[1024,256]{1,0:T(8,128)S(1)} %copy-done, bf16[1536,256]{1,0:T(8,128)(2,1)S(1)} %get-tuple-element.26.refs_2_, bf16[1536,256]{1,0:T(8,128)(2,1)S(1)} %get-tuple-element.27.refs_3_, ...), custom_call_target="tpu_custom_call", output_to_operand_aliasing={{}: (4, {})} | custom-call | flops 150994944 | bytes 2097152 | tf_op jit(solution)/shard_map/residual_rest/pallas_call | solution.py:377
  (49 shorter events, 4.4 us)
Async XLA Ops:
  1.6 0.9 %copy-start.4 = (f32[4,16,256]{2,1,0:T(8,128)S(1)}, f32[4,16,256]{2,1,0:T(8,128)}, u32[]{:S(2)}) copy-start(f32[4,16,256]{2,1,0:T(8,128)} %param.7) | copy-start | bytes 196612
  2.5 15.0 %collective-permute-start.5 = (f32[20,16,256]{2,1,0:T(8,128)S(1)}, f32[20,16,256]{2,1,0:T(8,128)S(1)}, u32[]{:S(2)}, u32[]{:S(2)}) collective-permute-start(f32[20,16,256]{2,1,0:T(8,128)S(1)} %pad_maximum_fusion.7.refs_2_.refs_4_), channel_id=1, source_target_pairs={{0,4},{2,6},{4,0},{6,2},{8,12},{10,14},{12,8},{14,10},{16,20},{18,... | collective-permute-start | bytes 983048 | tf_op jit(solution)/shard_map/ppermute | solution.py:43
  5.5 12.0 %collective-permute-start.8 = (f32[20,16,256]{2,1,0:T(8,128)S(1)}, f32[20,16,256]{2,1,0:T(8,128)S(1)}, u32[]{:S(2)}, u32[]{:S(2)}) collective-permute-start(f32[20,16,256]{2,1,0:T(8,128)S(1)} %pad_maximum_fusion.7.refs_2_.refs_4_), channel_id=1, source_target_pairs={{0,2},{2,0},{4,6},{6,4},{8,10},{10,8},{12,14},{14,12},{16,18},{18,... | collective-permute-start | bytes 983048 | tf_op jit(solution)/shard_map/ppermute | solution.py:43
  7.0 6.9 %collective-permute-start = (f32[8,16,256]{2,1,0:T(8,128)S(1)}, f32[8,16,256]{2,1,0:T(8,128)S(1)}, u32[]{:S(2)}, u32[]{:S(2)}) collective-permute-start(f32[8,16,256]{2,1,0:T(8,128)S(1)} %pad_maximum_fusion.10), channel_id=1, source_target_pairs={{0,24},{2,26},{4,28},{6,30},{8,16},{10,18},{12,20},{14,22},{16,8},... | collective-permute-start | bytes 393224 | tf_op jit(solution)/shard_map/ppermute | solution.py:43
  13.9 9.2 %collective-permute-start.1 = (f32[12,16,256]{2,1,0:T(8,128)S(1)}, f32[12,16,256]{2,1,0:T(8,128)S(1)}, u32[]{:S(2)}, u32[]{:S(2)}) collective-permute-start(f32[12,16,256]{2,1,0:T(8,128)S(1)} %bitcast.2), channel_id=1, source_target_pairs={{0,24},{2,26},{4,28},{6,30},{8,16},{10,18},{12,20},{14,22},{16,8},... | collective-permute-start | bytes 589832 | tf_op jit(solution)/shard_map/ppermute | solution.py:43
  17.6 9.2 %collective-permute-start.6 = (f32[18,16,256]{2,1,0:T(8,128)S(1)}, f32[18,16,256]{2,1,0:T(8,128)S(1)}, u32[]{:S(2)}, u32[]{:S(2)}) collective-permute-start(f32[18,16,256]{2,1,0:T(8,128)S(1)} %get-tuple-element.36), channel_id=1, source_target_pairs={{0,2},{2,0},{4,6},{6,4},{8,10},{10,8},{12,14},{14,12},{16,18},{18,... | collective-permute-start | bytes 884744 | tf_op jit(solution)/shard_map/ppermute | solution.py:43
  18.2 8.6 %collective-permute-start.9 = (f32[18,16,256]{2,1,0:T(8,128)S(1)}, f32[18,16,256]{2,1,0:T(8,128)S(1)}, u32[]{:S(2)}, u32[]{:S(2)}) collective-permute-start(f32[18,16,256]{2,1,0:T(8,128)S(1)} %get-tuple-element.35), channel_id=1, source_target_pairs={{0,4},{2,6},{4,0},{6,2},{8,12},{10,14},{12,8},{14,10},{16,20},{18,... | collective-permute-start | bytes 884744 | tf_op jit(solution)/shard_map/ppermute | solution.py:43
  18.7 8.1 %collective-permute-start.4 = (f32[16,16,256]{2,1,0:T(8,128)S(1)}, f32[16,16,256]{2,1,0:T(8,128)S(1)}, u32[]{:S(2)}, u32[]{:S(2)}) collective-permute-start(f32[16,16,256]{2,1,0:T(8,128)S(1)} %pad_maximum_fusion.8), channel_id=1, source_target_pairs={{0,8},{2,10},{4,12},{6,14},{8,0},{10,2},{12,4},{14,6},{16,24},{18,... | collective-permute-start | bytes 786440 | tf_op jit(solution)/shard_map/ppermute | solution.py:43
  23.1 19.7 %collective-permute-start.2 = (f32[24,16,256]{2,1,0:T(8,128)S(1)}, f32[24,16,256]{2,1,0:T(8,128)S(1)}, u32[]{:S(2)}, u32[]{:S(2)}) collective-permute-start(f32[24,16,256]{2,1,0:T(8,128)S(1)} %pad_maximum_fusion.2), channel_id=1, source_target_pairs={{0,8},{2,10},{4,12},{6,14},{8,0},{10,2},{12,4},{14,6},{16,24},{18,... | collective-permute-start | bytes 1179656 | tf_op jit(solution)/shard_map/ppermute | solution.py:43
  26.9 10.7 %collective-permute-start.7 = (f32[20,16,256]{2,1,0:T(8,128)S(1)}, f32[20,16,256]{2,1,0:T(8,128)S(1)}, u32[]{:S(2)}, u32[]{:S(2)}) collective-permute-start(f32[20,16,256]{2,1,0:T(8,128)S(1)} %get-tuple-element.31), channel_id=1, source_target_pairs={{0,4},{2,6},{4,0},{6,2},{8,12},{10,14},{12,8},{14,10},{16,20},{18,... | collective-permute-start | bytes 983048 | tf_op jit(solution)/shard_map/ppermute | solution.py:43
  28.8 10.4 %collective-permute-start.10 = (f32[20,16,256]{2,1,0:T(8,128)S(1)}, f32[20,16,256]{2,1,0:T(8,128)S(1)}, u32[]{:S(2)}, u32[]{:S(2)}) collective-permute-start(f32[20,16,256]{2,1,0:T(8,128)S(1)} %get-tuple-element.30), channel_id=1, source_target_pairs={{0,2},{2,0},{4,6},{6,4},{8,10},{10,8},{12,14},{14,12},{16,18},{18,... | collective-permute-start | bytes 983048 | tf_op jit(solution)/shard_map/ppermute | solution.py:43
  29.4 12.2 %collective-permute-start.3 = (f32[12,16,256]{2,1,0:T(8,128)S(1)}, f32[12,16,256]{2,1,0:T(8,128)S(1)}, u32[]{:S(2)}, u32[]{:S(2)}) collective-permute-start(f32[12,16,256]{2,1,0:T(8,128)S(1)} %collective-permute-done.1.refs_5_), channel_id=1, source_target_pairs={{0,4},{2,6},{4,0},{6,2},{8,12},{10,14},{12,8},{14,10},{16,20},{18,... | collective-permute-start | bytes 589832 | tf_op jit(solution)/shard_map/ppermute | solution.py:43
  30.8 12.0 %collective-permute-start.11 = (f32[12,16,256]{2,1,0:T(8,128)S(1)}, f32[12,16,256]{2,1,0:T(8,128)S(1)}, u32[]{:S(2)}, u32[]{:S(2)}) collective-permute-start(f32[12,16,256]{2,1,0:T(8,128)S(1)} %collective-permute-done.1.refs_5_), channel_id=1, source_target_pairs={{0,2},{2,0},{4,6},{6,4},{8,10},{10,8},{12,14},{14,12},{16,18},{18,... | collective-permute-start | bytes 589832 | tf_op jit(solution)/shard_map/ppermute | solution.py:43
  37.7 7.9 %collective-permute-start.12 = (f32[8,16,256]{2,1,0:T(8,128)S(1)}, f32[8,16,256]{2,1,0:T(8,128)S(1)}, u32[]{:S(2)}, u32[]{:S(2)}) collective-permute-start(f32[8,16,256]{2,1,0:T(8,128)S(1)} %slice.53), channel_id=1, source_target_pairs={{0,2},{2,0},{4,6},{6,4},{8,10},{10,8},{12,14},{14,12},{16,18},{18,... | collective-permute-start | bytes 393224 | tf_op jit(solution)/shard_map/ppermute | solution.py:43
  39.1 6.5 %copy-start = (f32[1024,256]{1,0:T(8,128)S(1)}, f32[1024,256]{1,0:T(8,128)}, u32[]{:S(2)}) copy-start(f32[1024,256]{1,0:T(8,128)} %refs_1_.4) | copy-start | bytes 3145732
  39.1 6.5 %collective-permute-start.13 = (f32[8,16,256]{2,1,0:T(8,128)S(1)}, f32[8,16,256]{2,1,0:T(8,128)S(1)}, u32[]{:S(2)}, u32[]{:S(2)}) collective-permute-start(f32[8,16,256]{2,1,0:T(8,128)S(1)} %slice.55), channel_id=1, source_target_pairs={{0,4},{2,6},{4,0},{6,2},{8,12},{10,14},{12,8},{14,10},{16,20},{18,... | collective-permute-start | bytes 393224 | tf_op jit(solution)/shard_map/ppermute | solution.py:43
  42.8 2.9 %copy-start.2 = (s32[4,4,4]{2,1,0:T(4,128)S(1)}, s32[4,4,4]{2,1,0:T(4,128)}, u32[]{:S(2)}) copy-start(s32[4,4,4]{2,1,0:T(4,128)} %refs_0_.3) | copy-start | bytes 772
  42.9 11.0 %collective-permute-start.16 = (f32[30,16,256]{2,1,0:T(8,128)S(1)}, f32[30,16,256]{2,1,0:T(8,128)S(1)}, u32[]{:S(2)}, u32[]{:S(2)}) collective-permute-start(f32[30,16,256]{2,1,0:T(8,128)S(1)} %get-tuple-element.29), channel_id=1, source_target_pairs={{0,2},{2,0},{4,6},{6,4},{8,10},{10,8},{12,14},{14,12},{16,18},{18,... | collective-permute-start | bytes 1474568 | tf_op jit(solution)/shard_map/ppermute | solution.py:43
  43.6 9.3 %collective-permute-start.17 = (f32[30,16,256]{2,1,0:T(8,128)S(1)}, f32[30,16,256]{2,1,0:T(8,128)S(1)}, u32[]{:S(2)}, u32[]{:S(2)}) collective-permute-start(f32[30,16,256]{2,1,0:T(8,128)S(1)} %get-tuple-element.28), channel_id=1, source_target_pairs={{0,4},{2,6},{4,0},{6,2},{8,12},{10,14},{12,8},{14,10},{16,20},{18,... | collective-permute-start | bytes 1474568 | tf_op jit(solution)/shard_map/ppermute | solution.py:43
  52.3 3.2 %collective-permute-start.14 = (f32[2,256,256]{2,1,0:T(8,128)S(1)}, f32[2,256,256]{2,1,0:T(8,128)S(1)}, u32[]{:S(2)}, u32[]{:S(2)}) collective-permute-start(f32[2,256,256]{2,1,0:T(8,128)S(1)} %get-tuple-element.23.own_ref), channel_id=1, source_target_pairs={{0,1},{1,0},{2,3},{3,2},{4,5},{5,4},{6,7},{7,6},{8,9},{9,8},{10,11... | collective-permute-start | bytes 1572872 | tf_op jit(solution)/shard_map/ppermute | solution.py:424
  52.4 3.1 %collective-permute-start.15 = (f32[2,256,256]{2,1,0:T(8,128)S(1)}, f32[2,256,256]{2,1,0:T(8,128)S(1)}, u32[]{:S(2)}, u32[]{:S(2)}) collective-permute-start(f32[2,256,256]{2,1,0:T(8,128)S(1)} %get-tuple-element.24), channel_id=1, source_target_pairs={{0,1},{1,0},{2,3},{3,2},{4,5},{5,4},{6,7},{7,6},{8,9},{9,8},{10,11... | collective-permute-start | bytes 1572872 | tf_op jit(solution)/shard_map/ppermute | solution.py:424
  52.9 11.4 %collective-permute-start.18 = (f32[12,16,256]{2,1,0:T(8,128)S(1)}, f32[12,16,256]{2,1,0:T(8,128)S(1)}, u32[]{:S(2)}, u32[]{:S(2)}) collective-permute-start(f32[12,16,256]{2,1,0:T(8,128)S(1)} %slice.56), channel_id=1, source_target_pairs={{0,2},{2,0},{4,6},{6,4},{8,10},{10,8},{12,14},{14,12},{16,18},{18,... | collective-permute-start | bytes 589832 | tf_op jit(solution)/shard_map/ppermute | solution.py:43
  54.0 10.3 %collective-permute-start.19 = (f32[12,16,256]{2,1,0:T(8,128)S(1)}, f32[12,16,256]{2,1,0:T(8,128)S(1)}, u32[]{:S(2)}, u32[]{:S(2)}) collective-permute-start(f32[12,16,256]{2,1,0:T(8,128)S(1)} %slice.57), channel_id=1, source_target_pairs={{0,4},{2,6},{4,0},{6,2},{8,12},{10,14},{12,8},{14,10},{16,20},{18,... | collective-permute-start | bytes 589832 | tf_op jit(solution)/shard_map/ppermute | solution.py:43
  55.6 2.0 %copy-start.1 = (s32[4,4,12]{2,1,0:T(4,128)S(1)}, s32[4,4,12]{2,1,0:T(4,128)}, u32[]{:S(2)}) copy-start(s32[4,4,12]{2,1,0:T(4,128)} %refs_0_.5) | copy-start | bytes 2308
  (1 other events, 0.8 us)

commit v10 on v8

--- a/solution.py
+++ b/solution.py
@@ -89,7 +89,7 @@
     late_across = send_both(onward(late_round, len(jacobian_line[-1][1]), [], axis), axis)
     right_side, _ = after((right_side, None), *late_parts)
     arrived = [own, *factor_line[1:], *jacobian_line[1:], *own_round, *second_round, *third_round, *factor_across]
-    return arrived + [*early_round, *late_round, *late_across], right_side
+    return arrived + [*early_round, *late_round], list(late_across), right_side
 
 
 def gather_whole(own, axis):
@@ -97,78 +97,61 @@
     return [(everything, [(owner, block) for owner in range(lax.axis_size(axis)) for _, block in own[1]])]
 
 
-def runs_of(pieces, begin, end):
-    chosen = []
+def places_of(pieces, begin, end):
+    arrays, places = [], {}
     for array, names in pieces:
-        runs = []
+        if not any(begin <= block < end for _, block in names):
+            continue
         for at, (owner, block) in enumerate(names):
-            if not begin <= block < end:
-                continue
-            if runs and runs[-1][0] + runs[-1][1] == at and names[at - 1] == (owner, block - 1):
-                runs[-1][1] += 1
-            else:
-                runs.append([at, 1, owner, block - begin])
-        if runs:
-            chosen.append((array, runs))
-    return chosen
-
-
-def place_rows(pieces, refs, relative, axis, panels, sem):
-    me = lax.axis_index(axis)
-    copies = []
-    for (array, runs), ref in zip(pieces, refs):
-        rows = array.shape[1]
-        for at, length, owner, block in runs:
-            row = pl.multiple_of((me ^ owner) * rows, rows) if relative else owner * rows
-            copies.append(
-                pltpu.make_async_copy(
-                    ref.at[pl.ds(at, length)],
-                    panels.at[pl.ds(block, length), pl.ds(row, rows), :],
-                    sem.at[len(copies)],
-                )
-            )
-    for copy in copies:
-        copy.start()
-    return copies
+            if begin <= block < end:
+                places.setdefault(owner, {})[block - begin] = (len(arrays), at)
+        arrays.append(array)
+    return arrays, places
+
+
+def row_of(owner, rows, relative):
+    return pl.multiple_of((lax.axis_index("rhs") ^ owner) * rows, rows) if relative else owner * rows
 
 
 def shapes(arrays):
     return [jax.ShapeDtypeStruct(shape, jnp.float32) for shape in arrays]
 
 
-def masked(rows, pattern_ref, s, block_rows):
-    wide = rows.shape[1]
-    blocks = wide // pattern_ref.shape[2]
-    together = max(1, 128 // blocks)
-    lane = lax.broadcasted_iota(jnp.int32, (1, together * blocks), 1)
-    bands = []
-    for a in range(pattern_ref.shape[1]):
-        weights = []
-        for first in range(0, pattern_ref.shape[2], together):
-            chosen = pattern_ref[s, a, first]
-            weight = jnp.full(lane.shape, chosen.astype(jnp.float32))
-            for c in range(1, min(together, pattern_ref.shape[2] - first)):
-                weight = jnp.where(lane >= c * blocks, pattern_ref[s, a, first + c].astype(jnp.float32), weight)
-            weights.append(weight)
-        weights = jnp.concatenate(weights, axis=1)[:, :wide]
-        bands.append(rows[a * block_rows : (a + 1) * block_rows] * weights)
-    return jnp.concatenate(bands, axis=0)
-
-
-def solve(pieces, relative, right_side, pattern, nodes, supers, size):
+def weights_of(pattern_ref, s, a, wide):
+    count = pattern_ref.shape[2]
+    step = wide // count
+    together = max(1, 128 // step)
+    lane = lax.broadcasted_iota(jnp.int32, (1, together * step), 1)
+    weights = []
+    for first in range(0, count, together):
+        weight = jnp.full(lane.shape, pattern_ref[s, a, first].astype(jnp.float32))
+        for c in range(1, min(together, count - first)):
+            weight = jnp.where(lane >= c * step, pattern_ref[s, a, first + c].astype(jnp.float32), weight)
+        weights.append(weight)
+    return jnp.concatenate(weights, axis=1)[:, :wide]
+
+
+def solve(arrays, places, relative, right_side, pattern, nodes, supers, size):
     columns = right_side.shape[1]
     extra = 0 if nodes == 1 else 1 if nodes == 2 else 2
     width = columns + extra * size
-    n = len(pieces)
-    n_copies = sum(len(runs) for _, runs in pieces)
+    n = len(arrays)
+    rows = arrays[0].shape[1]
 
     def kernel(*refs):
         pattern_ref, rhs_ref = refs[:2]
         piece_refs = refs[2 : 2 + n]
         sol_ref = refs[2 + n]
         extra_refs = refs[3 + n : 3 + n + extra]
-        down_ref, up_ref, panels, forward, sem = refs[3 + n + extra :]
-        copies = place_rows(pieces, piece_refs, relative, "rhs", panels, sem)
+        down_ref, up_ref, panels, forward = refs[3 + n + extra :]
+        for owner, blocks in places.items():
+            row = row_of(owner, rows, relative)
+            for block, (i, at) in blocks.items():
+                band = piece_refs[i][at]
+                if block >= supers:
+                    a = row // (size // pattern_ref.shape[1])
+                    band = band * weights_of(pattern_ref, block - supers, a, size)
+                panels[block, pl.ds(row, rows), :] = band
         index = lax.axis_index("node")
         below = jnp.where(index > 0, 1.0, 0.0)
         above = jnp.where(index < nodes - 1, 1.0, 0.0)
@@ -176,14 +159,11 @@
             jnp.int32, (size, size), 1
         )
         zeros = jnp.zeros((size, size), jnp.float32)
-        for copy in copies:
-            copy.wait()
 
         previous = None
         for s in range(supers):
             own = rhs_ref[s * size : (s + 1) * size, :]
-            low = masked(panels[supers + s], pattern_ref, s, size // pattern_ref.shape[1])
-            panels[supers + s] = low
+            low = panels[supers + s]
             if s == 0:
                 parts = [own]
                 if extra:
@@ -229,19 +209,18 @@
     out = pl.pallas_call(
         kernel,
         out_shape=shapes([(span, columns)] + [(span, size)] * extra + [leaving] * 2),
-        in_specs=[SMEM, VMEM] + [ANY] * n,
+        in_specs=[SMEM, VMEM] + [VMEM] * n,
         out_specs=[VMEM] * (3 + extra),
         scratch_shapes=[
             pltpu.VMEM((2 * supers, size, size), jnp.float32),
             pltpu.VMEM((supers, size, width), jnp.float32),
-            pltpu.SemaphoreType.DMA((n_copies,)),
         ],
         compiler_params=pltpu.CompilerParams(vmem_limit_bytes=VMEM_LIMIT),
         cost_estimate=pl.CostEstimate(
             flops=16 * supers * size * size * width, bytes_accessed=span * size, transcendentals=0
         ),
         name="solve",
-    )(pattern, right_side, *[array for array, _ in pieces])
+    )(pattern, right_side, *arrays)
     return out[0], out[1 : 1 + extra], out[1 + extra], out[2 + extra]
 
 
@@ -296,41 +275,56 @@
     return pl.pallas_call(kernel, out_shape=[windows, windows], name="windows")(sol, before, after)
 
 
-def subtract_product(pieces, relative, right_side, high, low, pattern, supers, size):
+def subtract_product(arrays, places, relative, right_side, high, low, pattern, supers, size, base=None):
     span, columns = right_side.shape
     wide = 3 * size
-    n = len(pieces)
-    n_copies = sum(len(runs) for _, runs in pieces)
+    n = len(arrays)
+    rows = arrays[0].shape[1]
+    extra = 0 if base is None else 1
 
     def kernel(*refs):
         pattern_ref, rhs_ref, high_ref, low_ref = refs[:4]
-        piece_refs = refs[4 : 4 + n]
-        out_ref, panels, sem = refs[4 + n :]
-        for copy in place_rows(pieces, piece_refs, relative, "rhs", panels, sem):
+        piece_refs = refs[4 + extra : 4 + extra + n]
+        out_ref = refs[4 + extra + n]
+        copies = []
+        for s in range(supers):
+            bands, starts = [], []
+            for owner, blocks in places.items():
+                row = row_of(owner, rows, relative)
+                band = [piece_refs[i][at] for i, at in (blocks[3 * s + c] for c in range(3))]
+                a = row // (size // pattern_ref.shape[1])
+                bands.append(jnp.concatenate(band, axis=1) * weights_of(pattern_ref, s, a, wide))
+                starts.append(s * size + row if not relative else pl.multiple_of(s * size + row, rows))
+            window = pl.ds(s * size, wide)
+            result = product(split(jnp.concatenate(bands, axis=0)), (high_ref[window, :], low_ref[window, :]))
+            for i, start in enumerate(starts):
+                value = rhs_ref[pl.ds(start, rows), :] - result[i * rows : (i + 1) * rows]
+                if base is None:
+                    out_ref[pl.ds(start, rows), :] = value
+                else:
+                    held, sem = refs[5 + extra + n :]
+                    at = len(copies)
+                    held[at] = value
+                    copies.append(pltpu.make_async_copy(held.at[at], out_ref.at[pl.ds(start, rows), :], sem.at[at]))
+                    copies[-1].start()
+        for copy in copies:
             copy.wait()
-        for s in range(supers):
-            rows = jnp.concatenate([panels[3 * s + c] for c in range(3)], axis=1)
-            panel = masked(rows, pattern_ref, s, size // pattern_ref.shape[1])
-            window = pl.ds(s * size, wide)
-            out_ref[s * size : (s + 1) * size, :] = rhs_ref[s * size : (s + 1) * size, :] - product(
-                split(panel), (high_ref[window, :], low_ref[window, :])
-            )
-
+
+    bands = supers * len(places)
+    scratch = [pltpu.VMEM((bands, rows, columns), jnp.float32), pltpu.SemaphoreType.DMA((bands,))]
     return pl.pallas_call(
         kernel,
         out_shape=shapes([(span, columns)])[0],
-        in_specs=[SMEM] + [VMEM] * 3 + [ANY] * n,
-        out_specs=VMEM,
-        scratch_shapes=[
-            pltpu.VMEM((3 * supers, size, size), jnp.float32),
-            pltpu.SemaphoreType.DMA((n_copies,)),
-        ],
+        in_specs=[SMEM] + [VMEM] * 3 + [ANY] * extra + [VMEM] * n,
+        out_specs=ANY if extra else VMEM,
+        input_output_aliases={4: 0} if extra else {},
+        scratch_shapes=scratch if extra else [],
         compiler_params=pltpu.CompilerParams(vmem_limit_bytes=VMEM_LIMIT),
         cost_estimate=pl.CostEstimate(
-            flops=6 * span * wide * columns, bytes_accessed=4 * span * (wide + 3 * columns), transcendentals=0
+            flops=6 * bands * rows * wide * columns, bytes_accessed=8 * bands * rows * wide, transcendentals=0
         ),
-        name="residual",
-    )(pattern, right_side, high, low, *[array for array, _ in pieces])
+        name="residual_rest" if extra else "residual",
+    )(pattern, right_side, high, low, *([base] if extra else []), *arrays)
 
 
 def dot(left, right):
@@ -353,13 +347,15 @@
     count = lax.axis_size("rhs")
     relative = count >= 16 and not count & (count - 1)
     if relative:
-        arrived, late = gather_panels(factor_own, jacobian_own, right_side, "rhs")
+        arrived, last, late = gather_panels(factor_own, jacobian_own, right_side, "rhs")
     else:
-        arrived, late = gather_whole(own, "rhs"), right_side
-    factor = runs_of(arrived, 0, 2 * supers)
-    jacobians = runs_of(arrived, 2 * supers, len(own[1]))
-
-    sol, parts, down, up = solve(factor, relative, late, factor_pattern, nodes, supers, size)
+        arrived, last, late = gather_whole(own, "rhs"), [], right_side
+    factor = places_of(arrived, 0, 2 * supers)
+    jacobians, places = places_of(arrived, 2 * supers, len(own[1]))
+    whole = {owner: blocks for owner, blocks in places.items() if len(blocks) == 3 * supers}
+    partial = set(places) - set(whole)
+
+    sol, parts, down, up = solve(*factor, relative, late, factor_pattern, nodes, supers, size)
     if nodes == 2:
         mail = [lax.ppermute(letter, "node", [(0, 1), (1, 0)]) for letter in (down, up)]
         sol, high, low = finish(sol, parts[0], down, *mail, supers)
@@ -380,7 +376,21 @@
             beneath = lax.ppermute(sol[span - size :], "node", upwards)
             beyond = lax.ppermute(sol[:size], "node", downwards)
         high, low = split_windows(sol, beneath, beyond)
-    residual = subtract_product(jacobians, relative, right_side, high, low, jacobian_pattern, supers, size)
+    subtract = functools.partial(
+        subtract_product,
+        relative=relative,
+        right_side=right_side,
+        high=high,
+        low=low,
+        pattern=jacobian_pattern,
+        supers=supers,
+        size=size,
+    )
+    residual = subtract(jacobians, whole)
+    if last:
+        arrays, rest = places_of([*arrived, *last] if partial else last, 2 * supers, len(own[1]))
+        rest = {owner: blocks for owner, blocks in rest.items() if owner not in whole}
+        residual = subtract(arrays, rest, base=residual)
     return sol, residual
 
 

time: 64.4 us -> 62.7 us (0.974)
  waiting for transfers between devices: 20.3 us -> 18.1 us
  Pallas kernels: 12.5 us -> 13.5 us
    ppermute x18, waiting for transfers between devices: 20.3 us -> 18.1 us  [sent(): lax.ppermute(array, axis, [(i, i ^ mask) for i in range(lax.axis_size(axi...]
    pallas_call x1 -> x2, Pallas kernels: 3.87 us -> 5.51 us  [subtract_product(): pl.pallas_call(kernel, out_shape=shapes([(span, columns)])[0], in_specs=[...]
  transfers between devices with their start and end apart: 20 -> 20, of which waited for: 8 -> 9; matrix products, arithmetic and copies ran while one was open for 1% -> 1% of each run, Pallas kernels for 13% -> 18%
where the time goes in v10:
time: 62.7 us; the launch traced here: 62.5 us
  starting transfers between devices  27.8 us (44%)
  waiting for transfers between devices  18.1 us (29%)
  Pallas kernels  13.5 us (22%)
  local copies, waits for them, and re-layouts  1.87 us (3%)
  between operations  0.81 us (1%)
    ppermute x18, starting transfers between devices, sent(): lax.ppermute(array, axis, [(i, i ^ mask) for i in range(lax.axis_size(axi...  27.2 us
    ppermute x18, waiting for transfers between devices, sent(): lax.ppermute(array, axis, [(i, i ^ mask) for i in range(lax.axis_size(axi...  18.1 us
    pallas_call x1, Pallas kernels, solve(): pl.pallas_call(kernel, out_shape=shapes([(span, columns)] + [(span, size)...  6.05 us
    pallas_call x2, Pallas kernels, subtract_product(): pl.pallas_call(kernel, out_shape=shapes([(span, columns)])[0], in_specs=[...  5.51 us
    pallas_call x1, Pallas kernels, finish(): pl.pallas_call(kernel, out_shape=shapes([(span, columns)]) + [windows, wi...  1.96 us
  transfers between devices with their start and end apart: 20, of which 9 were waited for; matrix products, arithmetic and copies ran while one was open for 1% of the time, Pallas kernels for 18%

profile of v10, /device:TPU:0, one launch (start us, length us, event | category | flops | bytes accessed | tf_op | source)
XLA Modules:
  0.0 62.5 jit_solution(10224779012782861915)
XLA Ops:
  0.6 0.9 %fusion = (f32[4,16,256]{2,1,0:T(8,128)S(1)}, f32[4,16,256]{2,1,0:T(8,128)S(1)}, f32[4,16,256]{2,1,0:T(8,128)S(1)}) fusion(f32[4,16,768]{2,1,0:T(8,128)} %param.10), kind=kLoop, calls=%fused_computation.11 | loop fusion | bytes 393216 | tf_op jit(solution)/shard_map/slice
  1.6 0.8 %copy-done.3 = f32[4,16,256]{2,1,0:T(8,128)S(1)} copy-done((f32[4,16,256]{2,1,0:T(8,128)S(1)}, f32[4,16,256]{2,1,0:T(8,128)}, u32[]{:S(2)}) %copy-start.3) | copy-done | bytes 65560
  2.5 3.0 %collective-permute-start.5 = (f32[20,16,256]{2,1,0:T(8,128)S(1)}, f32[20,16,256]{2,1,0:T(8,128)S(1)}, u32[]{:S(2)}, u32[]{:S(2)}) collective-permute-start(f32[20,16,256]{2,1,0:T(8,128)S(1)} %pad_maximum_fusion.7.refs_2_.refs_4_), channel_id=1, source_target_pairs={{0,4},{2,6},{4,0},{6,2},{8,12},{10,14},{12,8},{14,10},{16,20},{18,... | collective-permute-start | bytes 983048 | tf_op jit(solution)/shard_map/ppermute | solution.py:43
  5.5 1.5 %collective-permute-start.8 = (f32[20,16,256]{2,1,0:T(8,128)S(1)}, f32[20,16,256]{2,1,0:T(8,128)S(1)}, u32[]{:S(2)}, u32[]{:S(2)}) collective-permute-start(f32[20,16,256]{2,1,0:T(8,128)S(1)} %pad_maximum_fusion.7.refs_2_.refs_4_), channel_id=1, source_target_pairs={{0,2},{2,0},{4,6},{6,4},{8,10},{10,8},{12,14},{14,12},{16,18},{18,... | collective-permute-start | bytes 983048 | tf_op jit(solution)/shard_map/ppermute | solution.py:43
  7.0 3.7 %collective-permute-start = (f32[8,16,256]{2,1,0:T(8,128)S(1)}, f32[8,16,256]{2,1,0:T(8,128)S(1)}, u32[]{:S(2)}, u32[]{:S(2)}) collective-permute-start(f32[8,16,256]{2,1,0:T(8,128)S(1)} %pad_maximum_fusion.10), channel_id=1, source_target_pairs={{0,24},{2,26},{4,28},{6,30},{8,16},{10,18},{12,20},{14,22},{16,8},... | collective-permute-start | bytes 393224 | tf_op jit(solution)/shard_map/ppermute | solution.py:43
  10.7 3.2 %collective-permute-done.refs_3_ = f32[8,16,256]{2,1,0:T(8,128)S(1)} collective-permute-done((f32[8,16,256]{2,1,0:T(8,128)S(1)}, f32[8,16,256]{2,1,0:T(8,128)S(1)}, u32[]{:S(2)}, u32[]{:S(2)}) %collective-permute-start) | collective-permute-done | bytes 131104 | tf_op jit(solution)/shard_map/ppermute | solution.py:43
  13.9 3.6 %collective-permute-start.1 = (f32[12,16,256]{2,1,0:T(8,128)S(1)}, f32[12,16,256]{2,1,0:T(8,128)S(1)}, u32[]{:S(2)}, u32[]{:S(2)}) collective-permute-start(f32[12,16,256]{2,1,0:T(8,128)S(1)} %bitcast.2), channel_id=1, source_target_pairs={{0,24},{2,26},{4,28},{6,30},{8,16},{10,18},{12,20},{14,22},{16,8},... | collective-permute-start | bytes 589832 | tf_op jit(solution)/shard_map/ppermute | solution.py:43
  19.3 3.8 %collective-permute-done.1.refs_5_ = f32[12,16,256]{2,1,0:T(8,128)S(1)} collective-permute-done((f32[12,16,256]{2,1,0:T(8,128)S(1)}, f32[12,16,256]{2,1,0:T(8,128)S(1)}, u32[]{:S(2)}, u32[]{:S(2)}) %collective-permute-start.1) | collective-permute-done | bytes 196640 | tf_op jit(solution)/shard_map/ppermute | solution.py:43
  23.1 2.5 %collective-permute-start.2 = (f32[24,16,256]{2,1,0:T(8,128)S(1)}, f32[24,16,256]{2,1,0:T(8,128)S(1)}, u32[]{:S(2)}, u32[]{:S(2)}) collective-permute-start(f32[24,16,256]{2,1,0:T(8,128)S(1)} %pad_maximum_fusion.2), channel_id=1, source_target_pairs={{0,8},{2,10},{4,12},{6,14},{8,0},{10,2},{12,4},{14,6},{16,24},{18,... | collective-permute-start | bytes 1179656 | tf_op jit(solution)/shard_map/ppermute | solution.py:43
  25.6 1.2 %collective-permute-done.4.refs_4_ = f32[16,16,256]{2,1,0:T(8,128)S(1)} collective-permute-done((f32[16,16,256]{2,1,0:T(8,128)S(1)}, f32[16,16,256]{2,1,0:T(8,128)S(1)}, u32[]{:S(2)}, u32[]{:S(2)}) %collective-permute-start.4) | collective-permute-done | bytes 262176 | tf_op jit(solution)/shard_map/ppermute | solution.py:43
  26.9 1.8 %collective-permute-start.7 = (f32[20,16,256]{2,1,0:T(8,128)S(1)}, f32[20,16,256]{2,1,0:T(8,128)S(1)}, u32[]{:S(2)}, u32[]{:S(2)}) collective-permute-start(f32[20,16,256]{2,1,0:T(8,128)S(1)} %get-tuple-element.31), channel_id=1, source_target_pairs={{0,4},{2,6},{4,0},{6,2},{8,12},{10,14},{12,8},{14,10},{16,20},{18,... | collective-permute-start | bytes 983048 | tf_op jit(solution)/shard_map/ppermute | solution.py:43
  29.4 1.4 %collective-permute-start.3 = (f32[12,16,256]{2,1,0:T(8,128)S(1)}, f32[12,16,256]{2,1,0:T(8,128)S(1)}, u32[]{:S(2)}, u32[]{:S(2)}) collective-permute-start(f32[12,16,256]{2,1,0:T(8,128)S(1)} %collective-permute-done.1.refs_5_), channel_id=1, source_target_pairs={{0,4},{2,6},{4,0},{6,2},{8,12},{10,14},{12,8},{14,10},{16,20},{18,... | collective-permute-start | bytes 589832 | tf_op jit(solution)/shard_map/ppermute | solution.py:43
  31.1 6.6 %collective-permute-done.7.refs_10_ = f32[20,16,256]{2,1,0:T(8,128)S(1)} collective-permute-done((f32[20,16,256]{2,1,0:T(8,128)S(1)}, f32[20,16,256]{2,1,0:T(8,128)S(1)}, u32[]{:S(2)}, u32[]{:S(2)}) %collective-permute-start.7) | collective-permute-done | bytes 327712 | tf_op jit(solution)/shard_map/ppermute | solution.py:43
  37.7 1.4 %collective-permute-start.12 = (f32[8,16,256]{2,1,0:T(8,128)S(1)}, f32[8,16,256]{2,1,0:T(8,128)S(1)}, u32[]{:S(2)}, u32[]{:S(2)}) collective-permute-start(f32[8,16,256]{2,1,0:T(8,128)S(1)} %slice.53), channel_id=1, source_target_pairs={{0,2},{2,0},{4,6},{6,4},{8,10},{10,8},{12,14},{14,12},{16,18},{18,... | collective-permute-start | bytes 393224 | tf_op jit(solution)/shard_map/ppermute | solution.py:43
  39.8 1.8 %collective-permute-done.3.refs_12_ = f32[12,16,256]{2,1,0:T(8,128)S(1)} collective-permute-done((f32[12,16,256]{2,1,0:T(8,128)S(1)}, f32[12,16,256]{2,1,0:T(8,128)S(1)}, u32[]{:S(2)}, u32[]{:S(2)}) %collective-permute-start.3) | collective-permute-done | bytes 196640 | tf_op jit(solution)/shard_map/ppermute | solution.py:43
  41.6 1.2 %collective-permute-done.11.refs_11_ = f32[12,16,256]{2,1,0:T(8,128)S(1)} collective-permute-done((f32[12,16,256]{2,1,0:T(8,128)S(1)}, f32[12,16,256]{2,1,0:T(8,128)S(1)}, u32[]{:S(2)}, u32[]{:S(2)}) %collective-permute-start.11) | collective-permute-done | bytes 196640 | tf_op jit(solution)/shard_map/ppermute | solution.py:43
  42.9 0.7 %collective-permute-start.16 = (f32[30,16,256]{2,1,0:T(8,128)S(1)}, f32[30,16,256]{2,1,0:T(8,128)S(1)}, u32[]{:S(2)}, u32[]{:S(2)}) collective-permute-start(f32[30,16,256]{2,1,0:T(8,128)S(1)} %get-tuple-element.29), channel_id=1, source_target_pairs={{0,2},{2,0},{4,6},{6,4},{8,10},{10,8},{12,14},{14,12},{16,18},{18,... | collective-permute-start | bytes 1474568 | tf_op jit(solution)/shard_map/ppermute | solution.py:43
  43.6 1.9 %collective-permute-start.17 = (f32[30,16,256]{2,1,0:T(8,128)S(1)}, f32[30,16,256]{2,1,0:T(8,128)S(1)}, u32[]{:S(2)}, u32[]{:S(2)}) collective-permute-start(f32[30,16,256]{2,1,0:T(8,128)S(1)} %get-tuple-element.28), channel_id=1, source_target_pairs={{0,4},{2,6},{4,0},{6,2},{8,12},{10,14},{12,8},{14,10},{16,20},{18,... | collective-permute-start | bytes 1474568 | tf_op jit(solution)/shard_map/ppermute | solution.py:43
  45.6 6.1 %solve.1 = (f32[1024,256]{1,0:T(8,128)S(1)}, f32[1024,256]{1,0:T(8,128)S(1)}, f32[2,256,256]{2,1,0:T(8,128)S(1)}, f32[2,256,256]{2,1,0:T(8,128)S(1)}) custom-call(s32[4,4,4]{2,1,0:T(4,128)S(1)} %copy-done.2, f32[1024,256]{1,0:T(8,128)S(1)} %copy-done, f32[20,16,256]{2,1,0:T(8,128)S(1)} %pad_maximum_fusion.7.refs_2_.refs_4_, ...), custom_call_target="tpu_custom_call" | custom-call | flops 2147483648 | bytes 262144 | tf_op jit(solution)/shard_map/solve/pallas_call | solution.py:209
  52.5 1.5 %collective-permute-start.18 = (f32[12,16,256]{2,1,0:T(8,128)S(1)}, f32[12,16,256]{2,1,0:T(8,128)S(1)}, u32[]{:S(2)}, u32[]{:S(2)}) collective-permute-start(f32[12,16,256]{2,1,0:T(8,128)S(1)} %slice.56), channel_id=1, source_target_pairs={{0,2},{2,0},{4,6},{6,4},{8,10},{10,8},{12,14},{14,12},{16,18},{18,... | collective-permute-start | bytes 589832 | tf_op jit(solution)/shard_map/ppermute | solution.py:43
  54.0 1.0 %collective-permute-start.19 = (f32[12,16,256]{2,1,0:T(8,128)S(1)}, f32[12,16,256]{2,1,0:T(8,128)S(1)}, u32[]{:S(2)}, u32[]{:S(2)}) collective-permute-start(f32[12,16,256]{2,1,0:T(8,128)S(1)} %slice.57), channel_id=1, source_target_pairs={{0,4},{2,6},{4,0},{6,2},{8,12},{10,14},{12,8},{14,10},{16,20},{18,... | collective-permute-start | bytes 589832 | tf_op jit(solution)/shard_map/ppermute | solution.py:43
  55.0 2.0 %finish.1 = (f32[1024,256]{1,0:T(8,128)}, bf16[1536,256]{1,0:T(8,128)(2,1)S(1)}, bf16[1536,256]{1,0:T(8,128)(2,1)S(1)}) custom-call(f32[1024,256]{1,0:T(8,128)S(1)} %get-tuple-element.21.sol_ref, f32[1024,256]{1,0:T(8,128)S(1)} %get-tuple-element.22.part_ref, f32[2,256,256]{2,1,0:T(8,128)S(1)} %get-tuple-element.23.own_ref, ...), custom_call_target="tpu_custom_call" | custom-call | flops 100663296 | bytes 262144 | tf_op jit(solution)/shard_map/finish/pallas_call | solution.py:252
  56.9 3.3 %residual.1.refs_4_ = f32[1024,256]{1,0:T(8,128)} custom-call(s32[4,4,12]{2,1,0:T(4,128)S(1)} %copy-done.1, f32[1024,256]{1,0:T(8,128)S(1)} %copy-done, bf16[1536,256]{1,0:T(8,128)(2,1)S(1)} %get-tuple-element.26.refs_2_, bf16[1536,256]{1,0:T(8,128)(2,1)S(1)} %get-tuple-element.27.refs_3_, f32[20,16,256]{2,1,0:T(8,128)S(1)} %pad_maximum_fusion.7.refs_2_.refs_4_, ...), custom_call_target="tpu_custom_call" | custom-call | flops 1056964608 | bytes 5505024 | tf_op jit(solution)/shard_map/residual/pallas_call | solution.py:315
  60.2 2.3 %residual_rest.1 = f32[1024,256]{1,0:T(8,128)} custom-call(s32[4,4,12]{2,1,0:T(4,128)S(1)} %copy-done.1, f32[1024,256]{1,0:T(8,128)S(1)} %copy-done, bf16[1536,256]{1,0:T(8,128)(2,1)S(1)} %get-tuple-element.26.refs_2_, bf16[1536,256]{1,0:T(8,128)(2,1)S(1)} %get-tuple-element.27.refs_3_, ...), custom_call_target="tpu_custom_call", output_to_operand_aliasing={{}: (4, {})} | custom-call | flops 150994944 | bytes 786432 | tf_op jit(solution)/shard_map/residual_rest/pallas_call | solution.py:315
  (49 shorter events, 4.6 us)
Async XLA Ops:
  1.6 0.9 %copy-start.4 = (f32[4,16,256]{2,1,0:T(8,128)S(1)}, f32[4,16,256]{2,1,0:T(8,128)}, u32[]{:S(2)}) copy-start(f32[4,16,256]{2,1,0:T(8,128)} %param.7) | copy-start | bytes 196612
  2.5 15.0 %collective-permute-start.5 = (f32[20,16,256]{2,1,0:T(8,128)S(1)}, f32[20,16,256]{2,1,0:T(8,128)S(1)}, u32[]{:S(2)}, u32[]{:S(2)}) collective-permute-start(f32[20,16,256]{2,1,0:T(8,128)S(1)} %pad_maximum_fusion.7.refs_2_.refs_4_), channel_id=1, source_target_pairs={{0,4},{2,6},{4,0},{6,2},{8,12},{10,14},{12,8},{14,10},{16,20},{18,... | collective-permute-start | bytes 983048 | tf_op jit(solution)/shard_map/ppermute | solution.py:43
  5.5 12.0 %collective-permute-start.8 = (f32[20,16,256]{2,1,0:T(8,128)S(1)}, f32[20,16,256]{2,1,0:T(8,128)S(1)}, u32[]{:S(2)}, u32[]{:S(2)}) collective-permute-start(f32[20,16,256]{2,1,0:T(8,128)S(1)} %pad_maximum_fusion.7.refs_2_.refs_4_), channel_id=1, source_target_pairs={{0,2},{2,0},{4,6},{6,4},{8,10},{10,8},{12,14},{14,12},{16,18},{18,... | collective-permute-start | bytes 983048 | tf_op jit(solution)/shard_map/ppermute | solution.py:43
  7.0 6.9 %collective-permute-start = (f32[8,16,256]{2,1,0:T(8,128)S(1)}, f32[8,16,256]{2,1,0:T(8,128)S(1)}, u32[]{:S(2)}, u32[]{:S(2)}) collective-permute-start(f32[8,16,256]{2,1,0:T(8,128)S(1)} %pad_maximum_fusion.10), channel_id=1, source_target_pairs={{0,24},{2,26},{4,28},{6,30},{8,16},{10,18},{12,20},{14,22},{16,8},... | collective-permute-start | bytes 393224 | tf_op jit(solution)/shard_map/ppermute | solution.py:43
  13.9 9.2 %collective-permute-start.1 = (f32[12,16,256]{2,1,0:T(8,128)S(1)}, f32[12,16,256]{2,1,0:T(8,128)S(1)}, u32[]{:S(2)}, u32[]{:S(2)}) collective-permute-start(f32[12,16,256]{2,1,0:T(8,128)S(1)} %bitcast.2), channel_id=1, source_target_pairs={{0,24},{2,26},{4,28},{6,30},{8,16},{10,18},{12,20},{14,22},{16,8},... | collective-permute-start | bytes 589832 | tf_op jit(solution)/shard_map/ppermute | solution.py:43
  17.6 9.2 %collective-permute-start.6 = (f32[18,16,256]{2,1,0:T(8,128)S(1)}, f32[18,16,256]{2,1,0:T(8,128)S(1)}, u32[]{:S(2)}, u32[]{:S(2)}) collective-permute-start(f32[18,16,256]{2,1,0:T(8,128)S(1)} %get-tuple-element.36), channel_id=1, source_target_pairs={{0,2},{2,0},{4,6},{6,4},{8,10},{10,8},{12,14},{14,12},{16,18},{18,... | collective-permute-start | bytes 884744 | tf_op jit(solution)/shard_map/ppermute | solution.py:43
  18.2 8.6 %collective-permute-start.9 = (f32[18,16,256]{2,1,0:T(8,128)S(1)}, f32[18,16,256]{2,1,0:T(8,128)S(1)}, u32[]{:S(2)}, u32[]{:S(2)}) collective-permute-start(f32[18,16,256]{2,1,0:T(8,128)S(1)} %get-tuple-element.35), channel_id=1, source_target_pairs={{0,4},{2,6},{4,0},{6,2},{8,12},{10,14},{12,8},{14,10},{16,20},{18,... | collective-permute-start | bytes 884744 | tf_op jit(solution)/shard_map/ppermute | solution.py:43
  18.7 8.1 %collective-permute-start.4 = (f32[16,16,256]{2,1,0:T(8,128)S(1)}, f32[16,16,256]{2,1,0:T(8,128)S(1)}, u32[]{:S(2)}, u32[]{:S(2)}) collective-permute-start(f32[16,16,256]{2,1,0:T(8,128)S(1)} %pad_maximum_fusion.8), channel_id=1, source_target_pairs={{0,8},{2,10},{4,12},{6,14},{8,0},{10,2},{12,4},{14,6},{16,24},{18,... | collective-permute-start | bytes 786440 | tf_op jit(solution)/shard_map/ppermute | solution.py:43
  23.1 19.7 %collective-permute-start.2 = (f32[24,16,256]{2,1,0:T(8,128)S(1)}, f32[24,16,256]{2,1,0:T(8,128)S(1)}, u32[]{:S(2)}, u32[]{:S(2)}) collective-permute-start(f32[24,16,256]{2,1,0:T(8,128)S(1)} %pad_maximum_fusion.2), channel_id=1, source_target_pairs={{0,8},{2,10},{4,12},{6,14},{8,0},{10,2},{12,4},{14,6},{16,24},{18,... | collective-permute-start | bytes 1179656 | tf_op jit(solution)/shard_map/ppermute | solution.py:43
  26.9 10.7 %collective-permute-start.7 = (f32[20,16,256]{2,1,0:T(8,128)S(1)}, f32[20,16,256]{2,1,0:T(8,128)S(1)}, u32[]{:S(2)}, u32[]{:S(2)}) collective-permute-start(f32[20,16,256]{2,1,0:T(8,128)S(1)} %get-tuple-element.31), channel_id=1, source_target_pairs={{0,4},{2,6},{4,0},{6,2},{8,12},{10,14},{12,8},{14,10},{16,20},{18,... | collective-permute-start | bytes 983048 | tf_op jit(solution)/shard_map/ppermute | solution.py:43
  28.8 10.4 %collective-permute-start.10 = (f32[20,16,256]{2,1,0:T(8,128)S(1)}, f32[20,16,256]{2,1,0:T(8,128)S(1)}, u32[]{:S(2)}, u32[]{:S(2)}) collective-permute-start(f32[20,16,256]{2,1,0:T(8,128)S(1)} %get-tuple-element.30), channel_id=1, source_target_pairs={{0,2},{2,0},{4,6},{6,4},{8,10},{10,8},{12,14},{14,12},{16,18},{18,... | collective-permute-start | bytes 983048 | tf_op jit(solution)/shard_map/ppermute | solution.py:43
  29.4 12.2 %collective-permute-start.3 = (f32[12,16,256]{2,1,0:T(8,128)S(1)}, f32[12,16,256]{2,1,0:T(8,128)S(1)}, u32[]{:S(2)}, u32[]{:S(2)}) collective-permute-start(f32[12,16,256]{2,1,0:T(8,128)S(1)} %collective-permute-done.1.refs_5_), channel_id=1, source_target_pairs={{0,4},{2,6},{4,0},{6,2},{8,12},{10,14},{12,8},{14,10},{16,20},{18,... | collective-permute-start | bytes 589832 | tf_op jit(solution)/shard_map/ppermute | solution.py:43
  30.8 12.0 %collective-permute-start.11 = (f32[12,16,256]{2,1,0:T(8,128)S(1)}, f32[12,16,256]{2,1,0:T(8,128)S(1)}, u32[]{:S(2)}, u32[]{:S(2)}) collective-permute-start(f32[12,16,256]{2,1,0:T(8,128)S(1)} %collective-permute-done.1.refs_5_), channel_id=1, source_target_pairs={{0,2},{2,0},{4,6},{6,4},{8,10},{10,8},{12,14},{14,12},{16,18},{18,... | collective-permute-start | bytes 589832 | tf_op jit(solution)/shard_map/ppermute | solution.py:43
  37.7 7.9 %collective-permute-start.12 = (f32[8,16,256]{2,1,0:T(8,128)S(1)}, f32[8,16,256]{2,1,0:T(8,128)S(1)}, u32[]{:S(2)}, u32[]{:S(2)}) collective-permute-start(f32[8,16,256]{2,1,0:T(8,128)S(1)} %slice.53), channel_id=1, source_target_pairs={{0,2},{2,0},{4,6},{6,4},{8,10},{10,8},{12,14},{14,12},{16,18},{18,... | collective-permute-start | bytes 393224 | tf_op jit(solution)/shard_map/ppermute | solution.py:43
  39.1 6.5 %copy-start = (f32[1024,256]{1,0:T(8,128)S(1)}, f32[1024,256]{1,0:T(8,128)}, u32[]{:S(2)}) copy-start(f32[1024,256]{1,0:T(8,128)} %refs_1_.4) | copy-start | bytes 3145732
  39.1 6.5 %collective-permute-start.13 = (f32[8,16,256]{2,1,0:T(8,128)S(1)}, f32[8,16,256]{2,1,0:T(8,128)S(1)}, u32[]{:S(2)}, u32[]{:S(2)}) collective-permute-start(f32[8,16,256]{2,1,0:T(8,128)S(1)} %slice.55), channel_id=1, source_target_pairs={{0,4},{2,6},{4,0},{6,2},{8,12},{10,14},{12,8},{14,10},{16,20},{18,... | collective-permute-start | bytes 393224 | tf_op jit(solution)/shard_map/ppermute | solution.py:43
  42.8 2.9 %copy-start.2 = (s32[4,4,4]{2,1,0:T(4,128)S(1)}, s32[4,4,4]{2,1,0:T(4,128)}, u32[]{:S(2)}) copy-start(s32[4,4,4]{2,1,0:T(4,128)} %refs_0_.3) | copy-start | bytes 772
  42.9 11.0 %collective-permute-start.16 = (f32[30,16,256]{2,1,0:T(8,128)S(1)}, f32[30,16,256]{2,1,0:T(8,128)S(1)}, u32[]{:S(2)}, u32[]{:S(2)}) collective-permute-start(f32[30,16,256]{2,1,0:T(8,128)S(1)} %get-tuple-element.29), channel_id=1, source_target_pairs={{0,2},{2,0},{4,6},{6,4},{8,10},{10,8},{12,14},{14,12},{16,18},{18,... | collective-permute-start | bytes 1474568 | tf_op jit(solution)/shard_map/ppermute | solution.py:43
  43.6 8.8 %collective-permute-start.17 = (f32[30,16,256]{2,1,0:T(8,128)S(1)}, f32[30,16,256]{2,1,0:T(8,128)S(1)}, u32[]{:S(2)}, u32[]{:S(2)}) collective-permute-start(f32[30,16,256]{2,1,0:T(8,128)S(1)} %get-tuple-element.28), channel_id=1, source_target_pairs={{0,4},{2,6},{4,0},{6,2},{8,12},{10,14},{12,8},{14,10},{16,20},{18,... | collective-permute-start | bytes 1474568 | tf_op jit(solution)/shard_map/ppermute | solution.py:43
  51.7 3.3 %collective-permute-start.14 = (f32[2,256,256]{2,1,0:T(8,128)S(1)}, f32[2,256,256]{2,1,0:T(8,128)S(1)}, u32[]{:S(2)}, u32[]{:S(2)}) collective-permute-start(f32[2,256,256]{2,1,0:T(8,128)S(1)} %get-tuple-element.23.own_ref), channel_id=1, source_target_pairs={{0,1},{1,0},{2,3},{3,2},{4,5},{5,4},{6,7},{7,6},{8,9},{9,8},{10,11... | collective-permute-start | bytes 1572872 | tf_op jit(solution)/shard_map/ppermute | solution.py:360
  51.8 3.2 %collective-permute-start.15 = (f32[2,256,256]{2,1,0:T(8,128)S(1)}, f32[2,256,256]{2,1,0:T(8,128)S(1)}, u32[]{:S(2)}, u32[]{:S(2)}) collective-permute-start(f32[2,256,256]{2,1,0:T(8,128)S(1)} %get-tuple-element.24), channel_id=1, source_target_pairs={{0,1},{1,0},{2,3},{3,2},{4,5},{5,4},{6,7},{7,6},{8,9},{9,8},{10,11... | collective-permute-start | bytes 1572872 | tf_op jit(solution)/shard_map/ppermute | solution.py:360
  52.5 7.7 %collective-permute-start.18 = (f32[12,16,256]{2,1,0:T(8,128)S(1)}, f32[12,16,256]{2,1,0:T(8,128)S(1)}, u32[]{:S(2)}, u32[]{:S(2)}) collective-permute-start(f32[12,16,256]{2,1,0:T(8,128)S(1)} %slice.56), channel_id=1, source_target_pairs={{0,2},{2,0},{4,6},{6,4},{8,10},{10,8},{12,14},{14,12},{16,18},{18,... | collective-permute-start | bytes 589832 | tf_op jit(solution)/shard_map/ppermute | solution.py:43
  54.0 6.2 %collective-permute-start.19 = (f32[12,16,256]{2,1,0:T(8,128)S(1)}, f32[12,16,256]{2,1,0:T(8,128)S(1)}, u32[]{:S(2)}, u32[]{:S(2)}) collective-permute-start(f32[12,16,256]{2,1,0:T(8,128)S(1)} %slice.57), channel_id=1, source_target_pairs={{0,4},{2,6},{4,0},{6,2},{8,12},{10,14},{12,8},{14,10},{16,20},{18,... | collective-permute-start | bytes 589832 | tf_op jit(solution)/shard_map/ppermute | solution.py:43
  55.0 2.0 %copy-start.1 = (s32[4,4,12]{2,1,0:T(4,128)S(1)}, s32[4,4,12]{2,1,0:T(4,128)}, u32[]{:S(2)}) copy-start(s32[4,4,12]{2,1,0:T(4,128)} %refs_0_.5) | copy-start | bytes 2308
  (1 other events, 0.8 us)

commit v11 on v10

--- a/solution.py
+++ b/solution.py
@@ -59,37 +59,39 @@
     return sent(parts[0], axis, 1), sent(parts[1], axis, 2)
 
 
+def line_of(held, axis):
+    line, step = [held], lax.axis_size(axis) // 4
+    while step > 1:
+        line += [sent(part, axis, 4 * (step - 1)) for part in line]
+        step //= 2
+    return line
+
+
 def gather_panels(factor, jacobian, right_side, axis):
-    steps = lax.axis_size(axis) // 4
-    masks = []
-    while steps > 1:
-        masks.append(4 * (steps - 1))
-        steps //= 2
     own = joined(factor, jacobian)
-    factor_blocks = len(factor[1])
-
-    factor_line = [factor, sent(factor, axis, masks[0])]
-    jacobian_line = [jacobian, sent(after(jacobian, factor_line[1]), axis, masks[0])]
+    factor_line = line_of(factor, axis)
     own_round = around(own, axis)
-    second_round = send_both(onward(own_round, len(own[1]), factor_line[1:], axis), axis)
-    for mask in masks[1:]:
-        factor_line.append(sent(joined(*factor_line), axis, mask))
-    rest = joined(*factor_line[2:])
-    second_last = [after(part, rest) for part in second_round]
-    third_round = send_both(onward(second_last, factor_blocks, [rest], axis), axis)
-    for mask in masks[1:]:
-        jacobian_line.append(sent(joined(*jacobian_line), axis, mask))
-    early = joined(*jacobian_line[1:-1])
-    early_round = around(early, axis)
-    factor_parts = onward(third_round, len(rest[1]), [], axis)
+    near, far = joined(*factor_line[1:-1]), factor_line[-1]
+    second_parts = onward(own_round, len(own[1]), [near], axis)
+    second_round = send_both(second_parts, axis)
+    third_parts = onward(second_round, len(near[1]), [far], axis)
+    third_round = send_both(third_parts, axis)
+    factor_parts = onward(third_round, len(far[1]), [], axis)
     factor_across = send_both(factor_parts, axis)
-    early_last = [after(part, *factor_parts) for part in early_round]
-    late_parts = onward(early_last, len(early[1]), jacobian_line[-1:], axis)
-    late_round = send_both(late_parts, axis)
-    late_across = send_both(onward(late_round, len(jacobian_line[-1][1]), [], axis), axis)
-    right_side, _ = after((right_side, None), *late_parts)
+
+    jacobian_line = [after(jacobian, *second_parts)]
+    while len(jacobian_line) < len(factor_line).bit_length():
+        passed = joined(*jacobian_line)
+        jacobian_line.append(sent(passed, axis, factor_line[len(passed[1]) // len(jacobian[1])][1][0][0]))
+    near, far = joined(*jacobian_line[1:-1]), jacobian_line[-1]
+    near_round = around(near, axis)
+    near_last = [after(part, *factor_parts) for part in near_round]
+    far_parts = onward(near_last, len(near[1]), [far], axis)
+    far_round = send_both(far_parts, axis)
+    far_across = send_both(onward(far_round, len(far[1]), [], axis), axis)
+    right_side, _ = after((right_side, None), *far_parts)
     arrived = [own, *factor_line[1:], *jacobian_line[1:], *own_round, *second_round, *third_round, *factor_across]
-    return arrived + [*early_round, *late_round], list(late_across), right_side
+    return arrived + [*near_round, *far_round], list(far_across), right_side
 
 
 def gather_whole(own, axis):
@@ -155,43 +157,38 @@
         index = lax.axis_index("node")
         below = jnp.where(index > 0, 1.0, 0.0)
         above = jnp.where(index < nodes - 1, 1.0, 0.0)
-        on_diagonal = lax.broadcasted_iota(jnp.int32, (size, size), 0) == lax.broadcasted_iota(
-            jnp.int32, (size, size), 1
-        )
         zeros = jnp.zeros((size, size), jnp.float32)
 
+        inverse = [split(panels[s]) for s in range(supers)]
+        low = [split(panels[supers + s]) for s in range(supers)]
+        down = [product(inverse[s], low[s]) for s in range(supers)]
         previous = None
         for s in range(supers):
-            own = rhs_ref[s * size : (s + 1) * size, :]
-            low = panels[supers + s]
+            alone = product(inverse[s], split(rhs_ref[s * size : (s + 1) * size, :]))
             if s == 0:
-                parts = [own]
-                if extra:
-                    parts.append(low * -below)
-                if extra == 2:
-                    parts.append(zeros)
-                target = jnp.concatenate(parts, axis=1)
+                parts = [alone] + ([down[0] * -below] if extra else []) + [zeros] * (extra - 1)
+                previous = jnp.concatenate(parts, axis=1)
             else:
-                target = jnp.concatenate([own] + [zeros] * extra, axis=1) - product(split(low), split(previous))
-            previous = product(split(panels[s]), split(target))
+                alone = jnp.concatenate([alone] + [zeros] * extra, axis=1)
+                previous = alone - product(split(down[s]), split(previous))
             forward[s] = previous
 
-        entering = None
+        solved = None
         for s in reversed(range(supers)):
-            target = forward[s]
-            if s == supers - 1:
-                if extra:
-                    unit = jnp.where(on_diagonal, above, 0.0)
-                    shift = [jnp.zeros((size, columns), jnp.float32)] + [zeros] * (extra - 1) + [unit]
-                    target = target - jnp.concatenate(shift, axis=1)
+            turned = panels[s].T
+            alone = product(split(turned), split(forward[s]))
+            if s < supers - 1:
+                up = product(low[s + 1], inverse[s])
+                solved = alone - product(split(up.T), split(solved))
+            elif extra:
+                shift = [jnp.zeros((size, columns), jnp.float32)] + [zeros] * (extra - 1) + [turned * above]
+                solved = alone - jnp.concatenate(shift, axis=1)
             else:
-                target = target - entering
-            solved = product(split(panels[s].T), split(target))
+                solved = alone
             sol_ref[s * size : (s + 1) * size, :] = solved[:, :columns]
             for e, ref in enumerate(extra_refs):
                 ref[s * size : (s + 1) * size, :] = solved[:, columns + e * size : columns + (e + 1) * size]
-            if s > 0 or nodes > 1:
-                entering = product(split(panels[supers + s].T), split(solved))
+        entering = product(split(panels[supers].T), split(solved)) if nodes > 1 else None
 
         if nodes == 2:
             upper = index == 1

time: 62.7 us -> 63.8 us (1.018)
  waiting for transfers between devices: 18.1 us -> 19 us
  local copies, waits for them, and re-layouts: 1.87 us -> 2.6 us
    ppermute x18 -> x19, waiting for transfers between devices: 18.1 us -> 19 us  [sent(): lax.ppermute(array, axis, [(i, i ^ mask) for i in range(lax.axis_size(axi...]
    unnamed x10 -> x15, local copies, waits for them, and re-layouts: 0.85 us -> 1.59 us
    ppermute x18 -> x19, starting transfers between devices: 27.2 us -> 26.7 us  [sent(): lax.ppermute(array, axis, [(i, i ^ mask) for i in range(lax.axis_size(axi...]
  transfers between devices with their start and end apart: 20 -> 21, of which waited for: 9 -> 11; matrix products, arithmetic and copies ran while one was open for 1% -> 0% of each run, Pallas kernels for 18% -> 18%
where the time goes in v11:
time: 63.8 us; the launch traced here: 63.6 us
  starting transfers between devices  27.2 us (43%)
  waiting for transfers between devices  19 us (30%)
  Pallas kernels  13.6 us (21%)
  local copies, waits for them, and re-layouts  2.6 us (4%)
  between operations  0.81 us (1%)
    ppermute x19, starting transfers between devices, sent(): lax.ppermute(array, axis, [(i, i ^ mask) for i in range(lax.axis_size(axi...  26.7 us
    ppermute x19, waiting for transfers between devices, sent(): lax.ppermute(array, axis, [(i, i ^ mask) for i in range(lax.axis_size(axi...  19 us
    pallas_call x1, Pallas kernels, solve(): pl.pallas_call(kernel, out_shape=shapes([(span, columns)] + [(span, size)...  6.15 us
    pallas_call x2, Pallas kernels, subtract_product(): pl.pallas_call(kernel, out_shape=shapes([(span, columns)])[0], in_specs=[...  5.51 us
    pallas_call x1, Pallas kernels, finish(): pl.pallas_call(kernel, out_shape=shapes([(span, columns)]) + [windows, wi...  1.96 us
    unnamed x15, local copies, waits for them, and re-layouts  1.59 us
  transfers between devices with their start and end apart: 21, of which 11 were waited for; matrix products, arithmetic and copies ran while one was open for 0% of the time, Pallas kernels for 18%

profile of v11, /device:TPU:0, one launch (start us, length us, event | category | flops | bytes accessed | tf_op | source)
XLA Modules:
  0.0 63.6 jit_solution(503970648653865655)
XLA Ops:
  0.6 0.9 %fusion.1 = (f32[4,16,256]{2,1,0:T(8,128)S(1)}, f32[4,16,256]{2,1,0:T(8,128)S(1)}, f32[4,16,256]{2,1,0:T(8,128)S(1)}) fusion(f32[4,16,768]{2,1,0:T(8,128)} %param.10), kind=kLoop, calls=%fused_computation.12 | loop fusion | bytes 393216 | tf_op jit(solution)/shard_map/slice
  1.6 0.8 %copy-done.5 = f32[4,16,256]{2,1,0:T(8,128)S(1)} copy-done((f32[4,16,256]{2,1,0:T(8,128)S(1)}, f32[4,16,256]{2,1,0:T(8,128)}, u32[]{:S(2)}) %copy-start.5) | copy-done | bytes 65560
  2.5 3.0 %collective-permute-start.2 = (f32[20,16,256]{2,1,0:T(8,128)S(1)}, f32[20,16,256]{2,1,0:T(8,128)S(1)}, u32[]{:S(2)}, u32[]{:S(2)}) collective-permute-start(f32[20,16,256]{2,1,0:T(8,128)S(1)} %pad_maximum_fusion.5.refs_2_.refs_4_), channel_id=1, source_target_pairs={{0,4},{2,6},{4,0},{6,2},{8,12},{10,14},{12,8},{14,10},{16,20},{18,... | collective-permute-start | bytes 983048 | tf_op jit(solution)/shard_map/ppermute | solution.py:43
  5.5 1.5 %collective-permute-start.3 = (f32[20,16,256]{2,1,0:T(8,128)S(1)}, f32[20,16,256]{2,1,0:T(8,128)S(1)}, u32[]{:S(2)}, u32[]{:S(2)}) collective-permute-start(f32[20,16,256]{2,1,0:T(8,128)S(1)} %pad_maximum_fusion.5.refs_2_.refs_4_), channel_id=1, source_target_pairs={{0,2},{2,0},{4,6},{6,4},{8,10},{10,8},{12,14},{14,12},{16,18},{18,... | collective-permute-start | bytes 983048 | tf_op jit(solution)/shard_map/ppermute | solution.py:43
  7.0 3.7 %collective-permute-start = (f32[8,16,256]{2,1,0:T(8,128)S(1)}, f32[8,16,256]{2,1,0:T(8,128)S(1)}, u32[]{:S(2)}, u32[]{:S(2)}) collective-permute-start(f32[8,16,256]{2,1,0:T(8,128)S(1)} %constant_dynamic-update-slice_fusion), channel_id=1, source_target_pairs={{0,24},{2,26},{4,28},{6,30},{8,16},{10,18},{12,20},{14,22},{16,8},... | collective-permute-start | bytes 393224 | tf_op jit(solution)/shard_map/ppermute | solution.py:43
  10.7 2.5 %collective-permute-done.2.refs_7_.refs_8_ = f32[20,16,256]{2,1,0:T(8,128)S(1)} collective-permute-done((f32[20,16,256]{2,1,0:T(8,128)S(1)}, f32[20,16,256]{2,1,0:T(8,128)S(1)}, u32[]{:S(2)}, u32[]{:S(2)}) %collective-permute-start.2) | collective-permute-done | bytes 327712 | tf_op jit(solution)/shard_map/ppermute | solution.py:43
  15.1 1.4 %collective-permute-done.1.refs_4_ = f32[8,16,256]{2,1,0:T(8,128)S(1)} collective-permute-done((f32[8,16,256]{2,1,0:T(8,128)S(1)}, f32[8,16,256]{2,1,0:T(8,128)S(1)}, u32[]{:S(2)}, u32[]{:S(2)}) %collective-permute-start.1) | collective-permute-done | bytes 131104 | tf_op jit(solution)/shard_map/ppermute | solution.py:43
  17.2 1.0 %collective-permute-start.10 = (f32[26,16,256]{2,1,0:T(8,128)S(1)}, f32[26,16,256]{2,1,0:T(8,128)S(1)}, u32[]{:S(2)}, u32[]{:S(2)}) collective-permute-start(f32[26,16,256]{2,1,0:T(8,128)S(1)} %get-tuple-element.26), channel_id=1, source_target_pairs={{0,4},{2,6},{4,0},{6,2},{8,12},{10,14},{12,8},{14,10},{16,20},{18,... | collective-permute-start | bytes 1277960 | tf_op jit(solution)/shard_map/ppermute | solution.py:43
  18.2 3.6 %collective-permute-start.4 = (f32[12,16,256]{2,1,0:T(8,128)S(1)}, f32[12,16,256]{2,1,0:T(8,128)S(1)}, u32[]{:S(2)}, u32[]{:S(2)}) collective-permute-start(f32[12,16,256]{2,1,0:T(8,128)S(1)} %bitcast.2), channel_id=1, source_target_pairs={{0,24},{2,26},{4,28},{6,30},{8,16},{10,18},{12,20},{14,22},{16,8},... | collective-permute-start | bytes 589832 | tf_op jit(solution)/shard_map/ppermute | solution.py:43
  21.8 5.0 %collective-permute-done.4.refs_5_ = f32[12,16,256]{2,1,0:T(8,128)S(1)} collective-permute-done((f32[12,16,256]{2,1,0:T(8,128)S(1)}, f32[12,16,256]{2,1,0:T(8,128)S(1)}, u32[]{:S(2)}, u32[]{:S(2)}) %collective-permute-start.4) | collective-permute-done | bytes 196640 | tf_op jit(solution)/shard_map/ppermute | solution.py:43
  26.9 2.4 %collective-permute-start.5 = (f32[24,16,256]{2,1,0:T(8,128)S(1)}, f32[24,16,256]{2,1,0:T(8,128)S(1)}, u32[]{:S(2)}, u32[]{:S(2)}) collective-permute-start(f32[24,16,256]{2,1,0:T(8,128)S(1)} %pad_maximum_fusion.4), channel_id=1, source_target_pairs={{0,8},{2,10},{4,12},{6,14},{8,0},{10,2},{12,4},{14,6},{16,24},{18,... | collective-permute-start | bytes 1179656 | tf_op jit(solution)/shard_map/ppermute | solution.py:43
  29.5 0.8 %collective-permute-start.9 = (f32[16,16,256]{2,1,0:T(8,128)S(1)}, f32[16,16,256]{2,1,0:T(8,128)S(1)}, u32[]{:S(2)}, u32[]{:S(2)}) collective-permute-start(f32[16,16,256]{2,1,0:T(8,128)S(1)} %get-tuple-element.32), channel_id=1, source_target_pairs={{0,4},{2,6},{4,0},{6,2},{8,12},{10,14},{12,8},{14,10},{16,20},{18,... | collective-permute-start | bytes 786440 | tf_op jit(solution)/shard_map/ppermute | solution.py:43
  30.2 1.4 %collective-permute-start.11 = (f32[16,16,256]{2,1,0:T(8,128)S(1)}, f32[16,16,256]{2,1,0:T(8,128)S(1)}, u32[]{:S(2)}, u32[]{:S(2)}) collective-permute-start(f32[16,16,256]{2,1,0:T(8,128)S(1)} %get-tuple-element.31), channel_id=1, source_target_pairs={{0,2},{2,0},{4,6},{6,4},{8,10},{10,8},{12,14},{14,12},{16,18},{18,... | collective-permute-start | bytes 786440 | tf_op jit(solution)/shard_map/ppermute | solution.py:43
  32.1 1.5 %collective-permute-start.12 = (f32[12,16,256]{2,1,0:T(8,128)S(1)}, f32[12,16,256]{2,1,0:T(8,128)S(1)}, u32[]{:S(2)}, u32[]{:S(2)}) collective-permute-start(f32[12,16,256]{2,1,0:T(8,128)S(1)} %collective-permute-done.4.refs_5_), channel_id=1, source_target_pairs={{0,2},{2,0},{4,6},{6,4},{8,10},{10,8},{12,14},{14,12},{16,18},{18,... | collective-permute-start | bytes 589832 | tf_op jit(solution)/shard_map/ppermute | solution.py:43
  33.6 5.2 %collective-permute-done.9.refs_11_ = f32[16,16,256]{2,1,0:T(8,128)S(1)} collective-permute-done((f32[16,16,256]{2,1,0:T(8,128)S(1)}, f32[16,16,256]{2,1,0:T(8,128)S(1)}, u32[]{:S(2)}, u32[]{:S(2)}) %collective-permute-start.9) | collective-permute-done | bytes 262176 | tf_op jit(solution)/shard_map/ppermute | solution.py:43
  39.5 1.6 %collective-permute-start.14 = (f32[4,16,256]{2,1,0:T(8,128)S(1)}, f32[4,16,256]{2,1,0:T(8,128)S(1)}, u32[]{:S(2)}, u32[]{:S(2)}) collective-permute-start(f32[4,16,256]{2,1,0:T(8,128)S(1)} %slice.57), channel_id=1, source_target_pairs={{0,4},{2,6},{4,0},{6,2},{8,12},{10,14},{12,8},{14,10},{16,20},{18,... | collective-permute-start | bytes 196616 | tf_op jit(solution)/shard_map/ppermute | solution.py:43
  41.8 1.9 %collective-permute-start.17 = (f32[30,16,256]{2,1,0:T(8,128)S(1)}, f32[30,16,256]{2,1,0:T(8,128)S(1)}, u32[]{:S(2)}, u32[]{:S(2)}) collective-permute-start(f32[30,16,256]{2,1,0:T(8,128)S(1)} %get-tuple-element.25), channel_id=1, source_target_pairs={{0,2},{2,0},{4,6},{6,4},{8,10},{10,8},{12,14},{14,12},{16,18},{18,... | collective-permute-start | bytes 1474568 | tf_op jit(solution)/shard_map/ppermute | solution.py:43
  44.5 6.2 %solve.1 = (f32[1024,256]{1,0:T(8,128)S(1)}, f32[1024,256]{1,0:T(8,128)S(1)}, f32[2,256,256]{2,1,0:T(8,128)S(1)}, f32[2,256,256]{2,1,0:T(8,128)S(1)}) custom-call(s32[4,4,4]{2,1,0:T(4,128)S(1)} %copy-done.4, f32[1024,256]{1,0:T(8,128)S(1)} %copy-done, f32[20,16,256]{2,1,0:T(8,128)S(1)} %pad_maximum_fusion.5.refs_2_.refs_4_, ...), custom_call_target="tpu_custom_call" | custom-call | flops 2147483648 | bytes 262144 | tf_op jit(solution)/shard_map/solve/pallas_call | solution.py:206
  51.2 1.9 %collective-permute-done.18.refs_14_ = f32[30,16,256]{2,1,0:T(8,128)S(1)} collective-permute-done((f32[30,16,256]{2,1,0:T(8,128)S(1)}, f32[30,16,256]{2,1,0:T(8,128)S(1)}, u32[]{:S(2)}, u32[]{:S(2)}) %collective-permute-start.18) | collective-permute-done | bytes 491552 | tf_op jit(solution)/shard_map/ppermute | solution.py:43
  53.2 1.4 %collective-permute-start.19 = (f32[12,16,256]{2,1,0:T(8,128)S(1)}, f32[12,16,256]{2,1,0:T(8,128)S(1)}, u32[]{:S(2)}, u32[]{:S(2)}) collective-permute-start(f32[12,16,256]{2,1,0:T(8,128)S(1)} %slice.58), channel_id=1, source_target_pairs={{0,2},{2,0},{4,6},{6,4},{8,10},{10,8},{12,14},{14,12},{16,18},{18,... | collective-permute-start | bytes 589832 | tf_op jit(solution)/shard_map/ppermute | solution.py:43
  54.6 1.5 %collective-permute-start.20 = (f32[12,16,256]{2,1,0:T(8,128)S(1)}, f32[12,16,256]{2,1,0:T(8,128)S(1)}, u32[]{:S(2)}, u32[]{:S(2)}) collective-permute-start(f32[12,16,256]{2,1,0:T(8,128)S(1)} %slice.59), channel_id=1, source_target_pairs={{0,4},{2,6},{4,0},{6,2},{8,12},{10,14},{12,8},{14,10},{16,20},{18,... | collective-permute-start | bytes 589832 | tf_op jit(solution)/shard_map/ppermute | solution.py:43
  56.1 2.0 %finish.1 = (f32[1024,256]{1,0:T(8,128)}, bf16[1536,256]{1,0:T(8,128)(2,1)S(1)}, bf16[1536,256]{1,0:T(8,128)(2,1)S(1)}) custom-call(f32[1024,256]{1,0:T(8,128)S(1)} %get-tuple-element.17.sol_ref, f32[1024,256]{1,0:T(8,128)S(1)} %get-tuple-element.18.part_ref, f32[2,256,256]{2,1,0:T(8,128)S(1)} %get-tuple-element.19.own_ref, ...), custom_call_target="tpu_custom_call" | custom-call | flops 100663296 | bytes 262144 | tf_op jit(solution)/shard_map/finish/pallas_call | solution.py:249
  58.1 3.2 %residual.1.refs_4_ = f32[1024,256]{1,0:T(8,128)} custom-call(s32[4,4,12]{2,1,0:T(4,128)S(1)} %copy-done.3, f32[1024,256]{1,0:T(8,128)S(1)} %copy-done, bf16[1536,256]{1,0:T(8,128)(2,1)S(1)} %get-tuple-element.22.refs_2_, bf16[1536,256]{1,0:T(8,128)(2,1)S(1)} %get-tuple-element.23.refs_3_, f32[20,16,256]{2,1,0:T(8,128)S(1)} %pad_maximum_fusion.5.refs_2_.refs_4_, ...), custom_call_target="tpu_custom_call" | custom-call | flops 1056964608 | bytes 5505024 | tf_op jit(solution)/shard_map/residual/pallas_call | solution.py:312
  61.3 2.3 %residual_rest.1 = f32[1024,256]{1,0:T(8,128)} custom-call(s32[4,4,12]{2,1,0:T(4,128)S(1)} %copy-done.3, f32[1024,256]{1,0:T(8,128)S(1)} %copy-done, bf16[1536,256]{1,0:T(8,128)(2,1)S(1)} %get-tuple-element.22.refs_2_, bf16[1536,256]{1,0:T(8,128)(2,1)S(1)} %get-tuple-element.23.refs_3_, ...), custom_call_target="tpu_custom_call", output_to_operand_aliasing={{}: (4, {})} | custom-call | flops 150994944 | bytes 786432 | tf_op jit(solution)/shard_map/residual_rest/pallas_call | solution.py:312
  (56 shorter events, 6.0 us)
Async XLA Ops:
  2.5 10.7 %collective-permute-start.2 = (f32[20,16,256]{2,1,0:T(8,128)S(1)}, f32[20,16,256]{2,1,0:T(8,128)S(1)}, u32[]{:S(2)}, u32[]{:S(2)}) collective-permute-start(f32[20,16,256]{2,1,0:T(8,128)S(1)} %pad_maximum_fusion.5.refs_2_.refs_4_), channel_id=1, source_target_pairs={{0,4},{2,6},{4,0},{6,2},{8,12},{10,14},{12,8},{14,10},{16,20},{18,... | collective-permute-start | bytes 983048 | tf_op jit(solution)/shard_map/ppermute | solution.py:43
  5.5 9.2 %collective-permute-start.3 = (f32[20,16,256]{2,1,0:T(8,128)S(1)}, f32[20,16,256]{2,1,0:T(8,128)S(1)}, u32[]{:S(2)}, u32[]{:S(2)}) collective-permute-start(f32[20,16,256]{2,1,0:T(8,128)S(1)} %pad_maximum_fusion.5.refs_2_.refs_4_), channel_id=1, source_target_pairs={{0,2},{2,0},{4,6},{6,4},{8,10},{10,8},{12,14},{14,12},{16,18},{18,... | collective-permute-start | bytes 983048 | tf_op jit(solution)/shard_map/ppermute | solution.py:43
  7.0 8.1 %collective-permute-start = (f32[8,16,256]{2,1,0:T(8,128)S(1)}, f32[8,16,256]{2,1,0:T(8,128)S(1)}, u32[]{:S(2)}, u32[]{:S(2)}) collective-permute-start(f32[8,16,256]{2,1,0:T(8,128)S(1)} %constant_dynamic-update-slice_fusion), channel_id=1, source_target_pairs={{0,24},{2,26},{4,28},{6,30},{8,16},{10,18},{12,20},{14,22},{16,8},... | collective-permute-start | bytes 393224 | tf_op jit(solution)/shard_map/ppermute | solution.py:43
  10.7 5.8 %collective-permute-start.1 = (f32[8,16,256]{2,1,0:T(8,128)S(1)}, f32[8,16,256]{2,1,0:T(8,128)S(1)}, u32[]{:S(2)}, u32[]{:S(2)}) collective-permute-start(f32[8,16,256]{2,1,0:T(8,128)S(1)} %constant_dynamic-update-slice_fusion), channel_id=1, source_target_pairs={{0,8},{2,10},{4,12},{6,14},{8,0},{10,2},{12,4},{14,6},{16,24},{18,... | collective-permute-start | bytes 393224 | tf_op jit(solution)/shard_map/ppermute | solution.py:43
  16.6 12.7 %collective-permute-start.8 = (f32[26,16,256]{2,1,0:T(8,128)S(1)}, f32[26,16,256]{2,1,0:T(8,128)S(1)}, u32[]{:S(2)}, u32[]{:S(2)}) collective-permute-start(f32[26,16,256]{2,1,0:T(8,128)S(1)} %get-tuple-element.27), channel_id=1, source_target_pairs={{0,2},{2,0},{4,6},{6,4},{8,10},{10,8},{12,14},{14,12},{16,18},{18,... | collective-permute-start | bytes 1277960 | tf_op jit(solution)/shard_map/ppermute | solution.py:43
  17.2 12.1 %collective-permute-start.10 = (f32[26,16,256]{2,1,0:T(8,128)S(1)}, f32[26,16,256]{2,1,0:T(8,128)S(1)}, u32[]{:S(2)}, u32[]{:S(2)}) collective-permute-start(f32[26,16,256]{2,1,0:T(8,128)S(1)} %get-tuple-element.26), channel_id=1, source_target_pairs={{0,4},{2,6},{4,0},{6,2},{8,12},{10,14},{12,8},{14,10},{16,20},{18,... | collective-permute-start | bytes 1277960 | tf_op jit(solution)/shard_map/ppermute | solution.py:43
  18.2 8.6 %collective-permute-start.4 = (f32[12,16,256]{2,1,0:T(8,128)S(1)}, f32[12,16,256]{2,1,0:T(8,128)S(1)}, u32[]{:S(2)}, u32[]{:S(2)}) collective-permute-start(f32[12,16,256]{2,1,0:T(8,128)S(1)} %bitcast.2), channel_id=1, source_target_pairs={{0,24},{2,26},{4,28},{6,30},{8,16},{10,18},{12,20},{14,22},{16,8},... | collective-permute-start | bytes 589832 | tf_op jit(solution)/shard_map/ppermute | solution.py:43
  21.8 7.5 %collective-permute-start.7 = (f32[8,16,256]{2,1,0:T(8,128)S(1)}, f32[8,16,256]{2,1,0:T(8,128)S(1)}, u32[]{:S(2)}, u32[]{:S(2)}) collective-permute-start(f32[8,16,256]{2,1,0:T(8,128)S(1)} %collective-permute-done.refs_3_), channel_id=1, source_target_pairs={{0,8},{2,10},{4,12},{6,14},{8,0},{10,2},{12,4},{14,6},{16,24},{18,... | collective-permute-start | bytes 393224 | tf_op jit(solution)/shard_map/ppermute | solution.py:43
  26.9 14.8 %collective-permute-start.5 = (f32[24,16,256]{2,1,0:T(8,128)S(1)}, f32[24,16,256]{2,1,0:T(8,128)S(1)}, u32[]{:S(2)}, u32[]{:S(2)}) collective-permute-start(f32[24,16,256]{2,1,0:T(8,128)S(1)} %pad_maximum_fusion.4), channel_id=1, source_target_pairs={{0,8},{2,10},{4,12},{6,14},{8,0},{10,2},{12,4},{14,6},{16,24},{18,... | collective-permute-start | bytes 1179656 | tf_op jit(solution)/shard_map/ppermute | solution.py:43
  29.5 9.3 %collective-permute-start.9 = (f32[16,16,256]{2,1,0:T(8,128)S(1)}, f32[16,16,256]{2,1,0:T(8,128)S(1)}, u32[]{:S(2)}, u32[]{:S(2)}) collective-permute-start(f32[16,16,256]{2,1,0:T(8,128)S(1)} %get-tuple-element.32), channel_id=1, source_target_pairs={{0,4},{2,6},{4,0},{6,2},{8,12},{10,14},{12,8},{14,10},{16,20},{18,... | collective-permute-start | bytes 786440 | tf_op jit(solution)/shard_map/ppermute | solution.py:43
  30.2 9.2 %collective-permute-start.11 = (f32[16,16,256]{2,1,0:T(8,128)S(1)}, f32[16,16,256]{2,1,0:T(8,128)S(1)}, u32[]{:S(2)}, u32[]{:S(2)}) collective-permute-start(f32[16,16,256]{2,1,0:T(8,128)S(1)} %get-tuple-element.31), channel_id=1, source_target_pairs={{0,2},{2,0},{4,6},{6,4},{8,10},{10,8},{12,14},{14,12},{16,18},{18,... | collective-permute-start | bytes 786440 | tf_op jit(solution)/shard_map/ppermute | solution.py:43
  31.7 9.8 %collective-permute-start.6 = (f32[12,16,256]{2,1,0:T(8,128)S(1)}, f32[12,16,256]{2,1,0:T(8,128)S(1)}, u32[]{:S(2)}, u32[]{:S(2)}) collective-permute-start(f32[12,16,256]{2,1,0:T(8,128)S(1)} %collective-permute-done.4.refs_5_), channel_id=1, source_target_pairs={{0,4},{2,6},{4,0},{6,2},{8,12},{10,14},{12,8},{14,10},{16,20},{18,... | collective-permute-start | bytes 589832 | tf_op jit(solution)/shard_map/ppermute | solution.py:43
  32.1 9.6 %collective-permute-start.12 = (f32[12,16,256]{2,1,0:T(8,128)S(1)}, f32[12,16,256]{2,1,0:T(8,128)S(1)}, u32[]{:S(2)}, u32[]{:S(2)}) collective-permute-start(f32[12,16,256]{2,1,0:T(8,128)S(1)} %collective-permute-done.4.refs_5_), channel_id=1, source_target_pairs={{0,2},{2,0},{4,6},{6,4},{8,10},{10,8},{12,14},{14,12},{16,18},{18,... | collective-permute-start | bytes 589832 | tf_op jit(solution)/shard_map/ppermute | solution.py:43
  38.8 5.7 %copy-start = (f32[1024,256]{1,0:T(8,128)S(1)}, f32[1024,256]{1,0:T(8,128)}, u32[]{:S(2)}) copy-start(f32[1024,256]{1,0:T(8,128)} %refs_1_.4) | copy-start | bytes 3145732
  38.8 5.1 %collective-permute-start.13 = (f32[4,16,256]{2,1,0:T(8,128)S(1)}, f32[4,16,256]{2,1,0:T(8,128)S(1)}, u32[]{:S(2)}, u32[]{:S(2)}) collective-permute-start(f32[4,16,256]{2,1,0:T(8,128)S(1)} %slice.55), channel_id=1, source_target_pairs={{0,2},{2,0},{4,6},{6,4},{8,10},{10,8},{12,14},{14,12},{16,18},{18,... | collective-permute-start | bytes 196616 | tf_op jit(solution)/shard_map/ppermute | solution.py:43
  39.5 5.0 %collective-permute-start.14 = (f32[4,16,256]{2,1,0:T(8,128)S(1)}, f32[4,16,256]{2,1,0:T(8,128)S(1)}, u32[]{:S(2)}, u32[]{:S(2)}) collective-permute-start(f32[4,16,256]{2,1,0:T(8,128)S(1)} %slice.57), channel_id=1, source_target_pairs={{0,4},{2,6},{4,0},{6,2},{8,12},{10,14},{12,8},{14,10},{16,20},{18,... | collective-permute-start | bytes 196616 | tf_op jit(solution)/shard_map/ppermute | solution.py:43
  41.7 2.8 %copy-start.2 = (f32[20,16,256]{2,1,0:T(8,128)S(1)}, f32[20,16,256]{2,1,0:T(8,128)}, u32[]{:S(2)}) copy-start(f32[20,16,256]{2,1,0:T(8,128)} %copy-done.1) | copy-start | bytes 983044
  41.7 2.8 %copy-start.4 = (s32[4,4,4]{2,1,0:T(4,128)S(1)}, s32[4,4,4]{2,1,0:T(4,128)}, u32[]{:S(2)}) copy-start(s32[4,4,4]{2,1,0:T(4,128)} %refs_0_.3) | copy-start | bytes 772
  41.8 12.8 %collective-permute-start.17 = (f32[30,16,256]{2,1,0:T(8,128)S(1)}, f32[30,16,256]{2,1,0:T(8,128)S(1)}, u32[]{:S(2)}, u32[]{:S(2)}) collective-permute-start(f32[30,16,256]{2,1,0:T(8,128)S(1)} %get-tuple-element.25), channel_id=1, source_target_pairs={{0,2},{2,0},{4,6},{6,4},{8,10},{10,8},{12,14},{14,12},{16,18},{18,... | collective-permute-start | bytes 1474568 | tf_op jit(solution)/shard_map/ppermute | solution.py:43
  43.8 9.4 %collective-permute-start.18 = (f32[30,16,256]{2,1,0:T(8,128)S(1)}, f32[30,16,256]{2,1,0:T(8,128)S(1)}, u32[]{:S(2)}, u32[]{:S(2)}) collective-permute-start(f32[30,16,256]{2,1,0:T(8,128)S(1)} %get-tuple-element.24), channel_id=1, source_target_pairs={{0,4},{2,6},{4,0},{6,2},{8,12},{10,14},{12,8},{14,10},{16,20},{18,... | collective-permute-start | bytes 1474568 | tf_op jit(solution)/shard_map/ppermute | solution.py:43
  50.6 5.5 %collective-permute-start.15 = (f32[2,256,256]{2,1,0:T(8,128)S(1)}, f32[2,256,256]{2,1,0:T(8,128)S(1)}, u32[]{:S(2)}, u32[]{:S(2)}) collective-permute-start(f32[2,256,256]{2,1,0:T(8,128)S(1)} %get-tuple-element.19.own_ref), channel_id=1, source_target_pairs={{0,1},{1,0},{2,3},{3,2},{4,5},{5,4},{6,7},{7,6},{8,9},{9,8},{10,11... | collective-permute-start | bytes 1572872 | tf_op jit(solution)/shard_map/ppermute | solution.py:357
  50.7 5.4 %collective-permute-start.16 = (f32[2,256,256]{2,1,0:T(8,128)S(1)}, f32[2,256,256]{2,1,0:T(8,128)S(1)}, u32[]{:S(2)}, u32[]{:S(2)}) collective-permute-start(f32[2,256,256]{2,1,0:T(8,128)S(1)} %get-tuple-element.20), channel_id=1, source_target_pairs={{0,1},{1,0},{2,3},{3,2},{4,5},{5,4},{6,7},{7,6},{8,9},{9,8},{10,11... | collective-permute-start | bytes 1572872 | tf_op jit(solution)/shard_map/ppermute | solution.py:357
  53.2 8.2 %collective-permute-start.19 = (f32[12,16,256]{2,1,0:T(8,128)S(1)}, f32[12,16,256]{2,1,0:T(8,128)S(1)}, u32[]{:S(2)}, u32[]{:S(2)}) collective-permute-start(f32[12,16,256]{2,1,0:T(8,128)S(1)} %slice.58), channel_id=1, source_target_pairs={{0,2},{2,0},{4,6},{6,4},{8,10},{10,8},{12,14},{14,12},{16,18},{18,... | collective-permute-start | bytes 589832 | tf_op jit(solution)/shard_map/ppermute | solution.py:43
  54.6 6.7 %collective-permute-start.20 = (f32[12,16,256]{2,1,0:T(8,128)S(1)}, f32[12,16,256]{2,1,0:T(8,128)S(1)}, u32[]{:S(2)}, u32[]{:S(2)}) collective-permute-start(f32[12,16,256]{2,1,0:T(8,128)S(1)} %slice.59), channel_id=1, source_target_pairs={{0,4},{2,6},{4,0},{6,2},{8,12},{10,14},{12,8},{14,10},{16,20},{18,... | collective-permute-start | bytes 589832 | tf_op jit(solution)/shard_map/ppermute | solution.py:43
  (5 other events, 6.3 us)

commit v12 on v11

--- a/solution.py
+++ b/solution.py
@@ -11,7 +11,6 @@
 SMEM = pl.BlockSpec(memory_space=pltpu.SMEM)
 ANY = pl.BlockSpec(memory_space=pl.ANY)
 VMEM_LIMIT = 20 * 2**20
-PLAIN = (((1,), (0,)), ((), ()))
 
 
 def split(value):
@@ -19,9 +18,12 @@
     return high, (value - high.astype(jnp.float32)).astype(jnp.bfloat16)
 
 
-def product(left, right, dims=PLAIN):
-    dot = functools.partial(lax.dot_general, dimension_numbers=dims, preferred_element_type=jnp.float32)
-    return dot(left[0], right[1]) + dot(left[1], right[0]) + dot(left[0], right[0])
+def product(left, right):
+    return jnp.dot(
+        jnp.concatenate([left[1], left[0], left[0]], axis=1),
+        jnp.concatenate([right[0], right[1], right[0]], axis=0),
+        preferred_element_type=jnp.float32,
+    )
 
 
 def after(held, *others):
@@ -67,8 +69,7 @@
     return line
 
 
-def gather_panels(factor, jacobian, right_side, axis):
-    own = joined(factor, jacobian)
+def gather_panels(own, factor, jacobian, right_side, axis):
     factor_line = line_of(factor, axis)
     own_round = around(own, axis)
     near, far = joined(*factor_line[1:-1]), factor_line[-1]
@@ -92,6 +93,26 @@
     right_side, _ = after((right_side, None), *far_parts)
     arrived = [own, *factor_line[1:], *jacobian_line[1:], *own_round, *second_round, *third_round, *factor_across]
     return arrived + [*near_round, *far_round], list(far_across), right_side
+
+
+def pack(diag_inv, lower, jacobian):
+    supers, rows, size = diag_inv.shape
+
+    def kernel(diag_ref, lower_ref, jacobian_ref, factor_ref, blocks_ref, own_ref):
+        for s in range(supers):
+            factor_ref[s] = own_ref[s] = diag_ref[s]
+            factor_ref[supers + s] = own_ref[supers + s] = lower_ref[s]
+            for c in range(3):
+                block = jacobian_ref[s, :, c * size : (c + 1) * size]
+                blocks_ref[3 * s + c] = own_ref[2 * supers + 3 * s + c] = block
+
+    return pl.pallas_call(
+        kernel,
+        out_shape=shapes([(count * supers, rows, size) for count in (2, 3, 5)]),
+        in_specs=[VMEM] * 3,
+        out_specs=[VMEM] * 3,
+        name="pack",
+    )(diag_inv, lower, jacobian)
 
 
 def gather_whole(own, axis):
@@ -337,14 +358,14 @@
     def blocks_of(array, begin):
         return array, [(0, begin + block) for block in range(array.shape[0])]
 
-    factor_own = blocks_of(jnp.concatenate([diag_inv, lower]), 0)
-    shaped = jacobian.reshape(supers, rows, 3, size).swapaxes(1, 2).reshape(3 * supers, rows, size)
-    jacobian_own = blocks_of(shaped, 2 * supers)
-    own = joined(factor_own, jacobian_own)
+    factor_own, jacobian_own, own = pack(diag_inv, lower, jacobian)
+    factor_own = blocks_of(factor_own, 0)
+    jacobian_own = blocks_of(jacobian_own, 2 * supers)
+    own = blocks_of(own, 0)
     count = lax.axis_size("rhs")
     relative = count >= 16 and not count & (count - 1)
     if relative:
-        arrived, last, late = gather_panels(factor_own, jacobian_own, right_side, "rhs")
+        arrived, last, late = gather_panels(own, factor_own, jacobian_own, right_side, "rhs")
     else:
         arrived, last, late = gather_whole(own, "rhs"), [], right_side
     factor = places_of(arrived, 0, 2 * supers)

time: 63.8 us -> 63.9 us (level)
  local copies, waits for them, and re-layouts: 2.6 us -> 0.84 us
  Pallas kernels: 13.6 us -> 15.1 us
    pallas_call x0 -> x1, Pallas kernels: none -> 1.86 us  [pack(): pl.pallas_call(kernel, out_shape=shapes([(count * supers, rows, size) for...]
    slice x1 -> x0, local copies, waits for them, and re-layouts: 0.92 us -> none
    unnamed x15 -> x14, local copies, waits for them, and re-layouts: 1.59 us -> 0.75 us
  transfers between devices with their start and end apart: 21 -> 21, of which waited for: 11 -> 11; matrix products, arithmetic and copies ran while one was open for 0% -> 0% of each run, Pallas kernels for 18% -> 17%
where the time goes in v12:
time: 63.9 us; the launch traced here: 63.8 us
  starting transfers between devices  27.3 us (43%)
  waiting for transfers between devices  19.5 us (31%)
  Pallas kernels  15.1 us (24%)
  local copies, waits for them, and re-layouts  0.84 us (1%)
  between operations  0.8 us (1%)
    ppermute x19, starting transfers between devices, sent(): lax.ppermute(array, axis, [(i, i ^ mask) for i in range(lax.axis_size(axi...  26.7 us
    ppermute x19, waiting for transfers between devices, sent(): lax.ppermute(array, axis, [(i, i ^ mask) for i in range(lax.axis_size(axi...  19.5 us
    pallas_call x1, Pallas kernels, solve(): pl.pallas_call(kernel, out_shape=shapes([(span, columns)] + [(span, size)...  5.78 us
    pallas_call x2, Pallas kernels, subtract_product(): pl.pallas_call(kernel, out_shape=shapes([(span, columns)])[0], in_specs=[...  5.51 us
    pallas_call x1, Pallas kernels, finish(): pl.pallas_call(kernel, out_shape=shapes([(span, columns)]) + [windows, wi...  1.96 us
    pallas_call x1, Pallas kernels, pack(): pl.pallas_call(kernel, out_shape=shapes([(count * supers, rows, size) for...  1.86 us
  transfers between devices with their start and end apart: 21, of which 11 were waited for; matrix products, arithmetic and copies ran while one was open for 0% of the time, Pallas kernels for 17%

profile of v12, /device:TPU:0, one launch (start us, length us, event | category | flops | bytes accessed | tf_op | source)
XLA Modules:
  0.0 63.8 jit_solution(8511462040599779302)
XLA Ops:
  0.6 1.9 %pack.1 = (f32[8,16,256]{2,1,0:T(8,128)}, f32[12,16,256]{2,1,0:T(8,128)}, f32[20,16,256]{2,1,0:T(8,128)}) custom-call(f32[4,16,256]{2,1,0:T(8,128)} %diag_ref.1, f32[4,16,256]{2,1,0:T(8,128)} %lower_ref.1, f32[4,16,768]{2,1,0:T(8,128)} %jacobian_ref.1), custom_call_target="tpu_custom_call" | custom-call | tf_op jit(solution)/shard_map/pack/pallas_call | solution.py:109
  2.5 3.0 %collective-permute-start.2 = (f32[20,16,256]{2,1,0:T(8,128)}, f32[20,16,256]{2,1,0:T(8,128)S(1)}, u32[]{:S(2)}, u32[]{:S(2)}) collective-permute-start(f32[20,16,256]{2,1,0:T(8,128)} %get-tuple-element.18.refs_2_.refs_4_), channel_id=1, source_target_pairs={{0,4},{2,6},{4,0},{6,2},{8,12},{10,14},{12,8},{14,10},{16,20},{18,... | collective-permute-start | bytes 983048 | tf_op jit(solution)/shard_map/ppermute | solution.py:45
  5.5 1.5 %collective-permute-start.3 = (f32[20,16,256]{2,1,0:T(8,128)}, f32[20,16,256]{2,1,0:T(8,128)S(1)}, u32[]{:S(2)}, u32[]{:S(2)}) collective-permute-start(f32[20,16,256]{2,1,0:T(8,128)} %get-tuple-element.18.refs_2_.refs_4_), channel_id=1, source_target_pairs={{0,2},{2,0},{4,6},{6,4},{8,10},{10,8},{12,14},{14,12},{16,18},{18,... | collective-permute-start | bytes 983048 | tf_op jit(solution)/shard_map/ppermute | solution.py:45
  6.9 3.6 %collective-permute-start = (f32[8,16,256]{2,1,0:T(8,128)}, f32[8,16,256]{2,1,0:T(8,128)S(1)}, u32[]{:S(2)}, u32[]{:S(2)}) collective-permute-start(f32[8,16,256]{2,1,0:T(8,128)} %get-tuple-element.17), channel_id=1, source_target_pairs={{0,24},{2,26},{4,28},{6,30},{8,16},{10,18},{12,20},{14,22},{16,8},... | collective-permute-start | bytes 393224 | tf_op jit(solution)/shard_map/ppermute | solution.py:45
  10.6 2.8 %collective-permute-done.2.refs_7_.refs_8_ = f32[20,16,256]{2,1,0:T(8,128)S(1)} collective-permute-done((f32[20,16,256]{2,1,0:T(8,128)}, f32[20,16,256]{2,1,0:T(8,128)S(1)}, u32[]{:S(2)}, u32[]{:S(2)}) %collective-permute-start.2) | collective-permute-done | bytes 327712 | tf_op jit(solution)/shard_map/ppermute | solution.py:45
  14.1 0.7 %collective-permute-done.3.refs_6_.refs_7_ = f32[20,16,256]{2,1,0:T(8,128)S(1)} collective-permute-done((f32[20,16,256]{2,1,0:T(8,128)}, f32[20,16,256]{2,1,0:T(8,128)S(1)}, u32[]{:S(2)}, u32[]{:S(2)}) %collective-permute-start.3) | collective-permute-done | bytes 327712 | tf_op jit(solution)/shard_map/ppermute | solution.py:45
  15.2 1.4 %collective-permute-done.1.refs_4_ = f32[8,16,256]{2,1,0:T(8,128)S(1)} collective-permute-done((f32[8,16,256]{2,1,0:T(8,128)}, f32[8,16,256]{2,1,0:T(8,128)S(1)}, u32[]{:S(2)}, u32[]{:S(2)}) %collective-permute-start.1) | collective-permute-done | bytes 131104 | tf_op jit(solution)/shard_map/ppermute | solution.py:45
  17.4 1.0 %collective-permute-start.10 = (f32[26,16,256]{2,1,0:T(8,128)S(1)}, f32[26,16,256]{2,1,0:T(8,128)S(1)}, u32[]{:S(2)}, u32[]{:S(2)}) collective-permute-start(f32[26,16,256]{2,1,0:T(8,128)S(1)} %get-tuple-element.32), channel_id=1, source_target_pairs={{0,4},{2,6},{4,0},{6,2},{8,12},{10,14},{12,8},{14,10},{16,20},{18,... | collective-permute-start | bytes 1277960 | tf_op jit(solution)/shard_map/ppermute | solution.py:45
  18.4 3.6 %collective-permute-start.4 = (f32[12,16,256]{2,1,0:T(8,128)S(1)}, f32[12,16,256]{2,1,0:T(8,128)S(1)}, u32[]{:S(2)}, u32[]{:S(2)}) collective-permute-start(f32[12,16,256]{2,1,0:T(8,128)S(1)} %copy-done.6), channel_id=1, source_target_pairs={{0,24},{2,26},{4,28},{6,30},{8,16},{10,18},{12,20},{14,22},{16,8},... | collective-permute-start | bytes 589832 | tf_op jit(solution)/shard_map/ppermute | solution.py:45
  22.0 5.0 %collective-permute-done.4.refs_5_ = f32[12,16,256]{2,1,0:T(8,128)S(1)} collective-permute-done((f32[12,16,256]{2,1,0:T(8,128)S(1)}, f32[12,16,256]{2,1,0:T(8,128)S(1)}, u32[]{:S(2)}, u32[]{:S(2)}) %collective-permute-start.4) | collective-permute-done | bytes 196640 | tf_op jit(solution)/shard_map/ppermute | solution.py:45
  27.1 2.4 %collective-permute-start.5 = (f32[24,16,256]{2,1,0:T(8,128)S(1)}, f32[24,16,256]{2,1,0:T(8,128)S(1)}, u32[]{:S(2)}, u32[]{:S(2)}) collective-permute-start(f32[24,16,256]{2,1,0:T(8,128)S(1)} %pad_maximum_fusion.4), channel_id=1, source_target_pairs={{0,8},{2,10},{4,12},{6,14},{8,0},{10,2},{12,4},{14,6},{16,24},{18,... | collective-permute-start | bytes 1179656 | tf_op jit(solution)/shard_map/ppermute | solution.py:45
  29.6 0.8 %collective-permute-start.9 = (f32[16,16,256]{2,1,0:T(8,128)S(1)}, f32[16,16,256]{2,1,0:T(8,128)S(1)}, u32[]{:S(2)}, u32[]{:S(2)}) collective-permute-start(f32[16,16,256]{2,1,0:T(8,128)S(1)} %get-tuple-element.35), channel_id=1, source_target_pairs={{0,4},{2,6},{4,0},{6,2},{8,12},{10,14},{12,8},{14,10},{16,20},{18,... | collective-permute-start | bytes 786440 | tf_op jit(solution)/shard_map/ppermute | solution.py:45
  30.4 1.4 %collective-permute-start.11 = (f32[16,16,256]{2,1,0:T(8,128)S(1)}, f32[16,16,256]{2,1,0:T(8,128)S(1)}, u32[]{:S(2)}, u32[]{:S(2)}) collective-permute-start(f32[16,16,256]{2,1,0:T(8,128)S(1)} %get-tuple-element.34), channel_id=1, source_target_pairs={{0,2},{2,0},{4,6},{6,4},{8,10},{10,8},{12,14},{14,12},{16,18},{18,... | collective-permute-start | bytes 786440 | tf_op jit(solution)/shard_map/ppermute | solution.py:45
  32.2 1.5 %collective-permute-start.12 = (f32[12,16,256]{2,1,0:T(8,128)S(1)}, f32[12,16,256]{2,1,0:T(8,128)S(1)}, u32[]{:S(2)}, u32[]{:S(2)}) collective-permute-start(f32[12,16,256]{2,1,0:T(8,128)S(1)} %collective-permute-done.4.refs_5_), channel_id=1, source_target_pairs={{0,2},{2,0},{4,6},{6,4},{8,10},{10,8},{12,14},{14,12},{16,18},{18,... | collective-permute-start | bytes 589832 | tf_op jit(solution)/shard_map/ppermute | solution.py:45
  33.7 5.2 %collective-permute-done.9.refs_11_ = f32[16,16,256]{2,1,0:T(8,128)S(1)} collective-permute-done((f32[16,16,256]{2,1,0:T(8,128)S(1)}, f32[16,16,256]{2,1,0:T(8,128)S(1)}, u32[]{:S(2)}, u32[]{:S(2)}) %collective-permute-start.9) | collective-permute-done | bytes 262176 | tf_op jit(solution)/shard_map/ppermute | solution.py:45
  39.6 1.5 %collective-permute-start.14 = (f32[4,16,256]{2,1,0:T(8,128)S(1)}, f32[4,16,256]{2,1,0:T(8,128)S(1)}, u32[]{:S(2)}, u32[]{:S(2)}) collective-permute-start(f32[4,16,256]{2,1,0:T(8,128)S(1)} %slice.45), channel_id=1, source_target_pairs={{0,4},{2,6},{4,0},{6,2},{8,12},{10,14},{12,8},{14,10},{16,20},{18,... | collective-permute-start | bytes 196616 | tf_op jit(solution)/shard_map/ppermute | solution.py:45
  42.2 1.7 %collective-permute-start.17 = (f32[30,16,256]{2,1,0:T(8,128)S(1)}, f32[30,16,256]{2,1,0:T(8,128)S(1)}, u32[]{:S(2)}, u32[]{:S(2)}) collective-permute-start(f32[30,16,256]{2,1,0:T(8,128)S(1)} %get-tuple-element.31), channel_id=1, source_target_pairs={{0,2},{2,0},{4,6},{6,4},{8,10},{10,8},{12,14},{14,12},{16,18},{18,... | collective-permute-start | bytes 1474568 | tf_op jit(solution)/shard_map/ppermute | solution.py:45
  44.7 5.8 %solve.1 = (f32[1024,256]{1,0:T(8,128)S(1)}, f32[1024,256]{1,0:T(8,128)S(1)}, f32[2,256,256]{2,1,0:T(8,128)S(1)}, f32[2,256,256]{2,1,0:T(8,128)S(1)}) custom-call(s32[4,4,4]{2,1,0:T(4,128)S(1)} %copy-done.5, f32[1024,256]{1,0:T(8,128)S(1)} %copy-done, f32[20,16,256]{2,1,0:T(8,128)S(1)} %copy-done.3, f32[8,16,256]{2,1,0:T(8,128)S(1)} %collective-permute-done.refs_3_, ...), custom_call_target="tpu_custom_call" | custom-call | flops 2147483648 | bytes 262144 | tf_op jit(solution)/shard_map/solve/pallas_call | solution.py:227
  51.0 2.1 %collective-permute-done.18.refs_14_ = f32[30,16,256]{2,1,0:T(8,128)S(1)} collective-permute-done((f32[30,16,256]{2,1,0:T(8,128)S(1)}, f32[30,16,256]{2,1,0:T(8,128)S(1)}, u32[]{:S(2)}, u32[]{:S(2)}) %collective-permute-start.18) | collective-permute-done | bytes 491552 | tf_op jit(solution)/shard_map/ppermute | solution.py:45
  53.1 1.6 %collective-permute-start.19 = (f32[12,16,256]{2,1,0:T(8,128)S(1)}, f32[12,16,256]{2,1,0:T(8,128)S(1)}, u32[]{:S(2)}, u32[]{:S(2)}) collective-permute-start(f32[12,16,256]{2,1,0:T(8,128)S(1)} %slice.46), channel_id=1, source_target_pairs={{0,2},{2,0},{4,6},{6,4},{8,10},{10,8},{12,14},{14,12},{16,18},{18,... | collective-permute-start | bytes 589832 | tf_op jit(solution)/shard_map/ppermute | solution.py:45
  54.8 1.5 %collective-permute-start.20 = (f32[12,16,256]{2,1,0:T(8,128)S(1)}, f32[12,16,256]{2,1,0:T(8,128)S(1)}, u32[]{:S(2)}, u32[]{:S(2)}) collective-permute-start(f32[12,16,256]{2,1,0:T(8,128)S(1)} %slice.47), channel_id=1, source_target_pairs={{0,4},{2,6},{4,0},{6,2},{8,12},{10,14},{12,8},{14,10},{16,20},{18,... | collective-permute-start | bytes 589832 | tf_op jit(solution)/shard_map/ppermute | solution.py:45
  56.3 2.0 %finish.1 = (f32[1024,256]{1,0:T(8,128)}, bf16[1536,256]{1,0:T(8,128)(2,1)S(1)}, bf16[1536,256]{1,0:T(8,128)(2,1)S(1)}) custom-call(f32[1024,256]{1,0:T(8,128)S(1)} %get-tuple-element.23.sol_ref, f32[1024,256]{1,0:T(8,128)S(1)} %get-tuple-element.24.part_ref, f32[2,256,256]{2,1,0:T(8,128)S(1)} %get-tuple-element.25.own_ref, ...), custom_call_target="tpu_custom_call" | custom-call | flops 100663296 | bytes 262144 | tf_op jit(solution)/shard_map/finish/pallas_call | solution.py:270
  58.3 3.2 %residual.1.refs_4_ = f32[1024,256]{1,0:T(8,128)} custom-call(s32[4,4,12]{2,1,0:T(4,128)S(1)} %copy-done.4, f32[1024,256]{1,0:T(8,128)S(1)} %copy-done, bf16[1536,256]{1,0:T(8,128)(2,1)S(1)} %get-tuple-element.28.refs_2_, bf16[1536,256]{1,0:T(8,128)(2,1)S(1)} %get-tuple-element.29.refs_3_, f32[20,16,256]{2,1,0:T(8,128)S(1)} %copy-done.3, ...), custom_call_target="tpu_custom_call" | custom-call | flops 1056964608 | bytes 5505024 | tf_op jit(solution)/shard_map/residual/pallas_call | solution.py:333
  61.5 2.3 %residual_rest.1 = f32[1024,256]{1,0:T(8,128)} custom-call(s32[4,4,12]{2,1,0:T(4,128)S(1)} %copy-done.4, f32[1024,256]{1,0:T(8,128)S(1)} %copy-done, bf16[1536,256]{1,0:T(8,128)(2,1)S(1)} %get-tuple-element.28.refs_2_, bf16[1536,256]{1,0:T(8,128)(2,1)S(1)} %get-tuple-element.29.refs_3_, ...), custom_call_target="tpu_custom_call", output_to_operand_aliasing={{}: (4, {})} | custom-call | flops 150994944 | bytes 786432 | tf_op jit(solution)/shard_map/residual_rest/pallas_call | solution.py:333
  (52 shorter events, 5.4 us)
Async XLA Ops:
  2.5 10.9 %collective-permute-start.2 = (f32[20,16,256]{2,1,0:T(8,128)}, f32[20,16,256]{2,1,0:T(8,128)S(1)}, u32[]{:S(2)}, u32[]{:S(2)}) collective-permute-start(f32[20,16,256]{2,1,0:T(8,128)} %get-tuple-element.18.refs_2_.refs_4_), channel_id=1, source_target_pairs={{0,4},{2,6},{4,0},{6,2},{8,12},{10,14},{12,8},{14,10},{16,20},{18,... | collective-permute-start | bytes 983048 | tf_op jit(solution)/shard_map/ppermute | solution.py:45
  5.5 9.4 %collective-permute-start.3 = (f32[20,16,256]{2,1,0:T(8,128)}, f32[20,16,256]{2,1,0:T(8,128)S(1)}, u32[]{:S(2)}, u32[]{:S(2)}) collective-permute-start(f32[20,16,256]{2,1,0:T(8,128)} %get-tuple-element.18.refs_2_.refs_4_), channel_id=1, source_target_pairs={{0,2},{2,0},{4,6},{6,4},{8,10},{10,8},{12,14},{14,12},{16,18},{18,... | collective-permute-start | bytes 983048 | tf_op jit(solution)/shard_map/ppermute | solution.py:45
  6.9 8.2 %collective-permute-start = (f32[8,16,256]{2,1,0:T(8,128)}, f32[8,16,256]{2,1,0:T(8,128)S(1)}, u32[]{:S(2)}, u32[]{:S(2)}) collective-permute-start(f32[8,16,256]{2,1,0:T(8,128)} %get-tuple-element.17), channel_id=1, source_target_pairs={{0,24},{2,26},{4,28},{6,30},{8,16},{10,18},{12,20},{14,22},{16,8},... | collective-permute-start | bytes 393224 | tf_op jit(solution)/shard_map/ppermute | solution.py:45
  10.5 6.1 %collective-permute-start.1 = (f32[8,16,256]{2,1,0:T(8,128)}, f32[8,16,256]{2,1,0:T(8,128)S(1)}, u32[]{:S(2)}, u32[]{:S(2)}) collective-permute-start(f32[8,16,256]{2,1,0:T(8,128)} %get-tuple-element.17), channel_id=1, source_target_pairs={{0,8},{2,10},{4,12},{6,14},{8,0},{10,2},{12,4},{14,6},{16,24},{18,... | collective-permute-start | bytes 393224 | tf_op jit(solution)/shard_map/ppermute | solution.py:45
  14.9 3.6 %copy-start.6 = (f32[12,16,256]{2,1,0:T(8,128)S(1)}, f32[12,16,256]{2,1,0:T(8,128)}, u32[]{:S(2)}) copy-start(f32[12,16,256]{2,1,0:T(8,128)} %get-tuple-element.19) | copy-start | bytes 589828
  16.7 12.8 %collective-permute-start.8 = (f32[26,16,256]{2,1,0:T(8,128)S(1)}, f32[26,16,256]{2,1,0:T(8,128)S(1)}, u32[]{:S(2)}, u32[]{:S(2)}) collective-permute-start(f32[26,16,256]{2,1,0:T(8,128)S(1)} %get-tuple-element.33), channel_id=1, source_target_pairs={{0,2},{2,0},{4,6},{6,4},{8,10},{10,8},{12,14},{14,12},{16,18},{18,... | collective-permute-start | bytes 1277960 | tf_op jit(solution)/shard_map/ppermute | solution.py:45
  17.4 12.1 %collective-permute-start.10 = (f32[26,16,256]{2,1,0:T(8,128)S(1)}, f32[26,16,256]{2,1,0:T(8,128)S(1)}, u32[]{:S(2)}, u32[]{:S(2)}) collective-permute-start(f32[26,16,256]{2,1,0:T(8,128)S(1)} %get-tuple-element.32), channel_id=1, source_target_pairs={{0,4},{2,6},{4,0},{6,2},{8,12},{10,14},{12,8},{14,10},{16,20},{18,... | collective-permute-start | bytes 1277960 | tf_op jit(solution)/shard_map/ppermute | solution.py:45
  18.4 8.6 %collective-permute-start.4 = (f32[12,16,256]{2,1,0:T(8,128)S(1)}, f32[12,16,256]{2,1,0:T(8,128)S(1)}, u32[]{:S(2)}, u32[]{:S(2)}) collective-permute-start(f32[12,16,256]{2,1,0:T(8,128)S(1)} %copy-done.6), channel_id=1, source_target_pairs={{0,24},{2,26},{4,28},{6,30},{8,16},{10,18},{12,20},{14,22},{16,8},... | collective-permute-start | bytes 589832 | tf_op jit(solution)/shard_map/ppermute | solution.py:45
  22.0 7.5 %collective-permute-start.7 = (f32[8,16,256]{2,1,0:T(8,128)S(1)}, f32[8,16,256]{2,1,0:T(8,128)S(1)}, u32[]{:S(2)}, u32[]{:S(2)}) collective-permute-start(f32[8,16,256]{2,1,0:T(8,128)S(1)} %collective-permute-done.refs_3_), channel_id=1, source_target_pairs={{0,8},{2,10},{4,12},{6,14},{8,0},{10,2},{12,4},{14,6},{16,24},{18,... | collective-permute-start | bytes 393224 | tf_op jit(solution)/shard_map/ppermute | solution.py:45
  27.1 15.0 %collective-permute-start.5 = (f32[24,16,256]{2,1,0:T(8,128)S(1)}, f32[24,16,256]{2,1,0:T(8,128)S(1)}, u32[]{:S(2)}, u32[]{:S(2)}) collective-permute-start(f32[24,16,256]{2,1,0:T(8,128)S(1)} %pad_maximum_fusion.4), channel_id=1, source_target_pairs={{0,8},{2,10},{4,12},{6,14},{8,0},{10,2},{12,4},{14,6},{16,24},{18,... | collective-permute-start | bytes 1179656 | tf_op jit(solution)/shard_map/ppermute | solution.py:45
  29.6 9.3 %collective-permute-start.9 = (f32[16,16,256]{2,1,0:T(8,128)S(1)}, f32[16,16,256]{2,1,0:T(8,128)S(1)}, u32[]{:S(2)}, u32[]{:S(2)}) collective-permute-start(f32[16,16,256]{2,1,0:T(8,128)S(1)} %get-tuple-element.35), channel_id=1, source_target_pairs={{0,4},{2,6},{4,0},{6,2},{8,12},{10,14},{12,8},{14,10},{16,20},{18,... | collective-permute-start | bytes 786440 | tf_op jit(solution)/shard_map/ppermute | solution.py:45
  30.4 9.2 %collective-permute-start.11 = (f32[16,16,256]{2,1,0:T(8,128)S(1)}, f32[16,16,256]{2,1,0:T(8,128)S(1)}, u32[]{:S(2)}, u32[]{:S(2)}) collective-permute-start(f32[16,16,256]{2,1,0:T(8,128)S(1)} %get-tuple-element.34), channel_id=1, source_target_pairs={{0,2},{2,0},{4,6},{6,4},{8,10},{10,8},{12,14},{14,12},{16,18},{18,... | collective-permute-start | bytes 786440 | tf_op jit(solution)/shard_map/ppermute | solution.py:45
  31.8 9.8 %collective-permute-start.6 = (f32[12,16,256]{2,1,0:T(8,128)S(1)}, f32[12,16,256]{2,1,0:T(8,128)S(1)}, u32[]{:S(2)}, u32[]{:S(2)}) collective-permute-start(f32[12,16,256]{2,1,0:T(8,128)S(1)} %collective-permute-done.4.refs_5_), channel_id=1, source_target_pairs={{0,4},{2,6},{4,0},{6,2},{8,12},{10,14},{12,8},{14,10},{16,20},{18,... | collective-permute-start | bytes 589832 | tf_op jit(solution)/shard_map/ppermute | solution.py:45
  32.2 9.7 %collective-permute-start.12 = (f32[12,16,256]{2,1,0:T(8,128)S(1)}, f32[12,16,256]{2,1,0:T(8,128)S(1)}, u32[]{:S(2)}, u32[]{:S(2)}) collective-permute-start(f32[12,16,256]{2,1,0:T(8,128)S(1)} %collective-permute-done.4.refs_5_), channel_id=1, source_target_pairs={{0,2},{2,0},{4,6},{6,4},{8,10},{10,8},{12,14},{14,12},{16,18},{18,... | collective-permute-start | bytes 589832 | tf_op jit(solution)/shard_map/ppermute | solution.py:45
  38.9 5.7 %copy-start = (f32[1024,256]{1,0:T(8,128)S(1)}, f32[1024,256]{1,0:T(8,128)}, u32[]{:S(2)}) copy-start(f32[1024,256]{1,0:T(8,128)} %refs_1_.4) | copy-start | bytes 3145732
  38.9 5.1 %collective-permute-start.13 = (f32[4,16,256]{2,1,0:T(8,128)S(1)}, f32[4,16,256]{2,1,0:T(8,128)S(1)}, u32[]{:S(2)}, u32[]{:S(2)}) collective-permute-start(f32[4,16,256]{2,1,0:T(8,128)S(1)} %slice.43), channel_id=1, source_target_pairs={{0,2},{2,0},{4,6},{6,4},{8,10},{10,8},{12,14},{14,12},{16,18},{18,... | collective-permute-start | bytes 196616 | tf_op jit(solution)/shard_map/ppermute | solution.py:45
  39.6 5.0 %collective-permute-start.14 = (f32[4,16,256]{2,1,0:T(8,128)S(1)}, f32[4,16,256]{2,1,0:T(8,128)S(1)}, u32[]{:S(2)}, u32[]{:S(2)}) collective-permute-start(f32[4,16,256]{2,1,0:T(8,128)S(1)} %slice.45), channel_id=1, source_target_pairs={{0,4},{2,6},{4,0},{6,2},{8,12},{10,14},{12,8},{14,10},{16,20},{18,... | collective-permute-start | bytes 196616 | tf_op jit(solution)/shard_map/ppermute | solution.py:45
  42.0 2.6 %copy-start.2 = (f32[20,16,256]{2,1,0:T(8,128)S(1)}, f32[20,16,256]{2,1,0:T(8,128)}, u32[]{:S(2)}) copy-start(f32[20,16,256]{2,1,0:T(8,128)} %copy-done.1) | copy-start | bytes 983044
  42.2 12.6 %collective-permute-start.17 = (f32[30,16,256]{2,1,0:T(8,128)S(1)}, f32[30,16,256]{2,1,0:T(8,128)S(1)}, u32[]{:S(2)}, u32[]{:S(2)}) collective-permute-start(f32[30,16,256]{2,1,0:T(8,128)S(1)} %get-tuple-element.31), channel_id=1, source_target_pairs={{0,2},{2,0},{4,6},{6,4},{8,10},{10,8},{12,14},{14,12},{16,18},{18,... | collective-permute-start | bytes 1474568 | tf_op jit(solution)/shard_map/ppermute | solution.py:45
  43.9 9.2 %collective-permute-start.18 = (f32[30,16,256]{2,1,0:T(8,128)S(1)}, f32[30,16,256]{2,1,0:T(8,128)S(1)}, u32[]{:S(2)}, u32[]{:S(2)}) collective-permute-start(f32[30,16,256]{2,1,0:T(8,128)S(1)} %get-tuple-element.30), channel_id=1, source_target_pairs={{0,4},{2,6},{4,0},{6,2},{8,12},{10,14},{12,8},{14,10},{16,20},{18,... | collective-permute-start | bytes 1474568 | tf_op jit(solution)/shard_map/ppermute | solution.py:45
  50.4 5.8 %collective-permute-start.15 = (f32[2,256,256]{2,1,0:T(8,128)S(1)}, f32[2,256,256]{2,1,0:T(8,128)S(1)}, u32[]{:S(2)}, u32[]{:S(2)}) collective-permute-start(f32[2,256,256]{2,1,0:T(8,128)S(1)} %get-tuple-element.25.own_ref), channel_id=1, source_target_pairs={{0,1},{1,0},{2,3},{3,2},{4,5},{5,4},{6,7},{7,6},{8,9},{9,8},{10,11... | collective-permute-start | bytes 1572872 | tf_op jit(solution)/shard_map/ppermute | solution.py:378
  50.5 5.8 %collective-permute-start.16 = (f32[2,256,256]{2,1,0:T(8,128)S(1)}, f32[2,256,256]{2,1,0:T(8,128)S(1)}, u32[]{:S(2)}, u32[]{:S(2)}) collective-permute-start(f32[2,256,256]{2,1,0:T(8,128)S(1)} %get-tuple-element.26), channel_id=1, source_target_pairs={{0,1},{1,0},{2,3},{3,2},{4,5},{5,4},{6,7},{7,6},{8,9},{9,8},{10,11... | collective-permute-start | bytes 1572872 | tf_op jit(solution)/shard_map/ppermute | solution.py:378
  53.1 8.4 %collective-permute-start.19 = (f32[12,16,256]{2,1,0:T(8,128)S(1)}, f32[12,16,256]{2,1,0:T(8,128)S(1)}, u32[]{:S(2)}, u32[]{:S(2)}) collective-permute-start(f32[12,16,256]{2,1,0:T(8,128)S(1)} %slice.46), channel_id=1, source_target_pairs={{0,2},{2,0},{4,6},{6,4},{8,10},{10,8},{12,14},{14,12},{16,18},{18,... | collective-permute-start | bytes 589832 | tf_op jit(solution)/shard_map/ppermute | solution.py:45
  54.8 6.7 %collective-permute-start.20 = (f32[12,16,256]{2,1,0:T(8,128)S(1)}, f32[12,16,256]{2,1,0:T(8,128)S(1)}, u32[]{:S(2)}, u32[]{:S(2)}) collective-permute-start(f32[12,16,256]{2,1,0:T(8,128)S(1)} %slice.47), channel_id=1, source_target_pairs={{0,4},{2,6},{4,0},{6,2},{8,12},{10,14},{12,8},{14,10},{16,20},{18,... | collective-permute-start | bytes 589832 | tf_op jit(solution)/shard_map/ppermute | solution.py:45
  (5 other events, 9.7 us)

commit v13 on v12

--- a/solution.py
+++ b/solution.py
@@ -11,6 +11,7 @@
 SMEM = pl.BlockSpec(memory_space=pltpu.SMEM)
 ANY = pl.BlockSpec(memory_space=pl.ANY)
 VMEM_LIMIT = 20 * 2**20
+SMALL_LIMIT = 4 * 2**20
 
 
 def split(value):
@@ -111,6 +112,7 @@
         out_shape=shapes([(count * supers, rows, size) for count in (2, 3, 5)]),
         in_specs=[VMEM] * 3,
         out_specs=[VMEM] * 3,
+        compiler_params=pltpu.CompilerParams(vmem_limit_bytes=SMALL_LIMIT),
         name="pack",
     )(diag_inv, lower, jacobian)
 
@@ -140,21 +142,39 @@
     return [jax.ShapeDtypeStruct(shape, jnp.float32) for shape in arrays]
 
 
-def weights_of(pattern_ref, s, a, wide):
-    count = pattern_ref.shape[2]
+def widened(pattern, wide):
+    supers, bands, count = pattern.shape
     step = wide // count
     together = max(1, 128 // step)
-    lane = lax.broadcasted_iota(jnp.int32, (1, together * step), 1)
-    weights = []
-    for first in range(0, count, together):
-        weight = jnp.full(lane.shape, pattern_ref[s, a, first].astype(jnp.float32))
-        for c in range(1, min(together, count - first)):
-            weight = jnp.where(lane >= c * step, pattern_ref[s, a, first + c].astype(jnp.float32), weight)
-        weights.append(weight)
-    return jnp.concatenate(weights, axis=1)[:, :wide]
-
-
-def solve(arrays, places, relative, right_side, pattern, nodes, supers, size):
+
+    def kernel(pattern_ref, out_ref):
+        lane = lax.broadcasted_iota(jnp.int32, (1, together * step), 1)
+        for s in range(supers):
+            for a in range(bands):
+                for first in range(0, count, together):
+                    weight = jnp.full(lane.shape, pattern_ref[s, a, first].astype(jnp.float32))
+                    for c in range(1, min(together, count - first)):
+                        weight = jnp.where(lane >= c * step, pattern_ref[s, a, first + c].astype(jnp.float32), weight)
+                    end = min(first + together, count) * step
+                    row = s * bands + a
+                    out_ref[row : row + 1, first * step : end] = weight[:, : end - first * step]
+
+    return pl.pallas_call(
+        kernel,
+        out_shape=shapes([(supers * bands, wide)])[0],
+        in_specs=[SMEM],
+        out_specs=VMEM,
+        compiler_params=pltpu.CompilerParams(vmem_limit_bytes=SMALL_LIMIT),
+        name="widened",
+    )(pattern)
+
+
+def weights_of(weights_ref, s, row, supers, size):
+    bands = weights_ref.shape[0] // supers
+    return weights_ref[pl.ds(s * bands + row // (size // bands), 1), :]
+
+
+def solve(arrays, places, relative, right_side, weights, nodes, supers, size):
     columns = right_side.shape[1]
     extra = 0 if nodes == 1 else 1 if nodes == 2 else 2
     width = columns + extra * size
@@ -162,7 +182,7 @@
     rows = arrays[0].shape[1]
 
     def kernel(*refs):
-        pattern_ref, rhs_ref = refs[:2]
+        weights_ref, rhs_ref = refs[:2]
         piece_refs = refs[2 : 2 + n]
         sol_ref = refs[2 + n]
         extra_refs = refs[3 + n : 3 + n + extra]
@@ -172,8 +192,7 @@
             for block, (i, at) in blocks.items():
                 band = piece_refs[i][at]
                 if block >= supers:
-                    a = row // (size // pattern_ref.shape[1])
-                    band = band * weights_of(pattern_ref, block - supers, a, size)
+                    band = band * weights_of(weights_ref, block - supers, row, supers, size)
                 panels[block, pl.ds(row, rows), :] = band
         index = lax.axis_index("node")
         below = jnp.where(index > 0, 1.0, 0.0)
@@ -227,7 +246,7 @@
     out = pl.pallas_call(
         kernel,
         out_shape=shapes([(span, columns)] + [(span, size)] * extra + [leaving] * 2),
-        in_specs=[SMEM, VMEM] + [VMEM] * n,
+        in_specs=[VMEM] * (2 + n),
         out_specs=[VMEM] * (3 + extra),
         scratch_shapes=[
             pltpu.VMEM((2 * supers, size, size), jnp.float32),
@@ -238,7 +257,7 @@
             flops=16 * supers * size * size * width, bytes_accessed=span * size, transcendentals=0
         ),
         name="solve",
-    )(pattern, right_side, *arrays)
+    )(weights, right_side, *arrays)
     return out[0], out[1 : 1 + extra], out[1 + extra], out[2 + extra]
 
 
@@ -246,7 +265,7 @@
     span, columns = sol.shape
     size = span // supers
 
-    def kernel(sol_ref, part_ref, own_ref, mail_ref, beside_ref, out_ref, high_ref, low_ref):
+    def kernel(sol_ref, part_ref, own_ref, mail_ref, beside_ref, out_ref, high_ref, low_ref, held, sem):
         lower_one = lax.axis_index("node") == 0
         down = jnp.where(lower_one, own_ref[0], mail_ref[0])
         offset = jnp.where(lower_one, mail_ref[0], own_ref[0])
@@ -258,20 +277,28 @@
         def window(at, value):
             high_ref[at : at + size, :], low_ref[at : at + size, :] = split(value)
 
+        copies = []
         for at in range(0, span, size):
             value = sol_ref[at : at + size, :] + product(split(part_ref[at : at + size, :]), mine)
-            out_ref[at : at + size, :] = value
+            held[at : at + size, :] = value
+            copies.append(
+                pltpu.make_async_copy(held.at[at : at + size, :], out_ref.at[at : at + size, :], sem.at[at // size])
+            )
+            copies[-1].start()
             window(at + size, value)
         beside = beside_ref[0] + product(split(beside_ref[1]), other)
         window(0, jnp.where(lower_one, 0.0, beside))
         window(size + span, jnp.where(lower_one, beside, 0.0))
+        for copy in copies:
+            copy.wait()
 
     windows = jax.ShapeDtypeStruct((span + 2 * size, columns), jnp.bfloat16)
     return pl.pallas_call(
         kernel,
         out_shape=shapes([(span, columns)]) + [windows, windows],
         in_specs=[VMEM] * 5,
-        out_specs=[VMEM] * 3,
+        out_specs=[ANY, VMEM, VMEM],
+        scratch_shapes=[pltpu.VMEM((span, columns), jnp.float32), pltpu.SemaphoreType.DMA((supers,))],
         compiler_params=pltpu.CompilerParams(vmem_limit_bytes=VMEM_LIMIT),
         cost_estimate=pl.CostEstimate(
             flops=(span + 2 * size) * size * columns, bytes_accessed=span * columns, transcendentals=0
@@ -293,7 +320,7 @@
     return pl.pallas_call(kernel, out_shape=[windows, windows], name="windows")(sol, before, after)
 
 
-def subtract_product(arrays, places, relative, right_side, high, low, pattern, supers, size, base=None):
+def subtract_product(arrays, places, relative, right_side, high, low, weights, supers, size, base=None):
     span, columns = right_side.shape
     wide = 3 * size
     n = len(arrays)
@@ -301,48 +328,52 @@
     extra = 0 if base is None else 1
 
     def kernel(*refs):
-        pattern_ref, rhs_ref, high_ref, low_ref = refs[:4]
+        weights_ref, rhs_ref, high_ref, low_ref = refs[:4]
         piece_refs = refs[4 + extra : 4 + extra + n]
-        out_ref = refs[4 + extra + n]
+        out_ref, held, sem = refs[4 + extra + n :]
         copies = []
+
+        def write(source, target):
+            copies.append(pltpu.make_async_copy(source, target, sem.at[len(copies)]))
+            copies[-1].start()
+
         for s in range(supers):
             bands, starts = [], []
             for owner, blocks in places.items():
                 row = row_of(owner, rows, relative)
                 band = [piece_refs[i][at] for i, at in (blocks[3 * s + c] for c in range(3))]
-                a = row // (size // pattern_ref.shape[1])
-                bands.append(jnp.concatenate(band, axis=1) * weights_of(pattern_ref, s, a, wide))
+                bands.append(jnp.concatenate(band, axis=1) * weights_of(weights_ref, s, row, supers, size))
                 starts.append(s * size + row if not relative else pl.multiple_of(s * size + row, rows))
             window = pl.ds(s * size, wide)
             result = product(split(jnp.concatenate(bands, axis=0)), (high_ref[window, :], low_ref[window, :]))
             for i, start in enumerate(starts):
-                value = rhs_ref[pl.ds(start, rows), :] - result[i * rows : (i + 1) * rows]
-                if base is None:
-                    out_ref[pl.ds(start, rows), :] = value
-                else:
-                    held, sem = refs[5 + extra + n :]
-                    at = len(copies)
-                    held[at] = value
-                    copies.append(pltpu.make_async_copy(held.at[at], out_ref.at[pl.ds(start, rows), :], sem.at[at]))
-                    copies[-1].start()
+                at = (s * len(places) + i) * rows if extra else start
+                held[pl.ds(at, rows), :] = rhs_ref[pl.ds(start, rows), :] - result[i * rows : (i + 1) * rows]
+                if extra:
+                    write(held.at[pl.ds(at, rows), :], out_ref.at[pl.ds(start, rows), :])
+            if not extra:
+                whole = pl.ds(s * size, size)
+                write(held.at[whole, :], out_ref.at[whole, :])
         for copy in copies:
             copy.wait()
 
     bands = supers * len(places)
-    scratch = [pltpu.VMEM((bands, rows, columns), jnp.float32), pltpu.SemaphoreType.DMA((bands,))]
     return pl.pallas_call(
         kernel,
         out_shape=shapes([(span, columns)])[0],
-        in_specs=[SMEM] + [VMEM] * 3 + [ANY] * extra + [VMEM] * n,
-        out_specs=ANY if extra else VMEM,
+        in_specs=[VMEM] * 4 + [ANY] * extra + [VMEM] * n,
+        out_specs=ANY,
         input_output_aliases={4: 0} if extra else {},
-        scratch_shapes=scratch if extra else [],
+        scratch_shapes=[
+            pltpu.VMEM((bands * rows if extra else span, columns), jnp.float32),
+            pltpu.SemaphoreType.DMA((bands if extra else supers,)),
+        ],
         compiler_params=pltpu.CompilerParams(vmem_limit_bytes=VMEM_LIMIT),
         cost_estimate=pl.CostEstimate(
             flops=6 * bands * rows * wide * columns, bytes_accessed=8 * bands * rows * wide, transcendentals=0
         ),
         name="residual_rest" if extra else "residual",
-    )(pattern, right_side, high, low, *([base] if extra else []), *arrays)
+    )(weights, right_side, high, low, *([base] if extra else []), *arrays)
 
 
 def dot(left, right):
@@ -373,7 +404,7 @@
     whole = {owner: blocks for owner, blocks in places.items() if len(blocks) == 3 * supers}
     partial = set(places) - set(whole)
 
-    sol, parts, down, up = solve(*factor, relative, late, factor_pattern, nodes, supers, size)
+    sol, parts, down, up = solve(*factor, relative, late, widened(factor_pattern, size), nodes, supers, size)
     if nodes == 2:
         mail = [lax.ppermute(letter, "node", [(0, 1), (1, 0)]) for letter in (down, up)]
         sol, high, low = finish(sol, parts[0], down, *mail, supers)
@@ -400,7 +431,7 @@
         right_side=right_side,
         high=high,
         low=low,
-        pattern=jacobian_pattern,
+        weights=widened(jacobian_pattern, 3 * size),
         supers=supers,
         size=size,
     )

time: 63.9 us -> 63.6 us (level)
  Pallas kernels: 15.1 us -> 12.1 us
  local copies, waits for them, and re-layouts: 0.84 us -> 3.43 us
    unnamed x14 -> x16, local copies, waits for them, and re-layouts: 0.75 us -> 3.34 us
    pallas_call x1, Pallas kernels: 1.86 us -> 0.04 us  [pack(): pl.pallas_call(kernel, out_shape=shapes([(count * supers, rows, size) for...]
    pallas_call x2, Pallas kernels: 5.51 us -> 3.79 us  [subtract_product(): pl.pallas_call(kernel, out_shape=shapes([(span, columns)])[0], in_specs=[...]
    pallas_call x0 -> x2, Pallas kernels: none -> 1.47 us  [widened(): pl.pallas_call(kernel, out_shape=shapes([(supers * bands, wide)])[0], in_...]
    pallas_call x1, Pallas kernels: 5.78 us -> 4.98 us  [solve(): pl.pallas_call(kernel, out_shape=shapes([(span, columns)] + [(span, size)...]
  transfers between devices with their start and end apart: 21 -> 21, of which waited for: 11 -> 11; matrix products, arithmetic and copies ran while one was open for 0% -> 0% of each run, Pallas kernels for 17% -> 16%
where the time goes in v13:
time: 63.6 us; the launch traced here: 63.3 us
  starting transfers between devices  27.3 us (43%)
  waiting for transfers between devices  19.4 us (31%)
  Pallas kernels  12.1 us (19%)
  local copies, waits for them, and re-layouts  3.43 us (5%)
  between operations  0.85 us (1%)
    ppermute x19, starting transfers between devices, sent(): lax.ppermute(array, axis, [(i, i ^ mask) for i in range(lax.axis_size(axi...  26.7 us
    ppermute x19, waiting for transfers between devices, sent(): lax.ppermute(array, axis, [(i, i ^ mask) for i in range(lax.axis_size(axi...  19.4 us
    pallas_call x1, Pallas kernels, solve(): pl.pallas_call(kernel, out_shape=shapes([(span, columns)] + [(span, size)...  4.98 us
    pallas_call x2, Pallas kernels, subtract_product(): pl.pallas_call(kernel, out_shape=shapes([(span, columns)])[0], in_specs=[...  3.79 us
    unnamed x16, local copies, waits for them, and re-layouts  3.34 us
    pallas_call x1, Pallas kernels, finish(): pl.pallas_call(kernel, out_shape=shapes([(span, columns)]) + [windows, wi...  1.77 us
    pallas_call x2, Pallas kernels, widened(): pl.pallas_call(kernel, out_shape=shapes([(supers * bands, wide)])[0], in_...  1.47 us
  transfers between devices with their start and end apart: 21, of which 11 were waited for; matrix products, arithmetic and copies ran while one was open for 0% of the time, Pallas kernels for 16%

profile of v13, /device:TPU:0, one launch (start us, length us, event | category | flops | bytes accessed | tf_op | source)
XLA Modules:
  0.0 63.3 jit_solution(17000142233362331417)
XLA Ops:
  0.6 0.9 %copy-done.3 = f32[4,16,768]{2,1,0:T(8,128)S(1)} copy-done((f32[4,16,768]{2,1,0:T(8,128)S(1)}, f32[4,16,768]{2,1,0:T(8,128)}, u32[]{:S(2)}) %copy-start.3) | copy-done | bytes 196632
  1.6 0.8 %copy-done.4 = f32[4,16,256]{2,1,0:T(8,128)S(1)} copy-done((f32[4,16,256]{2,1,0:T(8,128)S(1)}, f32[4,16,256]{2,1,0:T(8,128)}, u32[]{:S(2)}) %copy-start.4) | copy-done | bytes 65560
  2.4 0.8 %copy-done.5 = f32[4,16,256]{2,1,0:T(8,128)S(1)} copy-done((f32[4,16,256]{2,1,0:T(8,128)S(1)}, f32[4,16,256]{2,1,0:T(8,128)}, u32[]{:S(2)}) %copy-start.5) | copy-done | bytes 65560
  3.3 3.0 %collective-permute-start.2 = (f32[20,16,256]{2,1,0:T(8,128)S(1)}, f32[20,16,256]{2,1,0:T(8,128)S(1)}, u32[]{:S(2)}, u32[]{:S(2)}) collective-permute-start(f32[20,16,256]{2,1,0:T(8,128)S(1)} %get-tuple-element.18.refs_2_.refs_4_), channel_id=1, source_target_pairs={{0,4},{2,6},{4,0},{6,2},{8,12},{10,14},{12,8},{14,10},{16,20},{18,... | collective-permute-start | bytes 983048 | tf_op jit(solution)/shard_map/ppermute | solution.py:46
  6.3 1.5 %collective-permute-start.3 = (f32[20,16,256]{2,1,0:T(8,128)S(1)}, f32[20,16,256]{2,1,0:T(8,128)S(1)}, u32[]{:S(2)}, u32[]{:S(2)}) collective-permute-start(f32[20,16,256]{2,1,0:T(8,128)S(1)} %get-tuple-element.18.refs_2_.refs_4_), channel_id=1, source_target_pairs={{0,2},{2,0},{4,6},{6,4},{8,10},{10,8},{12,14},{14,12},{16,18},{18,... | collective-permute-start | bytes 983048 | tf_op jit(solution)/shard_map/ppermute | solution.py:46
  7.8 3.6 %collective-permute-start = (f32[8,16,256]{2,1,0:T(8,128)S(1)}, f32[8,16,256]{2,1,0:T(8,128)S(1)}, u32[]{:S(2)}, u32[]{:S(2)}) collective-permute-start(f32[8,16,256]{2,1,0:T(8,128)S(1)} %get-tuple-element.17), channel_id=1, source_target_pairs={{0,24},{2,26},{4,28},{6,30},{8,16},{10,18},{12,20},{14,22},{16,8},... | collective-permute-start | bytes 393224 | tf_op jit(solution)/shard_map/ppermute | solution.py:46
  11.4 2.6 %collective-permute-done.2.refs_7_.refs_8_ = f32[20,16,256]{2,1,0:T(8,128)S(1)} collective-permute-done((f32[20,16,256]{2,1,0:T(8,128)S(1)}, f32[20,16,256]{2,1,0:T(8,128)S(1)}, u32[]{:S(2)}, u32[]{:S(2)}) %collective-permute-start.2) | collective-permute-done | bytes 327712 | tf_op jit(solution)/shard_map/ppermute | solution.py:46
  15.8 1.4 %collective-permute-done.1.refs_4_ = f32[8,16,256]{2,1,0:T(8,128)S(1)} collective-permute-done((f32[8,16,256]{2,1,0:T(8,128)S(1)}, f32[8,16,256]{2,1,0:T(8,128)S(1)}, u32[]{:S(2)}, u32[]{:S(2)}) %collective-permute-start.1) | collective-permute-done | bytes 131104 | tf_op jit(solution)/shard_map/ppermute | solution.py:46
  18.1 1.0 %collective-permute-start.10 = (f32[26,16,256]{2,1,0:T(8,128)S(1)}, f32[26,16,256]{2,1,0:T(8,128)S(1)}, u32[]{:S(2)}, u32[]{:S(2)}) collective-permute-start(f32[26,16,256]{2,1,0:T(8,128)S(1)} %get-tuple-element.32), channel_id=1, source_target_pairs={{0,4},{2,6},{4,0},{6,2},{8,12},{10,14},{12,8},{14,10},{16,20},{18,... | collective-permute-start | bytes 1277960 | tf_op jit(solution)/shard_map/ppermute | solution.py:46
  19.1 3.6 %collective-permute-start.4 = (f32[12,16,256]{2,1,0:T(8,128)S(1)}, f32[12,16,256]{2,1,0:T(8,128)S(1)}, u32[]{:S(2)}, u32[]{:S(2)}) collective-permute-start(f32[12,16,256]{2,1,0:T(8,128)S(1)} %get-tuple-element.19), channel_id=1, source_target_pairs={{0,24},{2,26},{4,28},{6,30},{8,16},{10,18},{12,20},{14,22},{16,8},... | collective-permute-start | bytes 589832 | tf_op jit(solution)/shard_map/ppermute | solution.py:46
  22.7 5.0 %collective-permute-done.4.refs_5_ = f32[12,16,256]{2,1,0:T(8,128)S(1)} collective-permute-done((f32[12,16,256]{2,1,0:T(8,128)S(1)}, f32[12,16,256]{2,1,0:T(8,128)S(1)}, u32[]{:S(2)}, u32[]{:S(2)}) %collective-permute-start.4) | collective-permute-done | bytes 196640 | tf_op jit(solution)/shard_map/ppermute | solution.py:46
  27.7 2.4 %collective-permute-start.5 = (f32[24,16,256]{2,1,0:T(8,128)S(1)}, f32[24,16,256]{2,1,0:T(8,128)S(1)}, u32[]{:S(2)}, u32[]{:S(2)}) collective-permute-start(f32[24,16,256]{2,1,0:T(8,128)S(1)} %pad_maximum_fusion.4), channel_id=1, source_target_pairs={{0,8},{2,10},{4,12},{6,14},{8,0},{10,2},{12,4},{14,6},{16,24},{18,... | collective-permute-start | bytes 1179656 | tf_op jit(solution)/shard_map/ppermute | solution.py:46
  31.1 1.4 %collective-permute-start.11 = (f32[16,16,256]{2,1,0:T(8,128)S(1)}, f32[16,16,256]{2,1,0:T(8,128)S(1)}, u32[]{:S(2)}, u32[]{:S(2)}) collective-permute-start(f32[16,16,256]{2,1,0:T(8,128)S(1)} %get-tuple-element.34), channel_id=1, source_target_pairs={{0,2},{2,0},{4,6},{6,4},{8,10},{10,8},{12,14},{14,12},{16,18},{18,... | collective-permute-start | bytes 786440 | tf_op jit(solution)/shard_map/ppermute | solution.py:46
  32.9 1.5 %collective-permute-start.12 = (f32[12,16,256]{2,1,0:T(8,128)S(1)}, f32[12,16,256]{2,1,0:T(8,128)S(1)}, u32[]{:S(2)}, u32[]{:S(2)}) collective-permute-start(f32[12,16,256]{2,1,0:T(8,128)S(1)} %collective-permute-done.4.refs_5_), channel_id=1, source_target_pairs={{0,2},{2,0},{4,6},{6,4},{8,10},{10,8},{12,14},{14,12},{16,18},{18,... | collective-permute-start | bytes 589832 | tf_op jit(solution)/shard_map/ppermute | solution.py:46
  35.1 4.5 %collective-permute-done.9.refs_11_ = f32[16,16,256]{2,1,0:T(8,128)S(1)} collective-permute-done((f32[16,16,256]{2,1,0:T(8,128)S(1)}, f32[16,16,256]{2,1,0:T(8,128)S(1)}, u32[]{:S(2)}, u32[]{:S(2)}) %collective-permute-start.9) | collective-permute-done | bytes 262176 | tf_op jit(solution)/shard_map/ppermute | solution.py:46
  40.3 1.5 %collective-permute-start.14 = (f32[4,16,256]{2,1,0:T(8,128)S(1)}, f32[4,16,256]{2,1,0:T(8,128)S(1)}, u32[]{:S(2)}, u32[]{:S(2)}) collective-permute-start(f32[4,16,256]{2,1,0:T(8,128)S(1)} %slice.45), channel_id=1, source_target_pairs={{0,4},{2,6},{4,0},{6,2},{8,12},{10,14},{12,8},{14,10},{16,20},{18,... | collective-permute-start | bytes 196616 | tf_op jit(solution)/shard_map/ppermute | solution.py:46
  42.8 1.7 %collective-permute-start.17 = (f32[30,16,256]{2,1,0:T(8,128)S(1)}, f32[30,16,256]{2,1,0:T(8,128)S(1)}, u32[]{:S(2)}, u32[]{:S(2)}) collective-permute-start(f32[30,16,256]{2,1,0:T(8,128)S(1)} %get-tuple-element.31), channel_id=1, source_target_pairs={{0,2},{2,0},{4,6},{6,4},{8,10},{10,8},{12,14},{14,12},{16,18},{18,... | collective-permute-start | bytes 1474568 | tf_op jit(solution)/shard_map/ppermute | solution.py:46
  45.3 5.0 %solve.1 = (f32[1024,256]{1,0:T(8,128)S(1)}, f32[1024,256]{1,0:T(8,128)S(1)}, f32[2,256,256]{2,1,0:T(8,128)S(1)}, f32[2,256,256]{2,1,0:T(8,128)S(1)}) custom-call(f32[16,256]{1,0:T(8,128)S(1)} %widened.2.refs_0_, f32[1024,256]{1,0:T(8,128)S(1)} %copy-done, f32[20,16,256]{2,1,0:T(8,128)S(1)} %get-tuple-element.18.refs_2_.refs_4_, ...), custom_call_target="tpu_custom_call" | custom-call | flops 2147483648 | bytes 262144 | tf_op jit(solution)/shard_map/solve/pallas_call | solution.py:246
  50.9 2.9 %collective-permute-done.18.refs_14_ = f32[30,16,256]{2,1,0:T(8,128)S(1)} collective-permute-done((f32[30,16,256]{2,1,0:T(8,128)S(1)}, f32[30,16,256]{2,1,0:T(8,128)S(1)}, u32[]{:S(2)}, u32[]{:S(2)}) %collective-permute-start.18) | collective-permute-done | bytes 491552 | tf_op jit(solution)/shard_map/ppermute | solution.py:46
  53.8 1.6 %collective-permute-start.19 = (f32[12,16,256]{2,1,0:T(8,128)S(1)}, f32[12,16,256]{2,1,0:T(8,128)S(1)}, u32[]{:S(2)}, u32[]{:S(2)}) collective-permute-start(f32[12,16,256]{2,1,0:T(8,128)S(1)} %slice.46), channel_id=1, source_target_pairs={{0,2},{2,0},{4,6},{6,4},{8,10},{10,8},{12,14},{14,12},{16,18},{18,... | collective-permute-start | bytes 589832 | tf_op jit(solution)/shard_map/ppermute | solution.py:46
  55.4 1.5 %collective-permute-start.20 = (f32[12,16,256]{2,1,0:T(8,128)S(1)}, f32[12,16,256]{2,1,0:T(8,128)S(1)}, u32[]{:S(2)}, u32[]{:S(2)}) collective-permute-start(f32[12,16,256]{2,1,0:T(8,128)S(1)} %slice.47), channel_id=1, source_target_pairs={{0,4},{2,6},{4,0},{6,2},{8,12},{10,14},{12,8},{14,10},{16,20},{18,... | collective-permute-start | bytes 589832 | tf_op jit(solution)/shard_map/ppermute | solution.py:46
  57.8 1.8 %finish.1 = (f32[1024,256]{1,0:T(8,128)}, bf16[1536,256]{1,0:T(8,128)(2,1)S(1)}, bf16[1536,256]{1,0:T(8,128)(2,1)S(1)}) custom-call(f32[1024,256]{1,0:T(8,128)S(1)} %get-tuple-element.23.sol_ref, f32[1024,256]{1,0:T(8,128)S(1)} %get-tuple-element.24.part_ref, f32[2,256,256]{2,1,0:T(8,128)S(1)} %get-tuple-element.25.own_ref, ...), custom_call_target="tpu_custom_call" | custom-call | flops 100663296 | bytes 262144 | tf_op jit(solution)/shard_map/finish/pallas_call | solution.py:296
  59.5 2.2 %residual.1.refs_4_ = f32[1024,256]{1,0:T(8,128)} custom-call(f32[16,768]{1,0:T(8,128)S(1)} %widened.3.refs_0_, f32[1024,256]{1,0:T(8,128)S(1)} %copy-done, bf16[1536,256]{1,0:T(8,128)(2,1)S(1)} %get-tuple-element.28.refs_2_, bf16[1536,256]{1,0:T(8,128)(2,1)S(1)} %get-tuple-element.29.refs_3_, f32[20,16,256]{2,1,0:T(8,128)S(1)} %get-tuple-element.18.refs_2_.refs_4_, ...), custom_call_target="tpu_custom_call" | custom-call | flops 1056964608 | bytes 5505024 | tf_op jit(solution)/shard_map/residual/pallas_call | solution.py:361
  61.7 1.6 %residual_rest.1 = f32[1024,256]{1,0:T(8,128)} custom-call(f32[16,768]{1,0:T(8,128)S(1)} %widened.3.refs_0_, f32[1024,256]{1,0:T(8,128)S(1)} %copy-done, bf16[1536,256]{1,0:T(8,128)(2,1)S(1)} %get-tuple-element.28.refs_2_, bf16[1536,256]{1,0:T(8,128)(2,1)S(1)} %get-tuple-element.29.refs_3_, ...), custom_call_target="tpu_custom_call", output_to_operand_aliasing={{}: (4, {})} | custom-call | flops 150994944 | bytes 786432 | tf_op jit(solution)/shard_map/residual_rest/pallas_call | solution.py:361
  (56 shorter events, 8.5 us)
Async XLA Ops:
  3.3 10.7 %collective-permute-start.2 = (f32[20,16,256]{2,1,0:T(8,128)S(1)}, f32[20,16,256]{2,1,0:T(8,128)S(1)}, u32[]{:S(2)}, u32[]{:S(2)}) collective-permute-start(f32[20,16,256]{2,1,0:T(8,128)S(1)} %get-tuple-element.18.refs_2_.refs_4_), channel_id=1, source_target_pairs={{0,4},{2,6},{4,0},{6,2},{8,12},{10,14},{12,8},{14,10},{16,20},{18,... | collective-permute-start | bytes 983048 | tf_op jit(solution)/shard_map/ppermute | solution.py:46
  6.3 9.2 %collective-permute-start.3 = (f32[20,16,256]{2,1,0:T(8,128)S(1)}, f32[20,16,256]{2,1,0:T(8,128)S(1)}, u32[]{:S(2)}, u32[]{:S(2)}) collective-permute-start(f32[20,16,256]{2,1,0:T(8,128)S(1)} %get-tuple-element.18.refs_2_.refs_4_), channel_id=1, source_target_pairs={{0,2},{2,0},{4,6},{6,4},{8,10},{10,8},{12,14},{14,12},{16,18},{18,... | collective-permute-start | bytes 983048 | tf_op jit(solution)/shard_map/ppermute | solution.py:46
  7.8 8.0 %collective-permute-start = (f32[8,16,256]{2,1,0:T(8,128)S(1)}, f32[8,16,256]{2,1,0:T(8,128)S(1)}, u32[]{:S(2)}, u32[]{:S(2)}) collective-permute-start(f32[8,16,256]{2,1,0:T(8,128)S(1)} %get-tuple-element.17), channel_id=1, source_target_pairs={{0,24},{2,26},{4,28},{6,30},{8,16},{10,18},{12,20},{14,22},{16,8},... | collective-permute-start | bytes 393224 | tf_op jit(solution)/shard_map/ppermute | solution.py:46
  11.4 5.8 %collective-permute-start.1 = (f32[8,16,256]{2,1,0:T(8,128)S(1)}, f32[8,16,256]{2,1,0:T(8,128)S(1)}, u32[]{:S(2)}, u32[]{:S(2)}) collective-permute-start(f32[8,16,256]{2,1,0:T(8,128)S(1)} %get-tuple-element.17), channel_id=1, source_target_pairs={{0,8},{2,10},{4,12},{6,14},{8,0},{10,2},{12,4},{14,6},{16,24},{18,... | collective-permute-start | bytes 393224 | tf_op jit(solution)/shard_map/ppermute | solution.py:46
  17.4 12.8 %collective-permute-start.8 = (f32[26,16,256]{2,1,0:T(8,128)S(1)}, f32[26,16,256]{2,1,0:T(8,128)S(1)}, u32[]{:S(2)}, u32[]{:S(2)}) collective-permute-start(f32[26,16,256]{2,1,0:T(8,128)S(1)} %get-tuple-element.33), channel_id=1, source_target_pairs={{0,2},{2,0},{4,6},{6,4},{8,10},{10,8},{12,14},{14,12},{16,18},{18,... | collective-permute-start | bytes 1277960 | tf_op jit(solution)/shard_map/ppermute | solution.py:46
  18.1 12.1 %collective-permute-start.10 = (f32[26,16,256]{2,1,0:T(8,128)S(1)}, f32[26,16,256]{2,1,0:T(8,128)S(1)}, u32[]{:S(2)}, u32[]{:S(2)}) collective-permute-start(f32[26,16,256]{2,1,0:T(8,128)S(1)} %get-tuple-element.32), channel_id=1, source_target_pairs={{0,4},{2,6},{4,0},{6,2},{8,12},{10,14},{12,8},{14,10},{16,20},{18,... | collective-permute-start | bytes 1277960 | tf_op jit(solution)/shard_map/ppermute | solution.py:46
  19.1 8.6 %collective-permute-start.4 = (f32[12,16,256]{2,1,0:T(8,128)S(1)}, f32[12,16,256]{2,1,0:T(8,128)S(1)}, u32[]{:S(2)}, u32[]{:S(2)}) collective-permute-start(f32[12,16,256]{2,1,0:T(8,128)S(1)} %get-tuple-element.19), channel_id=1, source_target_pairs={{0,24},{2,26},{4,28},{6,30},{8,16},{10,18},{12,20},{14,22},{16,8},... | collective-permute-start | bytes 589832 | tf_op jit(solution)/shard_map/ppermute | solution.py:46
  22.7 7.5 %collective-permute-start.7 = (f32[8,16,256]{2,1,0:T(8,128)S(1)}, f32[8,16,256]{2,1,0:T(8,128)S(1)}, u32[]{:S(2)}, u32[]{:S(2)}) collective-permute-start(f32[8,16,256]{2,1,0:T(8,128)S(1)} %collective-permute-done.refs_3_), channel_id=1, source_target_pairs={{0,8},{2,10},{4,12},{6,14},{8,0},{10,2},{12,4},{14,6},{16,24},{18,... | collective-permute-start | bytes 393224 | tf_op jit(solution)/shard_map/ppermute | solution.py:46
  27.7 15.0 %collective-permute-start.5 = (f32[24,16,256]{2,1,0:T(8,128)S(1)}, f32[24,16,256]{2,1,0:T(8,128)S(1)}, u32[]{:S(2)}, u32[]{:S(2)}) collective-permute-start(f32[24,16,256]{2,1,0:T(8,128)S(1)} %pad_maximum_fusion.4), channel_id=1, source_target_pairs={{0,8},{2,10},{4,12},{6,14},{8,0},{10,2},{12,4},{14,6},{16,24},{18,... | collective-permute-start | bytes 1179656 | tf_op jit(solution)/shard_map/ppermute | solution.py:46
  30.2 4.2 %copy-start.6 = (s32[4,4,4]{2,1,0:T(4,128)S(1)}, s32[4,4,4]{2,1,0:T(4,128)}, u32[]{:S(2)}) copy-start(s32[4,4,4]{2,1,0:T(4,128)} %pattern_ref.2) | copy-start | bytes 772
  30.3 9.3 %collective-permute-start.9 = (f32[16,16,256]{2,1,0:T(8,128)S(1)}, f32[16,16,256]{2,1,0:T(8,128)S(1)}, u32[]{:S(2)}, u32[]{:S(2)}) collective-permute-start(f32[16,16,256]{2,1,0:T(8,128)S(1)} %get-tuple-element.35), channel_id=1, source_target_pairs={{0,4},{2,6},{4,0},{6,2},{8,12},{10,14},{12,8},{14,10},{16,20},{18,... | collective-permute-start | bytes 786440 | tf_op jit(solution)/shard_map/ppermute | solution.py:46
  31.1 9.2 %collective-permute-start.11 = (f32[16,16,256]{2,1,0:T(8,128)S(1)}, f32[16,16,256]{2,1,0:T(8,128)S(1)}, u32[]{:S(2)}, u32[]{:S(2)}) collective-permute-start(f32[16,16,256]{2,1,0:T(8,128)S(1)} %get-tuple-element.34), channel_id=1, source_target_pairs={{0,2},{2,0},{4,6},{6,4},{8,10},{10,8},{12,14},{14,12},{16,18},{18,... | collective-permute-start | bytes 786440 | tf_op jit(solution)/shard_map/ppermute | solution.py:46
  32.5 9.9 %collective-permute-start.6 = (f32[12,16,256]{2,1,0:T(8,128)S(1)}, f32[12,16,256]{2,1,0:T(8,128)S(1)}, u32[]{:S(2)}, u32[]{:S(2)}) collective-permute-start(f32[12,16,256]{2,1,0:T(8,128)S(1)} %collective-permute-done.4.refs_5_), channel_id=1, source_target_pairs={{0,4},{2,6},{4,0},{6,2},{8,12},{10,14},{12,8},{14,10},{16,20},{18,... | collective-permute-start | bytes 589832 | tf_op jit(solution)/shard_map/ppermute | solution.py:46
  32.9 9.8 %collective-permute-start.12 = (f32[12,16,256]{2,1,0:T(8,128)S(1)}, f32[12,16,256]{2,1,0:T(8,128)S(1)}, u32[]{:S(2)}, u32[]{:S(2)}) collective-permute-start(f32[12,16,256]{2,1,0:T(8,128)S(1)} %collective-permute-done.4.refs_5_), channel_id=1, source_target_pairs={{0,2},{2,0},{4,6},{6,4},{8,10},{10,8},{12,14},{14,12},{16,18},{18,... | collective-permute-start | bytes 589832 | tf_op jit(solution)/shard_map/ppermute | solution.py:46
  39.6 5.7 %copy-start = (f32[1024,256]{1,0:T(8,128)S(1)}, f32[1024,256]{1,0:T(8,128)}, u32[]{:S(2)}) copy-start(f32[1024,256]{1,0:T(8,128)} %refs_1_.4) | copy-start | bytes 3145732
  39.6 5.1 %collective-permute-start.13 = (f32[4,16,256]{2,1,0:T(8,128)S(1)}, f32[4,16,256]{2,1,0:T(8,128)S(1)}, u32[]{:S(2)}, u32[]{:S(2)}) collective-permute-start(f32[4,16,256]{2,1,0:T(8,128)S(1)} %slice.43), channel_id=1, source_target_pairs={{0,2},{2,0},{4,6},{6,4},{8,10},{10,8},{12,14},{14,12},{16,18},{18,... | collective-permute-start | bytes 196616 | tf_op jit(solution)/shard_map/ppermute | solution.py:46
  40.3 5.0 %collective-permute-start.14 = (f32[4,16,256]{2,1,0:T(8,128)S(1)}, f32[4,16,256]{2,1,0:T(8,128)S(1)}, u32[]{:S(2)}, u32[]{:S(2)}) collective-permute-start(f32[4,16,256]{2,1,0:T(8,128)S(1)} %slice.45), channel_id=1, source_target_pairs={{0,4},{2,6},{4,0},{6,2},{8,12},{10,14},{12,8},{14,10},{16,20},{18,... | collective-permute-start | bytes 196616 | tf_op jit(solution)/shard_map/ppermute | solution.py:46
  42.8 12.6 %collective-permute-start.17 = (f32[30,16,256]{2,1,0:T(8,128)S(1)}, f32[30,16,256]{2,1,0:T(8,128)S(1)}, u32[]{:S(2)}, u32[]{:S(2)}) collective-permute-start(f32[30,16,256]{2,1,0:T(8,128)S(1)} %get-tuple-element.31), channel_id=1, source_target_pairs={{0,2},{2,0},{4,6},{6,4},{8,10},{10,8},{12,14},{14,12},{16,18},{18,... | collective-permute-start | bytes 1474568 | tf_op jit(solution)/shard_map/ppermute | solution.py:46
  44.5 9.3 %collective-permute-start.18 = (f32[30,16,256]{2,1,0:T(8,128)S(1)}, f32[30,16,256]{2,1,0:T(8,128)S(1)}, u32[]{:S(2)}, u32[]{:S(2)}) collective-permute-start(f32[30,16,256]{2,1,0:T(8,128)S(1)} %get-tuple-element.30), channel_id=1, source_target_pairs={{0,4},{2,6},{4,0},{6,2},{8,12},{10,14},{12,8},{14,10},{16,20},{18,... | collective-permute-start | bytes 1474568 | tf_op jit(solution)/shard_map/ppermute | solution.py:46
  50.3 7.4 %collective-permute-start.15 = (f32[2,256,256]{2,1,0:T(8,128)S(1)}, f32[2,256,256]{2,1,0:T(8,128)S(1)}, u32[]{:S(2)}, u32[]{:S(2)}) collective-permute-start(f32[2,256,256]{2,1,0:T(8,128)S(1)} %get-tuple-element.25.own_ref), channel_id=1, source_target_pairs={{0,1},{1,0},{2,3},{3,2},{4,5},{5,4},{6,7},{7,6},{8,9},{9,8},{10,11... | collective-permute-start | bytes 1572872 | tf_op jit(solution)/shard_map/ppermute | solution.py:409
  50.4 7.4 %collective-permute-start.16 = (f32[2,256,256]{2,1,0:T(8,128)S(1)}, f32[2,256,256]{2,1,0:T(8,128)S(1)}, u32[]{:S(2)}, u32[]{:S(2)}) collective-permute-start(f32[2,256,256]{2,1,0:T(8,128)S(1)} %get-tuple-element.26), channel_id=1, source_target_pairs={{0,1},{1,0},{2,3},{3,2},{4,5},{5,4},{6,7},{7,6},{8,9},{9,8},{10,11... | collective-permute-start | bytes 1572872 | tf_op jit(solution)/shard_map/ppermute | solution.py:409
  53.8 3.2 %copy-start.7 = (s32[4,4,12]{2,1,0:T(4,128)S(1)}, s32[4,4,12]{2,1,0:T(4,128)}, u32[]{:S(2)}) copy-start(s32[4,4,12]{2,1,0:T(4,128)} %pattern_ref.3) | copy-start | bytes 2308
  53.8 7.9 %collective-permute-start.19 = (f32[12,16,256]{2,1,0:T(8,128)S(1)}, f32[12,16,256]{2,1,0:T(8,128)S(1)}, u32[]{:S(2)}, u32[]{:S(2)}) collective-permute-start(f32[12,16,256]{2,1,0:T(8,128)S(1)} %slice.46), channel_id=1, source_target_pairs={{0,2},{2,0},{4,6},{6,4},{8,10},{10,8},{12,14},{14,12},{16,18},{18,... | collective-permute-start | bytes 589832 | tf_op jit(solution)/shard_map/ppermute | solution.py:46
  55.4 6.3 %collective-permute-start.20 = (f32[12,16,256]{2,1,0:T(8,128)S(1)}, f32[12,16,256]{2,1,0:T(8,128)S(1)}, u32[]{:S(2)}, u32[]{:S(2)}) collective-permute-start(f32[12,16,256]{2,1,0:T(8,128)S(1)} %slice.47), channel_id=1, source_target_pairs={{0,4},{2,6},{4,0},{6,2},{8,12},{10,14},{12,8},{14,10},{16,20},{18,... | collective-permute-start | bytes 589832 | tf_op jit(solution)/shard_map/ppermute | solution.py:46
  (6 other events, 7.7 us)

commit v14 on v13

--- a/solution.py
+++ b/solution.py
@@ -76,16 +76,17 @@
     near, far = joined(*factor_line[1:-1]), factor_line[-1]
     second_parts = onward(own_round, len(own[1]), [near], axis)
     second_round = send_both(second_parts, axis)
-    third_parts = onward(second_round, len(near[1]), [far], axis)
+    jacobian_line = line_of(after(jacobian, *second_parts), axis)
+    half = len(jacobian_line) // 2
+    j_near, j_far = joined(*jacobian_line[1:half]), joined(*jacobian_line[half:])
+    second_last = [after(part, *jacobian_line[1:-1]) for part in second_round]
+    third_parts = onward(second_last, len(near[1]), [far], axis)
     third_round = send_both(third_parts, axis)
-    factor_parts = onward(third_round, len(far[1]), [], axis)
+    third_last = [after(part, jacobian_line[-1]) for part in third_round]
+    factor_parts = onward(third_last, len(far[1]), [], axis)
     factor_across = send_both(factor_parts, axis)
 
-    jacobian_line = [after(jacobian, *second_parts)]
-    while len(jacobian_line) < len(factor_line).bit_length():
-        passed = joined(*jacobian_line)
-        jacobian_line.append(sent(passed, axis, factor_line[len(passed[1]) // len(jacobian[1])][1][0][0]))
-    near, far = joined(*jacobian_line[1:-1]), jacobian_line[-1]
+    near, far = j_near, j_far
     near_round = around(near, axis)
     near_last = [after(part, *factor_parts) for part in near_round]
     far_parts = onward(near_last, len(near[1]), [far], axis)
@@ -112,7 +113,6 @@
         out_shape=shapes([(count * supers, rows, size) for count in (2, 3, 5)]),
         in_specs=[VMEM] * 3,
         out_specs=[VMEM] * 3,
-        compiler_params=pltpu.CompilerParams(vmem_limit_bytes=SMALL_LIMIT),
         name="pack",
     )(diag_inv, lower, jacobian)
 
@@ -142,12 +142,11 @@
     return [jax.ShapeDtypeStruct(shape, jnp.float32) for shape in arrays]
 
 
-def widened(pattern, wide):
-    supers, bands, count = pattern.shape
-    step = wide // count
-    together = max(1, 128 // step)
-
-    def kernel(pattern_ref, out_ref):
+def widened(patterns, wides):
+    def widen(pattern_ref, out_ref):
+        supers, bands, count = pattern_ref.shape
+        step = out_ref.shape[1] // count
+        together = max(1, 128 // step)
         lane = lax.broadcasted_iota(jnp.int32, (1, together * step), 1)
         for s in range(supers):
             for a in range(bands):
@@ -159,14 +158,18 @@
                     row = s * bands + a
                     out_ref[row : row + 1, first * step : end] = weight[:, : end - first * step]
 
+    def kernel(*refs):
+        for pattern_ref, out_ref in zip(refs[: len(patterns)], refs[len(patterns) :]):
+            widen(pattern_ref, out_ref)
+
     return pl.pallas_call(
         kernel,
-        out_shape=shapes([(supers * bands, wide)])[0],
-        in_specs=[SMEM],
-        out_specs=VMEM,
+        out_shape=shapes([(p.shape[0] * p.shape[1], wide) for p, wide in zip(patterns, wides)]),
+        in_specs=[SMEM] * len(patterns),
+        out_specs=[VMEM] * len(patterns),
         compiler_params=pltpu.CompilerParams(vmem_limit_bytes=SMALL_LIMIT),
         name="widened",
-    )(pattern)
+    )(*patterns)
 
 
 def weights_of(weights_ref, s, row, supers, size):
@@ -404,7 +407,8 @@
     whole = {owner: blocks for owner, blocks in places.items() if len(blocks) == 3 * supers}
     partial = set(places) - set(whole)
 
-    sol, parts, down, up = solve(*factor, relative, late, widened(factor_pattern, size), nodes, supers, size)
+    factor_weights, jacobian_weights = widened([factor_pattern, jacobian_pattern], [size, 3 * size])
+    sol, parts, down, up = solve(*factor, relative, late, factor_weights, nodes, supers, size)
     if nodes == 2:
         mail = [lax.ppermute(letter, "node", [(0, 1), (1, 0)]) for letter in (down, up)]
         sol, high, low = finish(sol, parts[0], down, *mail, supers)
@@ -431,7 +435,7 @@
         right_side=right_side,
         high=high,
         low=low,
-        weights=widened(jacobian_pattern, 3 * size),
+        weights=jacobian_weights,
         supers=supers,
         size=size,
     )

time: 63.6 us -> 66.1 us (1.039)
  waiting for transfers between devices: 19.4 us -> 22.1 us
  local copies, waits for them, and re-layouts: 3.43 us -> 0.84 us
  starting transfers between devices: 27.3 us -> 28.7 us
  Pallas kernels: 12.1 us -> 13.3 us
    ppermute x19 -> x20, waiting for transfers between devices: 19.4 us -> 22.1 us  [sent(): lax.ppermute(array, axis, [(i, i ^ mask) for i in range(lax.axis_size(axi...]
    unnamed x16 -> x14, local copies, waits for them, and re-layouts: 3.34 us -> 0.75 us
    pallas_call x1, Pallas kernels: 0.04 us -> 1.86 us  [pack(): pl.pallas_call(kernel, out_shape=shapes([(count * supers, rows, size) for...]
    ppermute x19 -> x20, starting transfers between devices: 26.7 us -> 28.1 us  [sent(): lax.ppermute(array, axis, [(i, i ^ mask) for i in range(lax.axis_size(axi...]
    pallas_call x2 -> x1, Pallas kernels: 1.47 us -> 0.93 us  [widened(): pl.pallas_call(kernel, out_shape=shapes([(p.shape[0] * p.shape[1], wide)...]
  transfers between devices with their start and end apart: 21 -> 22, of which waited for: 11 -> 14; matrix products, arithmetic and copies ran while one was open for 0% -> 0% of each run, Pallas kernels for 16% -> 15%
where the time goes in v14:
time: 66.1 us; the launch traced here: 66 us
  starting transfers between devices  28.7 us (43%)
  waiting for transfers between devices  22.1 us (33%)
  Pallas kernels  13.3 us (20%)
  local copies, waits for them, and re-layouts  0.84 us (1%)
  between operations  0.81 us (1%)
    ppermute x20, starting transfers between devices, sent(): lax.ppermute(array, axis, [(i, i ^ mask) for i in range(lax.axis_size(axi...  28.1 us
    ppermute x20, waiting for transfers between devices, sent(): lax.ppermute(array, axis, [(i, i ^ mask) for i in range(lax.axis_size(axi...  22.1 us
    pallas_call x1, Pallas kernels, solve(): pl.pallas_call(kernel, out_shape=shapes([(span, columns)] + [(span, size)...  5 us
    pallas_call x2, Pallas kernels, subtract_product(): pl.pallas_call(kernel, out_shape=shapes([(span, columns)])[0], in_specs=[...  3.79 us
    pallas_call x1, Pallas kernels, pack(): pl.pallas_call(kernel, out_shape=shapes([(count * supers, rows, size) for...  1.86 us
    pallas_call x1, Pallas kernels, finish(): pl.pallas_call(kernel, out_shape=shapes([(span, columns)]) + [windows, wi...  1.76 us
  transfers between devices with their start and end apart: 22, of which 14 were waited for; matrix products, arithmetic and copies ran while one was open for 0% of the time, Pallas kernels for 15%

profile of v14, /device:TPU:0, one launch (start us, length us, event | category | flops | bytes accessed | tf_op | source)
XLA Modules:
  0.0 66.0 jit_solution(15654941663358929409)
XLA Ops:
  0.6 1.9 %pack.1 = (f32[8,16,256]{2,1,0:T(8,128)}, f32[12,16,256]{2,1,0:T(8,128)}, f32[20,16,256]{2,1,0:T(8,128)}) custom-call(f32[4,16,256]{2,1,0:T(8,128)} %diag_ref.1, f32[4,16,256]{2,1,0:T(8,128)} %lower_ref.1, f32[4,16,768]{2,1,0:T(8,128)} %jacobian_ref.1), custom_call_target="tpu_custom_call" | custom-call | tf_op jit(solution)/shard_map/pack/pallas_call | solution.py:111
  2.5 3.0 %collective-permute-start.2 = (f32[20,16,256]{2,1,0:T(8,128)}, f32[20,16,256]{2,1,0:T(8,128)S(1)}, u32[]{:S(2)}, u32[]{:S(2)}) collective-permute-start(f32[20,16,256]{2,1,0:T(8,128)} %get-tuple-element.25.refs_2_.refs_4_), channel_id=1, source_target_pairs={{0,4},{2,6},{4,0},{6,2},{8,12},{10,14},{12,8},{14,10},{16,20},{18,... | collective-permute-start | bytes 983048 | tf_op jit(solution)/shard_map/ppermute | solution.py:46
  5.5 1.5 %collective-permute-start.3 = (f32[20,16,256]{2,1,0:T(8,128)}, f32[20,16,256]{2,1,0:T(8,128)S(1)}, u32[]{:S(2)}, u32[]{:S(2)}) collective-permute-start(f32[20,16,256]{2,1,0:T(8,128)} %get-tuple-element.25.refs_2_.refs_4_), channel_id=1, source_target_pairs={{0,2},{2,0},{4,6},{6,4},{8,10},{10,8},{12,14},{14,12},{16,18},{18,... | collective-permute-start | bytes 983048 | tf_op jit(solution)/shard_map/ppermute | solution.py:46
  6.9 3.6 %collective-permute-start = (f32[8,16,256]{2,1,0:T(8,128)}, f32[8,16,256]{2,1,0:T(8,128)S(1)}, u32[]{:S(2)}, u32[]{:S(2)}) collective-permute-start(f32[8,16,256]{2,1,0:T(8,128)} %get-tuple-element.24), channel_id=1, source_target_pairs={{0,24},{2,26},{4,28},{6,30},{8,16},{10,18},{12,20},{14,22},{16,8},... | collective-permute-start | bytes 393224 | tf_op jit(solution)/shard_map/ppermute | solution.py:46
  10.6 2.8 %collective-permute-done.2.refs_7_.refs_9_ = f32[20,16,256]{2,1,0:T(8,128)S(1)} collective-permute-done((f32[20,16,256]{2,1,0:T(8,128)}, f32[20,16,256]{2,1,0:T(8,128)S(1)}, u32[]{:S(2)}, u32[]{:S(2)}) %collective-permute-start.2) | collective-permute-done | bytes 327712 | tf_op jit(solution)/shard_map/ppermute | solution.py:46
  15.2 1.4 %collective-permute-done.1.refs_4_ = f32[8,16,256]{2,1,0:T(8,128)S(1)} collective-permute-done((f32[8,16,256]{2,1,0:T(8,128)}, f32[8,16,256]{2,1,0:T(8,128)S(1)}, u32[]{:S(2)}, u32[]{:S(2)}) %collective-permute-start.1) | collective-permute-done | bytes 131104 | tf_op jit(solution)/shard_map/ppermute | solution.py:46
  18.4 3.6 %collective-permute-start.5 = (f32[12,16,256]{2,1,0:T(8,128)S(1)}, f32[12,16,256]{2,1,0:T(8,128)S(1)}, u32[]{:S(2)}, u32[]{:S(2)}) collective-permute-start(f32[12,16,256]{2,1,0:T(8,128)S(1)} %copy-done.6), channel_id=1, source_target_pairs={{0,24},{2,26},{4,28},{6,30},{8,16},{10,18},{12,20},{14,22},{16,8},... | collective-permute-start | bytes 589832 | tf_op jit(solution)/shard_map/ppermute | solution.py:46
  22.0 2.0 %collective-permute-start.8 = (f32[8,16,256]{2,1,0:T(8,128)S(1)}, f32[8,16,256]{2,1,0:T(8,128)S(1)}, u32[]{:S(2)}, u32[]{:S(2)}) collective-permute-start(f32[8,16,256]{2,1,0:T(8,128)S(1)} %collective-permute-done.refs_3_), channel_id=1, source_target_pairs={{0,8},{2,10},{4,12},{6,14},{8,0},{10,2},{12,4},{14,6},{16,24},{18,... | collective-permute-start | bytes 393224 | tf_op jit(solution)/shard_map/ppermute | solution.py:46
  24.1 4.0 %collective-permute-done.5.refs_5_ = f32[12,16,256]{2,1,0:T(8,128)S(1)} collective-permute-done((f32[12,16,256]{2,1,0:T(8,128)S(1)}, f32[12,16,256]{2,1,0:T(8,128)S(1)}, u32[]{:S(2)}, u32[]{:S(2)}) %collective-permute-start.5) | collective-permute-done | bytes 196640 | tf_op jit(solution)/shard_map/ppermute | solution.py:46
  28.1 3.0 %collective-permute-done.4.refs_6_ = f32[12,16,256]{2,1,0:T(8,128)S(1)} collective-permute-done((f32[12,16,256]{2,1,0:T(8,128)S(1)}, f32[12,16,256]{2,1,0:T(8,128)S(1)}, u32[]{:S(2)}, u32[]{:S(2)}) %collective-permute-start.4) | collective-permute-done | bytes 196640 | tf_op jit(solution)/shard_map/ppermute | solution.py:46
  31.1 1.5 %collective-permute-done.8.refs_5_ = f32[8,16,256]{2,1,0:T(8,128)S(1)} collective-permute-done((f32[8,16,256]{2,1,0:T(8,128)S(1)}, f32[8,16,256]{2,1,0:T(8,128)S(1)}, u32[]{:S(2)}, u32[]{:S(2)}) %collective-permute-start.8) | collective-permute-done | bytes 131104 | tf_op jit(solution)/shard_map/ppermute | solution.py:46
  33.6 1.5 %collective-permute-start.10 = (f32[16,16,256]{2,1,0:T(8,128)S(1)}, f32[16,16,256]{2,1,0:T(8,128)S(1)}, u32[]{:S(2)}, u32[]{:S(2)}) collective-permute-start(f32[16,16,256]{2,1,0:T(8,128)S(1)} %get-tuple-element.47), channel_id=1, source_target_pairs={{0,4},{2,6},{4,0},{6,2},{8,12},{10,14},{12,8},{14,10},{16,20},{18,... | collective-permute-start | bytes 786440 | tf_op jit(solution)/shard_map/ppermute | solution.py:46
  35.7 1.3 %collective-permute-start.7 = (f32[12,16,256]{2,1,0:T(8,128)S(1)}, f32[12,16,256]{2,1,0:T(8,128)S(1)}, u32[]{:S(2)}, u32[]{:S(2)}) collective-permute-start(f32[12,16,256]{2,1,0:T(8,128)S(1)} %collective-permute-done.5.refs_5_), channel_id=1, source_target_pairs={{0,4},{2,6},{4,0},{6,2},{8,12},{10,14},{12,8},{14,10},{16,20},{18,... | collective-permute-start | bytes 589832 | tf_op jit(solution)/shard_map/ppermute | solution.py:46
  37.0 1.5 %collective-permute-start.13 = (f32[12,16,256]{2,1,0:T(8,128)S(1)}, f32[12,16,256]{2,1,0:T(8,128)S(1)}, u32[]{:S(2)}, u32[]{:S(2)}) collective-permute-start(f32[12,16,256]{2,1,0:T(8,128)S(1)} %collective-permute-done.5.refs_5_), channel_id=1, source_target_pairs={{0,2},{2,0},{4,6},{6,4},{8,10},{10,8},{12,14},{14,12},{16,18},{18,... | collective-permute-start | bytes 589832 | tf_op jit(solution)/shard_map/ppermute | solution.py:46
  39.4 1.4 %collective-permute-done.6.refs_7_ = f32[12,16,256]{2,1,0:T(8,128)S(1)} collective-permute-done((f32[12,16,256]{2,1,0:T(8,128)S(1)}, f32[12,16,256]{2,1,0:T(8,128)S(1)}, u32[]{:S(2)}, u32[]{:S(2)}) %collective-permute-start.6) | collective-permute-done | bytes 196640 | tf_op jit(solution)/shard_map/ppermute | solution.py:46
  42.8 1.5 %collective-permute-start.15 = (f32[4,16,256]{2,1,0:T(8,128)S(1)}, f32[4,16,256]{2,1,0:T(8,128)S(1)}, u32[]{:S(2)}, u32[]{:S(2)}) collective-permute-start(f32[4,16,256]{2,1,0:T(8,128)S(1)} %slice.35), channel_id=1, source_target_pairs={{0,4},{2,6},{4,0},{6,2},{8,12},{10,14},{12,8},{14,10},{16,20},{18,... | collective-permute-start | bytes 196616 | tf_op jit(solution)/shard_map/ppermute | solution.py:46
  47.8 1.6 %collective-permute-done.14.refs_12_ = f32[4,16,256]{2,1,0:T(8,128)S(1)} collective-permute-done((f32[4,16,256]{2,1,0:T(8,128)S(1)}, f32[4,16,256]{2,1,0:T(8,128)S(1)}, u32[]{:S(2)}, u32[]{:S(2)}) %collective-permute-start.14) | collective-permute-done | bytes 65568 | tf_op jit(solution)/shard_map/ppermute | solution.py:46
  49.4 5.0 %solve.1 = (f32[1024,256]{1,0:T(8,128)S(1)}, f32[1024,256]{1,0:T(8,128)S(1)}, f32[2,256,256]{2,1,0:T(8,128)S(1)}, f32[2,256,256]{2,1,0:T(8,128)S(1)}) custom-call(f32[16,256]{1,0:T(8,128)S(1)} %get-tuple-element.22.refs_0_, f32[1024,256]{1,0:T(8,128)S(1)} %copy-done, f32[20,16,256]{2,1,0:T(8,128)S(1)} %copy-done.3, ...), custom_call_target="tpu_custom_call" | custom-call | flops 2147483648 | bytes 262144 | tf_op jit(solution)/shard_map/solve/pallas_call | solution.py:249
  55.0 2.2 %collective-permute-done.19.refs_15_ = f32[30,16,256]{2,1,0:T(8,128)S(1)} collective-permute-done((f32[30,16,256]{2,1,0:T(8,128)S(1)}, f32[30,16,256]{2,1,0:T(8,128)S(1)}, u32[]{:S(2)}, u32[]{:S(2)}) %collective-permute-start.19) | collective-permute-done | bytes 491552 | tf_op jit(solution)/shard_map/ppermute | solution.py:46
  57.2 1.5 %collective-permute-start.20 = (f32[12,16,256]{2,1,0:T(8,128)S(1)}, f32[12,16,256]{2,1,0:T(8,128)S(1)}, u32[]{:S(2)}, u32[]{:S(2)}) collective-permute-start(f32[12,16,256]{2,1,0:T(8,128)S(1)} %slice.42), channel_id=1, source_target_pairs={{0,2},{2,0},{4,6},{6,4},{8,10},{10,8},{12,14},{14,12},{16,18},{18,... | collective-permute-start | bytes 589832 | tf_op jit(solution)/shard_map/ppermute | solution.py:46
  58.7 1.2 %collective-permute-start.21 = (f32[12,16,256]{2,1,0:T(8,128)S(1)}, f32[12,16,256]{2,1,0:T(8,128)S(1)}, u32[]{:S(2)}, u32[]{:S(2)}) collective-permute-start(f32[12,16,256]{2,1,0:T(8,128)S(1)} %slice.43), channel_id=1, source_target_pairs={{0,4},{2,6},{4,0},{6,2},{8,12},{10,14},{12,8},{14,10},{16,20},{18,... | collective-permute-start | bytes 589832 | tf_op jit(solution)/shard_map/ppermute | solution.py:46
  59.9 1.8 %finish.1 = (f32[1024,256]{1,0:T(8,128)}, bf16[1536,256]{1,0:T(8,128)(2,1)S(1)}, bf16[1536,256]{1,0:T(8,128)(2,1)S(1)}) custom-call(f32[1024,256]{1,0:T(8,128)S(1)} %get-tuple-element.34.sol_ref, f32[1024,256]{1,0:T(8,128)S(1)} %get-tuple-element.35.part_ref, f32[2,256,256]{2,1,0:T(8,128)S(1)} %get-tuple-element.36.own_ref, ...), custom_call_target="tpu_custom_call" | custom-call | flops 100663296 | bytes 262144 | tf_op jit(solution)/shard_map/finish/pallas_call | solution.py:299
  61.6 2.2 %residual.1.refs_4_ = f32[1024,256]{1,0:T(8,128)} custom-call(f32[16,768]{1,0:T(8,128)S(1)} %get-tuple-element.39.refs_0_, f32[1024,256]{1,0:T(8,128)S(1)} %copy-done, bf16[1536,256]{1,0:T(8,128)(2,1)S(1)} %get-tuple-element.40.refs_2_, bf16[1536,256]{1,0:T(8,128)(2,1)S(1)} %get-tuple-element.41.refs_3_, f32[20,16,256]{2,1,0:T(8,128)S(1)} %copy-done.3, ...), custom_call_target="tpu_custom_call" | custom-call | flops 1056964608 | bytes 5505024 | tf_op jit(solution)/shard_map/residual/pallas_call | solution.py:364
  64.4 1.6 %residual_rest.1 = f32[1024,256]{1,0:T(8,128)} custom-call(f32[16,768]{1,0:T(8,128)S(1)} %get-tuple-element.39.refs_0_, f32[1024,256]{1,0:T(8,128)S(1)} %copy-done, bf16[1536,256]{1,0:T(8,128)(2,1)S(1)} %get-tuple-element.40.refs_2_, bf16[1536,256]{1,0:T(8,128)(2,1)S(1)} %get-tuple-element.41.refs_3_, ...), custom_call_target="tpu_custom_call", output_to_operand_aliasing={{}: (4, {})} | custom-call | flops 150994944 | bytes 786432 | tf_op jit(solution)/shard_map/residual_rest/pallas_call | solution.py:364
  (54 shorter events, 12.7 us)
Async XLA Ops:
  2.5 10.9 %collective-permute-start.2 = (f32[20,16,256]{2,1,0:T(8,128)}, f32[20,16,256]{2,1,0:T(8,128)S(1)}, u32[]{:S(2)}, u32[]{:S(2)}) collective-permute-start(f32[20,16,256]{2,1,0:T(8,128)} %get-tuple-element.25.refs_2_.refs_4_), channel_id=1, source_target_pairs={{0,4},{2,6},{4,0},{6,2},{8,12},{10,14},{12,8},{14,10},{16,20},{18,... | collective-permute-start | bytes 983048 | tf_op jit(solution)/shard_map/ppermute | solution.py:46
  5.5 9.4 %collective-permute-start.3 = (f32[20,16,256]{2,1,0:T(8,128)}, f32[20,16,256]{2,1,0:T(8,128)S(1)}, u32[]{:S(2)}, u32[]{:S(2)}) collective-permute-start(f32[20,16,256]{2,1,0:T(8,128)} %get-tuple-element.25.refs_2_.refs_4_), channel_id=1, source_target_pairs={{0,2},{2,0},{4,6},{6,4},{8,10},{10,8},{12,14},{14,12},{16,18},{18,... | collective-permute-start | bytes 983048 | tf_op jit(solution)/shard_map/ppermute | solution.py:46
  6.9 8.2 %collective-permute-start = (f32[8,16,256]{2,1,0:T(8,128)}, f32[8,16,256]{2,1,0:T(8,128)S(1)}, u32[]{:S(2)}, u32[]{:S(2)}) collective-permute-start(f32[8,16,256]{2,1,0:T(8,128)} %get-tuple-element.24), channel_id=1, source_target_pairs={{0,24},{2,26},{4,28},{6,30},{8,16},{10,18},{12,20},{14,22},{16,8},... | collective-permute-start | bytes 393224 | tf_op jit(solution)/shard_map/ppermute | solution.py:46
  10.5 6.1 %collective-permute-start.1 = (f32[8,16,256]{2,1,0:T(8,128)}, f32[8,16,256]{2,1,0:T(8,128)S(1)}, u32[]{:S(2)}, u32[]{:S(2)}) collective-permute-start(f32[8,16,256]{2,1,0:T(8,128)} %get-tuple-element.24), channel_id=1, source_target_pairs={{0,8},{2,10},{4,12},{6,14},{8,0},{10,2},{12,4},{14,6},{16,24},{18,... | collective-permute-start | bytes 393224 | tf_op jit(solution)/shard_map/ppermute | solution.py:46
  16.7 14.4 %collective-permute-start.9 = (f32[26,16,256]{2,1,0:T(8,128)S(1)}, f32[26,16,256]{2,1,0:T(8,128)S(1)}, u32[]{:S(2)}, u32[]{:S(2)}) collective-permute-start(f32[26,16,256]{2,1,0:T(8,128)S(1)} %get-tuple-element.45), channel_id=1, source_target_pairs={{0,2},{2,0},{4,6},{6,4},{8,10},{10,8},{12,14},{14,12},{16,18},{18,... | collective-permute-start | bytes 1277960 | tf_op jit(solution)/shard_map/ppermute | solution.py:46
  17.4 13.7 %collective-permute-start.11 = (f32[26,16,256]{2,1,0:T(8,128)S(1)}, f32[26,16,256]{2,1,0:T(8,128)S(1)}, u32[]{:S(2)}, u32[]{:S(2)}) collective-permute-start(f32[26,16,256]{2,1,0:T(8,128)S(1)} %get-tuple-element.44), channel_id=1, source_target_pairs={{0,4},{2,6},{4,0},{6,2},{8,12},{10,14},{12,8},{14,10},{16,20},{18,... | collective-permute-start | bytes 1277960 | tf_op jit(solution)/shard_map/ppermute | solution.py:46
  18.4 9.6 %collective-permute-start.5 = (f32[12,16,256]{2,1,0:T(8,128)S(1)}, f32[12,16,256]{2,1,0:T(8,128)S(1)}, u32[]{:S(2)}, u32[]{:S(2)}) collective-permute-start(f32[12,16,256]{2,1,0:T(8,128)S(1)} %copy-done.6), channel_id=1, source_target_pairs={{0,24},{2,26},{4,28},{6,30},{8,16},{10,18},{12,20},{14,22},{16,8},... | collective-permute-start | bytes 589832 | tf_op jit(solution)/shard_map/ppermute | solution.py:46
  22.0 9.1 %collective-permute-start.4 = (f32[12,16,256]{2,1,0:T(8,128)S(1)}, f32[12,16,256]{2,1,0:T(8,128)S(1)}, u32[]{:S(2)}, u32[]{:S(2)}) collective-permute-start(f32[12,16,256]{2,1,0:T(8,128)S(1)} %copy-done.6), channel_id=1, source_target_pairs={{0,8},{2,10},{4,12},{6,14},{8,0},{10,2},{12,4},{14,6},{16,24},{18,... | collective-permute-start | bytes 589832 | tf_op jit(solution)/shard_map/ppermute | solution.py:46
  22.0 10.6 %collective-permute-start.8 = (f32[8,16,256]{2,1,0:T(8,128)S(1)}, f32[8,16,256]{2,1,0:T(8,128)S(1)}, u32[]{:S(2)}, u32[]{:S(2)}) collective-permute-start(f32[8,16,256]{2,1,0:T(8,128)S(1)} %collective-permute-done.refs_3_), channel_id=1, source_target_pairs={{0,8},{2,10},{4,12},{6,14},{8,0},{10,2},{12,4},{14,6},{16,24},{18,... | collective-permute-start | bytes 393224 | tf_op jit(solution)/shard_map/ppermute | solution.py:46
  32.6 5.9 %copy-start.5 = (s32[4,4,12]{2,1,0:T(4,128)S(1)}, s32[4,4,12]{2,1,0:T(4,128)}, u32[]{:S(2)}) copy-start(s32[4,4,12]{2,1,0:T(4,128)} %refs_1_.3) | copy-start | bytes 2308
  32.7 9.2 %collective-permute-start.12 = (f32[16,16,256]{2,1,0:T(8,128)S(1)}, f32[16,16,256]{2,1,0:T(8,128)S(1)}, u32[]{:S(2)}, u32[]{:S(2)}) collective-permute-start(f32[16,16,256]{2,1,0:T(8,128)S(1)} %get-tuple-element.46), channel_id=1, source_target_pairs={{0,2},{2,0},{4,6},{6,4},{8,10},{10,8},{12,14},{14,12},{16,18},{18,... | collective-permute-start | bytes 786440 | tf_op jit(solution)/shard_map/ppermute | solution.py:46
  33.6 9.2 %collective-permute-start.10 = (f32[16,16,256]{2,1,0:T(8,128)S(1)}, f32[16,16,256]{2,1,0:T(8,128)S(1)}, u32[]{:S(2)}, u32[]{:S(2)}) collective-permute-start(f32[16,16,256]{2,1,0:T(8,128)S(1)} %get-tuple-element.47), channel_id=1, source_target_pairs={{0,4},{2,6},{4,0},{6,2},{8,12},{10,14},{12,8},{14,10},{16,20},{18,... | collective-permute-start | bytes 786440 | tf_op jit(solution)/shard_map/ppermute | solution.py:46
  35.1 5.7 %collective-permute-start.6 = (f32[12,16,256]{2,1,0:T(8,128)S(1)}, f32[12,16,256]{2,1,0:T(8,128)S(1)}, u32[]{:S(2)}, u32[]{:S(2)}) collective-permute-start(f32[12,16,256]{2,1,0:T(8,128)S(1)} %collective-permute-done.5.refs_5_), channel_id=1, source_target_pairs={{0,8},{2,10},{4,12},{6,14},{8,0},{10,2},{12,4},{14,6},{16,24},{18,... | collective-permute-start | bytes 589832 | tf_op jit(solution)/shard_map/ppermute | solution.py:46
  35.7 9.8 %collective-permute-start.7 = (f32[12,16,256]{2,1,0:T(8,128)S(1)}, f32[12,16,256]{2,1,0:T(8,128)S(1)}, u32[]{:S(2)}, u32[]{:S(2)}) collective-permute-start(f32[12,16,256]{2,1,0:T(8,128)S(1)} %collective-permute-done.5.refs_5_), channel_id=1, source_target_pairs={{0,4},{2,6},{4,0},{6,2},{8,12},{10,14},{12,8},{14,10},{16,20},{18,... | collective-permute-start | bytes 589832 | tf_op jit(solution)/shard_map/ppermute | solution.py:46
  37.0 8.4 %collective-permute-start.13 = (f32[12,16,256]{2,1,0:T(8,128)S(1)}, f32[12,16,256]{2,1,0:T(8,128)S(1)}, u32[]{:S(2)}, u32[]{:S(2)}) collective-permute-start(f32[12,16,256]{2,1,0:T(8,128)S(1)} %collective-permute-done.5.refs_5_), channel_id=1, source_target_pairs={{0,2},{2,0},{4,6},{6,4},{8,10},{10,8},{12,14},{14,12},{16,18},{18,... | collective-permute-start | bytes 589832 | tf_op jit(solution)/shard_map/ppermute | solution.py:46
  41.9 7.5 %copy-start = (f32[1024,256]{1,0:T(8,128)S(1)}, f32[1024,256]{1,0:T(8,128)}, u32[]{:S(2)}) copy-start(f32[1024,256]{1,0:T(8,128)} %refs_1_.6) | copy-start | bytes 3145732
  42.8 4.9 %collective-permute-start.15 = (f32[4,16,256]{2,1,0:T(8,128)S(1)}, f32[4,16,256]{2,1,0:T(8,128)S(1)}, u32[]{:S(2)}, u32[]{:S(2)}) collective-permute-start(f32[4,16,256]{2,1,0:T(8,128)S(1)} %slice.35), channel_id=1, source_target_pairs={{0,4},{2,6},{4,0},{6,2},{8,12},{10,14},{12,8},{14,10},{16,20},{18,... | collective-permute-start | bytes 196616 | tf_op jit(solution)/shard_map/ppermute | solution.py:46
  44.4 5.0 %collective-permute-start.14 = (f32[4,16,256]{2,1,0:T(8,128)S(1)}, f32[4,16,256]{2,1,0:T(8,128)S(1)}, u32[]{:S(2)}, u32[]{:S(2)}) collective-permute-start(f32[4,16,256]{2,1,0:T(8,128)S(1)} %slice.33), channel_id=1, source_target_pairs={{0,2},{2,0},{4,6},{6,4},{8,10},{10,8},{12,14},{14,12},{16,18},{18,... | collective-permute-start | bytes 196616 | tf_op jit(solution)/shard_map/ppermute | solution.py:46
  45.6 13.0 %collective-permute-start.18 = (f32[30,16,256]{2,1,0:T(8,128)S(1)}, f32[30,16,256]{2,1,0:T(8,128)S(1)}, u32[]{:S(2)}, u32[]{:S(2)}) collective-permute-start(f32[30,16,256]{2,1,0:T(8,128)S(1)} %get-tuple-element.43), channel_id=1, source_target_pairs={{0,2},{2,0},{4,6},{6,4},{8,10},{10,8},{12,14},{14,12},{16,18},{18,... | collective-permute-start | bytes 1474568 | tf_op jit(solution)/shard_map/ppermute | solution.py:46
  46.7 10.5 %collective-permute-start.19 = (f32[30,16,256]{2,1,0:T(8,128)S(1)}, f32[30,16,256]{2,1,0:T(8,128)S(1)}, u32[]{:S(2)}, u32[]{:S(2)}) collective-permute-start(f32[30,16,256]{2,1,0:T(8,128)S(1)} %get-tuple-element.42), channel_id=1, source_target_pairs={{0,4},{2,6},{4,0},{6,2},{8,12},{10,14},{12,8},{14,10},{16,20},{18,... | collective-permute-start | bytes 1474568 | tf_op jit(solution)/shard_map/ppermute | solution.py:46
  54.4 5.5 %collective-permute-start.16 = (f32[2,256,256]{2,1,0:T(8,128)S(1)}, f32[2,256,256]{2,1,0:T(8,128)S(1)}, u32[]{:S(2)}, u32[]{:S(2)}) collective-permute-start(f32[2,256,256]{2,1,0:T(8,128)S(1)} %get-tuple-element.36.own_ref), channel_id=1, source_target_pairs={{0,1},{1,0},{2,3},{3,2},{4,5},{5,4},{6,7},{7,6},{8,9},{9,8},{10,11... | collective-permute-start | bytes 1572872 | tf_op jit(solution)/shard_map/ppermute | solution.py:413
  54.5 5.4 %collective-permute-start.17 = (f32[2,256,256]{2,1,0:T(8,128)S(1)}, f32[2,256,256]{2,1,0:T(8,128)S(1)}, u32[]{:S(2)}, u32[]{:S(2)}) collective-permute-start(f32[2,256,256]{2,1,0:T(8,128)S(1)} %get-tuple-element.37), channel_id=1, source_target_pairs={{0,1},{1,0},{2,3},{3,2},{4,5},{5,4},{6,7},{7,6},{8,9},{9,8},{10,11... | collective-permute-start | bytes 1572872 | tf_op jit(solution)/shard_map/ppermute | solution.py:413
  57.2 6.7 %collective-permute-start.20 = (f32[12,16,256]{2,1,0:T(8,128)S(1)}, f32[12,16,256]{2,1,0:T(8,128)S(1)}, u32[]{:S(2)}, u32[]{:S(2)}) collective-permute-start(f32[12,16,256]{2,1,0:T(8,128)S(1)} %slice.42), channel_id=1, source_target_pairs={{0,2},{2,0},{4,6},{6,4},{8,10},{10,8},{12,14},{14,12},{16,18},{18,... | collective-permute-start | bytes 589832 | tf_op jit(solution)/shard_map/ppermute | solution.py:46
  58.7 5.7 %collective-permute-start.21 = (f32[12,16,256]{2,1,0:T(8,128)S(1)}, f32[12,16,256]{2,1,0:T(8,128)S(1)}, u32[]{:S(2)}, u32[]{:S(2)}) collective-permute-start(f32[12,16,256]{2,1,0:T(8,128)S(1)} %slice.43), channel_id=1, source_target_pairs={{0,4},{2,6},{4,0},{6,2},{8,12},{10,14},{12,8},{14,10},{16,20},{18,... | collective-permute-start | bytes 589832 | tf_op jit(solution)/shard_map/ppermute | solution.py:46
  (6 other events, 19.8 us)

commit v15 on v14

--- a/solution.py
+++ b/solution.py
@@ -62,12 +62,21 @@
     return sent(parts[0], axis, 1), sent(parts[1], axis, 2)
 
 
+def masks_of(axis):
+    masks, step = [], lax.axis_size(axis) // 4
+    while step > 1:
+        masks.append(4 * (step - 1))
+        step //= 2
+    return masks
+
+
 def line_of(held, axis):
-    line, step = [held], lax.axis_size(axis) // 4
-    while step > 1:
-        line += [sent(part, axis, 4 * (step - 1)) for part in line]
-        step //= 2
-    return line
+    *masks, last = masks_of(axis)
+    beside = sent(held, axis, last)
+    line = [held]
+    for mask in masks:
+        line += [sent(part, axis, mask) for part in line]
+    return line + [beside] + [sent(part, axis, last) for part in line[1:]]
 
 
 def gather_panels(own, factor, jacobian, right_side, axis):
@@ -76,17 +85,15 @@
     near, far = joined(*factor_line[1:-1]), factor_line[-1]
     second_parts = onward(own_round, len(own[1]), [near], axis)
     second_round = send_both(second_parts, axis)
-    jacobian_line = line_of(after(jacobian, *second_parts), axis)
-    half = len(jacobian_line) // 2
-    j_near, j_far = joined(*jacobian_line[1:half]), joined(*jacobian_line[half:])
-    second_last = [after(part, *jacobian_line[1:-1]) for part in second_round]
-    third_parts = onward(second_last, len(near[1]), [far], axis)
+    third_parts = onward(second_round, len(near[1]), [far], axis)
     third_round = send_both(third_parts, axis)
-    third_last = [after(part, jacobian_line[-1]) for part in third_round]
-    factor_parts = onward(third_last, len(far[1]), [], axis)
+    factor_parts = onward(third_round, len(far[1]), [], axis)
     factor_across = send_both(factor_parts, axis)
 
-    near, far = j_near, j_far
+    jacobian_line = [after(jacobian, *second_parts)]
+    for mask in masks_of(axis):
+        jacobian_line.append(sent(joined(*jacobian_line), axis, mask))
+    near, far = joined(*jacobian_line[1:-1]), jacobian_line[-1]
     near_round = around(near, axis)
     near_last = [after(part, *factor_parts) for part in near_round]
     far_parts = onward(near_last, len(near[1]), [far], axis)
@@ -97,20 +104,24 @@
     return arrived + [*near_round, *far_round], list(far_across), right_side
 
 
-def pack(diag_inv, lower, jacobian):
+def pack(diag_inv, lower, jacobian, spare):
     supers, rows, size = diag_inv.shape
+    kept = 3 * supers - spare
 
     def kernel(diag_ref, lower_ref, jacobian_ref, factor_ref, blocks_ref, own_ref):
+        def block(q):
+            return jacobian_ref[q // 3, :, q % 3 * size : (q % 3 + 1) * size]
+
         for s in range(supers):
             factor_ref[s] = own_ref[s] = diag_ref[s]
             factor_ref[supers + s] = own_ref[supers + s] = lower_ref[s]
-            for c in range(3):
-                block = jacobian_ref[s, :, c * size : (c + 1) * size]
-                blocks_ref[3 * s + c] = own_ref[2 * supers + 3 * s + c] = block
+        for k in range(kept):
+            value = jnp.where(lax.axis_index("node") == 0, block(k + 1), block(k)) if spare else block(k)
+            blocks_ref[k] = own_ref[2 * supers + k] = value
 
     return pl.pallas_call(
         kernel,
-        out_shape=shapes([(count * supers, rows, size) for count in (2, 3, 5)]),
+        out_shape=shapes([(count, rows, size) for count in (2 * supers, kept, 2 * supers + kept)]),
         in_specs=[VMEM] * 3,
         out_specs=[VMEM] * 3,
         name="pack",
@@ -177,6 +188,19 @@
     return weights_ref[pl.ds(s * bands + row // (size // bands), 1), :]
 
 
+def cuts_of(size):
+    third = -(-4 * size // 24) * 8
+    return [0, third, 2 * third, 4 * size]
+
+
+def parts_of(i, size):
+    cuts = cuts_of(size)
+    for k, (first, last) in enumerate(zip(cuts, cuts[1:])):
+        begin, end = max(first, i * size), min(last, (i + 1) * size)
+        if begin < end:
+            yield k, begin - first, begin - i * size, end - i * size
+
+
 def solve(arrays, places, relative, right_side, weights, nodes, supers, size):
     columns = right_side.shape[1]
     extra = 0 if nodes == 1 else 1 if nodes == 2 else 2
@@ -189,7 +213,7 @@
         piece_refs = refs[2 : 2 + n]
         sol_ref = refs[2 + n]
         extra_refs = refs[3 + n : 3 + n + extra]
-        down_ref, up_ref, panels, forward = refs[3 + n + extra :]
+        *leaving_refs, panels, forward = refs[3 + n + extra :]
         for owner, blocks in places.items():
             row = row_of(owner, rows, relative)
             for block, (i, at) in blocks.items():
@@ -236,21 +260,27 @@
         if nodes == 2:
             upper = index == 1
             span = supers * size
-            down_ref[0] = jnp.where(upper, entering[:, :columns], forward[supers - 1, :, :columns])
-            down_ref[1] = entering[:, columns:]
-            up_ref[0] = jnp.where(upper, sol_ref[:size, :], sol_ref[span - size :, :])
-            up_ref[1] = jnp.where(upper, extra_refs[0][:size, :], extra_refs[0][span - size :, :])
+            letters = [
+                jnp.where(upper, entering[:, :columns], forward[supers - 1, :, :columns]),
+                entering[:, columns:],
+                jnp.where(upper, sol_ref[:size, :], sol_ref[span - size :, :]),
+                jnp.where(upper, extra_refs[0][:size, :], extra_refs[0][span - size :, :]),
+            ]
+            for i, letter in enumerate(letters):
+                for k, row, begin, end in parts_of(i, size):
+                    leaving_refs[k][row : row + end - begin, :] = letter[begin:end]
         else:
-            down_ref[...] = forward[supers - 1]
-            up_ref[...] = entering if nodes > 1 else forward[0]
+            leaving_refs[0][...] = forward[supers - 1]
+            leaving_refs[1][...] = entering if nodes > 1 else forward[0]
 
     span = supers * size
-    leaving = (2, size, columns) if nodes == 2 else (size, width)
+    cuts = cuts_of(size)
+    leaving = [(e - b, columns) for b, e in zip(cuts, cuts[1:])] if nodes == 2 else [(size, width)] * 2
     out = pl.pallas_call(
         kernel,
-        out_shape=shapes([(span, columns)] + [(span, size)] * extra + [leaving] * 2),
+        out_shape=shapes([(span, columns)] + [(span, size)] * extra + leaving),
         in_specs=[VMEM] * (2 + n),
-        out_specs=[VMEM] * (3 + extra),
+        out_specs=[VMEM] * (1 + extra + len(leaving)),
         scratch_shapes=[
             pltpu.VMEM((2 * supers, size, size), jnp.float32),
             pltpu.VMEM((supers, size, width), jnp.float32),
@@ -261,18 +291,25 @@
         ),
         name="solve",
     )(weights, right_side, *arrays)
-    return out[0], out[1 : 1 + extra], out[1 + extra], out[2 + extra]
-
-
-def finish(sol, part, own_mail, mail, beside_mail, supers):
+    return out[0], out[1 : 1 + extra], out[1 + extra :]
+
+
+def finish(sol, part, own_mail, mail, supers):
     span, columns = sol.shape
     size = span // supers
-
-    def kernel(sol_ref, part_ref, own_ref, mail_ref, beside_ref, out_ref, high_ref, low_ref, held, sem):
+    n = len(mail)
+
+    def kernel(sol_ref, part_ref, *refs):
+        own_refs, mail_refs, (out_ref, high_ref, low_ref, held, sem) = refs[:n], refs[n : 2 * n], refs[2 * n :]
+
+        def letter(piece_refs, i):
+            parts = [piece_refs[k][row : row + end - begin, :] for k, row, begin, end in parts_of(i, size)]
+            return jnp.concatenate(parts, axis=0)
+
         lower_one = lax.axis_index("node") == 0
-        down = jnp.where(lower_one, own_ref[0], mail_ref[0])
-        offset = jnp.where(lower_one, mail_ref[0], own_ref[0])
-        matrix = jnp.where(lower_one, mail_ref[1], own_ref[1])
+        down = jnp.where(lower_one, letter(own_refs, 0), letter(mail_refs, 0))
+        offset = jnp.where(lower_one, letter(mail_refs, 0), letter(own_refs, 0))
+        matrix = jnp.where(lower_one, letter(mail_refs, 1), letter(own_refs, 1))
         up = offset + product(split(matrix), split(down))
         mine = split(jnp.where(lower_one, up, down))
         other = split(jnp.where(lower_one, down, up))
@@ -289,7 +326,7 @@
             )
             copies[-1].start()
             window(at + size, value)
-        beside = beside_ref[0] + product(split(beside_ref[1]), other)
+        beside = letter(mail_refs, 2) + product(split(letter(mail_refs, 3)), other)
         window(0, jnp.where(lower_one, 0.0, beside))
         window(size + span, jnp.where(lower_one, beside, 0.0))
         for copy in copies:
@@ -299,7 +336,7 @@
     return pl.pallas_call(
         kernel,
         out_shape=shapes([(span, columns)]) + [windows, windows],
-        in_specs=[VMEM] * 5,
+        in_specs=[VMEM] * (2 + 2 * n),
         out_specs=[ANY, VMEM, VMEM],
         scratch_shapes=[pltpu.VMEM((span, columns), jnp.float32), pltpu.SemaphoreType.DMA((supers,))],
         compiler_params=pltpu.CompilerParams(vmem_limit_bytes=VMEM_LIMIT),
@@ -307,7 +344,7 @@
             flops=(span + 2 * size) * size * columns, bytes_accessed=span * columns, transcendentals=0
         ),
         name="finish",
-    )(sol, part, own_mail, mail, beside_mail)
+    )(sol, part, *own_mail, *mail)
 
 
 def split_windows(sol, before, after):
@@ -323,7 +360,7 @@
     return pl.pallas_call(kernel, out_shape=[windows, windows], name="windows")(sol, before, after)
 
 
-def subtract_product(arrays, places, relative, right_side, high, low, weights, supers, size, base=None):
+def subtract_product(arrays, places, relative, right_side, high, low, weights, supers, size, spare, base=None):
     span, columns = right_side.shape
     wide = 3 * size
     n = len(arrays)
@@ -336,6 +373,15 @@
         out_ref, held, sem = refs[4 + extra + n :]
         copies = []
 
+        def block_of(blocks, q):
+            def held_as(k):
+                if not 0 <= k < 3 * supers - spare:
+                    return jnp.zeros((rows, size), jnp.float32)
+                i, at = blocks[k]
+                return piece_refs[i][at]
+
+            return jnp.where(lax.axis_index("node") == 0, held_as(q - 1), held_as(q)) if spare else held_as(q)
+
         def write(source, target):
             copies.append(pltpu.make_async_copy(source, target, sem.at[len(copies)]))
             copies[-1].start()
@@ -344,7 +390,7 @@
             bands, starts = [], []
             for owner, blocks in places.items():
                 row = row_of(owner, rows, relative)
-                band = [piece_refs[i][at] for i, at in (blocks[3 * s + c] for c in range(3))]
+                band = [block_of(blocks, 3 * s + c) for c in range(3)]
                 bands.append(jnp.concatenate(band, axis=1) * weights_of(weights_ref, s, row, supers, size))
                 starts.append(s * size + row if not relative else pl.multiple_of(s * size + row, rows))
             window = pl.ds(s * size, wide)
@@ -392,7 +438,8 @@
     def blocks_of(array, begin):
         return array, [(0, begin + block) for block in range(array.shape[0])]
 
-    factor_own, jacobian_own, own = pack(diag_inv, lower, jacobian)
+    spare = 1 if nodes == 2 else 0
+    factor_own, jacobian_own, own = pack(diag_inv, lower, jacobian, spare)
     factor_own = blocks_of(factor_own, 0)
     jacobian_own = blocks_of(jacobian_own, 2 * supers)
     own = blocks_of(own, 0)
@@ -404,20 +451,21 @@
         arrived, last, late = gather_whole(own, "rhs"), [], right_side
     factor = places_of(arrived, 0, 2 * supers)
     jacobians, places = places_of(arrived, 2 * supers, len(own[1]))
-    whole = {owner: blocks for owner, blocks in places.items() if len(blocks) == 3 * supers}
+    whole = {owner: blocks for owner, blocks in places.items() if len(blocks) == 3 * supers - spare}
     partial = set(places) - set(whole)
 
     factor_weights, jacobian_weights = widened([factor_pattern, jacobian_pattern], [size, 3 * size])
-    sol, parts, down, up = solve(*factor, relative, late, factor_weights, nodes, supers, size)
+    sol, parts, leaving = solve(*factor, relative, late, factor_weights, nodes, supers, size)
     if nodes == 2:
-        mail = [lax.ppermute(letter, "node", [(0, 1), (1, 0)]) for letter in (down, up)]
-        sol, high, low = finish(sol, parts[0], down, *mail, supers)
+        mail = [lax.ppermute(piece, "node", [(0, 1), (1, 0)]) for piece in leaving]
+        sol, high, low = finish(sol, parts[0], leaving, mail, supers)
     else:
         beneath = beyond = jnp.zeros((size, columns), jnp.float32)
         if nodes > 1:
             upwards = [(i, i + 1) for i in range(nodes - 1)]
             downwards = [(i + 1, i) for i in range(nodes - 1)]
             below = above = beneath
+            down, up = leaving
             for _ in range(nodes - 1):
                 below = lax.ppermute(
                     down[:, :columns] + dot(down[:, columns : columns + size], below), "node", upwards
@@ -438,6 +486,7 @@
         weights=jacobian_weights,
         supers=supers,
         size=size,
+        spare=spare,
     )
     residual = subtract(jacobians, whole)
     if last:

time: 66.1 us -> 58 us (0.88)
  starting transfers between devices: 28.7 us -> 24.3 us
  waiting for transfers between devices: 22.1 us -> 18 us
    ppermute x20 -> x19, starting transfers between devices: 28.1 us -> 23.7 us  [sent(): lax.ppermute(array, axis, [(i, i ^ mask) for i in range(lax.axis_size(axi...]
    ppermute x20 -> x19, waiting for transfers between devices: 22.1 us -> 18 us  [sent(): lax.ppermute(array, axis, [(i, i ^ mask) for i in range(lax.axis_size(axi...]
  transfers between devices with their start and end apart: 22 -> 22, of which waited for: 14 -> 12; matrix products, arithmetic and copies ran while one was open for 0% -> 0% of each run, Pallas kernels for 15% -> 17%
where the time goes in v15:
time: 58 us; the launch traced here: 57.8 us
  starting transfers between devices  24.3 us (42%)
  waiting for transfers between devices  18 us (31%)
  Pallas kernels  13.4 us (23%)
  local copies, waits for them, and re-layouts  1.1 us (2%)
  between operations  0.83 us (1%)
    ppermute x19, starting transfers between devices, sent(): lax.ppermute(array, axis, [(i, i ^ mask) for i in range(lax.axis_size(axi...  23.7 us
    ppermute x19, waiting for transfers between devices, sent(): lax.ppermute(array, axis, [(i, i ^ mask) for i in range(lax.axis_size(axi...  18 us
    pallas_call x1, Pallas kernels, solve(): pl.pallas_call(kernel, out_shape=shapes([(span, columns)] + [(span, size)...  4.97 us
    pallas_call x2, Pallas kernels, subtract_product(): pl.pallas_call(kernel, out_shape=shapes([(span, columns)])[0], in_specs=[...  3.82 us
    pallas_call x1, Pallas kernels, pack(): pl.pallas_call(kernel, out_shape=shapes([(count, rows, size) for count in...  1.86 us
    pallas_call x1, Pallas kernels, finish(): pl.pallas_call(kernel, out_shape=shapes([(span, columns)]) + [windows, wi...  1.77 us
  transfers between devices with their start and end apart: 22, of which 12 were waited for; matrix products, arithmetic and copies ran while one was open for 0% of the time, Pallas kernels for 17%

profile of v15, /device:TPU:0, one launch (start us, length us, event | category | flops | bytes accessed | tf_op | source)
XLA Modules:
  0.0 57.8 jit_solution(565547743194471584)
XLA Ops:
  0.6 1.9 %pack.1 = (f32[8,16,256]{2,1,0:T(8,128)}, f32[11,16,256]{2,1,0:T(8,128)}, f32[19,16,256]{2,1,0:T(8,128)}) custom-call(f32[4,16,256]{2,1,0:T(8,128)} %diag_ref.1, f32[4,16,256]{2,1,0:T(8,128)} %lower_ref.1, f32[4,16,768]{2,1,0:T(8,128)} %jacobian_ref.1), custom_call_target="tpu_custom_call" | custom-call | tf_op jit(solution)/shard_map/pack/pallas_call | solution.py:122
  2.5 3.0 %collective-permute-start.2 = (f32[19,16,256]{2,1,0:T(8,128)}, f32[19,16,256]{2,1,0:T(8,128)S(1)}, u32[]{:S(2)}, u32[]{:S(2)}) collective-permute-start(f32[19,16,256]{2,1,0:T(8,128)} %get-tuple-element.22.refs_2_.refs_4_), channel_id=1, source_target_pairs={{0,4},{2,6},{4,0},{6,2},{8,12},{10,14},{12,8},{14,10},{16,20},{18,... | collective-permute-start | bytes 933896 | tf_op jit(solution)/shard_map/ppermute | solution.py:46
  5.5 1.5 %collective-permute-start.3 = (f32[19,16,256]{2,1,0:T(8,128)}, f32[19,16,256]{2,1,0:T(8,128)S(1)}, u32[]{:S(2)}, u32[]{:S(2)}) collective-permute-start(f32[19,16,256]{2,1,0:T(8,128)} %get-tuple-element.22.refs_2_.refs_4_), channel_id=1, source_target_pairs={{0,2},{2,0},{4,6},{6,4},{8,10},{10,8},{12,14},{14,12},{16,18},{18,... | collective-permute-start | bytes 933896 | tf_op jit(solution)/shard_map/ppermute | solution.py:46
  7.0 3.6 %collective-permute-start = (f32[8,16,256]{2,1,0:T(8,128)}, f32[8,16,256]{2,1,0:T(8,128)S(1)}, u32[]{:S(2)}, u32[]{:S(2)}) collective-permute-start(f32[8,16,256]{2,1,0:T(8,128)} %get-tuple-element.21), channel_id=1, source_target_pairs={{0,24},{2,26},{4,28},{6,30},{8,16},{10,18},{12,20},{14,22},{16,8},... | collective-permute-start | bytes 393224 | tf_op jit(solution)/shard_map/ppermute | solution.py:46
  10.6 2.5 %collective-permute-done.2.refs_7_.refs_8_ = f32[19,16,256]{2,1,0:T(8,128)S(1)} collective-permute-done((f32[19,16,256]{2,1,0:T(8,128)}, f32[19,16,256]{2,1,0:T(8,128)S(1)}, u32[]{:S(2)}, u32[]{:S(2)}) %collective-permute-start.2) | collective-permute-done | bytes 311328 | tf_op jit(solution)/shard_map/ppermute | solution.py:46
  13.0 2.1 %collective-permute-done.refs_3_ = f32[8,16,256]{2,1,0:T(8,128)S(1)} collective-permute-done((f32[8,16,256]{2,1,0:T(8,128)}, f32[8,16,256]{2,1,0:T(8,128)S(1)}, u32[]{:S(2)}, u32[]{:S(2)}) %collective-permute-start) | collective-permute-done | bytes 131104 | tf_op jit(solution)/shard_map/ppermute | solution.py:46
  15.2 1.4 %collective-permute-done.1.refs_4_ = f32[8,16,256]{2,1,0:T(8,128)S(1)} collective-permute-done((f32[8,16,256]{2,1,0:T(8,128)}, f32[8,16,256]{2,1,0:T(8,128)S(1)}, u32[]{:S(2)}, u32[]{:S(2)}) %collective-permute-start.1) | collective-permute-done | bytes 131104 | tf_op jit(solution)/shard_map/ppermute | solution.py:46
  18.2 2.1 %collective-permute-start.4 = (f32[11,16,256]{2,1,0:T(8,128)S(1)}, f32[11,16,256]{2,1,0:T(8,128)S(1)}, u32[]{:S(2)}, u32[]{:S(2)}) collective-permute-start(f32[11,16,256]{2,1,0:T(8,128)S(1)} %copy-done.6), channel_id=1, source_target_pairs={{0,24},{2,26},{4,28},{6,30},{8,16},{10,18},{12,20},{14,22},{16,8},... | collective-permute-start | bytes 540680 | tf_op jit(solution)/shard_map/ppermute | solution.py:46
  20.3 6.4 %collective-permute-done.4.refs_5_ = f32[11,16,256]{2,1,0:T(8,128)S(1)} collective-permute-done((f32[11,16,256]{2,1,0:T(8,128)S(1)}, f32[11,16,256]{2,1,0:T(8,128)S(1)}, u32[]{:S(2)}, u32[]{:S(2)}) %collective-permute-start.4) | collective-permute-done | bytes 180256 | tf_op jit(solution)/shard_map/ppermute | solution.py:46
  26.7 1.7 %collective-permute-start.5 = (f32[22,16,256]{2,1,0:T(8,128)S(1)}, f32[22,16,256]{2,1,0:T(8,128)S(1)}, u32[]{:S(2)}, u32[]{:S(2)}) collective-permute-start(f32[22,16,256]{2,1,0:T(8,128)S(1)} %pad_maximum_fusion.4), channel_id=1, source_target_pairs={{0,8},{2,10},{4,12},{6,14},{8,0},{10,2},{12,4},{14,6},{16,24},{18,... | collective-permute-start | bytes 1081352 | tf_op jit(solution)/shard_map/ppermute | solution.py:46
  28.5 1.0 %collective-permute-start.9 = (f32[16,16,256]{2,1,0:T(8,128)S(1)}, f32[16,16,256]{2,1,0:T(8,128)S(1)}, u32[]{:S(2)}, u32[]{:S(2)}) collective-permute-start(f32[16,16,256]{2,1,0:T(8,128)S(1)} %get-tuple-element.37), channel_id=1, source_target_pairs={{0,4},{2,6},{4,0},{6,2},{8,12},{10,14},{12,8},{14,10},{16,20},{18,... | collective-permute-start | bytes 786440 | tf_op jit(solution)/shard_map/ppermute | solution.py:46
  29.6 1.2 %collective-permute-start.11 = (f32[16,16,256]{2,1,0:T(8,128)S(1)}, f32[16,16,256]{2,1,0:T(8,128)S(1)}, u32[]{:S(2)}, u32[]{:S(2)}) collective-permute-start(f32[16,16,256]{2,1,0:T(8,128)S(1)} %get-tuple-element.36), channel_id=1, source_target_pairs={{0,2},{2,0},{4,6},{6,4},{8,10},{10,8},{12,14},{14,12},{16,18},{18,... | collective-permute-start | bytes 786440 | tf_op jit(solution)/shard_map/ppermute | solution.py:46
  31.6 1.0 %collective-permute-start.6 = (f32[11,16,256]{2,1,0:T(8,128)S(1)}, f32[11,16,256]{2,1,0:T(8,128)S(1)}, u32[]{:S(2)}, u32[]{:S(2)}) collective-permute-start(f32[11,16,256]{2,1,0:T(8,128)S(1)} %collective-permute-done.4.refs_5_), channel_id=1, source_target_pairs={{0,4},{2,6},{4,0},{6,2},{8,12},{10,14},{12,8},{14,10},{16,20},{18,... | collective-permute-start | bytes 540680 | tf_op jit(solution)/shard_map/ppermute | solution.py:46
  32.7 0.9 %widened.1 = (f32[16,256]{1,0:T(8,128)S(1)}, f32[16,768]{1,0:T(8,128)S(1)}) custom-call(s32[4,4,4]{2,1,0:T(4,128)S(1)} %copy-done.4, s32[4,4,12]{2,1,0:T(4,128)S(1)} %copy-done.5), custom_call_target="tpu_custom_call" | custom-call | tf_op jit(solution)/shard_map/widened/pallas_call | solution.py:176
  33.6 3.1 %collective-permute-done.9.refs_11_ = f32[16,16,256]{2,1,0:T(8,128)S(1)} collective-permute-done((f32[16,16,256]{2,1,0:T(8,128)S(1)}, f32[16,16,256]{2,1,0:T(8,128)S(1)}, u32[]{:S(2)}, u32[]{:S(2)}) %collective-permute-start.9) | collective-permute-done | bytes 262176 | tf_op jit(solution)/shard_map/ppermute | solution.py:46
  36.7 1.1 %collective-permute-start.13 = (f32[4,16,256]{2,1,0:T(8,128)S(1)}, f32[4,16,256]{2,1,0:T(8,128)S(1)}, u32[]{:S(2)}, u32[]{:S(2)}) collective-permute-start(f32[4,16,256]{2,1,0:T(8,128)S(1)} %slice.43), channel_id=1, source_target_pairs={{0,2},{2,0},{4,6},{6,4},{8,10},{10,8},{12,14},{14,12},{16,18},{18,... | collective-permute-start | bytes 196616 | tf_op jit(solution)/shard_map/ppermute | solution.py:46
  40.3 1.2 %collective-permute-start.19 = (f32[27,16,256]{2,1,0:T(8,128)S(1)}, f32[27,16,256]{2,1,0:T(8,128)S(1)}, u32[]{:S(2)}, u32[]{:S(2)}) collective-permute-start(f32[27,16,256]{2,1,0:T(8,128)S(1)} %pad_maximum_fusion.1), channel_id=1, source_target_pairs={{0,4},{2,6},{4,0},{6,2},{8,12},{10,14},{12,8},{14,10},{16,20},{18,... | collective-permute-start | bytes 1327112 | tf_op jit(solution)/shard_map/ppermute | solution.py:46
  41.5 1.3 %collective-permute-start.18 = (f32[28,16,256]{2,1,0:T(8,128)S(1)}, f32[28,16,256]{2,1,0:T(8,128)S(1)}, u32[]{:S(2)}, u32[]{:S(2)}) collective-permute-start(f32[28,16,256]{2,1,0:T(8,128)S(1)} %pad_maximum_fusion), channel_id=1, source_target_pairs={{0,2},{2,0},{4,6},{6,4},{8,10},{10,8},{12,14},{14,12},{16,18},{18,... | collective-permute-start | bytes 1376264 | tf_op jit(solution)/shard_map/ppermute | solution.py:46
  42.9 5.0 %solve.1 = (f32[1024,256]{1,0:T(8,128)S(1)}, f32[1024,256]{1,0:T(8,128)S(1)}, f32[344,256]{1,0:T(8,128)S(1)}, f32[344,256]{1,0:T(8,128)S(1)}, f32[336,256]{1,0:T(8,128)S(1)}) custom-call(f32[16,256]{1,0:T(8,128)S(1)} %get-tuple-element.19.refs_0_, f32[1024,256]{1,0:T(8,128)S(1)} %copy-done, f32[19,16,256]{2,1,0:T(8,128)S(1)} %copy-done.3, ...), custom_call_target="tpu_custom_call" | custom-call | flops 2147483648 | bytes 262144 | tf_op jit(solution)/shard_map/solve/pallas_call | solution.py:279
  48.8 1.2 %collective-permute-start.20 = (f32[11,16,256]{2,1,0:T(8,128)S(1)}, f32[11,16,256]{2,1,0:T(8,128)S(1)}, u32[]{:S(2)}, u32[]{:S(2)}) collective-permute-start(f32[11,16,256]{2,1,0:T(8,128)S(1)} %slice.46), channel_id=1, source_target_pairs={{0,2},{2,0},{4,6},{6,4},{8,10},{10,8},{12,14},{14,12},{16,18},{18,... | collective-permute-start | bytes 540680 | tf_op jit(solution)/shard_map/ppermute | solution.py:46
  50.1 1.1 %collective-permute-start.21 = (f32[11,16,256]{2,1,0:T(8,128)S(1)}, f32[11,16,256]{2,1,0:T(8,128)S(1)}, u32[]{:S(2)}, u32[]{:S(2)}) collective-permute-start(f32[11,16,256]{2,1,0:T(8,128)S(1)} %slice.47), channel_id=1, source_target_pairs={{0,4},{2,6},{4,0},{6,2},{8,12},{10,14},{12,8},{14,10},{16,20},{18,... | collective-permute-start | bytes 540680 | tf_op jit(solution)/shard_map/ppermute | solution.py:46
  51.2 1.8 %finish.1 = (f32[1024,256]{1,0:T(8,128)}, bf16[1536,256]{1,0:T(8,128)(2,1)S(1)}, bf16[1536,256]{1,0:T(8,128)(2,1)S(1)}) custom-call(f32[1024,256]{1,0:T(8,128)S(1)} %get-tuple-element.27.sol_ref, f32[1024,256]{1,0:T(8,128)S(1)} %get-tuple-element.28.part_ref, f32[344,256]{1,0:T(8,128)S(1)} %get-tuple-element.29.refs_0_, ...), custom_call_target="tpu_custom_call" | custom-call | flops 100663296 | bytes 262144 | tf_op jit(solution)/shard_map/finish/pallas_call | solution.py:336
  53.0 2.3 %residual.1.refs_4_ = f32[1024,256]{1,0:T(8,128)} custom-call(f32[16,768]{1,0:T(8,128)S(1)} %get-tuple-element.33.refs_0_, f32[1024,256]{1,0:T(8,128)S(1)} %copy-done, bf16[1536,256]{1,0:T(8,128)(2,1)S(1)} %get-tuple-element.34.refs_2_, bf16[1536,256]{1,0:T(8,128)(2,1)S(1)} %get-tuple-element.35.refs_3_, f32[19,16,256]{2,1,0:T(8,128)S(1)} %copy-done.3, ...), custom_call_target="tpu_custom_call" | custom-call | flops 1056964608 | bytes 5505024 | tf_op jit(solution)/shard_map/residual/pallas_call | solution.py:410
  56.3 1.6 %residual_rest.1 = f32[1024,256]{1,0:T(8,128)} custom-call(f32[16,768]{1,0:T(8,128)S(1)} %get-tuple-element.33.refs_0_, f32[1024,256]{1,0:T(8,128)S(1)} %copy-done, bf16[1536,256]{1,0:T(8,128)(2,1)S(1)} %get-tuple-element.34.refs_2_, bf16[1536,256]{1,0:T(8,128)(2,1)S(1)} %get-tuple-element.35.refs_3_, ...), custom_call_target="tpu_custom_call", output_to_operand_aliasing={{}: (4, {})} | custom-call | flops 150994944 | bytes 786432 | tf_op jit(solution)/shard_map/residual_rest/pallas_call | solution.py:410
  (57 shorter events, 7.3 us)
Async XLA Ops:
  2.5 10.5 %collective-permute-start.2 = (f32[19,16,256]{2,1,0:T(8,128)}, f32[19,16,256]{2,1,0:T(8,128)S(1)}, u32[]{:S(2)}, u32[]{:S(2)}) collective-permute-start(f32[19,16,256]{2,1,0:T(8,128)} %get-tuple-element.22.refs_2_.refs_4_), channel_id=1, source_target_pairs={{0,4},{2,6},{4,0},{6,2},{8,12},{10,14},{12,8},{14,10},{16,20},{18,... | collective-permute-start | bytes 933896 | tf_op jit(solution)/shard_map/ppermute | solution.py:46
  5.5 11.8 %collective-permute-start.3 = (f32[19,16,256]{2,1,0:T(8,128)}, f32[19,16,256]{2,1,0:T(8,128)S(1)}, u32[]{:S(2)}, u32[]{:S(2)}) collective-permute-start(f32[19,16,256]{2,1,0:T(8,128)} %get-tuple-element.22.refs_2_.refs_4_), channel_id=1, source_target_pairs={{0,2},{2,0},{4,6},{6,4},{8,10},{10,8},{12,14},{14,12},{16,18},{18,... | collective-permute-start | bytes 933896 | tf_op jit(solution)/shard_map/ppermute | solution.py:46
  7.0 8.2 %collective-permute-start = (f32[8,16,256]{2,1,0:T(8,128)}, f32[8,16,256]{2,1,0:T(8,128)S(1)}, u32[]{:S(2)}, u32[]{:S(2)}) collective-permute-start(f32[8,16,256]{2,1,0:T(8,128)} %get-tuple-element.21), channel_id=1, source_target_pairs={{0,24},{2,26},{4,28},{6,30},{8,16},{10,18},{12,20},{14,22},{16,8},... | collective-permute-start | bytes 393224 | tf_op jit(solution)/shard_map/ppermute | solution.py:46
  10.6 6.1 %collective-permute-start.1 = (f32[8,16,256]{2,1,0:T(8,128)}, f32[8,16,256]{2,1,0:T(8,128)S(1)}, u32[]{:S(2)}, u32[]{:S(2)}) collective-permute-start(f32[8,16,256]{2,1,0:T(8,128)} %get-tuple-element.21), channel_id=1, source_target_pairs={{0,8},{2,10},{4,12},{6,14},{8,0},{10,2},{12,4},{14,6},{16,24},{18,... | collective-permute-start | bytes 393224 | tf_op jit(solution)/shard_map/ppermute | solution.py:46
  16.6 11.8 %collective-permute-start.8 = (f32[26,16,256]{2,1,0:T(8,128)S(1)}, f32[26,16,256]{2,1,0:T(8,128)S(1)}, u32[]{:S(2)}, u32[]{:S(2)}) collective-permute-start(f32[26,16,256]{2,1,0:T(8,128)S(1)} %pad_maximum_fusion.2), channel_id=1, source_target_pairs={{0,2},{2,0},{4,6},{6,4},{8,10},{10,8},{12,14},{14,12},{16,18},{18,... | collective-permute-start | bytes 1277960 | tf_op jit(solution)/shard_map/ppermute | solution.py:46
  17.3 11.1 %collective-permute-start.10 = (f32[25,16,256]{2,1,0:T(8,128)S(1)}, f32[25,16,256]{2,1,0:T(8,128)S(1)}, u32[]{:S(2)}, u32[]{:S(2)}) collective-permute-start(f32[25,16,256]{2,1,0:T(8,128)S(1)} %pad_maximum_fusion.3), channel_id=1, source_target_pairs={{0,4},{2,6},{4,0},{6,2},{8,12},{10,14},{12,8},{14,10},{16,20},{18,... | collective-permute-start | bytes 1228808 | tf_op jit(solution)/shard_map/ppermute | solution.py:46
  18.2 8.5 %collective-permute-start.4 = (f32[11,16,256]{2,1,0:T(8,128)S(1)}, f32[11,16,256]{2,1,0:T(8,128)S(1)}, u32[]{:S(2)}, u32[]{:S(2)}) collective-permute-start(f32[11,16,256]{2,1,0:T(8,128)S(1)} %copy-done.6), channel_id=1, source_target_pairs={{0,24},{2,26},{4,28},{6,30},{8,16},{10,18},{12,20},{14,22},{16,8},... | collective-permute-start | bytes 540680 | tf_op jit(solution)/shard_map/ppermute | solution.py:46
  20.3 8.1 %collective-permute-start.7 = (f32[8,16,256]{2,1,0:T(8,128)S(1)}, f32[8,16,256]{2,1,0:T(8,128)S(1)}, u32[]{:S(2)}, u32[]{:S(2)}) collective-permute-start(f32[8,16,256]{2,1,0:T(8,128)S(1)} %collective-permute-done.refs_3_), channel_id=1, source_target_pairs={{0,8},{2,10},{4,12},{6,14},{8,0},{10,2},{12,4},{14,6},{16,24},{18,... | collective-permute-start | bytes 393224 | tf_op jit(solution)/shard_map/ppermute | solution.py:46
  26.7 13.5 %collective-permute-start.5 = (f32[22,16,256]{2,1,0:T(8,128)S(1)}, f32[22,16,256]{2,1,0:T(8,128)S(1)}, u32[]{:S(2)}, u32[]{:S(2)}) collective-permute-start(f32[22,16,256]{2,1,0:T(8,128)S(1)} %pad_maximum_fusion.4), channel_id=1, source_target_pairs={{0,8},{2,10},{4,12},{6,14},{8,0},{10,2},{12,4},{14,6},{16,24},{18,... | collective-permute-start | bytes 1081352 | tf_op jit(solution)/shard_map/ppermute | solution.py:46
  28.5 4.2 %copy-start.4 = (s32[4,4,4]{2,1,0:T(4,128)S(1)}, s32[4,4,4]{2,1,0:T(4,128)}, u32[]{:S(2)}) copy-start(s32[4,4,4]{2,1,0:T(4,128)} %refs_0_.1) | copy-start | bytes 772
  28.5 8.1 %collective-permute-start.9 = (f32[16,16,256]{2,1,0:T(8,128)S(1)}, f32[16,16,256]{2,1,0:T(8,128)S(1)}, u32[]{:S(2)}, u32[]{:S(2)}) collective-permute-start(f32[16,16,256]{2,1,0:T(8,128)S(1)} %get-tuple-element.37), channel_id=1, source_target_pairs={{0,4},{2,6},{4,0},{6,2},{8,12},{10,14},{12,8},{14,10},{16,20},{18,... | collective-permute-start | bytes 786440 | tf_op jit(solution)/shard_map/ppermute | solution.py:46
  29.6 8.2 %collective-permute-start.11 = (f32[16,16,256]{2,1,0:T(8,128)S(1)}, f32[16,16,256]{2,1,0:T(8,128)S(1)}, u32[]{:S(2)}, u32[]{:S(2)}) collective-permute-start(f32[16,16,256]{2,1,0:T(8,128)S(1)} %get-tuple-element.36), channel_id=1, source_target_pairs={{0,2},{2,0},{4,6},{6,4},{8,10},{10,8},{12,14},{14,12},{16,18},{18,... | collective-permute-start | bytes 786440 | tf_op jit(solution)/shard_map/ppermute | solution.py:46
  30.7 8.3 %collective-permute-start.12 = (f32[11,16,256]{2,1,0:T(8,128)S(1)}, f32[11,16,256]{2,1,0:T(8,128)S(1)}, u32[]{:S(2)}, u32[]{:S(2)}) collective-permute-start(f32[11,16,256]{2,1,0:T(8,128)S(1)} %collective-permute-done.4.refs_5_), channel_id=1, source_target_pairs={{0,2},{2,0},{4,6},{6,4},{8,10},{10,8},{12,14},{14,12},{16,18},{18,... | collective-permute-start | bytes 540680 | tf_op jit(solution)/shard_map/ppermute | solution.py:46
  31.6 7.9 %collective-permute-start.6 = (f32[11,16,256]{2,1,0:T(8,128)S(1)}, f32[11,16,256]{2,1,0:T(8,128)S(1)}, u32[]{:S(2)}, u32[]{:S(2)}) collective-permute-start(f32[11,16,256]{2,1,0:T(8,128)S(1)} %collective-permute-done.4.refs_5_), channel_id=1, source_target_pairs={{0,4},{2,6},{4,0},{6,2},{8,12},{10,14},{12,8},{14,10},{16,20},{18,... | collective-permute-start | bytes 540680 | tf_op jit(solution)/shard_map/ppermute | solution.py:46
  36.7 6.1 %collective-permute-start.13 = (f32[4,16,256]{2,1,0:T(8,128)S(1)}, f32[4,16,256]{2,1,0:T(8,128)S(1)}, u32[]{:S(2)}, u32[]{:S(2)}) collective-permute-start(f32[4,16,256]{2,1,0:T(8,128)S(1)} %slice.43), channel_id=1, source_target_pairs={{0,2},{2,0},{4,6},{6,4},{8,10},{10,8},{12,14},{14,12},{16,18},{18,... | collective-permute-start | bytes 196616 | tf_op jit(solution)/shard_map/ppermute | solution.py:46
  37.8 5.1 %copy-start = (f32[1024,256]{1,0:T(8,128)S(1)}, f32[1024,256]{1,0:T(8,128)}, u32[]{:S(2)}) copy-start(f32[1024,256]{1,0:T(8,128)} %refs_1_.6) | copy-start | bytes 3145732
  37.8 5.1 %collective-permute-start.14 = (f32[4,16,256]{2,1,0:T(8,128)S(1)}, f32[4,16,256]{2,1,0:T(8,128)S(1)}, u32[]{:S(2)}, u32[]{:S(2)}) collective-permute-start(f32[4,16,256]{2,1,0:T(8,128)S(1)} %slice.45), channel_id=1, source_target_pairs={{0,4},{2,6},{4,0},{6,2},{8,12},{10,14},{12,8},{14,10},{16,20},{18,... | collective-permute-start | bytes 196616 | tf_op jit(solution)/shard_map/ppermute | solution.py:46
  40.3 8.5 %collective-permute-start.19 = (f32[27,16,256]{2,1,0:T(8,128)S(1)}, f32[27,16,256]{2,1,0:T(8,128)S(1)}, u32[]{:S(2)}, u32[]{:S(2)}) collective-permute-start(f32[27,16,256]{2,1,0:T(8,128)S(1)} %pad_maximum_fusion.1), channel_id=1, source_target_pairs={{0,4},{2,6},{4,0},{6,2},{8,12},{10,14},{12,8},{14,10},{16,20},{18,... | collective-permute-start | bytes 1327112 | tf_op jit(solution)/shard_map/ppermute | solution.py:46
  41.5 8.5 %collective-permute-start.18 = (f32[28,16,256]{2,1,0:T(8,128)S(1)}, f32[28,16,256]{2,1,0:T(8,128)S(1)}, u32[]{:S(2)}, u32[]{:S(2)}) collective-permute-start(f32[28,16,256]{2,1,0:T(8,128)S(1)} %pad_maximum_fusion), channel_id=1, source_target_pairs={{0,2},{2,0},{4,6},{6,4},{8,10},{10,8},{12,14},{14,12},{16,18},{18,... | collective-permute-start | bytes 1376264 | tf_op jit(solution)/shard_map/ppermute | solution.py:46
  47.9 3.3 %collective-permute-start.15 = (f32[344,256]{1,0:T(8,128)S(1)}, f32[344,256]{1,0:T(8,128)S(1)}, u32[]{:S(2)}, u32[]{:S(2)}) collective-permute-start(f32[344,256]{1,0:T(8,128)S(1)} %get-tuple-element.29.refs_0_), channel_id=1, source_target_pairs={{0,1},{1,0},{2,3},{3,2},{4,5},{5,4},{6,7},{7,6},{8,9},{9,8},{10,11... | collective-permute-start | bytes 1056776 | tf_op jit(solution)/shard_map/ppermute | solution.py:460
  48.0 3.2 %collective-permute-start.16 = (f32[344,256]{1,0:T(8,128)S(1)}, f32[344,256]{1,0:T(8,128)S(1)}, u32[]{:S(2)}, u32[]{:S(2)}) collective-permute-start(f32[344,256]{1,0:T(8,128)S(1)} %get-tuple-element.30.refs_1_), channel_id=1, source_target_pairs={{0,1},{1,0},{2,3},{3,2},{4,5},{5,4},{6,7},{7,6},{8,9},{9,8},{10,11... | collective-permute-start | bytes 1056776 | tf_op jit(solution)/shard_map/ppermute | solution.py:460
  48.5 2.7 %collective-permute-start.17 = (f32[336,256]{1,0:T(8,128)S(1)}, f32[336,256]{1,0:T(8,128)S(1)}, u32[]{:S(2)}, u32[]{:S(2)}) collective-permute-start(f32[336,256]{1,0:T(8,128)S(1)} %get-tuple-element.31.refs_2_), channel_id=1, source_target_pairs={{0,1},{1,0},{2,3},{3,2},{4,5},{5,4},{6,7},{7,6},{8,9},{9,8},{10,11... | collective-permute-start | bytes 1032200 | tf_op jit(solution)/shard_map/ppermute | solution.py:460
  48.8 6.7 %collective-permute-start.20 = (f32[11,16,256]{2,1,0:T(8,128)S(1)}, f32[11,16,256]{2,1,0:T(8,128)S(1)}, u32[]{:S(2)}, u32[]{:S(2)}) collective-permute-start(f32[11,16,256]{2,1,0:T(8,128)S(1)} %slice.46), channel_id=1, source_target_pairs={{0,2},{2,0},{4,6},{6,4},{8,10},{10,8},{12,14},{14,12},{16,18},{18,... | collective-permute-start | bytes 540680 | tf_op jit(solution)/shard_map/ppermute | solution.py:46
  50.1 6.2 %collective-permute-start.21 = (f32[11,16,256]{2,1,0:T(8,128)S(1)}, f32[11,16,256]{2,1,0:T(8,128)S(1)}, u32[]{:S(2)}, u32[]{:S(2)}) collective-permute-start(f32[11,16,256]{2,1,0:T(8,128)S(1)} %slice.47), channel_id=1, source_target_pairs={{0,4},{2,6},{4,0},{6,2},{8,12},{10,14},{12,8},{14,10},{16,20},{18,... | collective-permute-start | bytes 540680 | tf_op jit(solution)/shard_map/ppermute | solution.py:46
  (6 other events, 11.5 us)

commit v16 on v15

--- a/solution.py
+++ b/solution.py
@@ -85,15 +85,15 @@
     near, far = joined(*factor_line[1:-1]), factor_line[-1]
     second_parts = onward(own_round, len(own[1]), [near], axis)
     second_round = send_both(second_parts, axis)
-    third_parts = onward(second_round, len(near[1]), [far], axis)
+    jacobian_line = line_of(after(jacobian, *second_parts), axis)
+    second_last = [after(part, jacobian_line[1]) for part in second_round]
+    third_parts = onward(second_last, len(near[1]), [far], axis)
     third_round = send_both(third_parts, axis)
     factor_parts = onward(third_round, len(far[1]), [], axis)
     factor_across = send_both(factor_parts, axis)
 
-    jacobian_line = [after(jacobian, *second_parts)]
-    for mask in masks_of(axis):
-        jacobian_line.append(sent(joined(*jacobian_line), axis, mask))
-    near, far = joined(*jacobian_line[1:-1]), jacobian_line[-1]
+    half = len(jacobian_line) // 2
+    near, far = joined(*jacobian_line[1:half]), joined(*jacobian_line[half:])
     near_round = around(near, axis)
     near_last = [after(part, *factor_parts) for part in near_round]
     far_parts = onward(near_last, len(near[1]), [far], axis)

time: 58 us -> 59.1 us (1.019)
  waiting for transfers between devices: 18 us -> 19.3 us
    ppermute x19 -> x20, waiting for transfers between devices: 18 us -> 19.3 us  [sent(): lax.ppermute(array, axis, [(i, i ^ mask) for i in range(lax.axis_size(axi...]
    ppermute x19 -> x20, starting transfers between devices: 23.7 us -> 23.6 us  [sent(): lax.ppermute(array, axis, [(i, i ^ mask) for i in range(lax.axis_size(axi...]
  transfers between devices with their start and end apart: 22 -> 23, of which waited for: 12 -> 12; matrix products, arithmetic and copies ran while one was open for 0% -> 0% of each run, Pallas kernels for 17% -> 17%
where the time goes in v16:
time: 59.1 us; the launch traced here: 59 us
  starting transfers between devices  24.2 us (41%)
  waiting for transfers between devices  19.3 us (33%)
  Pallas kernels  13.4 us (23%)
  local copies, waits for them, and re-layouts  1.08 us (2%)
  between operations  0.82 us (1%)
    ppermute x20, starting transfers between devices, sent(): lax.ppermute(array, axis, [(i, i ^ mask) for i in range(lax.axis_size(axi...  23.6 us
    ppermute x20, waiting for transfers between devices, sent(): lax.ppermute(array, axis, [(i, i ^ mask) for i in range(lax.axis_size(axi...  19.3 us
    pallas_call x1, Pallas kernels, solve(): pl.pallas_call(kernel, out_shape=shapes([(span, columns)] + [(span, size)...  4.99 us
    pallas_call x2, Pallas kernels, subtract_product(): pl.pallas_call(kernel, out_shape=shapes([(span, columns)])[0], in_specs=[...  3.81 us
    pallas_call x1, Pallas kernels, pack(): pl.pallas_call(kernel, out_shape=shapes([(count, rows, size) for count in...  1.86 us
    pallas_call x1, Pallas kernels, finish(): pl.pallas_call(kernel, out_shape=shapes([(span, columns)]) + [windows, wi...  1.77 us
  transfers between devices with their start and end apart: 23, of which 12 were waited for; matrix products, arithmetic and copies ran while one was open for 0% of the time, Pallas kernels for 17%

profile of v16, /device:TPU:0, one launch (start us, length us, event | category | flops | bytes accessed | tf_op | source)
XLA Modules:
  0.0 59.0 jit_solution(13616620544118343973)
XLA Ops:
  0.6 1.9 %pack.1 = (f32[8,16,256]{2,1,0:T(8,128)}, f32[11,16,256]{2,1,0:T(8,128)}, f32[19,16,256]{2,1,0:T(8,128)}) custom-call(f32[4,16,256]{2,1,0:T(8,128)} %diag_ref.1, f32[4,16,256]{2,1,0:T(8,128)} %lower_ref.1, f32[4,16,768]{2,1,0:T(8,128)} %jacobian_ref.1), custom_call_target="tpu_custom_call" | custom-call | tf_op jit(solution)/shard_map/pack/pallas_call | solution.py:122
  2.5 3.0 %collective-permute-start.2 = (f32[19,16,256]{2,1,0:T(8,128)}, f32[19,16,256]{2,1,0:T(8,128)S(1)}, u32[]{:S(2)}, u32[]{:S(2)}) collective-permute-start(f32[19,16,256]{2,1,0:T(8,128)} %get-tuple-element.24.refs_2_.refs_4_), channel_id=1, source_target_pairs={{0,4},{2,6},{4,0},{6,2},{8,12},{10,14},{12,8},{14,10},{16,20},{18,... | collective-permute-start | bytes 933896 | tf_op jit(solution)/shard_map/ppermute | solution.py:46
  5.5 1.5 %collective-permute-start.3 = (f32[19,16,256]{2,1,0:T(8,128)}, f32[19,16,256]{2,1,0:T(8,128)S(1)}, u32[]{:S(2)}, u32[]{:S(2)}) collective-permute-start(f32[19,16,256]{2,1,0:T(8,128)} %get-tuple-element.24.refs_2_.refs_4_), channel_id=1, source_target_pairs={{0,2},{2,0},{4,6},{6,4},{8,10},{10,8},{12,14},{14,12},{16,18},{18,... | collective-permute-start | bytes 933896 | tf_op jit(solution)/shard_map/ppermute | solution.py:46
  7.0 3.6 %collective-permute-start = (f32[8,16,256]{2,1,0:T(8,128)}, f32[8,16,256]{2,1,0:T(8,128)S(1)}, u32[]{:S(2)}, u32[]{:S(2)}) collective-permute-start(f32[8,16,256]{2,1,0:T(8,128)} %get-tuple-element.23), channel_id=1, source_target_pairs={{0,24},{2,26},{4,28},{6,30},{8,16},{10,18},{12,20},{14,22},{16,8},... | collective-permute-start | bytes 393224 | tf_op jit(solution)/shard_map/ppermute | solution.py:46
  10.6 2.5 %collective-permute-done.2.refs_7_.refs_9_ = f32[19,16,256]{2,1,0:T(8,128)S(1)} collective-permute-done((f32[19,16,256]{2,1,0:T(8,128)}, f32[19,16,256]{2,1,0:T(8,128)S(1)}, u32[]{:S(2)}, u32[]{:S(2)}) %collective-permute-start.2) | collective-permute-done | bytes 311328 | tf_op jit(solution)/shard_map/ppermute | solution.py:46
  13.0 2.1 %collective-permute-done.refs_3_ = f32[8,16,256]{2,1,0:T(8,128)S(1)} collective-permute-done((f32[8,16,256]{2,1,0:T(8,128)}, f32[8,16,256]{2,1,0:T(8,128)S(1)}, u32[]{:S(2)}, u32[]{:S(2)}) %collective-permute-start) | collective-permute-done | bytes 131104 | tf_op jit(solution)/shard_map/ppermute | solution.py:46
  15.2 1.4 %collective-permute-done.1.refs_4_ = f32[8,16,256]{2,1,0:T(8,128)S(1)} collective-permute-done((f32[8,16,256]{2,1,0:T(8,128)}, f32[8,16,256]{2,1,0:T(8,128)S(1)}, u32[]{:S(2)}, u32[]{:S(2)}) %collective-permute-start.1) | collective-permute-done | bytes 131104 | tf_op jit(solution)/shard_map/ppermute | solution.py:46
  18.2 2.1 %collective-permute-start.5 = (f32[11,16,256]{2,1,0:T(8,128)S(1)}, f32[11,16,256]{2,1,0:T(8,128)S(1)}, u32[]{:S(2)}, u32[]{:S(2)}) collective-permute-start(f32[11,16,256]{2,1,0:T(8,128)S(1)} %copy-done.6), channel_id=1, source_target_pairs={{0,24},{2,26},{4,28},{6,30},{8,16},{10,18},{12,20},{14,22},{16,8},... | collective-permute-start | bytes 540680 | tf_op jit(solution)/shard_map/ppermute | solution.py:46
  20.3 6.4 %collective-permute-done.5.refs_5_ = f32[11,16,256]{2,1,0:T(8,128)S(1)} collective-permute-done((f32[11,16,256]{2,1,0:T(8,128)S(1)}, f32[11,16,256]{2,1,0:T(8,128)S(1)}, u32[]{:S(2)}, u32[]{:S(2)}) %collective-permute-start.5) | collective-permute-done | bytes 180256 | tf_op jit(solution)/shard_map/ppermute | solution.py:46
  27.6 1.2 %collective-permute-start.10 = (f32[16,16,256]{2,1,0:T(8,128)S(1)}, f32[16,16,256]{2,1,0:T(8,128)S(1)}, u32[]{:S(2)}, u32[]{:S(2)}) collective-permute-start(f32[16,16,256]{2,1,0:T(8,128)S(1)} %get-tuple-element.41), channel_id=1, source_target_pairs={{0,4},{2,6},{4,0},{6,2},{8,12},{10,14},{12,8},{14,10},{16,20},{18,... | collective-permute-start | bytes 786440 | tf_op jit(solution)/shard_map/ppermute | solution.py:46
  28.7 1.2 %collective-permute-start.12 = (f32[16,16,256]{2,1,0:T(8,128)S(1)}, f32[16,16,256]{2,1,0:T(8,128)S(1)}, u32[]{:S(2)}, u32[]{:S(2)}) collective-permute-start(f32[16,16,256]{2,1,0:T(8,128)S(1)} %get-tuple-element.40), channel_id=1, source_target_pairs={{0,2},{2,0},{4,6},{6,4},{8,10},{10,8},{12,14},{14,12},{16,18},{18,... | collective-permute-start | bytes 786440 | tf_op jit(solution)/shard_map/ppermute | solution.py:46
  30.8 0.9 %collective-permute-start.7 = (f32[11,16,256]{2,1,0:T(8,128)S(1)}, f32[11,16,256]{2,1,0:T(8,128)S(1)}, u32[]{:S(2)}, u32[]{:S(2)}) collective-permute-start(f32[11,16,256]{2,1,0:T(8,128)S(1)} %collective-permute-done.5.refs_5_), channel_id=1, source_target_pairs={{0,4},{2,6},{4,0},{6,2},{8,12},{10,14},{12,8},{14,10},{16,20},{18,... | collective-permute-start | bytes 540680 | tf_op jit(solution)/shard_map/ppermute | solution.py:46
  31.7 1.1 %collective-permute-start.4 = (f32[11,16,256]{2,1,0:T(8,128)S(1)}, f32[11,16,256]{2,1,0:T(8,128)S(1)}, u32[]{:S(2)}, u32[]{:S(2)}) collective-permute-start(f32[11,16,256]{2,1,0:T(8,128)S(1)} %copy-done.6), channel_id=1, source_target_pairs={{0,8},{2,10},{4,12},{6,14},{8,0},{10,2},{12,4},{14,6},{16,24},{18,... | collective-permute-start | bytes 540680 | tf_op jit(solution)/shard_map/ppermute | solution.py:46
  32.8 3.1 %collective-permute-done.10.refs_11_ = f32[16,16,256]{2,1,0:T(8,128)S(1)} collective-permute-done((f32[16,16,256]{2,1,0:T(8,128)S(1)}, f32[16,16,256]{2,1,0:T(8,128)S(1)}, u32[]{:S(2)}, u32[]{:S(2)}) %collective-permute-start.10) | collective-permute-done | bytes 262176 | tf_op jit(solution)/shard_map/ppermute | solution.py:46
  36.2 0.9 %widened.1 = (f32[16,256]{1,0:T(8,128)S(1)}, f32[16,768]{1,0:T(8,128)S(1)}) custom-call(s32[4,4,4]{2,1,0:T(4,128)S(1)} %copy-done.4, s32[4,4,12]{2,1,0:T(4,128)S(1)} %copy-done.5), custom_call_target="tpu_custom_call" | custom-call | tf_op jit(solution)/shard_map/widened/pallas_call | solution.py:176
  37.1 1.2 %collective-permute-start.14 = (f32[4,16,256]{2,1,0:T(8,128)S(1)}, f32[4,16,256]{2,1,0:T(8,128)S(1)}, u32[]{:S(2)}, u32[]{:S(2)}) collective-permute-start(f32[4,16,256]{2,1,0:T(8,128)S(1)} %slice.42), channel_id=1, source_target_pairs={{0,2},{2,0},{4,6},{6,4},{8,10},{10,8},{12,14},{14,12},{16,18},{18,... | collective-permute-start | bytes 196616 | tf_op jit(solution)/shard_map/ppermute | solution.py:46
  38.9 1.3 %collective-permute-start.15 = (f32[4,16,256]{2,1,0:T(8,128)S(1)}, f32[4,16,256]{2,1,0:T(8,128)S(1)}, u32[]{:S(2)}, u32[]{:S(2)}) collective-permute-start(f32[4,16,256]{2,1,0:T(8,128)S(1)} %slice.43), channel_id=1, source_target_pairs={{0,4},{2,6},{4,0},{6,2},{8,12},{10,14},{12,8},{14,10},{16,20},{18,... | collective-permute-start | bytes 196616 | tf_op jit(solution)/shard_map/ppermute | solution.py:46
  42.2 1.1 %collective-permute-start.19 = (f32[28,16,256]{2,1,0:T(8,128)S(1)}, f32[28,16,256]{2,1,0:T(8,128)S(1)}, u32[]{:S(2)}, u32[]{:S(2)}) collective-permute-start(f32[28,16,256]{2,1,0:T(8,128)S(1)} %pad_maximum_fusion), channel_id=1, source_target_pairs={{0,2},{2,0},{4,6},{6,4},{8,10},{10,8},{12,14},{14,12},{16,18},{18,... | collective-permute-start | bytes 1376264 | tf_op jit(solution)/shard_map/ppermute | solution.py:46
  44.0 5.0 %solve.1 = (f32[1024,256]{1,0:T(8,128)S(1)}, f32[1024,256]{1,0:T(8,128)S(1)}, f32[344,256]{1,0:T(8,128)S(1)}, f32[344,256]{1,0:T(8,128)S(1)}, f32[336,256]{1,0:T(8,128)S(1)}) custom-call(f32[16,256]{1,0:T(8,128)S(1)} %get-tuple-element.21.refs_0_, f32[1024,256]{1,0:T(8,128)S(1)} %copy-done, f32[19,16,256]{2,1,0:T(8,128)S(1)} %copy-done.3, ...), custom_call_target="tpu_custom_call" | custom-call | flops 2147483648 | bytes 262144 | tf_op jit(solution)/shard_map/solve/pallas_call | solution.py:279
  49.8 1.2 %collective-permute-start.21 = (f32[11,16,256]{2,1,0:T(8,128)S(1)}, f32[11,16,256]{2,1,0:T(8,128)S(1)}, u32[]{:S(2)}, u32[]{:S(2)}) collective-permute-start(f32[11,16,256]{2,1,0:T(8,128)S(1)} %slice.44), channel_id=1, source_target_pairs={{0,2},{2,0},{4,6},{6,4},{8,10},{10,8},{12,14},{14,12},{16,18},{18,... | collective-permute-start | bytes 540680 | tf_op jit(solution)/shard_map/ppermute | solution.py:46
  51.1 1.1 %collective-permute-start.22 = (f32[11,16,256]{2,1,0:T(8,128)S(1)}, f32[11,16,256]{2,1,0:T(8,128)S(1)}, u32[]{:S(2)}, u32[]{:S(2)}) collective-permute-start(f32[11,16,256]{2,1,0:T(8,128)S(1)} %slice.45), channel_id=1, source_target_pairs={{0,4},{2,6},{4,0},{6,2},{8,12},{10,14},{12,8},{14,10},{16,20},{18,... | collective-permute-start | bytes 540680 | tf_op jit(solution)/shard_map/ppermute | solution.py:46
  52.2 1.8 %finish.1 = (f32[1024,256]{1,0:T(8,128)}, bf16[1536,256]{1,0:T(8,128)(2,1)S(1)}, bf16[1536,256]{1,0:T(8,128)(2,1)S(1)}) custom-call(f32[1024,256]{1,0:T(8,128)S(1)} %get-tuple-element.31.sol_ref, f32[1024,256]{1,0:T(8,128)S(1)} %get-tuple-element.32.part_ref, f32[344,256]{1,0:T(8,128)S(1)} %get-tuple-element.33.refs_0_, ...), custom_call_target="tpu_custom_call" | custom-call | flops 100663296 | bytes 262144 | tf_op jit(solution)/shard_map/finish/pallas_call | solution.py:336
  54.0 2.2 %residual.1.refs_4_ = f32[1024,256]{1,0:T(8,128)} custom-call(f32[16,768]{1,0:T(8,128)S(1)} %get-tuple-element.37.refs_0_, f32[1024,256]{1,0:T(8,128)S(1)} %copy-done, bf16[1536,256]{1,0:T(8,128)(2,1)S(1)} %get-tuple-element.38.refs_2_, bf16[1536,256]{1,0:T(8,128)(2,1)S(1)} %get-tuple-element.39.refs_3_, f32[19,16,256]{2,1,0:T(8,128)S(1)} %copy-done.3, ...), custom_call_target="tpu_custom_call" | custom-call | flops 1056964608 | bytes 5505024 | tf_op jit(solution)/shard_map/residual/pallas_call | solution.py:410
  57.4 1.6 %residual_rest.1 = f32[1024,256]{1,0:T(8,128)} custom-call(f32[16,768]{1,0:T(8,128)S(1)} %get-tuple-element.37.refs_0_, f32[1024,256]{1,0:T(8,128)S(1)} %copy-done, bf16[1536,256]{1,0:T(8,128)(2,1)S(1)} %get-tuple-element.38.refs_2_, bf16[1536,256]{1,0:T(8,128)(2,1)S(1)} %get-tuple-element.39.refs_3_, ...), custom_call_target="tpu_custom_call", output_to_operand_aliasing={{}: (4, {})} | custom-call | flops 150994944 | bytes 786432 | tf_op jit(solution)/shard_map/residual_rest/pallas_call | solution.py:410
  (58 shorter events, 8.8 us)
Async XLA Ops:
  2.5 10.5 %collective-permute-start.2 = (f32[19,16,256]{2,1,0:T(8,128)}, f32[19,16,256]{2,1,0:T(8,128)S(1)}, u32[]{:S(2)}, u32[]{:S(2)}) collective-permute-start(f32[19,16,256]{2,1,0:T(8,128)} %get-tuple-element.24.refs_2_.refs_4_), channel_id=1, source_target_pairs={{0,4},{2,6},{4,0},{6,2},{8,12},{10,14},{12,8},{14,10},{16,20},{18,... | collective-permute-start | bytes 933896 | tf_op jit(solution)/shard_map/ppermute | solution.py:46
  5.5 11.8 %collective-permute-start.3 = (f32[19,16,256]{2,1,0:T(8,128)}, f32[19,16,256]{2,1,0:T(8,128)S(1)}, u32[]{:S(2)}, u32[]{:S(2)}) collective-permute-start(f32[19,16,256]{2,1,0:T(8,128)} %get-tuple-element.24.refs_2_.refs_4_), channel_id=1, source_target_pairs={{0,2},{2,0},{4,6},{6,4},{8,10},{10,8},{12,14},{14,12},{16,18},{18,... | collective-permute-start | bytes 933896 | tf_op jit(solution)/shard_map/ppermute | solution.py:46
  7.0 8.2 %collective-permute-start = (f32[8,16,256]{2,1,0:T(8,128)}, f32[8,16,256]{2,1,0:T(8,128)S(1)}, u32[]{:S(2)}, u32[]{:S(2)}) collective-permute-start(f32[8,16,256]{2,1,0:T(8,128)} %get-tuple-element.23), channel_id=1, source_target_pairs={{0,24},{2,26},{4,28},{6,30},{8,16},{10,18},{12,20},{14,22},{16,8},... | collective-permute-start | bytes 393224 | tf_op jit(solution)/shard_map/ppermute | solution.py:46
  10.6 6.1 %collective-permute-start.1 = (f32[8,16,256]{2,1,0:T(8,128)}, f32[8,16,256]{2,1,0:T(8,128)S(1)}, u32[]{:S(2)}, u32[]{:S(2)}) collective-permute-start(f32[8,16,256]{2,1,0:T(8,128)} %get-tuple-element.23), channel_id=1, source_target_pairs={{0,8},{2,10},{4,12},{6,14},{8,0},{10,2},{12,4},{14,6},{16,24},{18,... | collective-permute-start | bytes 393224 | tf_op jit(solution)/shard_map/ppermute | solution.py:46
  16.6 10.8 %collective-permute-start.9 = (f32[26,16,256]{2,1,0:T(8,128)S(1)}, f32[26,16,256]{2,1,0:T(8,128)S(1)}, u32[]{:S(2)}, u32[]{:S(2)}) collective-permute-start(f32[26,16,256]{2,1,0:T(8,128)S(1)} %pad_maximum_fusion.2), channel_id=1, source_target_pairs={{0,2},{2,0},{4,6},{6,4},{8,10},{10,8},{12,14},{14,12},{16,18},{18,... | collective-permute-start | bytes 1277960 | tf_op jit(solution)/shard_map/ppermute | solution.py:46
  17.3 10.1 %collective-permute-start.11 = (f32[25,16,256]{2,1,0:T(8,128)S(1)}, f32[25,16,256]{2,1,0:T(8,128)S(1)}, u32[]{:S(2)}, u32[]{:S(2)}) collective-permute-start(f32[25,16,256]{2,1,0:T(8,128)S(1)} %pad_maximum_fusion.3), channel_id=1, source_target_pairs={{0,4},{2,6},{4,0},{6,2},{8,12},{10,14},{12,8},{14,10},{16,20},{18,... | collective-permute-start | bytes 1228808 | tf_op jit(solution)/shard_map/ppermute | solution.py:46
  18.2 8.5 %collective-permute-start.5 = (f32[11,16,256]{2,1,0:T(8,128)S(1)}, f32[11,16,256]{2,1,0:T(8,128)S(1)}, u32[]{:S(2)}, u32[]{:S(2)}) collective-permute-start(f32[11,16,256]{2,1,0:T(8,128)S(1)} %copy-done.6), channel_id=1, source_target_pairs={{0,24},{2,26},{4,28},{6,30},{8,16},{10,18},{12,20},{14,22},{16,8},... | collective-permute-start | bytes 540680 | tf_op jit(solution)/shard_map/ppermute | solution.py:46
  20.3 7.2 %collective-permute-start.8 = (f32[8,16,256]{2,1,0:T(8,128)S(1)}, f32[8,16,256]{2,1,0:T(8,128)S(1)}, u32[]{:S(2)}, u32[]{:S(2)}) collective-permute-start(f32[8,16,256]{2,1,0:T(8,128)S(1)} %collective-permute-done.refs_3_), channel_id=1, source_target_pairs={{0,8},{2,10},{4,12},{6,14},{8,0},{10,2},{12,4},{14,6},{16,24},{18,... | collective-permute-start | bytes 393224 | tf_op jit(solution)/shard_map/ppermute | solution.py:46
  27.5 8.6 %copy-start.5 = (s32[4,4,12]{2,1,0:T(4,128)S(1)}, s32[4,4,12]{2,1,0:T(4,128)}, u32[]{:S(2)}) copy-start(s32[4,4,12]{2,1,0:T(4,128)} %refs_1_.3) | copy-start | bytes 2308
  27.6 8.3 %collective-permute-start.10 = (f32[16,16,256]{2,1,0:T(8,128)S(1)}, f32[16,16,256]{2,1,0:T(8,128)S(1)}, u32[]{:S(2)}, u32[]{:S(2)}) collective-permute-start(f32[16,16,256]{2,1,0:T(8,128)S(1)} %get-tuple-element.41), channel_id=1, source_target_pairs={{0,4},{2,6},{4,0},{6,2},{8,12},{10,14},{12,8},{14,10},{16,20},{18,... | collective-permute-start | bytes 786440 | tf_op jit(solution)/shard_map/ppermute | solution.py:46
  28.7 8.4 %collective-permute-start.12 = (f32[16,16,256]{2,1,0:T(8,128)S(1)}, f32[16,16,256]{2,1,0:T(8,128)S(1)}, u32[]{:S(2)}, u32[]{:S(2)}) collective-permute-start(f32[16,16,256]{2,1,0:T(8,128)S(1)} %get-tuple-element.40), channel_id=1, source_target_pairs={{0,2},{2,0},{4,6},{6,4},{8,10},{10,8},{12,14},{14,12},{16,18},{18,... | collective-permute-start | bytes 786440 | tf_op jit(solution)/shard_map/ppermute | solution.py:46
  29.9 9.0 %collective-permute-start.13 = (f32[11,16,256]{2,1,0:T(8,128)S(1)}, f32[11,16,256]{2,1,0:T(8,128)S(1)}, u32[]{:S(2)}, u32[]{:S(2)}) collective-permute-start(f32[11,16,256]{2,1,0:T(8,128)S(1)} %collective-permute-done.5.refs_5_), channel_id=1, source_target_pairs={{0,2},{2,0},{4,6},{6,4},{8,10},{10,8},{12,14},{14,12},{16,18},{18,... | collective-permute-start | bytes 540680 | tf_op jit(solution)/shard_map/ppermute | solution.py:46
  30.8 9.5 %collective-permute-start.7 = (f32[11,16,256]{2,1,0:T(8,128)S(1)}, f32[11,16,256]{2,1,0:T(8,128)S(1)}, u32[]{:S(2)}, u32[]{:S(2)}) collective-permute-start(f32[11,16,256]{2,1,0:T(8,128)S(1)} %collective-permute-done.5.refs_5_), channel_id=1, source_target_pairs={{0,4},{2,6},{4,0},{6,2},{8,12},{10,14},{12,8},{14,10},{16,20},{18,... | collective-permute-start | bytes 540680 | tf_op jit(solution)/shard_map/ppermute | solution.py:46
  31.7 9.3 %collective-permute-start.4 = (f32[11,16,256]{2,1,0:T(8,128)S(1)}, f32[11,16,256]{2,1,0:T(8,128)S(1)}, u32[]{:S(2)}, u32[]{:S(2)}) collective-permute-start(f32[11,16,256]{2,1,0:T(8,128)S(1)} %copy-done.6), channel_id=1, source_target_pairs={{0,8},{2,10},{4,12},{6,14},{8,0},{10,2},{12,4},{14,6},{16,24},{18,... | collective-permute-start | bytes 540680 | tf_op jit(solution)/shard_map/ppermute | solution.py:46
  35.9 5.5 %collective-permute-start.6 = (f32[11,16,256]{2,1,0:T(8,128)S(1)}, f32[11,16,256]{2,1,0:T(8,128)S(1)}, u32[]{:S(2)}, u32[]{:S(2)}) collective-permute-start(f32[11,16,256]{2,1,0:T(8,128)S(1)} %collective-permute-done.5.refs_5_), channel_id=1, source_target_pairs={{0,8},{2,10},{4,12},{6,14},{8,0},{10,2},{12,4},{14,6},{16,24},{18,... | collective-permute-start | bytes 540680 | tf_op jit(solution)/shard_map/ppermute | solution.py:46
  37.1 6.1 %collective-permute-start.14 = (f32[4,16,256]{2,1,0:T(8,128)S(1)}, f32[4,16,256]{2,1,0:T(8,128)S(1)}, u32[]{:S(2)}, u32[]{:S(2)}) collective-permute-start(f32[4,16,256]{2,1,0:T(8,128)S(1)} %slice.42), channel_id=1, source_target_pairs={{0,2},{2,0},{4,6},{6,4},{8,10},{10,8},{12,14},{14,12},{16,18},{18,... | collective-permute-start | bytes 196616 | tf_op jit(solution)/shard_map/ppermute | solution.py:46
  38.9 5.0 %collective-permute-start.15 = (f32[4,16,256]{2,1,0:T(8,128)S(1)}, f32[4,16,256]{2,1,0:T(8,128)S(1)}, u32[]{:S(2)}, u32[]{:S(2)}) collective-permute-start(f32[4,16,256]{2,1,0:T(8,128)S(1)} %slice.43), channel_id=1, source_target_pairs={{0,4},{2,6},{4,0},{6,2},{8,12},{10,14},{12,8},{14,10},{16,20},{18,... | collective-permute-start | bytes 196616 | tf_op jit(solution)/shard_map/ppermute | solution.py:46
  41.4 8.4 %collective-permute-start.20 = (f32[27,16,256]{2,1,0:T(8,128)S(1)}, f32[27,16,256]{2,1,0:T(8,128)S(1)}, u32[]{:S(2)}, u32[]{:S(2)}) collective-permute-start(f32[27,16,256]{2,1,0:T(8,128)S(1)} %pad_maximum_fusion.1), channel_id=1, source_target_pairs={{0,4},{2,6},{4,0},{6,2},{8,12},{10,14},{12,8},{14,10},{16,20},{18,... | collective-permute-start | bytes 1327112 | tf_op jit(solution)/shard_map/ppermute | solution.py:46
  42.2 8.8 %collective-permute-start.19 = (f32[28,16,256]{2,1,0:T(8,128)S(1)}, f32[28,16,256]{2,1,0:T(8,128)S(1)}, u32[]{:S(2)}, u32[]{:S(2)}) collective-permute-start(f32[28,16,256]{2,1,0:T(8,128)S(1)} %pad_maximum_fusion), channel_id=1, source_target_pairs={{0,2},{2,0},{4,6},{6,4},{8,10},{10,8},{12,14},{14,12},{16,18},{18,... | collective-permute-start | bytes 1376264 | tf_op jit(solution)/shard_map/ppermute | solution.py:46
  49.0 3.2 %collective-permute-start.16 = (f32[344,256]{1,0:T(8,128)S(1)}, f32[344,256]{1,0:T(8,128)S(1)}, u32[]{:S(2)}, u32[]{:S(2)}) collective-permute-start(f32[344,256]{1,0:T(8,128)S(1)} %get-tuple-element.33.refs_0_), channel_id=1, source_target_pairs={{0,1},{1,0},{2,3},{3,2},{4,5},{5,4},{6,7},{7,6},{8,9},{9,8},{10,11... | collective-permute-start | bytes 1056776 | tf_op jit(solution)/shard_map/ppermute | solution.py:460
  49.1 3.1 %collective-permute-start.17 = (f32[344,256]{1,0:T(8,128)S(1)}, f32[344,256]{1,0:T(8,128)S(1)}, u32[]{:S(2)}, u32[]{:S(2)}) collective-permute-start(f32[344,256]{1,0:T(8,128)S(1)} %get-tuple-element.34.refs_1_), channel_id=1, source_target_pairs={{0,1},{1,0},{2,3},{3,2},{4,5},{5,4},{6,7},{7,6},{8,9},{9,8},{10,11... | collective-permute-start | bytes 1056776 | tf_op jit(solution)/shard_map/ppermute | solution.py:460
  49.5 2.6 %collective-permute-start.18 = (f32[336,256]{1,0:T(8,128)S(1)}, f32[336,256]{1,0:T(8,128)S(1)}, u32[]{:S(2)}, u32[]{:S(2)}) collective-permute-start(f32[336,256]{1,0:T(8,128)S(1)} %get-tuple-element.35.refs_2_), channel_id=1, source_target_pairs={{0,1},{1,0},{2,3},{3,2},{4,5},{5,4},{6,7},{7,6},{8,9},{9,8},{10,11... | collective-permute-start | bytes 1032200 | tf_op jit(solution)/shard_map/ppermute | solution.py:460
  49.8 6.8 %collective-permute-start.21 = (f32[11,16,256]{2,1,0:T(8,128)S(1)}, f32[11,16,256]{2,1,0:T(8,128)S(1)}, u32[]{:S(2)}, u32[]{:S(2)}) collective-permute-start(f32[11,16,256]{2,1,0:T(8,128)S(1)} %slice.44), channel_id=1, source_target_pairs={{0,2},{2,0},{4,6},{6,4},{8,10},{10,8},{12,14},{14,12},{16,18},{18,... | collective-permute-start | bytes 540680 | tf_op jit(solution)/shard_map/ppermute | solution.py:46
  51.1 6.3 %collective-permute-start.22 = (f32[11,16,256]{2,1,0:T(8,128)S(1)}, f32[11,16,256]{2,1,0:T(8,128)S(1)}, u32[]{:S(2)}, u32[]{:S(2)}) collective-permute-start(f32[11,16,256]{2,1,0:T(8,128)S(1)} %slice.45), channel_id=1, source_target_pairs={{0,4},{2,6},{4,0},{6,2},{8,12},{10,14},{12,8},{14,10},{16,20},{18,... | collective-permute-start | bytes 540680 | tf_op jit(solution)/shard_map/ppermute | solution.py:46
  (7 other events, 21.5 us)

commit v17 on v15

--- a/solution.py
+++ b/solution.py
@@ -108,22 +108,38 @@
     supers, rows, size = diag_inv.shape
     kept = 3 * supers - spare
 
-    def kernel(diag_ref, lower_ref, jacobian_ref, factor_ref, blocks_ref, own_ref):
-        def block(q):
-            return jacobian_ref[q // 3, :, q % 3 * size : (q % 3 + 1) * size]
-
-        for s in range(supers):
-            factor_ref[s] = own_ref[s] = diag_ref[s]
-            factor_ref[supers + s] = own_ref[supers + s] = lower_ref[s]
-        for k in range(kept):
-            value = jnp.where(lax.axis_index("node") == 0, block(k + 1), block(k)) if spare else block(k)
-            blocks_ref[k] = own_ref[2 * supers + k] = value
+    def kernel(diag_ref, lower_ref, jacobian_ref, factor_ref, blocks_ref, own_ref, sem):
+        def move(first, last):
+            copies = []
+
+            def start(source, target):
+                copies.append(pltpu.make_async_copy(source, target, sem.at[len(copies)]))
+                copies[-1].start()
+
+            for ref, base in ((own_ref, 2 * supers), (blocks_ref, 0)):
+                for c in range(3):
+                    begin, end = max(c * supers, first), min((c + 1) * supers, last)
+                    band = jacobian_ref.at[pl.ds(begin - c * supers, end - begin), :, pl.ds(c * size, size)]
+                    start(band, ref.at[pl.ds(base + begin - first, end - begin)])
+            for ref in (own_ref, factor_ref):
+                start(diag_ref, ref.at[pl.ds(0, supers)])
+                start(lower_ref, ref.at[pl.ds(supers, supers)])
+            for copy in copies:
+                copy.wait()
+
+        if spare:
+            pl.when(lax.axis_index("node") == 0)(lambda: move(1, 3 * supers))
+            pl.when(lax.axis_index("node") != 0)(lambda: move(0, kept))
+        else:
+            move(0, kept)
 
     return pl.pallas_call(
         kernel,
         out_shape=shapes([(count, rows, size) for count in (2 * supers, kept, 2 * supers + kept)]),
-        in_specs=[VMEM] * 3,
-        out_specs=[VMEM] * 3,
+        in_specs=[ANY] * 3,
+        out_specs=[ANY] * 3,
+        scratch_shapes=[pltpu.SemaphoreType.DMA((10,))],
+        compiler_params=pltpu.CompilerParams(vmem_limit_bytes=60 * 2**20),
         name="pack",
     )(diag_inv, lower, jacobian)
 
@@ -390,7 +406,7 @@
             bands, starts = [], []
             for owner, blocks in places.items():
                 row = row_of(owner, rows, relative)
-                band = [block_of(blocks, 3 * s + c) for c in range(3)]
+                band = [block_of(blocks, c * supers + s) for c in range(3)]
                 bands.append(jnp.concatenate(band, axis=1) * weights_of(weights_ref, s, row, supers, size))
                 starts.append(s * size + row if not relative else pl.multiple_of(s * size + row, rows))
             window = pl.ds(s * size, wide)

time: 58 us -> 76.4 us (1.32)
  Pallas kernels: 13.4 us -> 31.6 us
    pallas_call x1, Pallas kernels: 1.86 us -> 20.1 us  [pack(): pl.pallas_call(kernel, out_shape=shapes([(count, rows, size) for count in...]
  transfers between devices with their start and end apart: 22 -> 22, of which waited for: 12 -> 12; matrix products, arithmetic and copies ran while one was open for 0% -> 0% of each run, Pallas kernels for 17% -> 13%
where the time goes in v17:
time: 76.4 us; the launch traced here: 76.2 us
  Pallas kernels  31.6 us (41%)
  starting transfers between devices  24.3 us (32%)
  waiting for transfers between devices  18.2 us (24%)
  local copies, waits for them, and re-layouts  1.1 us (1%)
  between operations  0.84 us (1%)
    ppermute x19, starting transfers between devices, sent(): lax.ppermute(array, axis, [(i, i ^ mask) for i in range(lax.axis_size(axi...  23.7 us
    pallas_call x1, Pallas kernels, pack(): pl.pallas_call(kernel, out_shape=shapes([(count, rows, size) for count in...  20.1 us
    ppermute x19, waiting for transfers between devices, sent(): lax.ppermute(array, axis, [(i, i ^ mask) for i in range(lax.axis_size(axi...  18.2 us
    pallas_call x1, Pallas kernels, solve(): pl.pallas_call(kernel, out_shape=shapes([(span, columns)] + [(span, size)...  4.97 us
    pallas_call x2, Pallas kernels, subtract_product(): pl.pallas_call(kernel, out_shape=shapes([(span, columns)])[0], in_specs=[...  3.82 us
    pallas_call x1, Pallas kernels, finish(): pl.pallas_call(kernel, out_shape=shapes([(span, columns)]) + [windows, wi...  1.77 us
  transfers between devices with their start and end apart: 22, of which 12 were waited for; matrix products, arithmetic and copies ran while one was open for 0% of the time, Pallas kernels for 13%

profile of v17, /device:TPU:0, one launch (start us, length us, event | category | flops | bytes accessed | tf_op | source)
XLA Modules:
  0.0 76.2 jit_solution(17428457410382739693)
XLA Ops:
  0.6 20.1 %pack.1 = (f32[8,16,256]{2,1,0:T(8,128)}, f32[11,16,256]{2,1,0:T(8,128)}, f32[19,16,256]{2,1,0:T(8,128)}) custom-call(f32[4,16,256]{2,1,0:T(8,128)} %diag_ref.1, f32[4,16,256]{2,1,0:T(8,128)} %lower_ref.1, f32[4,16,768]{2,1,0:T(8,128)} %jacobian_ref.1), custom_call_target="tpu_custom_call" | custom-call | tf_op jit(solution)/shard_map/pack/pallas_call | solution.py:136
  20.7 3.0 %collective-permute-start.2 = (f32[19,16,256]{2,1,0:T(8,128)}, f32[19,16,256]{2,1,0:T(8,128)S(1)}, u32[]{:S(2)}, u32[]{:S(2)}) collective-permute-start(f32[19,16,256]{2,1,0:T(8,128)} %get-tuple-element.22.refs_2_.refs_4_), channel_id=1, source_target_pairs={{0,4},{2,6},{4,0},{6,2},{8,12},{10,14},{12,8},{14,10},{16,20},{18,... | collective-permute-start | bytes 933896 | tf_op jit(solution)/shard_map/ppermute | solution.py:46
  23.7 1.5 %collective-permute-start.3 = (f32[19,16,256]{2,1,0:T(8,128)}, f32[19,16,256]{2,1,0:T(8,128)S(1)}, u32[]{:S(2)}, u32[]{:S(2)}) collective-permute-start(f32[19,16,256]{2,1,0:T(8,128)} %get-tuple-element.22.refs_2_.refs_4_), channel_id=1, source_target_pairs={{0,2},{2,0},{4,6},{6,4},{8,10},{10,8},{12,14},{14,12},{16,18},{18,... | collective-permute-start | bytes 933896 | tf_op jit(solution)/shard_map/ppermute | solution.py:46
  25.2 3.6 %collective-permute-start = (f32[8,16,256]{2,1,0:T(8,128)}, f32[8,16,256]{2,1,0:T(8,128)S(1)}, u32[]{:S(2)}, u32[]{:S(2)}) collective-permute-start(f32[8,16,256]{2,1,0:T(8,128)} %get-tuple-element.21), channel_id=1, source_target_pairs={{0,24},{2,26},{4,28},{6,30},{8,16},{10,18},{12,20},{14,22},{16,8},... | collective-permute-start | bytes 393224 | tf_op jit(solution)/shard_map/ppermute | solution.py:46
  28.8 2.5 %collective-permute-done.2.refs_7_.refs_8_ = f32[19,16,256]{2,1,0:T(8,128)S(1)} collective-permute-done((f32[19,16,256]{2,1,0:T(8,128)}, f32[19,16,256]{2,1,0:T(8,128)S(1)}, u32[]{:S(2)}, u32[]{:S(2)}) %collective-permute-start.2) | collective-permute-done | bytes 311328 | tf_op jit(solution)/shard_map/ppermute | solution.py:46
  31.3 2.1 %collective-permute-done.refs_3_ = f32[8,16,256]{2,1,0:T(8,128)S(1)} collective-permute-done((f32[8,16,256]{2,1,0:T(8,128)}, f32[8,16,256]{2,1,0:T(8,128)S(1)}, u32[]{:S(2)}, u32[]{:S(2)}) %collective-permute-start) | collective-permute-done | bytes 131104 | tf_op jit(solution)/shard_map/ppermute | solution.py:46
  33.5 1.4 %collective-permute-done.1.refs_4_ = f32[8,16,256]{2,1,0:T(8,128)S(1)} collective-permute-done((f32[8,16,256]{2,1,0:T(8,128)}, f32[8,16,256]{2,1,0:T(8,128)S(1)}, u32[]{:S(2)}, u32[]{:S(2)}) %collective-permute-start.1) | collective-permute-done | bytes 131104 | tf_op jit(solution)/shard_map/ppermute | solution.py:46
  36.5 2.1 %collective-permute-start.4 = (f32[11,16,256]{2,1,0:T(8,128)S(1)}, f32[11,16,256]{2,1,0:T(8,128)S(1)}, u32[]{:S(2)}, u32[]{:S(2)}) collective-permute-start(f32[11,16,256]{2,1,0:T(8,128)S(1)} %copy-done.6), channel_id=1, source_target_pairs={{0,24},{2,26},{4,28},{6,30},{8,16},{10,18},{12,20},{14,22},{16,8},... | collective-permute-start | bytes 540680 | tf_op jit(solution)/shard_map/ppermute | solution.py:46
  38.6 6.4 %collective-permute-done.4.refs_5_ = f32[11,16,256]{2,1,0:T(8,128)S(1)} collective-permute-done((f32[11,16,256]{2,1,0:T(8,128)S(1)}, f32[11,16,256]{2,1,0:T(8,128)S(1)}, u32[]{:S(2)}, u32[]{:S(2)}) %collective-permute-start.4) | collective-permute-done | bytes 180256 | tf_op jit(solution)/shard_map/ppermute | solution.py:46
  45.0 1.7 %collective-permute-start.5 = (f32[22,16,256]{2,1,0:T(8,128)S(1)}, f32[22,16,256]{2,1,0:T(8,128)S(1)}, u32[]{:S(2)}, u32[]{:S(2)}) collective-permute-start(f32[22,16,256]{2,1,0:T(8,128)S(1)} %pad_maximum_fusion.4), channel_id=1, source_target_pairs={{0,8},{2,10},{4,12},{6,14},{8,0},{10,2},{12,4},{14,6},{16,24},{18,... | collective-permute-start | bytes 1081352 | tf_op jit(solution)/shard_map/ppermute | solution.py:46
  46.9 1.1 %collective-permute-start.9 = (f32[16,16,256]{2,1,0:T(8,128)S(1)}, f32[16,16,256]{2,1,0:T(8,128)S(1)}, u32[]{:S(2)}, u32[]{:S(2)}) collective-permute-start(f32[16,16,256]{2,1,0:T(8,128)S(1)} %get-tuple-element.37), channel_id=1, source_target_pairs={{0,4},{2,6},{4,0},{6,2},{8,12},{10,14},{12,8},{14,10},{16,20},{18,... | collective-permute-start | bytes 786440 | tf_op jit(solution)/shard_map/ppermute | solution.py:46
  47.9 1.1 %collective-permute-start.11 = (f32[16,16,256]{2,1,0:T(8,128)S(1)}, f32[16,16,256]{2,1,0:T(8,128)S(1)}, u32[]{:S(2)}, u32[]{:S(2)}) collective-permute-start(f32[16,16,256]{2,1,0:T(8,128)S(1)} %get-tuple-element.36), channel_id=1, source_target_pairs={{0,2},{2,0},{4,6},{6,4},{8,10},{10,8},{12,14},{14,12},{16,18},{18,... | collective-permute-start | bytes 786440 | tf_op jit(solution)/shard_map/ppermute | solution.py:46
  50.0 1.0 %collective-permute-start.6 = (f32[11,16,256]{2,1,0:T(8,128)S(1)}, f32[11,16,256]{2,1,0:T(8,128)S(1)}, u32[]{:S(2)}, u32[]{:S(2)}) collective-permute-start(f32[11,16,256]{2,1,0:T(8,128)S(1)} %collective-permute-done.4.refs_5_), channel_id=1, source_target_pairs={{0,4},{2,6},{4,0},{6,2},{8,12},{10,14},{12,8},{14,10},{16,20},{18,... | collective-permute-start | bytes 540680 | tf_op jit(solution)/shard_map/ppermute | solution.py:46
  51.0 0.9 %widened.1 = (f32[16,256]{1,0:T(8,128)S(1)}, f32[16,768]{1,0:T(8,128)S(1)}) custom-call(s32[4,4,4]{2,1,0:T(4,128)S(1)} %copy-done.4, s32[4,4,12]{2,1,0:T(4,128)S(1)} %copy-done.5), custom_call_target="tpu_custom_call" | custom-call | tf_op jit(solution)/shard_map/widened/pallas_call | solution.py:192
  51.9 3.1 %collective-permute-done.9.refs_11_ = f32[16,16,256]{2,1,0:T(8,128)S(1)} collective-permute-done((f32[16,16,256]{2,1,0:T(8,128)S(1)}, f32[16,16,256]{2,1,0:T(8,128)S(1)}, u32[]{:S(2)}, u32[]{:S(2)}) %collective-permute-start.9) | collective-permute-done | bytes 262176 | tf_op jit(solution)/shard_map/ppermute | solution.py:46
  55.1 1.1 %collective-permute-start.13 = (f32[4,16,256]{2,1,0:T(8,128)S(1)}, f32[4,16,256]{2,1,0:T(8,128)S(1)}, u32[]{:S(2)}, u32[]{:S(2)}) collective-permute-start(f32[4,16,256]{2,1,0:T(8,128)S(1)} %slice.43), channel_id=1, source_target_pairs={{0,2},{2,0},{4,6},{6,4},{8,10},{10,8},{12,14},{14,12},{16,18},{18,... | collective-permute-start | bytes 196616 | tf_op jit(solution)/shard_map/ppermute | solution.py:46
  58.6 1.2 %collective-permute-start.19 = (f32[27,16,256]{2,1,0:T(8,128)S(1)}, f32[27,16,256]{2,1,0:T(8,128)S(1)}, u32[]{:S(2)}, u32[]{:S(2)}) collective-permute-start(f32[27,16,256]{2,1,0:T(8,128)S(1)} %pad_maximum_fusion.1), channel_id=1, source_target_pairs={{0,4},{2,6},{4,0},{6,2},{8,12},{10,14},{12,8},{14,10},{16,20},{18,... | collective-permute-start | bytes 1327112 | tf_op jit(solution)/shard_map/ppermute | solution.py:46
  59.9 1.3 %collective-permute-start.18 = (f32[28,16,256]{2,1,0:T(8,128)S(1)}, f32[28,16,256]{2,1,0:T(8,128)S(1)}, u32[]{:S(2)}, u32[]{:S(2)}) collective-permute-start(f32[28,16,256]{2,1,0:T(8,128)S(1)} %pad_maximum_fusion), channel_id=1, source_target_pairs={{0,2},{2,0},{4,6},{6,4},{8,10},{10,8},{12,14},{14,12},{16,18},{18,... | collective-permute-start | bytes 1376264 | tf_op jit(solution)/shard_map/ppermute | solution.py:46
  61.3 5.0 %solve.1 = (f32[1024,256]{1,0:T(8,128)S(1)}, f32[1024,256]{1,0:T(8,128)S(1)}, f32[344,256]{1,0:T(8,128)S(1)}, f32[344,256]{1,0:T(8,128)S(1)}, f32[336,256]{1,0:T(8,128)S(1)}) custom-call(f32[16,256]{1,0:T(8,128)S(1)} %get-tuple-element.19.refs_0_, f32[1024,256]{1,0:T(8,128)S(1)} %copy-done, f32[19,16,256]{2,1,0:T(8,128)S(1)} %copy-done.3, ...), custom_call_target="tpu_custom_call" | custom-call | flops 2147483648 | bytes 262144 | tf_op jit(solution)/shard_map/solve/pallas_call | solution.py:295
  67.2 1.1 %collective-permute-start.20 = (f32[11,16,256]{2,1,0:T(8,128)S(1)}, f32[11,16,256]{2,1,0:T(8,128)S(1)}, u32[]{:S(2)}, u32[]{:S(2)}) collective-permute-start(f32[11,16,256]{2,1,0:T(8,128)S(1)} %slice.46), channel_id=1, source_target_pairs={{0,2},{2,0},{4,6},{6,4},{8,10},{10,8},{12,14},{14,12},{16,18},{18,... | collective-permute-start | bytes 540680 | tf_op jit(solution)/shard_map/ppermute | solution.py:46
  68.4 1.1 %collective-permute-start.21 = (f32[11,16,256]{2,1,0:T(8,128)S(1)}, f32[11,16,256]{2,1,0:T(8,128)S(1)}, u32[]{:S(2)}, u32[]{:S(2)}) collective-permute-start(f32[11,16,256]{2,1,0:T(8,128)S(1)} %slice.47), channel_id=1, source_target_pairs={{0,4},{2,6},{4,0},{6,2},{8,12},{10,14},{12,8},{14,10},{16,20},{18,... | collective-permute-start | bytes 540680 | tf_op jit(solution)/shard_map/ppermute | solution.py:46
  69.5 1.8 %finish.1 = (f32[1024,256]{1,0:T(8,128)}, bf16[1536,256]{1,0:T(8,128)(2,1)S(1)}, bf16[1536,256]{1,0:T(8,128)(2,1)S(1)}) custom-call(f32[1024,256]{1,0:T(8,128)S(1)} %get-tuple-element.27.sol_ref, f32[1024,256]{1,0:T(8,128)S(1)} %get-tuple-element.28.part_ref, f32[344,256]{1,0:T(8,128)S(1)} %get-tuple-element.29.refs_0_, ...), custom_call_target="tpu_custom_call" | custom-call | flops 100663296 | bytes 262144 | tf_op jit(solution)/shard_map/finish/pallas_call | solution.py:352
  71.3 2.2 %residual.1.refs_4_ = f32[1024,256]{1,0:T(8,128)} custom-call(f32[16,768]{1,0:T(8,128)S(1)} %get-tuple-element.33.refs_0_, f32[1024,256]{1,0:T(8,128)S(1)} %copy-done, bf16[1536,256]{1,0:T(8,128)(2,1)S(1)} %get-tuple-element.34.refs_2_, bf16[1536,256]{1,0:T(8,128)(2,1)S(1)} %get-tuple-element.35.refs_3_, f32[19,16,256]{2,1,0:T(8,128)S(1)} %copy-done.3, ...), custom_call_target="tpu_custom_call" | custom-call | flops 1056964608 | bytes 5505024 | tf_op jit(solution)/shard_map/residual/pallas_call | solution.py:426
  74.6 1.6 %residual_rest.1 = f32[1024,256]{1,0:T(8,128)} custom-call(f32[16,768]{1,0:T(8,128)S(1)} %get-tuple-element.33.refs_0_, f32[1024,256]{1,0:T(8,128)S(1)} %copy-done, bf16[1536,256]{1,0:T(8,128)(2,1)S(1)} %get-tuple-element.34.refs_2_, bf16[1536,256]{1,0:T(8,128)(2,1)S(1)} %get-tuple-element.35.refs_3_, ...), custom_call_target="tpu_custom_call", output_to_operand_aliasing={{}: (4, {})} | custom-call | flops 150994944 | bytes 786432 | tf_op jit(solution)/shard_map/residual_rest/pallas_call | solution.py:426
  (57 shorter events, 7.3 us)
Async XLA Ops:
  20.7 10.6 %collective-permute-start.2 = (f32[19,16,256]{2,1,0:T(8,128)}, f32[19,16,256]{2,1,0:T(8,128)S(1)}, u32[]{:S(2)}, u32[]{:S(2)}) collective-permute-start(f32[19,16,256]{2,1,0:T(8,128)} %get-tuple-element.22.refs_2_.refs_4_), channel_id=1, source_target_pairs={{0,4},{2,6},{4,0},{6,2},{8,12},{10,14},{12,8},{14,10},{16,20},{18,... | collective-permute-start | bytes 933896 | tf_op jit(solution)/shard_map/ppermute | solution.py:46
  23.7 11.8 %collective-permute-start.3 = (f32[19,16,256]{2,1,0:T(8,128)}, f32[19,16,256]{2,1,0:T(8,128)S(1)}, u32[]{:S(2)}, u32[]{:S(2)}) collective-permute-start(f32[19,16,256]{2,1,0:T(8,128)} %get-tuple-element.22.refs_2_.refs_4_), channel_id=1, source_target_pairs={{0,2},{2,0},{4,6},{6,4},{8,10},{10,8},{12,14},{14,12},{16,18},{18,... | collective-permute-start | bytes 933896 | tf_op jit(solution)/shard_map/ppermute | solution.py:46
  25.2 8.2 %collective-permute-start = (f32[8,16,256]{2,1,0:T(8,128)}, f32[8,16,256]{2,1,0:T(8,128)S(1)}, u32[]{:S(2)}, u32[]{:S(2)}) collective-permute-start(f32[8,16,256]{2,1,0:T(8,128)} %get-tuple-element.21), channel_id=1, source_target_pairs={{0,24},{2,26},{4,28},{6,30},{8,16},{10,18},{12,20},{14,22},{16,8},... | collective-permute-start | bytes 393224 | tf_op jit(solution)/shard_map/ppermute | solution.py:46
  28.8 6.1 %collective-permute-start.1 = (f32[8,16,256]{2,1,0:T(8,128)}, f32[8,16,256]{2,1,0:T(8,128)S(1)}, u32[]{:S(2)}, u32[]{:S(2)}) collective-permute-start(f32[8,16,256]{2,1,0:T(8,128)} %get-tuple-element.21), channel_id=1, source_target_pairs={{0,8},{2,10},{4,12},{6,14},{8,0},{10,2},{12,4},{14,6},{16,24},{18,... | collective-permute-start | bytes 393224 | tf_op jit(solution)/shard_map/ppermute | solution.py:46
  34.9 11.8 %collective-permute-start.8 = (f32[26,16,256]{2,1,0:T(8,128)S(1)}, f32[26,16,256]{2,1,0:T(8,128)S(1)}, u32[]{:S(2)}, u32[]{:S(2)}) collective-permute-start(f32[26,16,256]{2,1,0:T(8,128)S(1)} %pad_maximum_fusion.2), channel_id=1, source_target_pairs={{0,2},{2,0},{4,6},{6,4},{8,10},{10,8},{12,14},{14,12},{16,18},{18,... | collective-permute-start | bytes 1277960 | tf_op jit(solution)/shard_map/ppermute | solution.py:46
  35.6 11.1 %collective-permute-start.10 = (f32[25,16,256]{2,1,0:T(8,128)S(1)}, f32[25,16,256]{2,1,0:T(8,128)S(1)}, u32[]{:S(2)}, u32[]{:S(2)}) collective-permute-start(f32[25,16,256]{2,1,0:T(8,128)S(1)} %pad_maximum_fusion.3), channel_id=1, source_target_pairs={{0,4},{2,6},{4,0},{6,2},{8,12},{10,14},{12,8},{14,10},{16,20},{18,... | collective-permute-start | bytes 1228808 | tf_op jit(solution)/shard_map/ppermute | solution.py:46
  36.5 8.5 %collective-permute-start.4 = (f32[11,16,256]{2,1,0:T(8,128)S(1)}, f32[11,16,256]{2,1,0:T(8,128)S(1)}, u32[]{:S(2)}, u32[]{:S(2)}) collective-permute-start(f32[11,16,256]{2,1,0:T(8,128)S(1)} %copy-done.6), channel_id=1, source_target_pairs={{0,24},{2,26},{4,28},{6,30},{8,16},{10,18},{12,20},{14,22},{16,8},... | collective-permute-start | bytes 540680 | tf_op jit(solution)/shard_map/ppermute | solution.py:46
  38.6 8.2 %collective-permute-start.7 = (f32[8,16,256]{2,1,0:T(8,128)S(1)}, f32[8,16,256]{2,1,0:T(8,128)S(1)}, u32[]{:S(2)}, u32[]{:S(2)}) collective-permute-start(f32[8,16,256]{2,1,0:T(8,128)S(1)} %collective-permute-done.refs_3_), channel_id=1, source_target_pairs={{0,8},{2,10},{4,12},{6,14},{8,0},{10,2},{12,4},{14,6},{16,24},{18,... | collective-permute-start | bytes 393224 | tf_op jit(solution)/shard_map/ppermute | solution.py:46
  45.0 13.5 %collective-permute-start.5 = (f32[22,16,256]{2,1,0:T(8,128)S(1)}, f32[22,16,256]{2,1,0:T(8,128)S(1)}, u32[]{:S(2)}, u32[]{:S(2)}) collective-permute-start(f32[22,16,256]{2,1,0:T(8,128)S(1)} %pad_maximum_fusion.4), channel_id=1, source_target_pairs={{0,8},{2,10},{4,12},{6,14},{8,0},{10,2},{12,4},{14,6},{16,24},{18,... | collective-permute-start | bytes 1081352 | tf_op jit(solution)/shard_map/ppermute | solution.py:46
  46.8 4.2 %copy-start.4 = (s32[4,4,4]{2,1,0:T(4,128)S(1)}, s32[4,4,4]{2,1,0:T(4,128)}, u32[]{:S(2)}) copy-start(s32[4,4,4]{2,1,0:T(4,128)} %refs_0_.1) | copy-start | bytes 772
  46.9 8.2 %collective-permute-start.9 = (f32[16,16,256]{2,1,0:T(8,128)S(1)}, f32[16,16,256]{2,1,0:T(8,128)S(1)}, u32[]{:S(2)}, u32[]{:S(2)}) collective-permute-start(f32[16,16,256]{2,1,0:T(8,128)S(1)} %get-tuple-element.37), channel_id=1, source_target_pairs={{0,4},{2,6},{4,0},{6,2},{8,12},{10,14},{12,8},{14,10},{16,20},{18,... | collective-permute-start | bytes 786440 | tf_op jit(solution)/shard_map/ppermute | solution.py:46
  47.9 8.2 %collective-permute-start.11 = (f32[16,16,256]{2,1,0:T(8,128)S(1)}, f32[16,16,256]{2,1,0:T(8,128)S(1)}, u32[]{:S(2)}, u32[]{:S(2)}) collective-permute-start(f32[16,16,256]{2,1,0:T(8,128)S(1)} %get-tuple-element.36), channel_id=1, source_target_pairs={{0,2},{2,0},{4,6},{6,4},{8,10},{10,8},{12,14},{14,12},{16,18},{18,... | collective-permute-start | bytes 786440 | tf_op jit(solution)/shard_map/ppermute | solution.py:46
  49.1 8.3 %collective-permute-start.12 = (f32[11,16,256]{2,1,0:T(8,128)S(1)}, f32[11,16,256]{2,1,0:T(8,128)S(1)}, u32[]{:S(2)}, u32[]{:S(2)}) collective-permute-start(f32[11,16,256]{2,1,0:T(8,128)S(1)} %collective-permute-done.4.refs_5_), channel_id=1, source_target_pairs={{0,2},{2,0},{4,6},{6,4},{8,10},{10,8},{12,14},{14,12},{16,18},{18,... | collective-permute-start | bytes 540680 | tf_op jit(solution)/shard_map/ppermute | solution.py:46
  50.0 7.9 %collective-permute-start.6 = (f32[11,16,256]{2,1,0:T(8,128)S(1)}, f32[11,16,256]{2,1,0:T(8,128)S(1)}, u32[]{:S(2)}, u32[]{:S(2)}) collective-permute-start(f32[11,16,256]{2,1,0:T(8,128)S(1)} %collective-permute-done.4.refs_5_), channel_id=1, source_target_pairs={{0,4},{2,6},{4,0},{6,2},{8,12},{10,14},{12,8},{14,10},{16,20},{18,... | collective-permute-start | bytes 540680 | tf_op jit(solution)/shard_map/ppermute | solution.py:46
  55.1 6.1 %collective-permute-start.13 = (f32[4,16,256]{2,1,0:T(8,128)S(1)}, f32[4,16,256]{2,1,0:T(8,128)S(1)}, u32[]{:S(2)}, u32[]{:S(2)}) collective-permute-start(f32[4,16,256]{2,1,0:T(8,128)S(1)} %slice.43), channel_id=1, source_target_pairs={{0,2},{2,0},{4,6},{6,4},{8,10},{10,8},{12,14},{14,12},{16,18},{18,... | collective-permute-start | bytes 196616 | tf_op jit(solution)/shard_map/ppermute | solution.py:46
  56.1 5.1 %copy-start = (f32[1024,256]{1,0:T(8,128)S(1)}, f32[1024,256]{1,0:T(8,128)}, u32[]{:S(2)}) copy-start(f32[1024,256]{1,0:T(8,128)} %refs_1_.6) | copy-start | bytes 3145732
  56.2 5.1 %collective-permute-start.14 = (f32[4,16,256]{2,1,0:T(8,128)S(1)}, f32[4,16,256]{2,1,0:T(8,128)S(1)}, u32[]{:S(2)}, u32[]{:S(2)}) collective-permute-start(f32[4,16,256]{2,1,0:T(8,128)S(1)} %slice.45), channel_id=1, source_target_pairs={{0,4},{2,6},{4,0},{6,2},{8,12},{10,14},{12,8},{14,10},{16,20},{18,... | collective-permute-start | bytes 196616 | tf_op jit(solution)/shard_map/ppermute | solution.py:46
  58.6 8.6 %collective-permute-start.19 = (f32[27,16,256]{2,1,0:T(8,128)S(1)}, f32[27,16,256]{2,1,0:T(8,128)S(1)}, u32[]{:S(2)}, u32[]{:S(2)}) collective-permute-start(f32[27,16,256]{2,1,0:T(8,128)S(1)} %pad_maximum_fusion.1), channel_id=1, source_target_pairs={{0,4},{2,6},{4,0},{6,2},{8,12},{10,14},{12,8},{14,10},{16,20},{18,... | collective-permute-start | bytes 1327112 | tf_op jit(solution)/shard_map/ppermute | solution.py:46
  59.9 8.5 %collective-permute-start.18 = (f32[28,16,256]{2,1,0:T(8,128)S(1)}, f32[28,16,256]{2,1,0:T(8,128)S(1)}, u32[]{:S(2)}, u32[]{:S(2)}) collective-permute-start(f32[28,16,256]{2,1,0:T(8,128)S(1)} %pad_maximum_fusion), channel_id=1, source_target_pairs={{0,2},{2,0},{4,6},{6,4},{8,10},{10,8},{12,14},{14,12},{16,18},{18,... | collective-permute-start | bytes 1376264 | tf_op jit(solution)/shard_map/ppermute | solution.py:46
  66.2 3.3 %collective-permute-start.15 = (f32[344,256]{1,0:T(8,128)S(1)}, f32[344,256]{1,0:T(8,128)S(1)}, u32[]{:S(2)}, u32[]{:S(2)}) collective-permute-start(f32[344,256]{1,0:T(8,128)S(1)} %get-tuple-element.29.refs_0_), channel_id=1, source_target_pairs={{0,1},{1,0},{2,3},{3,2},{4,5},{5,4},{6,7},{7,6},{8,9},{9,8},{10,11... | collective-permute-start | bytes 1056776 | tf_op jit(solution)/shard_map/ppermute | solution.py:476
  66.3 3.2 %collective-permute-start.16 = (f32[344,256]{1,0:T(8,128)S(1)}, f32[344,256]{1,0:T(8,128)S(1)}, u32[]{:S(2)}, u32[]{:S(2)}) collective-permute-start(f32[344,256]{1,0:T(8,128)S(1)} %get-tuple-element.30.refs_1_), channel_id=1, source_target_pairs={{0,1},{1,0},{2,3},{3,2},{4,5},{5,4},{6,7},{7,6},{8,9},{9,8},{10,11... | collective-permute-start | bytes 1056776 | tf_op jit(solution)/shard_map/ppermute | solution.py:476
  66.8 2.7 %collective-permute-start.17 = (f32[336,256]{1,0:T(8,128)S(1)}, f32[336,256]{1,0:T(8,128)S(1)}, u32[]{:S(2)}, u32[]{:S(2)}) collective-permute-start(f32[336,256]{1,0:T(8,128)S(1)} %get-tuple-element.31.refs_2_), channel_id=1, source_target_pairs={{0,1},{1,0},{2,3},{3,2},{4,5},{5,4},{6,7},{7,6},{8,9},{9,8},{10,11... | collective-permute-start | bytes 1032200 | tf_op jit(solution)/shard_map/ppermute | solution.py:476
  67.2 6.7 %collective-permute-start.20 = (f32[11,16,256]{2,1,0:T(8,128)S(1)}, f32[11,16,256]{2,1,0:T(8,128)S(1)}, u32[]{:S(2)}, u32[]{:S(2)}) collective-permute-start(f32[11,16,256]{2,1,0:T(8,128)S(1)} %slice.46), channel_id=1, source_target_pairs={{0,2},{2,0},{4,6},{6,4},{8,10},{10,8},{12,14},{14,12},{16,18},{18,... | collective-permute-start | bytes 540680 | tf_op jit(solution)/shard_map/ppermute | solution.py:46
  68.4 6.2 %collective-permute-start.21 = (f32[11,16,256]{2,1,0:T(8,128)S(1)}, f32[11,16,256]{2,1,0:T(8,128)S(1)}, u32[]{:S(2)}, u32[]{:S(2)}) collective-permute-start(f32[11,16,256]{2,1,0:T(8,128)S(1)} %slice.47), channel_id=1, source_target_pairs={{0,4},{2,6},{4,0},{6,2},{8,12},{10,14},{12,8},{14,10},{16,20},{18,... | collective-permute-start | bytes 540680 | tf_op jit(solution)/shard_map/ppermute | solution.py:46
  (6 other events, 11.5 us)

commit v18 on v15

--- a/solution.py
+++ b/solution.py
@@ -56,6 +56,28 @@
     second = joined(*more, cut(pair[1], half, size))
     first = joined(*more, cut(pair[0], 0, half))
     return second, first
+
+
+def onward_joined(pair, size, more, axis):
+    half = size // 2
+    second, first = more[1] + pair[1][1][half:size], more[1] + pair[0][1][:half]
+    length = len(more[1])
+
+    def kernel(first_ref, second_ref, more_ref, to_first_ref, to_second_ref):
+        to_first_ref[:length] = to_second_ref[:length] = more_ref[...]
+        to_first_ref[length:] = second_ref[half:size]
+        to_second_ref[length:] = first_ref[:half]
+
+    out = pl.pallas_call(
+        kernel,
+        out_shape=shapes([(len(names), *more[0].shape[1:]) for names in (second, first)]),
+        in_specs=[VMEM] * 3,
+        out_specs=[VMEM] * 2,
+        compiler_params=pltpu.CompilerParams(vmem_limit_bytes=SMALL_LIMIT),
+        cost_estimate=pl.CostEstimate(flops=0, bytes_accessed=4 * more[0].size, transcendentals=0),
+        name="onward",
+    )(pair[0][0], pair[1][0], more[0])
+    return (out[0], second), (out[1], first)
 
 
 def send_both(parts, axis):
@@ -96,7 +118,7 @@
     near, far = joined(*jacobian_line[1:-1]), jacobian_line[-1]
     near_round = around(near, axis)
     near_last = [after(part, *factor_parts) for part in near_round]
-    far_parts = onward(near_last, len(near[1]), [far], axis)
+    far_parts = onward_joined(near_last, len(near[1]), far, axis)
     far_round = send_both(far_parts, axis)
     far_across = send_both(onward(far_round, len(far[1]), [], axis), axis)
     right_side, _ = after((right_side, None), *far_parts)

time: 58 us -> 58.8 us (1.014)
  waiting for transfers between devices: 18 us -> 19.2 us
  local copies, waits for them, and re-layouts: 1.1 us -> 0.41 us
    ppermute x19, waiting for transfers between devices: 18 us -> 19.2 us  [sent(): lax.ppermute(array, axis, [(i, i ^ mask) for i in range(lax.axis_size(axi...]
    unnamed x14 -> x10, local copies, waits for them, and re-layouts: 1.01 us -> 0.33 us
  transfers between devices with their start and end apart: 22 -> 22, of which waited for: 12 -> 9; matrix products, arithmetic and copies ran while one was open for 0% -> 0% of each run, Pallas kernels for 17% -> 17%
where the time goes in v18:
time: 58.8 us; the launch traced here: 58.6 us
  starting transfers between devices  24.6 us (42%)
  waiting for transfers between devices  19.2 us (33%)
  Pallas kernels  13.4 us (23%)
  between operations  0.82 us (1%)
    ppermute x19, starting transfers between devices, sent(): lax.ppermute(array, axis, [(i, i ^ mask) for i in range(lax.axis_size(axi...  24 us
    ppermute x19, waiting for transfers between devices, sent(): lax.ppermute(array, axis, [(i, i ^ mask) for i in range(lax.axis_size(axi...  19.2 us
    pallas_call x1, Pallas kernels, solve(): pl.pallas_call(kernel, out_shape=shapes([(span, columns)] + [(span, size)...  4.99 us
    pallas_call x2, Pallas kernels, subtract_product(): pl.pallas_call(kernel, out_shape=shapes([(span, columns)])[0], in_specs=[...  3.82 us
    pallas_call x1, Pallas kernels, pack(): pl.pallas_call(kernel, out_shape=shapes([(count, rows, size) for count in...  1.86 us
    pallas_call x1, Pallas kernels, finish(): pl.pallas_call(kernel, out_shape=shapes([(span, columns)]) + [windows, wi...  1.77 us
  transfers between devices with their start and end apart: 22, of which 9 were waited for; matrix products, arithmetic and copies ran while one was open for 0% of the time, Pallas kernels for 17%

profile of v18, /device:TPU:0, one launch (start us, length us, event | category | flops | bytes accessed | tf_op | source)
XLA Modules:
  0.0 58.6 jit_solution(11367489524905695665)
XLA Ops:
  0.6 1.9 %pack.1 = (f32[8,16,256]{2,1,0:T(8,128)}, f32[11,16,256]{2,1,0:T(8,128)}, f32[19,16,256]{2,1,0:T(8,128)}) custom-call(f32[4,16,256]{2,1,0:T(8,128)} %diag_ref.1, f32[4,16,256]{2,1,0:T(8,128)} %lower_ref.1, f32[4,16,768]{2,1,0:T(8,128)} %jacobian_ref.1), custom_call_target="tpu_custom_call" | custom-call | tf_op jit(solution)/shard_map/pack/pallas_call | solution.py:144
  2.5 3.0 %collective-permute-start.2 = (f32[19,16,256]{2,1,0:T(8,128)}, f32[19,16,256]{2,1,0:T(8,128)S(1)}, u32[]{:S(2)}, u32[]{:S(2)}) collective-permute-start(f32[19,16,256]{2,1,0:T(8,128)} %get-tuple-element.24.refs_2_.refs_4_), channel_id=1, source_target_pairs={{0,4},{2,6},{4,0},{6,2},{8,12},{10,14},{12,8},{14,10},{16,20},{18,... | collective-permute-start | bytes 933896 | tf_op jit(solution)/shard_map/ppermute | solution.py:46
  5.5 1.5 %collective-permute-start.3 = (f32[19,16,256]{2,1,0:T(8,128)}, f32[19,16,256]{2,1,0:T(8,128)S(1)}, u32[]{:S(2)}, u32[]{:S(2)}) collective-permute-start(f32[19,16,256]{2,1,0:T(8,128)} %get-tuple-element.24.refs_2_.refs_4_), channel_id=1, source_target_pairs={{0,2},{2,0},{4,6},{6,4},{8,10},{10,8},{12,14},{14,12},{16,18},{18,... | collective-permute-start | bytes 933896 | tf_op jit(solution)/shard_map/ppermute | solution.py:46
  7.0 3.6 %collective-permute-start = (f32[8,16,256]{2,1,0:T(8,128)}, f32[8,16,256]{2,1,0:T(8,128)S(1)}, u32[]{:S(2)}, u32[]{:S(2)}) collective-permute-start(f32[8,16,256]{2,1,0:T(8,128)} %get-tuple-element.23), channel_id=1, source_target_pairs={{0,24},{2,26},{4,28},{6,30},{8,16},{10,18},{12,20},{14,22},{16,8},... | collective-permute-start | bytes 393224 | tf_op jit(solution)/shard_map/ppermute | solution.py:46
  10.6 2.5 %collective-permute-done.2.refs_7_.refs_8_ = f32[19,16,256]{2,1,0:T(8,128)S(1)} collective-permute-done((f32[19,16,256]{2,1,0:T(8,128)}, f32[19,16,256]{2,1,0:T(8,128)S(1)}, u32[]{:S(2)}, u32[]{:S(2)}) %collective-permute-start.2) | collective-permute-done | bytes 311328 | tf_op jit(solution)/shard_map/ppermute | solution.py:46
  13.0 2.1 %collective-permute-done.refs_3_ = f32[8,16,256]{2,1,0:T(8,128)S(1)} collective-permute-done((f32[8,16,256]{2,1,0:T(8,128)}, f32[8,16,256]{2,1,0:T(8,128)S(1)}, u32[]{:S(2)}, u32[]{:S(2)}) %collective-permute-start) | collective-permute-done | bytes 131104 | tf_op jit(solution)/shard_map/ppermute | solution.py:46
  15.2 1.4 %collective-permute-done.1.refs_4_ = f32[8,16,256]{2,1,0:T(8,128)S(1)} collective-permute-done((f32[8,16,256]{2,1,0:T(8,128)}, f32[8,16,256]{2,1,0:T(8,128)S(1)}, u32[]{:S(2)}, u32[]{:S(2)}) %collective-permute-start.1) | collective-permute-done | bytes 131104 | tf_op jit(solution)/shard_map/ppermute | solution.py:46
  18.2 2.1 %collective-permute-start.4 = (f32[11,16,256]{2,1,0:T(8,128)S(1)}, f32[11,16,256]{2,1,0:T(8,128)S(1)}, u32[]{:S(2)}, u32[]{:S(2)}) collective-permute-start(f32[11,16,256]{2,1,0:T(8,128)S(1)} %copy-done.4), channel_id=1, source_target_pairs={{0,24},{2,26},{4,28},{6,30},{8,16},{10,18},{12,20},{14,22},{16,8},... | collective-permute-start | bytes 540680 | tf_op jit(solution)/shard_map/ppermute | solution.py:46
  20.3 6.4 %collective-permute-done.4.refs_5_ = f32[11,16,256]{2,1,0:T(8,128)S(1)} collective-permute-done((f32[11,16,256]{2,1,0:T(8,128)S(1)}, f32[11,16,256]{2,1,0:T(8,128)S(1)}, u32[]{:S(2)}, u32[]{:S(2)}) %collective-permute-start.4) | collective-permute-done | bytes 180256 | tf_op jit(solution)/shard_map/ppermute | solution.py:46
  26.7 1.7 %collective-permute-start.12 = (f32[22,16,256]{2,1,0:T(8,128)S(1)}, f32[22,16,256]{2,1,0:T(8,128)S(1)}, u32[]{:S(2)}, u32[]{:S(2)}) collective-permute-start(f32[22,16,256]{2,1,0:T(8,128)S(1)} %pad_maximum_fusion.2), channel_id=1, source_target_pairs={{0,8},{2,10},{4,12},{6,14},{8,0},{10,2},{12,4},{14,6},{16,24},{18,... | collective-permute-start | bytes 1081352 | tf_op jit(solution)/shard_map/ppermute | solution.py:46
  28.5 1.1 %collective-permute-start.8 = (f32[16,16,256]{2,1,0:T(8,128)S(1)}, f32[16,16,256]{2,1,0:T(8,128)S(1)}, u32[]{:S(2)}, u32[]{:S(2)}) collective-permute-start(f32[16,16,256]{2,1,0:T(8,128)S(1)} %get-tuple-element.41), channel_id=1, source_target_pairs={{0,4},{2,6},{4,0},{6,2},{8,12},{10,14},{12,8},{14,10},{16,20},{18,... | collective-permute-start | bytes 786440 | tf_op jit(solution)/shard_map/ppermute | solution.py:46
  29.6 1.1 %collective-permute-start.10 = (f32[16,16,256]{2,1,0:T(8,128)S(1)}, f32[16,16,256]{2,1,0:T(8,128)S(1)}, u32[]{:S(2)}, u32[]{:S(2)}) collective-permute-start(f32[16,16,256]{2,1,0:T(8,128)S(1)} %get-tuple-element.40), channel_id=1, source_target_pairs={{0,2},{2,0},{4,6},{6,4},{8,10},{10,8},{12,14},{14,12},{16,18},{18,... | collective-permute-start | bytes 786440 | tf_op jit(solution)/shard_map/ppermute | solution.py:46
  30.7 1.1 %collective-permute-start.11 = (f32[11,16,256]{2,1,0:T(8,128)S(1)}, f32[11,16,256]{2,1,0:T(8,128)S(1)}, u32[]{:S(2)}, u32[]{:S(2)}) collective-permute-start(f32[11,16,256]{2,1,0:T(8,128)S(1)} %collective-permute-done.4.refs_5_), channel_id=1, source_target_pairs={{0,4},{2,6},{4,0},{6,2},{8,12},{10,14},{12,8},{14,10},{16,20},{18,... | collective-permute-start | bytes 540680 | tf_op jit(solution)/shard_map/ppermute | solution.py:46
  32.6 4.0 %collective-permute-done.8.refs_11_ = f32[16,16,256]{2,1,0:T(8,128)S(1)} collective-permute-done((f32[16,16,256]{2,1,0:T(8,128)S(1)}, f32[16,16,256]{2,1,0:T(8,128)S(1)}, u32[]{:S(2)}, u32[]{:S(2)}) %collective-permute-start.8) | collective-permute-done | bytes 262176 | tf_op jit(solution)/shard_map/ppermute | solution.py:46
  36.7 1.2 %collective-permute-start.13 = (f32[4,16,256]{2,1,0:T(8,128)S(1)}, f32[4,16,256]{2,1,0:T(8,128)S(1)}, u32[]{:S(2)}, u32[]{:S(2)}) collective-permute-start(f32[4,16,256]{2,1,0:T(8,128)S(1)} %slice.35), channel_id=1, source_target_pairs={{0,2},{2,0},{4,6},{6,4},{8,10},{10,8},{12,14},{14,12},{16,18},{18,... | collective-permute-start | bytes 196616 | tf_op jit(solution)/shard_map/ppermute | solution.py:46
  39.5 1.4 %collective-permute-done.5.first_ref.refs_11_ = f32[11,16,256]{2,1,0:T(8,128)S(1)} collective-permute-done((f32[11,16,256]{2,1,0:T(8,128)S(1)}, f32[11,16,256]{2,1,0:T(8,128)S(1)}, u32[]{:S(2)}, u32[]{:S(2)}) %collective-permute-start.5) | collective-permute-done | bytes 180256 | tf_op jit(solution)/shard_map/ppermute | solution.py:46
  42.0 1.6 %collective-permute-start.19 = (f32[27,16,256]{2,1,0:T(8,128)S(1)}, f32[27,16,256]{2,1,0:T(8,128)S(1)}, u32[]{:S(2)}, u32[]{:S(2)}) collective-permute-start(f32[27,16,256]{2,1,0:T(8,128)S(1)} %get-tuple-element.29), channel_id=1, source_target_pairs={{0,4},{2,6},{4,0},{6,2},{8,12},{10,14},{12,8},{14,10},{16,20},{18,... | collective-permute-start | bytes 1327112 | tf_op jit(solution)/shard_map/ppermute | solution.py:46
  43.6 5.0 %solve.1 = (f32[1024,256]{1,0:T(8,128)S(1)}, f32[1024,256]{1,0:T(8,128)S(1)}, f32[344,256]{1,0:T(8,128)S(1)}, f32[344,256]{1,0:T(8,128)S(1)}, f32[336,256]{1,0:T(8,128)S(1)}) custom-call(f32[16,256]{1,0:T(8,128)S(1)} %get-tuple-element.21.refs_0_, f32[1024,256]{1,0:T(8,128)S(1)} %copy-done, f32[19,16,256]{2,1,0:T(8,128)S(1)} %copy-done.1, ...), custom_call_target="tpu_custom_call" | custom-call | flops 2147483648 | bytes 262144 | tf_op jit(solution)/shard_map/solve/pallas_call | solution.py:301
  49.2 1.1 %collective-permute-done.19.refs_14_ = f32[27,16,256]{2,1,0:T(8,128)S(1)} collective-permute-done((f32[27,16,256]{2,1,0:T(8,128)S(1)}, f32[27,16,256]{2,1,0:T(8,128)S(1)}, u32[]{:S(2)}, u32[]{:S(2)}) %collective-permute-start.19) | collective-permute-done | bytes 442400 | tf_op jit(solution)/shard_map/ppermute | solution.py:46
  50.3 1.2 %collective-permute-start.20 = (f32[11,16,256]{2,1,0:T(8,128)S(1)}, f32[11,16,256]{2,1,0:T(8,128)S(1)}, u32[]{:S(2)}, u32[]{:S(2)}) collective-permute-start(f32[11,16,256]{2,1,0:T(8,128)S(1)} %slice.38), channel_id=1, source_target_pairs={{0,2},{2,0},{4,6},{6,4},{8,10},{10,8},{12,14},{14,12},{16,18},{18,... | collective-permute-start | bytes 540680 | tf_op jit(solution)/shard_map/ppermute | solution.py:46
  51.5 1.3 %collective-permute-start.21 = (f32[11,16,256]{2,1,0:T(8,128)S(1)}, f32[11,16,256]{2,1,0:T(8,128)S(1)}, u32[]{:S(2)}, u32[]{:S(2)}) collective-permute-start(f32[11,16,256]{2,1,0:T(8,128)S(1)} %slice.39), channel_id=1, source_target_pairs={{0,4},{2,6},{4,0},{6,2},{8,12},{10,14},{12,8},{14,10},{16,20},{18,... | collective-permute-start | bytes 540680 | tf_op jit(solution)/shard_map/ppermute | solution.py:46
  52.9 1.8 %finish.1 = (f32[1024,256]{1,0:T(8,128)}, bf16[1536,256]{1,0:T(8,128)(2,1)S(1)}, bf16[1536,256]{1,0:T(8,128)(2,1)S(1)}) custom-call(f32[1024,256]{1,0:T(8,128)S(1)} %get-tuple-element.31.sol_ref, f32[1024,256]{1,0:T(8,128)S(1)} %get-tuple-element.32.part_ref, f32[344,256]{1,0:T(8,128)S(1)} %get-tuple-element.33.refs_0_, ...), custom_call_target="tpu_custom_call" | custom-call | flops 100663296 | bytes 262144 | tf_op jit(solution)/shard_map/finish/pallas_call | solution.py:358
  54.6 2.3 %residual.1.refs_4_ = f32[1024,256]{1,0:T(8,128)} custom-call(f32[16,768]{1,0:T(8,128)S(1)} %get-tuple-element.37.refs_0_, f32[1024,256]{1,0:T(8,128)S(1)} %copy-done, bf16[1536,256]{1,0:T(8,128)(2,1)S(1)} %get-tuple-element.38.refs_2_, bf16[1536,256]{1,0:T(8,128)(2,1)S(1)} %get-tuple-element.39.refs_3_, f32[19,16,256]{2,1,0:T(8,128)S(1)} %copy-done.1, ...), custom_call_target="tpu_custom_call" | custom-call | flops 1056964608 | bytes 5505024 | tf_op jit(solution)/shard_map/residual/pallas_call | solution.py:432
  57.1 1.6 %residual_rest.1 = f32[1024,256]{1,0:T(8,128)} custom-call(f32[16,768]{1,0:T(8,128)S(1)} %get-tuple-element.37.refs_0_, f32[1024,256]{1,0:T(8,128)S(1)} %copy-done, bf16[1536,256]{1,0:T(8,128)(2,1)S(1)} %get-tuple-element.38.refs_2_, bf16[1536,256]{1,0:T(8,128)(2,1)S(1)} %get-tuple-element.39.refs_3_, ...), custom_call_target="tpu_custom_call", output_to_operand_aliasing={{}: (4, {})} | custom-call | flops 150994944 | bytes 786432 | tf_op jit(solution)/shard_map/residual_rest/pallas_call | solution.py:432
  (49 shorter events, 6.0 us)
Async XLA Ops:
  2.5 10.5 %collective-permute-start.2 = (f32[19,16,256]{2,1,0:T(8,128)}, f32[19,16,256]{2,1,0:T(8,128)S(1)}, u32[]{:S(2)}, u32[]{:S(2)}) collective-permute-start(f32[19,16,256]{2,1,0:T(8,128)} %get-tuple-element.24.refs_2_.refs_4_), channel_id=1, source_target_pairs={{0,4},{2,6},{4,0},{6,2},{8,12},{10,14},{12,8},{14,10},{16,20},{18,... | collective-permute-start | bytes 933896 | tf_op jit(solution)/shard_map/ppermute | solution.py:46
  5.5 11.8 %collective-permute-start.3 = (f32[19,16,256]{2,1,0:T(8,128)}, f32[19,16,256]{2,1,0:T(8,128)S(1)}, u32[]{:S(2)}, u32[]{:S(2)}) collective-permute-start(f32[19,16,256]{2,1,0:T(8,128)} %get-tuple-element.24.refs_2_.refs_4_), channel_id=1, source_target_pairs={{0,2},{2,0},{4,6},{6,4},{8,10},{10,8},{12,14},{14,12},{16,18},{18,... | collective-permute-start | bytes 933896 | tf_op jit(solution)/shard_map/ppermute | solution.py:46
  7.0 8.2 %collective-permute-start = (f32[8,16,256]{2,1,0:T(8,128)}, f32[8,16,256]{2,1,0:T(8,128)S(1)}, u32[]{:S(2)}, u32[]{:S(2)}) collective-permute-start(f32[8,16,256]{2,1,0:T(8,128)} %get-tuple-element.23), channel_id=1, source_target_pairs={{0,24},{2,26},{4,28},{6,30},{8,16},{10,18},{12,20},{14,22},{16,8},... | collective-permute-start | bytes 393224 | tf_op jit(solution)/shard_map/ppermute | solution.py:46
  10.6 6.1 %collective-permute-start.1 = (f32[8,16,256]{2,1,0:T(8,128)}, f32[8,16,256]{2,1,0:T(8,128)S(1)}, u32[]{:S(2)}, u32[]{:S(2)}) collective-permute-start(f32[8,16,256]{2,1,0:T(8,128)} %get-tuple-element.23), channel_id=1, source_target_pairs={{0,8},{2,10},{4,12},{6,14},{8,0},{10,2},{12,4},{14,6},{16,24},{18,... | collective-permute-start | bytes 393224 | tf_op jit(solution)/shard_map/ppermute | solution.py:46
  16.6 11.8 %collective-permute-start.7 = (f32[26,16,256]{2,1,0:T(8,128)S(1)}, f32[26,16,256]{2,1,0:T(8,128)S(1)}, u32[]{:S(2)}, u32[]{:S(2)}) collective-permute-start(f32[26,16,256]{2,1,0:T(8,128)S(1)} %pad_maximum_fusion), channel_id=1, source_target_pairs={{0,2},{2,0},{4,6},{6,4},{8,10},{10,8},{12,14},{14,12},{16,18},{18,... | collective-permute-start | bytes 1277960 | tf_op jit(solution)/shard_map/ppermute | solution.py:46
  17.3 11.1 %collective-permute-start.9 = (f32[25,16,256]{2,1,0:T(8,128)S(1)}, f32[25,16,256]{2,1,0:T(8,128)S(1)}, u32[]{:S(2)}, u32[]{:S(2)}) collective-permute-start(f32[25,16,256]{2,1,0:T(8,128)S(1)} %pad_maximum_fusion.1), channel_id=1, source_target_pairs={{0,4},{2,6},{4,0},{6,2},{8,12},{10,14},{12,8},{14,10},{16,20},{18,... | collective-permute-start | bytes 1228808 | tf_op jit(solution)/shard_map/ppermute | solution.py:46
  18.2 8.5 %collective-permute-start.4 = (f32[11,16,256]{2,1,0:T(8,128)S(1)}, f32[11,16,256]{2,1,0:T(8,128)S(1)}, u32[]{:S(2)}, u32[]{:S(2)}) collective-permute-start(f32[11,16,256]{2,1,0:T(8,128)S(1)} %copy-done.4), channel_id=1, source_target_pairs={{0,24},{2,26},{4,28},{6,30},{8,16},{10,18},{12,20},{14,22},{16,8},... | collective-permute-start | bytes 540680 | tf_op jit(solution)/shard_map/ppermute | solution.py:46
  20.3 8.1 %collective-permute-start.6 = (f32[8,16,256]{2,1,0:T(8,128)S(1)}, f32[8,16,256]{2,1,0:T(8,128)S(1)}, u32[]{:S(2)}, u32[]{:S(2)}) collective-permute-start(f32[8,16,256]{2,1,0:T(8,128)S(1)} %collective-permute-done.refs_3_), channel_id=1, source_target_pairs={{0,8},{2,10},{4,12},{6,14},{8,0},{10,2},{12,4},{14,6},{16,24},{18,... | collective-permute-start | bytes 393224 | tf_op jit(solution)/shard_map/ppermute | solution.py:46
  26.7 14.2 %collective-permute-start.12 = (f32[22,16,256]{2,1,0:T(8,128)S(1)}, f32[22,16,256]{2,1,0:T(8,128)S(1)}, u32[]{:S(2)}, u32[]{:S(2)}) collective-permute-start(f32[22,16,256]{2,1,0:T(8,128)S(1)} %pad_maximum_fusion.2), channel_id=1, source_target_pairs={{0,8},{2,10},{4,12},{6,14},{8,0},{10,2},{12,4},{14,6},{16,24},{18,... | collective-permute-start | bytes 1081352 | tf_op jit(solution)/shard_map/ppermute | solution.py:46
  28.4 15.2 %copy-start = (f32[1024,256]{1,0:T(8,128)S(1)}, f32[1024,256]{1,0:T(8,128)}, u32[]{:S(2)}) copy-start(f32[1024,256]{1,0:T(8,128)} %refs_1_.6) | copy-start | bytes 3145732
  28.5 8.1 %collective-permute-start.8 = (f32[16,16,256]{2,1,0:T(8,128)S(1)}, f32[16,16,256]{2,1,0:T(8,128)S(1)}, u32[]{:S(2)}, u32[]{:S(2)}) collective-permute-start(f32[16,16,256]{2,1,0:T(8,128)S(1)} %get-tuple-element.41), channel_id=1, source_target_pairs={{0,4},{2,6},{4,0},{6,2},{8,12},{10,14},{12,8},{14,10},{16,20},{18,... | collective-permute-start | bytes 786440 | tf_op jit(solution)/shard_map/ppermute | solution.py:46
  29.6 8.3 %collective-permute-start.10 = (f32[16,16,256]{2,1,0:T(8,128)S(1)}, f32[16,16,256]{2,1,0:T(8,128)S(1)}, u32[]{:S(2)}, u32[]{:S(2)}) collective-permute-start(f32[16,16,256]{2,1,0:T(8,128)S(1)} %get-tuple-element.40), channel_id=1, source_target_pairs={{0,2},{2,0},{4,6},{6,4},{8,10},{10,8},{12,14},{14,12},{16,18},{18,... | collective-permute-start | bytes 786440 | tf_op jit(solution)/shard_map/ppermute | solution.py:46
  30.7 8.8 %collective-permute-start.11 = (f32[11,16,256]{2,1,0:T(8,128)S(1)}, f32[11,16,256]{2,1,0:T(8,128)S(1)}, u32[]{:S(2)}, u32[]{:S(2)}) collective-permute-start(f32[11,16,256]{2,1,0:T(8,128)S(1)} %collective-permute-done.4.refs_5_), channel_id=1, source_target_pairs={{0,4},{2,6},{4,0},{6,2},{8,12},{10,14},{12,8},{14,10},{16,20},{18,... | collective-permute-start | bytes 540680 | tf_op jit(solution)/shard_map/ppermute | solution.py:46
  31.8 9.1 %collective-permute-start.5 = (f32[11,16,256]{2,1,0:T(8,128)S(1)}, f32[11,16,256]{2,1,0:T(8,128)S(1)}, u32[]{:S(2)}, u32[]{:S(2)}) collective-permute-start(f32[11,16,256]{2,1,0:T(8,128)S(1)} %collective-permute-done.4.refs_5_), channel_id=1, source_target_pairs={{0,2},{2,0},{4,6},{6,4},{8,10},{10,8},{12,14},{14,12},{16,18},{18,... | collective-permute-start | bytes 540680 | tf_op jit(solution)/shard_map/ppermute | solution.py:46
  36.7 6.9 %collective-permute-start.13 = (f32[4,16,256]{2,1,0:T(8,128)S(1)}, f32[4,16,256]{2,1,0:T(8,128)S(1)}, u32[]{:S(2)}, u32[]{:S(2)}) collective-permute-start(f32[4,16,256]{2,1,0:T(8,128)S(1)} %slice.35), channel_id=1, source_target_pairs={{0,2},{2,0},{4,6},{6,4},{8,10},{10,8},{12,14},{14,12},{16,18},{18,... | collective-permute-start | bytes 196616 | tf_op jit(solution)/shard_map/ppermute | solution.py:46
  37.9 5.7 %collective-permute-start.14 = (f32[4,16,256]{2,1,0:T(8,128)S(1)}, f32[4,16,256]{2,1,0:T(8,128)S(1)}, u32[]{:S(2)}, u32[]{:S(2)}) collective-permute-start(f32[4,16,256]{2,1,0:T(8,128)S(1)} %slice.37), channel_id=1, source_target_pairs={{0,4},{2,6},{4,0},{6,2},{8,12},{10,14},{12,8},{14,10},{16,20},{18,... | collective-permute-start | bytes 196616 | tf_op jit(solution)/shard_map/ppermute | solution.py:46
  39.4 4.2 %copy-start.1 = (f32[19,16,256]{2,1,0:T(8,128)S(1)}, f32[19,16,256]{2,1,0:T(8,128)}, u32[]{:S(2)}) copy-start(f32[19,16,256]{2,1,0:T(8,128)} %get-tuple-element.24.refs_2_.refs_4_) | copy-start | bytes 933892
  41.0 10.5 %collective-permute-start.18 = (f32[28,16,256]{2,1,0:T(8,128)S(1)}, f32[28,16,256]{2,1,0:T(8,128)S(1)}, u32[]{:S(2)}, u32[]{:S(2)}) collective-permute-start(f32[28,16,256]{2,1,0:T(8,128)S(1)} %get-tuple-element.28), channel_id=1, source_target_pairs={{0,2},{2,0},{4,6},{6,4},{8,10},{10,8},{12,14},{14,12},{16,18},{18,... | collective-permute-start | bytes 1376264 | tf_op jit(solution)/shard_map/ppermute | solution.py:46
  42.0 8.3 %collective-permute-start.19 = (f32[27,16,256]{2,1,0:T(8,128)S(1)}, f32[27,16,256]{2,1,0:T(8,128)S(1)}, u32[]{:S(2)}, u32[]{:S(2)}) collective-permute-start(f32[27,16,256]{2,1,0:T(8,128)S(1)} %get-tuple-element.29), channel_id=1, source_target_pairs={{0,4},{2,6},{4,0},{6,2},{8,12},{10,14},{12,8},{14,10},{16,20},{18,... | collective-permute-start | bytes 1327112 | tf_op jit(solution)/shard_map/ppermute | solution.py:46
  48.6 4.3 %collective-permute-start.15 = (f32[344,256]{1,0:T(8,128)S(1)}, f32[344,256]{1,0:T(8,128)S(1)}, u32[]{:S(2)}, u32[]{:S(2)}) collective-permute-start(f32[344,256]{1,0:T(8,128)S(1)} %get-tuple-element.33.refs_0_), channel_id=1, source_target_pairs={{0,1},{1,0},{2,3},{3,2},{4,5},{5,4},{6,7},{7,6},{8,9},{9,8},{10,11... | collective-permute-start | bytes 1056776 | tf_op jit(solution)/shard_map/ppermute | solution.py:482
  48.7 4.2 %collective-permute-start.16 = (f32[344,256]{1,0:T(8,128)S(1)}, f32[344,256]{1,0:T(8,128)S(1)}, u32[]{:S(2)}, u32[]{:S(2)}) collective-permute-start(f32[344,256]{1,0:T(8,128)S(1)} %get-tuple-element.34.refs_1_), channel_id=1, source_target_pairs={{0,1},{1,0},{2,3},{3,2},{4,5},{5,4},{6,7},{7,6},{8,9},{9,8},{10,11... | collective-permute-start | bytes 1056776 | tf_op jit(solution)/shard_map/ppermute | solution.py:482
  49.2 3.7 %collective-permute-start.17 = (f32[336,256]{1,0:T(8,128)S(1)}, f32[336,256]{1,0:T(8,128)S(1)}, u32[]{:S(2)}, u32[]{:S(2)}) collective-permute-start(f32[336,256]{1,0:T(8,128)S(1)} %get-tuple-element.35.refs_2_), channel_id=1, source_target_pairs={{0,1},{1,0},{2,3},{3,2},{4,5},{5,4},{6,7},{7,6},{8,9},{9,8},{10,11... | collective-permute-start | bytes 1032200 | tf_op jit(solution)/shard_map/ppermute | solution.py:482
  50.3 6.6 %collective-permute-start.20 = (f32[11,16,256]{2,1,0:T(8,128)S(1)}, f32[11,16,256]{2,1,0:T(8,128)S(1)}, u32[]{:S(2)}, u32[]{:S(2)}) collective-permute-start(f32[11,16,256]{2,1,0:T(8,128)S(1)} %slice.38), channel_id=1, source_target_pairs={{0,2},{2,0},{4,6},{6,4},{8,10},{10,8},{12,14},{14,12},{16,18},{18,... | collective-permute-start | bytes 540680 | tf_op jit(solution)/shard_map/ppermute | solution.py:46
  51.5 5.6 %collective-permute-start.21 = (f32[11,16,256]{2,1,0:T(8,128)S(1)}, f32[11,16,256]{2,1,0:T(8,128)S(1)}, u32[]{:S(2)}, u32[]{:S(2)}) collective-permute-start(f32[11,16,256]{2,1,0:T(8,128)S(1)} %slice.39), channel_id=1, source_target_pairs={{0,4},{2,6},{4,0},{6,2},{8,12},{10,14},{12,8},{14,10},{16,20},{18,... | collective-permute-start | bytes 540680 | tf_op jit(solution)/shard_map/ppermute | solution.py:46
  (3 other events, 4.5 us)

commit v19 on v18

--- a/solution.py
+++ b/solution.py
@@ -101,10 +101,11 @@
     return line + [beside] + [sent(part, axis, last) for part in line[1:]]
 
 
-def gather_panels(own, factor, jacobian, right_side, axis):
+def gather_panels(own, factor, jacobian, right_side, tables, axis):
     factor_line = line_of(factor, axis)
     own_round = around(own, axis)
     near, far = joined(*factor_line[1:-1]), factor_line[-1]
+    far = after(far, *[(table, None) for table in tables])
     second_parts = onward(own_round, len(own[1]), [near], axis)
     second_round = send_both(second_parts, axis)
     third_parts = onward(second_round, len(near[1]), [far], axis)
@@ -465,10 +466,11 @@
     factor_own = blocks_of(factor_own, 0)
     jacobian_own = blocks_of(jacobian_own, 2 * supers)
     own = blocks_of(own, 0)
+    tables = factor_weights, jacobian_weights = widened([factor_pattern, jacobian_pattern], [size, 3 * size])
     count = lax.axis_size("rhs")
     relative = count >= 16 and not count & (count - 1)
     if relative:
-        arrived, last, late = gather_panels(own, factor_own, jacobian_own, right_side, "rhs")
+        arrived, last, late = gather_panels(own, factor_own, jacobian_own, right_side, tables, "rhs")
     else:
         arrived, last, late = gather_whole(own, "rhs"), [], right_side
     factor = places_of(arrived, 0, 2 * supers)
@@ -476,7 +478,6 @@
     whole = {owner: blocks for owner, blocks in places.items() if len(blocks) == 3 * supers - spare}
     partial = set(places) - set(whole)
 
-    factor_weights, jacobian_weights = widened([factor_pattern, jacobian_pattern], [size, 3 * size])
     sol, parts, leaving = solve(*factor, relative, late, factor_weights, nodes, supers, size)
     if nodes == 2:
         mail = [lax.ppermute(piece, "node", [(0, 1), (1, 0)]) for piece in leaving]

time: 58.8 us -> 58.6 us (level)
  transfers between devices with their start and end apart: 22 -> 22, of which waited for: 9 -> 8; matrix products, arithmetic and copies ran while one was open for 0% -> 0% of each run, Pallas kernels for 17% -> 17%
where the time goes in v19:
time: 58.6 us; the launch traced here: 58.5 us
  starting transfers between devices  24.1 us (41%)
  waiting for transfers between devices  19.6 us (33%)
  Pallas kernels  13.5 us (23%)
  between operations  0.83 us (1%)
    ppermute x19, starting transfers between devices, sent(): lax.ppermute(array, axis, [(i, i ^ mask) for i in range(lax.axis_size(axi...  23.4 us
    ppermute x19, waiting for transfers between devices, sent(): lax.ppermute(array, axis, [(i, i ^ mask) for i in range(lax.axis_size(axi...  19.6 us
    pallas_call x1, Pallas kernels, solve(): pl.pallas_call(kernel, out_shape=shapes([(span, columns)] + [(span, size)...  5 us
    pallas_call x2, Pallas kernels, subtract_product(): pl.pallas_call(kernel, out_shape=shapes([(span, columns)])[0], in_specs=[...  3.82 us
    pallas_call x1, Pallas kernels, pack(): pl.pallas_call(kernel, out_shape=shapes([(count, rows, size) for count in...  1.86 us
    pallas_call x1, Pallas kernels, finish(): pl.pallas_call(kernel, out_shape=shapes([(span, columns)]) + [windows, wi...  1.77 us
  transfers between devices with their start and end apart: 22, of which 8 were waited for; matrix products, arithmetic and copies ran while one was open for 0% of the time, Pallas kernels for 17%

profile of v19, /device:TPU:0, one launch (start us, length us, event | category | flops | bytes accessed | tf_op | source)
XLA Modules:
  0.0 58.5 jit_solution(1328540557734246343)
XLA Ops:
  0.6 1.9 %pack.1 = (f32[8,16,256]{2,1,0:T(8,128)}, f32[11,16,256]{2,1,0:T(8,128)}, f32[19,16,256]{2,1,0:T(8,128)}) custom-call(f32[4,16,256]{2,1,0:T(8,128)} %diag_ref.1, f32[4,16,256]{2,1,0:T(8,128)} %lower_ref.1, f32[4,16,768]{2,1,0:T(8,128)} %jacobian_ref.1), custom_call_target="tpu_custom_call" | custom-call | tf_op jit(solution)/shard_map/pack/pallas_call | solution.py:145
  2.5 3.0 %collective-permute-start.2 = (f32[19,16,256]{2,1,0:T(8,128)}, f32[19,16,256]{2,1,0:T(8,128)S(1)}, u32[]{:S(2)}, u32[]{:S(2)}) collective-permute-start(f32[19,16,256]{2,1,0:T(8,128)} %get-tuple-element.25.refs_2_.refs_4_), channel_id=1, source_target_pairs={{0,4},{2,6},{4,0},{6,2},{8,12},{10,14},{12,8},{14,10},{16,20},{18,... | collective-permute-start | bytes 933896 | tf_op jit(solution)/shard_map/ppermute | solution.py:46
  5.5 1.5 %collective-permute-start.3 = (f32[19,16,256]{2,1,0:T(8,128)}, f32[19,16,256]{2,1,0:T(8,128)S(1)}, u32[]{:S(2)}, u32[]{:S(2)}) collective-permute-start(f32[19,16,256]{2,1,0:T(8,128)} %get-tuple-element.25.refs_2_.refs_4_), channel_id=1, source_target_pairs={{0,2},{2,0},{4,6},{6,4},{8,10},{10,8},{12,14},{14,12},{16,18},{18,... | collective-permute-start | bytes 933896 | tf_op jit(solution)/shard_map/ppermute | solution.py:46
  7.0 3.6 %collective-permute-start = (f32[8,16,256]{2,1,0:T(8,128)}, f32[8,16,256]{2,1,0:T(8,128)S(1)}, u32[]{:S(2)}, u32[]{:S(2)}) collective-permute-start(f32[8,16,256]{2,1,0:T(8,128)} %get-tuple-element.24), channel_id=1, source_target_pairs={{0,24},{2,26},{4,28},{6,30},{8,16},{10,18},{12,20},{14,22},{16,8},... | collective-permute-start | bytes 393224 | tf_op jit(solution)/shard_map/ppermute | solution.py:46
  10.6 2.5 %collective-permute-done.2.refs_7_.refs_8_ = f32[19,16,256]{2,1,0:T(8,128)S(1)} collective-permute-done((f32[19,16,256]{2,1,0:T(8,128)}, f32[19,16,256]{2,1,0:T(8,128)S(1)}, u32[]{:S(2)}, u32[]{:S(2)}) %collective-permute-start.2) | collective-permute-done | bytes 311328 | tf_op jit(solution)/shard_map/ppermute | solution.py:46
  13.0 2.1 %collective-permute-done.refs_3_ = f32[8,16,256]{2,1,0:T(8,128)S(1)} collective-permute-done((f32[8,16,256]{2,1,0:T(8,128)}, f32[8,16,256]{2,1,0:T(8,128)S(1)}, u32[]{:S(2)}, u32[]{:S(2)}) %collective-permute-start) | collective-permute-done | bytes 131104 | tf_op jit(solution)/shard_map/ppermute | solution.py:46
  15.2 1.4 %collective-permute-done.1.refs_4_ = f32[8,16,256]{2,1,0:T(8,128)S(1)} collective-permute-done((f32[8,16,256]{2,1,0:T(8,128)}, f32[8,16,256]{2,1,0:T(8,128)S(1)}, u32[]{:S(2)}, u32[]{:S(2)}) %collective-permute-start.1) | collective-permute-done | bytes 131104 | tf_op jit(solution)/shard_map/ppermute | solution.py:46
  18.2 2.1 %collective-permute-start.4 = (f32[11,16,256]{2,1,0:T(8,128)S(1)}, f32[11,16,256]{2,1,0:T(8,128)S(1)}, u32[]{:S(2)}, u32[]{:S(2)}) collective-permute-start(f32[11,16,256]{2,1,0:T(8,128)S(1)} %copy-done.4), channel_id=1, source_target_pairs={{0,24},{2,26},{4,28},{6,30},{8,16},{10,18},{12,20},{14,22},{16,8},... | collective-permute-start | bytes 540680 | tf_op jit(solution)/shard_map/ppermute | solution.py:46
  20.3 0.9 %widened.1 = (f32[16,256]{1,0:T(8,128)S(1)}, f32[16,768]{1,0:T(8,128)S(1)}) custom-call(s32[4,4,4]{2,1,0:T(4,128)S(1)} %copy-done.2, s32[4,4,12]{2,1,0:T(4,128)S(1)} %copy-done.3), custom_call_target="tpu_custom_call" | custom-call | tf_op jit(solution)/shard_map/widened/pallas_call | solution.py:199
  21.3 6.3 %collective-permute-done.6.refs_5_ = f32[8,16,256]{2,1,0:T(8,128)S(1)} collective-permute-done((f32[8,16,256]{2,1,0:T(8,128)S(1)}, f32[8,16,256]{2,1,0:T(8,128)S(1)}, u32[]{:S(2)}, u32[]{:S(2)}) %collective-permute-start.6) | collective-permute-done | bytes 131104 | tf_op jit(solution)/shard_map/ppermute | solution.py:46
  28.5 1.0 %collective-permute-start.8 = (f32[16,16,256]{2,1,0:T(8,128)S(1)}, f32[16,16,256]{2,1,0:T(8,128)S(1)}, u32[]{:S(2)}, u32[]{:S(2)}) collective-permute-start(f32[16,16,256]{2,1,0:T(8,128)S(1)} %get-tuple-element.43), channel_id=1, source_target_pairs={{0,4},{2,6},{4,0},{6,2},{8,12},{10,14},{12,8},{14,10},{16,20},{18,... | collective-permute-start | bytes 786440 | tf_op jit(solution)/shard_map/ppermute | solution.py:46
  29.5 1.2 %collective-permute-start.10 = (f32[16,16,256]{2,1,0:T(8,128)S(1)}, f32[16,16,256]{2,1,0:T(8,128)S(1)}, u32[]{:S(2)}, u32[]{:S(2)}) collective-permute-start(f32[16,16,256]{2,1,0:T(8,128)S(1)} %get-tuple-element.42), channel_id=1, source_target_pairs={{0,2},{2,0},{4,6},{6,4},{8,10},{10,8},{12,14},{14,12},{16,18},{18,... | collective-permute-start | bytes 786440 | tf_op jit(solution)/shard_map/ppermute | solution.py:46
  30.7 1.1 %collective-permute-start.11 = (f32[11,16,256]{2,1,0:T(8,128)S(1)}, f32[11,16,256]{2,1,0:T(8,128)S(1)}, u32[]{:S(2)}, u32[]{:S(2)}) collective-permute-start(f32[11,16,256]{2,1,0:T(8,128)S(1)} %collective-permute-done.4.refs_5_), channel_id=1, source_target_pairs={{0,4},{2,6},{4,0},{6,2},{8,12},{10,14},{12,8},{14,10},{16,20},{18,... | collective-permute-start | bytes 540680 | tf_op jit(solution)/shard_map/ppermute | solution.py:46
  32.6 4.2 %collective-permute-done.8.refs_11_ = f32[16,16,256]{2,1,0:T(8,128)S(1)} collective-permute-done((f32[16,16,256]{2,1,0:T(8,128)S(1)}, f32[16,16,256]{2,1,0:T(8,128)S(1)}, u32[]{:S(2)}, u32[]{:S(2)}) %collective-permute-start.8) | collective-permute-done | bytes 262176 | tf_op jit(solution)/shard_map/ppermute | solution.py:46
  38.7 1.2 %collective-permute-done.11.second_ref.refs_12_ = f32[11,16,256]{2,1,0:T(8,128)S(1)} collective-permute-done((f32[11,16,256]{2,1,0:T(8,128)S(1)}, f32[11,16,256]{2,1,0:T(8,128)S(1)}, u32[]{:S(2)}, u32[]{:S(2)}) %collective-permute-start.11) | collective-permute-done | bytes 180256 | tf_op jit(solution)/shard_map/ppermute | solution.py:46
  40.8 1.2 %collective-permute-start.18 = (f32[28,16,256]{2,1,0:T(8,128)S(1)}, f32[28,16,256]{2,1,0:T(8,128)S(1)}, u32[]{:S(2)}, u32[]{:S(2)}) collective-permute-start(f32[28,16,256]{2,1,0:T(8,128)S(1)} %get-tuple-element.31), channel_id=1, source_target_pairs={{0,2},{2,0},{4,6},{6,4},{8,10},{10,8},{12,14},{14,12},{16,18},{18,... | collective-permute-start | bytes 1376264 | tf_op jit(solution)/shard_map/ppermute | solution.py:46
  42.0 1.6 %collective-permute-start.19 = (f32[27,16,256]{2,1,0:T(8,128)S(1)}, f32[27,16,256]{2,1,0:T(8,128)S(1)}, u32[]{:S(2)}, u32[]{:S(2)}) collective-permute-start(f32[27,16,256]{2,1,0:T(8,128)S(1)} %get-tuple-element.32), channel_id=1, source_target_pairs={{0,4},{2,6},{4,0},{6,2},{8,12},{10,14},{12,8},{14,10},{16,20},{18,... | collective-permute-start | bytes 1327112 | tf_op jit(solution)/shard_map/ppermute | solution.py:46
  43.6 5.0 %solve.1 = (f32[1024,256]{1,0:T(8,128)S(1)}, f32[1024,256]{1,0:T(8,128)S(1)}, f32[344,256]{1,0:T(8,128)S(1)}, f32[344,256]{1,0:T(8,128)S(1)}, f32[336,256]{1,0:T(8,128)S(1)}) custom-call(f32[16,256]{1,0:T(8,128)S(1)} %get-tuple-element.22.refs_0_, f32[1024,256]{1,0:T(8,128)S(1)} %copy-done, f32[19,16,256]{2,1,0:T(8,128)S(1)} %copy-done.1, ...), custom_call_target="tpu_custom_call" | custom-call | flops 2147483648 | bytes 262144 | tf_op jit(solution)/shard_map/solve/pallas_call | solution.py:302
  49.2 1.0 %collective-permute-done.19.refs_14_ = f32[27,16,256]{2,1,0:T(8,128)S(1)} collective-permute-done((f32[27,16,256]{2,1,0:T(8,128)S(1)}, f32[27,16,256]{2,1,0:T(8,128)S(1)}, u32[]{:S(2)}, u32[]{:S(2)}) %collective-permute-start.19) | collective-permute-done | bytes 442400 | tf_op jit(solution)/shard_map/ppermute | solution.py:46
  50.3 1.0 %collective-permute-start.20 = (f32[11,16,256]{2,1,0:T(8,128)S(1)}, f32[11,16,256]{2,1,0:T(8,128)S(1)}, u32[]{:S(2)}, u32[]{:S(2)}) collective-permute-start(f32[11,16,256]{2,1,0:T(8,128)S(1)} %slice.38), channel_id=1, source_target_pairs={{0,2},{2,0},{4,6},{6,4},{8,10},{10,8},{12,14},{14,12},{16,18},{18,... | collective-permute-start | bytes 540680 | tf_op jit(solution)/shard_map/ppermute | solution.py:46
  51.3 1.6 %collective-permute-start.21 = (f32[11,16,256]{2,1,0:T(8,128)S(1)}, f32[11,16,256]{2,1,0:T(8,128)S(1)}, u32[]{:S(2)}, u32[]{:S(2)}) collective-permute-start(f32[11,16,256]{2,1,0:T(8,128)S(1)} %slice.39), channel_id=1, source_target_pairs={{0,4},{2,6},{4,0},{6,2},{8,12},{10,14},{12,8},{14,10},{16,20},{18,... | collective-permute-start | bytes 540680 | tf_op jit(solution)/shard_map/ppermute | solution.py:46
  52.9 1.8 %finish.1 = (f32[1024,256]{1,0:T(8,128)}, bf16[1536,256]{1,0:T(8,128)(2,1)S(1)}, bf16[1536,256]{1,0:T(8,128)(2,1)S(1)}) custom-call(f32[1024,256]{1,0:T(8,128)S(1)} %get-tuple-element.34.sol_ref, f32[1024,256]{1,0:T(8,128)S(1)} %get-tuple-element.35.part_ref, f32[344,256]{1,0:T(8,128)S(1)} %get-tuple-element.36.refs_0_, ...), custom_call_target="tpu_custom_call" | custom-call | flops 100663296 | bytes 262144 | tf_op jit(solution)/shard_map/finish/pallas_call | solution.py:359
  54.6 2.3 %residual.1.refs_4_ = f32[1024,256]{1,0:T(8,128)} custom-call(f32[16,768]{1,0:T(8,128)S(1)} %get-tuple-element.27.refs_0_, f32[1024,256]{1,0:T(8,128)S(1)} %copy-done, bf16[1536,256]{1,0:T(8,128)(2,1)S(1)} %get-tuple-element.40.refs_2_, bf16[1536,256]{1,0:T(8,128)(2,1)S(1)} %get-tuple-element.41.refs_3_, f32[19,16,256]{2,1,0:T(8,128)S(1)} %copy-done.1, ...), custom_call_target="tpu_custom_call" | custom-call | flops 1056964608 | bytes 5505024 | tf_op jit(solution)/shard_map/residual/pallas_call | solution.py:433
  56.9 1.6 %residual_rest.1 = f32[1024,256]{1,0:T(8,128)} custom-call(f32[16,768]{1,0:T(8,128)S(1)} %get-tuple-element.27.refs_0_, f32[1024,256]{1,0:T(8,128)S(1)} %copy-done, bf16[1536,256]{1,0:T(8,128)(2,1)S(1)} %get-tuple-element.40.refs_2_, bf16[1536,256]{1,0:T(8,128)(2,1)S(1)} %get-tuple-element.41.refs_3_, ...), custom_call_target="tpu_custom_call", output_to_operand_aliasing={{}: (4, {})} | custom-call | flops 150994944 | bytes 786432 | tf_op jit(solution)/shard_map/residual_rest/pallas_call | solution.py:433
  (49 shorter events, 6.7 us)
Async XLA Ops:
  2.5 10.5 %collective-permute-start.2 = (f32[19,16,256]{2,1,0:T(8,128)}, f32[19,16,256]{2,1,0:T(8,128)S(1)}, u32[]{:S(2)}, u32[]{:S(2)}) collective-permute-start(f32[19,16,256]{2,1,0:T(8,128)} %get-tuple-element.25.refs_2_.refs_4_), channel_id=1, source_target_pairs={{0,4},{2,6},{4,0},{6,2},{8,12},{10,14},{12,8},{14,10},{16,20},{18,... | collective-permute-start | bytes 933896 | tf_op jit(solution)/shard_map/ppermute | solution.py:46
  5.5 11.8 %collective-permute-start.3 = (f32[19,16,256]{2,1,0:T(8,128)}, f32[19,16,256]{2,1,0:T(8,128)S(1)}, u32[]{:S(2)}, u32[]{:S(2)}) collective-permute-start(f32[19,16,256]{2,1,0:T(8,128)} %get-tuple-element.25.refs_2_.refs_4_), channel_id=1, source_target_pairs={{0,2},{2,0},{4,6},{6,4},{8,10},{10,8},{12,14},{14,12},{16,18},{18,... | collective-permute-start | bytes 933896 | tf_op jit(solution)/shard_map/ppermute | solution.py:46
  7.0 8.2 %collective-permute-start = (f32[8,16,256]{2,1,0:T(8,128)}, f32[8,16,256]{2,1,0:T(8,128)S(1)}, u32[]{:S(2)}, u32[]{:S(2)}) collective-permute-start(f32[8,16,256]{2,1,0:T(8,128)} %get-tuple-element.24), channel_id=1, source_target_pairs={{0,24},{2,26},{4,28},{6,30},{8,16},{10,18},{12,20},{14,22},{16,8},... | collective-permute-start | bytes 393224 | tf_op jit(solution)/shard_map/ppermute | solution.py:46
  10.6 6.1 %collective-permute-start.1 = (f32[8,16,256]{2,1,0:T(8,128)}, f32[8,16,256]{2,1,0:T(8,128)S(1)}, u32[]{:S(2)}, u32[]{:S(2)}) collective-permute-start(f32[8,16,256]{2,1,0:T(8,128)} %get-tuple-element.24), channel_id=1, source_target_pairs={{0,8},{2,10},{4,12},{6,14},{8,0},{10,2},{12,4},{14,6},{16,24},{18,... | collective-permute-start | bytes 393224 | tf_op jit(solution)/shard_map/ppermute | solution.py:46
  16.6 11.8 %collective-permute-start.7 = (f32[26,16,256]{2,1,0:T(8,128)S(1)}, f32[26,16,256]{2,1,0:T(8,128)S(1)}, u32[]{:S(2)}, u32[]{:S(2)}) collective-permute-start(f32[26,16,256]{2,1,0:T(8,128)S(1)} %pad_maximum_fusion), channel_id=1, source_target_pairs={{0,2},{2,0},{4,6},{6,4},{8,10},{10,8},{12,14},{14,12},{16,18},{18,... | collective-permute-start | bytes 1277960 | tf_op jit(solution)/shard_map/ppermute | solution.py:46
  17.3 11.1 %collective-permute-start.9 = (f32[25,16,256]{2,1,0:T(8,128)S(1)}, f32[25,16,256]{2,1,0:T(8,128)S(1)}, u32[]{:S(2)}, u32[]{:S(2)}) collective-permute-start(f32[25,16,256]{2,1,0:T(8,128)S(1)} %pad_maximum_fusion.1), channel_id=1, source_target_pairs={{0,4},{2,6},{4,0},{6,2},{8,12},{10,14},{12,8},{14,10},{16,20},{18,... | collective-permute-start | bytes 1228808 | tf_op jit(solution)/shard_map/ppermute | solution.py:46
  18.2 9.4 %collective-permute-start.4 = (f32[11,16,256]{2,1,0:T(8,128)S(1)}, f32[11,16,256]{2,1,0:T(8,128)S(1)}, u32[]{:S(2)}, u32[]{:S(2)}) collective-permute-start(f32[11,16,256]{2,1,0:T(8,128)S(1)} %copy-done.4), channel_id=1, source_target_pairs={{0,24},{2,26},{4,28},{6,30},{8,16},{10,18},{12,20},{14,22},{16,8},... | collective-permute-start | bytes 540680 | tf_op jit(solution)/shard_map/ppermute | solution.py:46
  20.3 7.2 %collective-permute-start.6 = (f32[8,16,256]{2,1,0:T(8,128)S(1)}, f32[8,16,256]{2,1,0:T(8,128)S(1)}, u32[]{:S(2)}, u32[]{:S(2)}) collective-permute-start(f32[8,16,256]{2,1,0:T(8,128)S(1)} %collective-permute-done.refs_3_), channel_id=1, source_target_pairs={{0,8},{2,10},{4,12},{6,14},{8,0},{10,2},{12,4},{14,6},{16,24},{18,... | collective-permute-start | bytes 393224 | tf_op jit(solution)/shard_map/ppermute | solution.py:46
  27.6 13.1 %collective-permute-start.12 = (f32[22,16,256]{2,1,0:T(8,128)S(1)}, f32[22,16,256]{2,1,0:T(8,128)S(1)}, u32[]{:S(2)}, u32[]{:S(2)}) collective-permute-start(f32[22,16,256]{2,1,0:T(8,128)S(1)} %pad_maximum_fusion.2), channel_id=1, source_target_pairs={{0,8},{2,10},{4,12},{6,14},{8,0},{10,2},{12,4},{14,6},{16,24},{18,... | collective-permute-start | bytes 1081352 | tf_op jit(solution)/shard_map/ppermute | solution.py:46
  28.4 15.1 %copy-start = (f32[1024,256]{1,0:T(8,128)S(1)}, f32[1024,256]{1,0:T(8,128)}, u32[]{:S(2)}) copy-start(f32[1024,256]{1,0:T(8,128)} %refs_1_.6) | copy-start | bytes 3145732
  28.5 8.3 %collective-permute-start.8 = (f32[16,16,256]{2,1,0:T(8,128)S(1)}, f32[16,16,256]{2,1,0:T(8,128)S(1)}, u32[]{:S(2)}, u32[]{:S(2)}) collective-permute-start(f32[16,16,256]{2,1,0:T(8,128)S(1)} %get-tuple-element.43), channel_id=1, source_target_pairs={{0,4},{2,6},{4,0},{6,2},{8,12},{10,14},{12,8},{14,10},{16,20},{18,... | collective-permute-start | bytes 786440 | tf_op jit(solution)/shard_map/ppermute | solution.py:46
  29.5 8.2 %collective-permute-start.10 = (f32[16,16,256]{2,1,0:T(8,128)S(1)}, f32[16,16,256]{2,1,0:T(8,128)S(1)}, u32[]{:S(2)}, u32[]{:S(2)}) collective-permute-start(f32[16,16,256]{2,1,0:T(8,128)S(1)} %get-tuple-element.42), channel_id=1, source_target_pairs={{0,2},{2,0},{4,6},{6,4},{8,10},{10,8},{12,14},{14,12},{16,18},{18,... | collective-permute-start | bytes 786440 | tf_op jit(solution)/shard_map/ppermute | solution.py:46
  30.7 9.1 %collective-permute-start.11 = (f32[11,16,256]{2,1,0:T(8,128)S(1)}, f32[11,16,256]{2,1,0:T(8,128)S(1)}, u32[]{:S(2)}, u32[]{:S(2)}) collective-permute-start(f32[11,16,256]{2,1,0:T(8,128)S(1)} %collective-permute-done.4.refs_5_), channel_id=1, source_target_pairs={{0,4},{2,6},{4,0},{6,2},{8,12},{10,14},{12,8},{14,10},{16,20},{18,... | collective-permute-start | bytes 540680 | tf_op jit(solution)/shard_map/ppermute | solution.py:46
  31.8 8.9 %collective-permute-start.5 = (f32[11,16,256]{2,1,0:T(8,128)S(1)}, f32[11,16,256]{2,1,0:T(8,128)S(1)}, u32[]{:S(2)}, u32[]{:S(2)}) collective-permute-start(f32[11,16,256]{2,1,0:T(8,128)S(1)} %collective-permute-done.4.refs_5_), channel_id=1, source_target_pairs={{0,2},{2,0},{4,6},{6,4},{8,10},{10,8},{12,14},{14,12},{16,18},{18,... | collective-permute-start | bytes 540680 | tf_op jit(solution)/shard_map/ppermute | solution.py:46
  36.9 6.7 %collective-permute-start.13 = (f32[4,16,256]{2,1,0:T(8,128)S(1)}, f32[4,16,256]{2,1,0:T(8,128)S(1)}, u32[]{:S(2)}, u32[]{:S(2)}) collective-permute-start(f32[4,16,256]{2,1,0:T(8,128)S(1)} %slice.35), channel_id=1, source_target_pairs={{0,2},{2,0},{4,6},{6,4},{8,10},{10,8},{12,14},{14,12},{16,18},{18,... | collective-permute-start | bytes 196616 | tf_op jit(solution)/shard_map/ppermute | solution.py:46
  37.8 5.8 %copy-start.1 = (f32[19,16,256]{2,1,0:T(8,128)S(1)}, f32[19,16,256]{2,1,0:T(8,128)}, u32[]{:S(2)}) copy-start(f32[19,16,256]{2,1,0:T(8,128)} %get-tuple-element.25.refs_2_.refs_4_) | copy-start | bytes 933892
  37.8 5.8 %collective-permute-start.14 = (f32[4,16,256]{2,1,0:T(8,128)S(1)}, f32[4,16,256]{2,1,0:T(8,128)S(1)}, u32[]{:S(2)}, u32[]{:S(2)}) collective-permute-start(f32[4,16,256]{2,1,0:T(8,128)S(1)} %slice.37), channel_id=1, source_target_pairs={{0,4},{2,6},{4,0},{6,2},{8,12},{10,14},{12,8},{14,10},{16,20},{18,... | collective-permute-start | bytes 196616 | tf_op jit(solution)/shard_map/ppermute | solution.py:46
  40.8 10.5 %collective-permute-start.18 = (f32[28,16,256]{2,1,0:T(8,128)S(1)}, f32[28,16,256]{2,1,0:T(8,128)S(1)}, u32[]{:S(2)}, u32[]{:S(2)}) collective-permute-start(f32[28,16,256]{2,1,0:T(8,128)S(1)} %get-tuple-element.31), channel_id=1, source_target_pairs={{0,2},{2,0},{4,6},{6,4},{8,10},{10,8},{12,14},{14,12},{16,18},{18,... | collective-permute-start | bytes 1376264 | tf_op jit(solution)/shard_map/ppermute | solution.py:46
  42.0 8.3 %collective-permute-start.19 = (f32[27,16,256]{2,1,0:T(8,128)S(1)}, f32[27,16,256]{2,1,0:T(8,128)S(1)}, u32[]{:S(2)}, u32[]{:S(2)}) collective-permute-start(f32[27,16,256]{2,1,0:T(8,128)S(1)} %get-tuple-element.32), channel_id=1, source_target_pairs={{0,4},{2,6},{4,0},{6,2},{8,12},{10,14},{12,8},{14,10},{16,20},{18,... | collective-permute-start | bytes 1327112 | tf_op jit(solution)/shard_map/ppermute | solution.py:46
  48.6 4.3 %collective-permute-start.15 = (f32[344,256]{1,0:T(8,128)S(1)}, f32[344,256]{1,0:T(8,128)S(1)}, u32[]{:S(2)}, u32[]{:S(2)}) collective-permute-start(f32[344,256]{1,0:T(8,128)S(1)} %get-tuple-element.36.refs_0_), channel_id=1, source_target_pairs={{0,1},{1,0},{2,3},{3,2},{4,5},{5,4},{6,7},{7,6},{8,9},{9,8},{10,11... | collective-permute-start | bytes 1056776 | tf_op jit(solution)/shard_map/ppermute | solution.py:483
  48.7 4.2 %collective-permute-start.16 = (f32[344,256]{1,0:T(8,128)S(1)}, f32[344,256]{1,0:T(8,128)S(1)}, u32[]{:S(2)}, u32[]{:S(2)}) collective-permute-start(f32[344,256]{1,0:T(8,128)S(1)} %get-tuple-element.37.refs_1_), channel_id=1, source_target_pairs={{0,1},{1,0},{2,3},{3,2},{4,5},{5,4},{6,7},{7,6},{8,9},{9,8},{10,11... | collective-permute-start | bytes 1056776 | tf_op jit(solution)/shard_map/ppermute | solution.py:483
  49.2 3.7 %collective-permute-start.17 = (f32[336,256]{1,0:T(8,128)S(1)}, f32[336,256]{1,0:T(8,128)S(1)}, u32[]{:S(2)}, u32[]{:S(2)}) collective-permute-start(f32[336,256]{1,0:T(8,128)S(1)} %get-tuple-element.38.refs_2_), channel_id=1, source_target_pairs={{0,1},{1,0},{2,3},{3,2},{4,5},{5,4},{6,7},{7,6},{8,9},{9,8},{10,11... | collective-permute-start | bytes 1032200 | tf_op jit(solution)/shard_map/ppermute | solution.py:483
  50.3 6.6 %collective-permute-start.20 = (f32[11,16,256]{2,1,0:T(8,128)S(1)}, f32[11,16,256]{2,1,0:T(8,128)S(1)}, u32[]{:S(2)}, u32[]{:S(2)}) collective-permute-start(f32[11,16,256]{2,1,0:T(8,128)S(1)} %slice.38), channel_id=1, source_target_pairs={{0,2},{2,0},{4,6},{6,4},{8,10},{10,8},{12,14},{14,12},{16,18},{18,... | collective-permute-start | bytes 540680 | tf_op jit(solution)/shard_map/ppermute | solution.py:46
  51.3 5.7 %collective-permute-start.21 = (f32[11,16,256]{2,1,0:T(8,128)S(1)}, f32[11,16,256]{2,1,0:T(8,128)S(1)}, u32[]{:S(2)}, u32[]{:S(2)}) collective-permute-start(f32[11,16,256]{2,1,0:T(8,128)S(1)} %slice.39), channel_id=1, source_target_pairs={{0,4},{2,6},{4,0},{6,2},{8,12},{10,14},{12,8},{14,10},{16,20},{18,... | collective-permute-start | bytes 540680 | tf_op jit(solution)/shard_map/ppermute | solution.py:46
  (3 other events, 7.0 us)
